TPU v7x, 128 devices: a whole 4x4x4 slice. The times are simulated.
128 devices in a mesh: dp: 8 (over y, x_hi), ctx: 16 (over x_lo, z, core).
Axes of the slice: x: 4 (x_hi: 2, x_lo: 2; x = x_hi * 2 + x_lo), y: 4, z: 4, core: 2. Of those that a mesh axis runs over, the one named last changes fastest.
Arguments:
- tokens: bfloat16 [8, 2048, 2048], P('dp', 'ctx'), may hold values from -6 to 6
- segments: int32 [8, 2048], P('dp', 'ctx'), may hold values from 0 to 31, as said below
- cotangent: bfloat16 [8, 2048, 2048], P('dp', 'ctx'), may hold values from -6 to 6
- norm_attn: bfloat16 [2048], P('dp'), may hold values from 0.5 to 1.5
- norm_ffn: bfloat16 [2048], P('dp'), may hold values from 0.5 to 1.5
- wqkv: bfloat16 [2048, 2560], P('dp'), may hold values from -0.125 to 0.125
- wo: bfloat16 [2048, 2048], P('dp'), may hold values from -0.5 to 0.5
- w1: bfloat16 [2048, 5632], P('dp'), may hold values from -0.125 to 0.125
- w3: bfloat16 [2048, 5632], P('dp'), may hold values from -0.125 to 0.125
- w2: bfloat16 [5632, 2048], P('dp'), may hold values from -0.078125 to 0.078125
Outputs:
- output: float32 [8, 2048, 2048], P('dp', 'ctx')
- input_grad: float32 [8, 2048, 2048], P('dp', 'ctx')
- grad_norm_attn: float32 [2048], P('dp')
- grad_norm_ffn: float32 [2048], P('dp')
- grad_wqkv: float32 [2048, 2560], P('dp')
- grad_wo: float32 [2048, 2048], P('dp')
- grad_w1: float32 [2048, 5632], P('dp')
- grad_w3: float32 [2048, 5632], P('dp')
- grad_w2: float32 [5632, 2048], P('dp')
Inputs may be any that keep to these rules, and one draw needn't show every extreme that they name: `segments`: document numbers start at 0 and rise by one at each new document, so a document's tokens are contiguous; every sequence holds all 32 documents.
All inputs are finite; a program needn't handle non-finite values.
Results may differ from a plain program's by a relative error of at most 0.025.
Values may be sent and summed in bfloat16 or wider, within the bound.
A program may use at most 384 MiB of HBM per device.

v0:
```python
from functools import partial

import jax
import jax.numpy as jnp
from jax import lax
from jax.sharding import PartitionSpec as P

HEADS = 32
KV_HEADS = 4
HEAD_DIM = 64
COUNT = 32
QDIM = 2048
KVDIM = 256


EPS = 1e-05
THETA = 10000.0


def entering(x, axis, combine, identity):
    devices, index = (lax.axis_size(axis), lax.axis_index(axis))
    everything = lax.all_gather(x, axis)
    start = jnp.broadcast_to(jnp.asarray(identity, x.dtype), x.shape)

    def lap(k, before):
        reached = k < index
        new = combine(before, everything[k])
        return jnp.where(reached, new, before)

    return lax.fori_loop(0, devices, lap, start)


def rms(v, gain):
    return v * lax.rsqrt(jnp.mean(v * v, axis=-1, keepdims=True) + EPS) * gain


def rms_back(v, gain, grad):
    scale = lax.rsqrt(jnp.mean(v * v, axis=-1, keepdims=True) + EPS)
    unit = v * scale
    gain_grad = jnp.sum(grad * unit, axis=0)
    inner = grad * gain
    return (scale * (inner - unit * jnp.mean(inner * unit, axis=-1, keepdims=True)), gain_grad)


def rotate(v, cosine, sine):
    half = v.shape[-1] // 2
    turned = jnp.concatenate([-v[..., half:], v[..., :half]], axis=-1)
    return v * cosine[:, None, :] + turned * sine[:, None, :]


def rotate_back(w, cosine, sine):
    half = w.shape[-1] // 2
    moved = w * sine[:, None, :]
    turned = jnp.concatenate([moved[..., half:], -moved[..., :half]], axis=-1)
    return w * cosine[:, None, :] + turned


def add_counts(earlier, later):
    return earlier + later


def masked_scores(visible, query_head, key_head):
    raw = jnp.einsum("tgd,sd->gts", query_head, key_head, preferred_element_type=jnp.float32)
    return jnp.where(visible[None], raw * (1.0 / HEAD_DIM**0.5), -1e30)


def head_forward(visible, args):
    query_head, key_head, value_head = args
    scores = masked_scores(visible, query_head, key_head)
    top = jnp.max(scores, axis=-1, keepdims=True)
    summed = jnp.sum(jnp.exp(scores - top), axis=-1, keepdims=True)
    logsum = top + jnp.log(summed)
    probs = jnp.exp(scores - logsum).astype(jnp.bfloat16)
    out = jnp.einsum("gts,sd->tgd", probs, value_head, preferred_element_type=jnp.float32)
    return (out, logsum)


def head_backward(visible, args):
    query_head, key_head, value_head, grad_head, logsum = args
    scale = 1.0 / HEAD_DIM**0.5
    probs = jnp.exp(masked_scores(visible, query_head, key_head) - logsum)
    probs_low = probs.astype(jnp.bfloat16)
    grad_probs = jnp.einsum(
        "tgd,sd->gts", grad_head, value_head, preferred_element_type=jnp.float32
    )
    delta = jnp.sum(probs * grad_probs, axis=-1, keepdims=True)
    grad_scores = (probs * (grad_probs - delta)).astype(jnp.bfloat16)
    grad_query = (
        jnp.einsum("gts,sd->tgd", grad_scores, key_head, preferred_element_type=jnp.float32) * scale
    )
    grad_key = (
        jnp.einsum("gts,tgd->sd", grad_scores, query_head, preferred_element_type=jnp.float32)
        * scale
    )
    grad_value = jnp.einsum("gts,tgd->sd", probs_low, grad_head, preferred_element_type=jnp.float32)
    return (grad_query, grad_key, grad_value)


def body(tokens, segments, cotangent, norm_attn, norm_ffn, wqkv, wo, w1, w3, w2):
    fetched = (
        lax.all_gather(wqkv, "dp", axis=0, tiled=True),
        lax.all_gather(wo, "dp", axis=0, tiled=True),
        lax.all_gather(w1, "dp", axis=0, tiled=True),
        lax.all_gather(w3, "dp", axis=0, tiled=True),
        lax.all_gather(w2, "dp", axis=0, tiled=True),
        lax.all_gather(norm_attn, "dp", axis=0, tiled=True),
        lax.all_gather(norm_ffn, "dp", axis=0, tiled=True),
    )
    full_qkv, full_out, full_gate, full_up, full_down, gain_attn, gain_ffn = fetched
    x_rows = tokens[0].astype(jnp.float32)
    doc_ids = segments[0]
    tok = doc_ids.shape[0]
    group = HEADS // KV_HEADS
    kinds = jnp.arange(COUNT, dtype=jnp.int32)
    member = (doc_ids[:, None] == kinds[None, :]).astype(jnp.int32)
    earlier = entering(jnp.sum(member, axis=0), "ctx", add_counts, jnp.zeros((COUNT,), jnp.int32))
    local = jnp.arange(tok, dtype=jnp.int32)
    same_doc = (doc_ids[:, None] == doc_ids[None, :]) & (local[None, :] < local[:, None])
    place = jnp.sum(same_doc.astype(jnp.int32), axis=1) + jnp.sum(member * earlier[None, :], axis=1)
    global_index = lax.axis_index("ctx") * tok + local
    doc_start = global_index - place
    freq = THETA ** (-jnp.arange(HEAD_DIM // 2, dtype=jnp.float32) * 2.0 / HEAD_DIM)
    angle = place.astype(jnp.float32)[:, None] * freq[None, :]
    cosine = jnp.concatenate([jnp.cos(angle), jnp.cos(angle)], axis=-1)
    sine = jnp.concatenate([jnp.sin(angle), jnp.sin(angle)], axis=-1)
    norm_one = rms(x_rows, gain_attn.astype(jnp.float32)).astype(jnp.bfloat16)
    mixed = jnp.dot(norm_one, full_qkv, preferred_element_type=jnp.float32)
    query = rotate(mixed[:, :QDIM].reshape(tok, HEADS, HEAD_DIM), cosine, sine).astype(jnp.bfloat16)
    key_rows = rotate(mixed[:, QDIM : QDIM + KVDIM].reshape(tok, KV_HEADS, HEAD_DIM), cosine, sine)
    key_rows = key_rows.astype(jnp.bfloat16).reshape(tok, KVDIM)
    value_rows = mixed[:, QDIM + KVDIM :].astype(jnp.bfloat16)
    all_keys, all_values = (
        lax.all_gather(key_rows, "ctx", axis=0, tiled=True),
        lax.all_gather(value_rows, "ctx", axis=0, tiled=True),
    )
    total = all_keys.shape[0]
    key_index = jnp.arange(total, dtype=jnp.int32)
    visible = (key_index[None, :] <= global_index[:, None]) & (
        key_index[None, :] >= doc_start[:, None]
    )
    query_heads = query.reshape(tok, KV_HEADS, group, HEAD_DIM).transpose(1, 0, 2, 3)
    key_heads = all_keys.reshape(total, KV_HEADS, HEAD_DIM).transpose(1, 0, 2)
    value_heads = all_values.reshape(total, KV_HEADS, HEAD_DIM).transpose(1, 0, 2)
    attended, logsum = lax.map(
        partial(head_forward, visible), (query_heads, key_heads, value_heads)
    )
    heads_out = attended.transpose(1, 0, 2, 3).reshape(tok, QDIM).astype(jnp.bfloat16)
    resid = x_rows + jnp.dot(heads_out, full_out, preferred_element_type=jnp.float32)
    norm_two = rms(resid, gain_ffn.astype(jnp.float32)).astype(jnp.bfloat16)
    gate = jnp.dot(norm_two, full_gate, preferred_element_type=jnp.float32)
    up = jnp.dot(norm_two, full_up, preferred_element_type=jnp.float32)
    hidden = (jax.nn.silu(gate) * up).astype(jnp.bfloat16)
    result = resid + jnp.dot(hidden, full_down, preferred_element_type=jnp.float32)
    fetched = (
        lax.all_gather(wqkv, "dp", axis=0, tiled=True),
        lax.all_gather(wo, "dp", axis=0, tiled=True),
        lax.all_gather(w1, "dp", axis=0, tiled=True),
        lax.all_gather(w3, "dp", axis=0, tiled=True),
        lax.all_gather(w2, "dp", axis=0, tiled=True),
        lax.all_gather(norm_attn, "dp", axis=0, tiled=True),
        lax.all_gather(norm_ffn, "dp", axis=0, tiled=True),
    )
    full_qkv, full_out, full_gate, full_up, full_down, gain_attn, gain_ffn = fetched
    grad_out = cotangent[0]
    grad_hidden = jnp.einsum("td,fd->tf", grad_out, full_down, preferred_element_type=jnp.float32)
    sigma = jax.nn.sigmoid(gate)
    grad_gate = (grad_hidden * up * sigma * (1.0 + gate * (1.0 - sigma))).astype(jnp.bfloat16)
    grad_up = (grad_hidden * gate * sigma).astype(jnp.bfloat16)
    grad_norm_two = jnp.einsum(
        "tf,df->td", grad_gate, full_gate, preferred_element_type=jnp.float32
    )
    grad_norm_two = grad_norm_two + jnp.einsum(
        "tf,df->td", grad_up, full_up, preferred_element_type=jnp.float32
    )
    back_two, gain_two_grad = rms_back(resid, gain_ffn.astype(jnp.float32), grad_norm_two)
    grad_resid = grad_out.astype(jnp.float32) + back_two
    resid_low = grad_resid.astype(jnp.bfloat16)
    grad_heads = jnp.einsum(
        "td,qd->tq", resid_low, full_out, preferred_element_type=jnp.float32
    ).astype(jnp.bfloat16)
    grad_heads_split = grad_heads.reshape(tok, KV_HEADS, group, HEAD_DIM).transpose(1, 0, 2, 3)
    grad_query, key_part, value_part = lax.map(
        partial(head_backward, visible),
        (query_heads, key_heads, value_heads, grad_heads_split, logsum),
    )
    key_part = key_part.transpose(1, 0, 2).reshape(total, KVDIM)
    value_part = value_part.transpose(1, 0, 2).reshape(total, KVDIM)
    key_grad, value_grad = (
        lax.psum_scatter(
            key_part.astype(jnp.bfloat16), "ctx", scatter_dimension=0, tiled=True
        ).astype(jnp.float32),
        lax.psum_scatter(
            value_part.astype(jnp.bfloat16), "ctx", scatter_dimension=0, tiled=True
        ).astype(jnp.float32),
    )
    grad_query = grad_query.transpose(1, 0, 2, 3).reshape(tok, HEADS, HEAD_DIM)
    query_pre = rotate_back(grad_query, cosine, sine).reshape(tok, QDIM)
    key_pre = rotate_back(key_grad.reshape(tok, KV_HEADS, HEAD_DIM), cosine, sine).reshape(
        tok, KVDIM
    )
    grad_mixed = jnp.concatenate([query_pre, key_pre, value_grad], axis=1).astype(jnp.bfloat16)
    grad_norm_one = jnp.einsum(
        "tc,dc->td", grad_mixed, full_qkv, preferred_element_type=jnp.float32
    )
    back_one, gain_one_grad = rms_back(x_rows, gain_attn.astype(jnp.float32), grad_norm_one)
    grad_in = grad_resid + back_one
    qkv_term = jnp.einsum("td,tc->dc", norm_one, grad_mixed, preferred_element_type=jnp.float32)
    out_term = jnp.einsum("tq,td->qd", heads_out, resid_low, preferred_element_type=jnp.float32)
    gate_both = jnp.concatenate([grad_gate, grad_up], axis=1)
    qkv_piece, out_piece, attn_gain, ffn_gain = (
        lax.psum_scatter(
            qkv_term.astype(jnp.bfloat16), "dp", scatter_dimension=0, tiled=True
        ).astype(jnp.float32),
        lax.psum_scatter(
            out_term.astype(jnp.bfloat16), "dp", scatter_dimension=0, tiled=True
        ).astype(jnp.float32),
        lax.psum_scatter(
            gain_one_grad.astype(jnp.bfloat16), "dp", scatter_dimension=0, tiled=True
        ).astype(jnp.float32),
        lax.psum_scatter(
            gain_two_grad.astype(jnp.bfloat16), "dp", scatter_dimension=0, tiled=True
        ).astype(jnp.float32),
    )
    rows = norm_two
    gate_piece = lax.psum_scatter(
        jnp.einsum("tr,tc->rc", rows, gate_both, preferred_element_type=jnp.float32).astype(
            jnp.bfloat16
        ),
        "dp",
        scatter_dimension=0,
        tiled=True,
    )
    rows = hidden
    down_piece = lax.psum_scatter(
        jnp.einsum("tr,td->rd", rows, grad_out, preferred_element_type=jnp.float32).astype(
            jnp.bfloat16
        ),
        "dp",
        scatter_dimension=0,
        tiled=True,
    )
    summed = (
        lax.psum(qkv_piece.astype(jnp.bfloat16), "ctx").astype(jnp.float32),
        lax.psum(out_piece.astype(jnp.bfloat16), "ctx").astype(jnp.float32),
        lax.psum(attn_gain.astype(jnp.bfloat16), "ctx").astype(jnp.float32),
        lax.psum(ffn_gain.astype(jnp.bfloat16), "ctx").astype(jnp.float32),
        lax.psum(gate_piece, "ctx").astype(jnp.float32),
        lax.psum(down_piece, "ctx").astype(jnp.float32),
    )
    qkv_grad, out_grad, attn_gain_grad, ffn_gain_grad, gate_up_grad, down_grad = summed
    half_cols = gate_up_grad.shape[1] // 2
    return (
        result[None],
        grad_in[None],
        attn_gain_grad,
        ffn_gain_grad,
        qkv_grad,
        out_grad,
        gate_up_grad[:, :half_cols],
        gate_up_grad[:, half_cols:],
        down_grad,
    )


def solution(mesh):
    return jax.shard_map(
        body,
        mesh=mesh,
        in_specs=(
            P("dp", "ctx", None),
            P("dp", "ctx"),
            P("dp", "ctx", None),
            P("dp"),
            P("dp"),
            P("dp", None),
            P("dp", None),
            P("dp", None),
            P("dp", None),
            P("dp", None),
        ),
        out_specs=(
            P("dp", "ctx", None),
            P("dp", "ctx", None),
            P("dp"),
            P("dp"),
            P("dp", None),
            P("dp", None),
            P("dp", None),
            P("dp", None),
            P("dp", None),
        ),
        check_vma=False,
    )
```

profile of v0, /device:TPU:1, one launch (start us, length us, event | category | flops | bytes accessed | tf_op | source)
XLA Modules:
  0.0 2415.3 jit_solution(4199943283030216873)
XLA Ops:
  8.6 20.7 all-gather.1
  32.2 14.8 all-reduce
  48.4 90.7 %all-gather.11.cloned.1.call-done = bf16[2048,2560]{1,0:T(8,128)(2,1)} async-done(((bf16[256,2560]{1,0:T(8,128)(2,1)}), bf16[2048,2560]{1,0:T(8,128)(2,1)}) %all-gather.11.cloned.1.call-update) | async-done | bytes 10485776 | tf_op jit(solution)/shard_map/all_gather | solution.py:101
  150.4 15.2 all-gather.2
  179.2 32.6 %all-gather.15.cloned.1.call-done = bf16[2048,256]{1,0:T(8,128)(2,1)} async-done(((bf16[128,256]{1,0:T(8,128)(2,1)}), bf16[2048,256]{1,0:T(8,128)(2,1)}) %all-gather.15.cloned.1.call-update) | async-done | bytes 1048592 | tf_op jit(solution)/shard_map/all_gather | solution.py:133
  213.4 27.6 %while.45 = (s32[]{:T(128)}, bf16[4,128,8,64]{1,3,2,0:T(8,128)(2,1)S(1)}, f32[4,8,128,1]{2,1,3,0:T(8,128)}, bf16[4,2048,64]{1,2,0:T(8,128)(2,1)}, bf16[4,2048,64...) while((s32[]{:T(128)}, ...), condition=%wide.region_9.10_spmd.clone.clone, body=%wide.region_6.9_spmd.clone.sunk.clone | while | flops 560724992 | bytes 27167840 | solution.py:144
  241.0 79.3 %all-gather.17.cloned.1.call-done = bf16[2048,2048]{1,0:T(8,128)(2,1)} async-done(((bf16[256,2048]{1,0:T(8,128)(2,1)}), bf16[2048,2048]{1,0:T(8,128)(2,1)}) %all-gather.17.cloned.1.call-update) | async-done | bytes 8388624 | tf_op jit(solution)/shard_map/all_gather | solution.py:102
  325.2 234.6 %all-gather.19.cloned.1.call-done = bf16[2048,5632]{1,0:T(8,128)(2,1)} async-done(((bf16[256,5632]{1,0:T(8,128)(2,1)}), bf16[2048,5632]{1,0:T(8,128)(2,1)}) %all-gather.19.cloned.1.call-update) | async-done | bytes 23068688 | tf_op jit(solution)/shard_map/all_gather | solution.py:103
  572.2 227.1 %all-gather.21.cloned.1.call-done = bf16[2048,5632]{1,0:T(8,128)(2,1)} async-done(((bf16[256,5632]{1,0:T(8,128)(2,1)}), bf16[2048,5632]{1,0:T(8,128)(2,1)}) %all-gather.21.cloned.1.call-update) | async-done | bytes 23068688 | tf_op jit(solution)/shard_map/all_gather | solution.py:104
  811.7 227.3 %all-gather.23.cloned.1.call-done = bf16[5632,2048]{1,0:T(8,128)(2,1)} async-done(((bf16[704,2048]{1,0:T(8,128)(2,1)}), bf16[5632,2048]{1,0:T(8,128)(2,1)}) %all-gather.23.cloned.1.call-update) | async-done | bytes 23068688 | tf_op jit(solution)/shard_map/all_gather | solution.py:105
  1039.0 15.2 multiply_convert_fusion
  1054.1 23.7 fusion.105
  1077.9 13.8 multiply_reduce_fusion
  1099.8 62.7 %while.46 = (s32[]{:T(128)}, f32[4,128,8,64]{1,3,2,0:T(8,128)}, bf16[4,2048,64]{1,2,0:T(8,128)(2,1)}, bf16[4,2048,64]{1,2,0:T(8,128)(2,1)}, bf16[4,2048,64]{1,2,...) while((s32[]{:T(128)}, f32[4,128,8,64]{1,3,2,0:T(8,128)}, ...), condition=%wide.region_14.15_spmd.clone.clone, body=%wide.region_12.14_spmd.clone.sunk.clone | while | flops 1374616576 | bytes 83396840 | solution.py:182
  1174.6 46.4 %reduce-scatter.19.cloned.1.call-done = bf16[128,256]{1,0:T(8,128)(2,1)} async-done(((bf16[2048,256]{1,0:T(8,128)(2,1)}), bf16[128,256]{1,0:T(8,128)(2,1)}) %reduce-scatter.19.cloned.1.call-update) | async-done | bytes 65552
  1222.1 62.2 %reduce-scatter.21.cloned.1.call-done = bf16[128,256]{1,0:T(8,128)(2,1)} async-done(((bf16[2048,256]{1,0:T(8,128)(2,1)}), bf16[128,256]{1,0:T(8,128)(2,1)}) %reduce-scatter.21.cloned.1.call-update) | async-done | bytes 65552
  1306.9 20.7 convolution_convert_fusion
  1327.9 76.2 %reduce-scatter.15.cloned.1.call-done = bf16[256,2048]{1,0:T(8,128)(2,1)} async-done(((bf16[2048,2048]{1,0:T(8,128)(2,1)}), bf16[256,2048]{1,0:T(8,128)(2,1)}) %reduce-scatter.15.cloned.1.call-update) | async-done | bytes 1048592 | tf_op jit(solution)/shard_map/reduce_scatter | solution.py:214
  1404.1 134.6 %reduce-scatter.13.cloned.1.call-done = bf16[256,2560]{1,0:T(8,128)(2,1)} async-done(((bf16[2048,2560]{1,0:T(8,128)(2,1)}), bf16[256,2560]{1,0:T(8,128)(2,1)}) %reduce-scatter.13.cloned.1.call-update) | async-done | bytes 1310736 | tf_op jit(solution)/shard_map/reduce_scatter | solution.py:211
  1538.6 246.1 %reduce-scatter.17.cloned.1.call-done = bf16[704,2048]{1,0:T(8,128)(2,1)} async-done(((bf16[5632,2048]{1,0:T(8,128)(2,1)}), bf16[704,2048]{1,0:T(8,128)(2,1)}) %reduce-scatter.17.cloned.1.call-update) | async-done | bytes 2883600 | tf_op jit(solution)/shard_map/reduce_scatter | solution.py:234
  1784.7 453.4 %reduce-scatter.23.cloned.1.call-done = bf16[256,11264]{1,0:T(8,128)(2,1)} async-done(((bf16[2048,11264]{1,0:T(8,128)(2,1)}), bf16[256,11264]{1,0:T(8,128)(2,1)}) %reduce-scatter.23.cloned.1.call-update) | async-done | bytes 5767184
  2259.3 20.5 all-reduce.6
  2279.9 32.3 %all-reduce.4 = (bf16[256]{0:T(256)(128)(2,1)S(1)}, bf16[256]{0:T(256)(128)(2,1)S(1)}) all-reduce(bf16[256]{0:T(256)(128)(2,1)S(1)} %dynamic-slice.2, bf16[256]{0:T(256)(128)(2,1)S(1)} %dynamic-slice.4), channel_id=1, replica_groups=mesh['dp'=8,'ctx'=16] {'ctx'}, use_global_device_ids=true, to_apply=%region_20.21 | all-reduce | flops 512 | bytes 2048 | tf_op jit(solution)/shard_map/psum | solution.py:245
  2314.7 78.2 %all-reduce.9.cloned.1.call-done = (bf16[256,2560]{1,0:T(8,128)(2,1)}, bf16[256,2048]{1,0:T(8,128)(2,1)}, bf16[256,11264]{1,0:T(8,128)(2,1)}, bf16[704,2048]{1,0:T(8,128)(2,1)}) async-done(((bf16[256,2560]{1,0:T(8,128)(2,1)}, bf16[256,2048]{1,0:T(8,128)(2,1)}, bf16[256,11264]{1,0:T(8,128)(2,1)}, bf16[704,2048]{1,0:T(8,128)(2,1)}), (bf16[256,2560]{1,0:T(8,128)(2,1)}, bf16[256,2048]{1,0:T(8,128)(2,1)}, ...) | async-done | bytes 11010064 | tf_op jit(solution)/shard_map/psum | solution.py:243
  (270 shorter events, 233.0 us)
Async XLA Ops:
  7.2 131.9 %all-gather.11.cloned.1.call-start = ((), (), s32[]{:S(2)}) async-start(), calls=%async_computation.6 | async-start | bytes 11796480 | tf_op jit(solution)/shard_map/all_gather | solution.py:101
  7.9 169.1 %all-gather.13.cloned.1.call-start = ((), (), s32[]{:S(2)}) async-start(), calls=%async_computation.7 | async-start | bytes 1114112 | tf_op jit(solution)/shard_map/all_gather | solution.py:134
  29.3 115.6 %copy-start.25 = (f32[8,1,256]{2,1,0:T(1,128)}, f32[8,1,256]{2,1,0:T(1,128)S(1)}, u32[]{:S(2)}) copy-start(f32[8,1,256]{2,1,0:T(1,128)S(1)} %convert_element_type.185) | copy-start | bytes 24580
  145.6 66.3 %all-gather.15.cloned.1.call-start = ((), (), s32[]{:S(2)}) async-start(), calls=%async_computation.8 | async-start | bytes 1114112 | tf_op jit(solution)/shard_map/all_gather | solution.py:133
  147.8 172.4 %all-gather.17.cloned.1.call-start = ((), (), s32[]{:S(2)}) async-start(), calls=%async_computation.9 | async-start | bytes 9437184 | tf_op jit(solution)/shard_map/all_gather | solution.py:102
  148.4 411.4 %all-gather.19.cloned.1.call-start = ((), (), s32[]{:S(2)}) async-start(), calls=%async_computation.10 | async-start | bytes 25952256 | tf_op jit(solution)/shard_map/all_gather | solution.py:103
  149.0 650.3 %all-gather.21.cloned.1.call-start = ((), (), s32[]{:S(2)}) async-start(), calls=%async_computation.11 | async-start | bytes 25952256 | tf_op jit(solution)/shard_map/all_gather | solution.py:104
  149.6 889.4 %all-gather.23.cloned.1.call-start = ((), (), s32[]{:S(2)}) async-start(), calls=%async_computation.12 | async-start | bytes 25952256 | tf_op jit(solution)/shard_map/all_gather | solution.py:105
  150.3 1070.8 %reduce-scatter.19.cloned.1.call-start = ((), (), s32[]{:S(2)}) async-start(), calls=%async_computation.16 | async-start | bytes 1114112
  325.0 766.7 %copy-start = (f32[128,2048]{1,0:T(8,128)}, f32[128,2048]{1,0:T(8,128)S(1)}, u32[]{:S(2)}) copy-start(f32[128,2048]{1,0:T(8,128)S(1)} %get-tuple-element.329) | copy-start | bytes 3145732
  325.1 247.1 %copy-start.30 = (f32[128]{0:T(128)}, f32[128]{0:T(128)S(1)}, u32[]{:S(2)}) copy-start(f32[128]{0:T(128)S(1)} %add_rsqrt_fusion) | copy-start | bytes 1540
  325.2 474.1 %copy-start.9 = (bf16[128,2048]{1,0:T(8,128)(2,1)}, bf16[128,2048]{1,0:T(8,128)(2,1)S(1)}, u32[]{:S(2)}) copy-start(bf16[128,2048]{1,0:T(8,128)(2,1)S(1)} %multiply_convert_fusion.3) | copy-start | bytes 1572868
  1164.8 119.5 %reduce-scatter.21.cloned.1.call-start = ((), (), s32[]{:S(2)}) async-start(), calls=%async_computation.17 | async-start | bytes 1114112
  1167.1 236.9 %reduce-scatter.15.cloned.1.call-start = ((), (), s32[]{:S(2)}) async-start(), calls=%async_computation.14 | async-start | bytes 9437184 | tf_op jit(solution)/shard_map/reduce_scatter | solution.py:214
  1172.7 112.5 %copy-start.4 = (bf16[1,128,2048]{2,1,0:T(8,128)(2,1)S(1)}, bf16[1,128,2048]{2,1,0:T(8,128)(2,1)}, u32[]{:S(2)}) copy-start(bf16[1,128,2048]{2,1,0:T(8,128)(2,1)} %param.16) | copy-start | bytes 1572868
  1172.7 112.5 %copy-start.26 = (f32[8,1,256]{2,1,0:T(1,128)S(1)}, f32[8,1,256]{2,1,0:T(1,128)}, u32[]{:S(2)}) copy-start(f32[8,1,256]{2,1,0:T(1,128)} %copy-done.25) | copy-start | bytes 24580
  1172.8 112.5 %copy-start.29 = (f32[128]{0:T(128)S(1)}, f32[128]{0:T(128)}, u32[]{:S(2)}) copy-start(f32[128]{0:T(128)} %copy-done.28) | copy-start | bytes 1540
  1172.8 365.9 %reduce-scatter.13.cloned.1.call-start = ((), (), s32[]{:S(2)}) async-start(), calls=%async_computation.13 | async-start | bytes 11796480 | tf_op jit(solution)/shard_map/reduce_scatter | solution.py:211
  1174.6 110.6 %copy-start.15 = (bf16[128,2048]{0,1:T(8,128)(2,1)}, bf16[128,2048]{0,1:T(8,128)(2,1)S(1)}, u32[]{:S(2)}) copy-start(bf16[128,2048]{0,1:T(8,128)(2,1)S(1)} %fusion.84) | copy-start | bytes 1572868
  1292.2 492.5 %reduce-scatter.17.cloned.1.call-start = ((), (), s32[]{:S(2)}) async-start(), calls=%async_computation.15 | async-start | bytes 25952256 | tf_op jit(solution)/shard_map/reduce_scatter | solution.py:234
  1305.9 932.2 %reduce-scatter.23.cloned.1.call-start = ((), (), s32[]{:S(2)}) async-start(), calls=%async_computation.18 | async-start | bytes 51904512
  1327.6 910.5 %copy-start.34 = (u32[128]{0:T(128)S(1)}, u32[128]{0:T(128)}, u32[]{:S(2)}) copy-start(u32[128]{0:T(128)} %constant.112) | copy-start | bytes 1540
  1327.6 911.8 %copy-start.1 = (f32[128,2048]{1,0:T(8,128)S(1)}, f32[128,2048]{1,0:T(8,128)}, u32[]{:S(2)}) copy-start(f32[128,2048]{1,0:T(8,128)} %copy-done) | copy-start | bytes 3145732
  1327.6 1065.4 %all-reduce.9.cloned.1.call-start = ((), (), s32[]{:S(2)}) async-start(), calls=%async_computation.19 | async-start | bytes 22020096 | tf_op jit(solution)/shard_map/psum | solution.py:243
  (37 other events, 633.2 us)
Sparse Core Ops, SparseCore 0:
  10.3 128.7 all-gather.10
  145.7 31.2 all-gather.12
  179.3 32.5 all-gather.14
  214.1 106.1 all-gather.16
  322.4 237.3 all-gather.18
  561.9 237.3 all-gather.20
  801.6 237.3 all-gather.22
  1164.9 56.1 reduce-scatter.18
  1224.2 60.0 reduce-scatter.20
  1288.0 116.0 reduce-scatter.14
  1408.4 130.1 reduce-scatter.12
  1543.0 241.6 reduce-scatter.16
  1789.2 448.8 reduce-scatter.22
  2240.7 152.2 all-reduce.8
where the time goes:
time: 2420 us
  waiting for transfers between devices  2000 us (83%)
  matrix products  222 us (9%)
  blocking collectives  104 us (4%)
  other arithmetic  39.5 us (2%)
  local copies, waits for them, and re-layouts  29.5 us (1%)
    unnamed x17, waiting for transfers between devices  565 us
    reduce_scatter x1, waiting for transfers between devices, body(): lax.psum_scatter(jnp.einsum('tr,td->rd', rows, grad_out, preferred_elemen...  246 us
    all_gather x1, waiting for transfers between devices, body(): lax.all_gather(w1, 'dp', axis=0, tiled=True)  235 us
    all_gather x1, waiting for transfers between devices, body(): lax.all_gather(w2, 'dp', axis=0, tiled=True)  227 us
    all_gather x1, waiting for transfers between devices, body(): lax.all_gather(w3, 'dp', axis=0, tiled=True)  227 us
    reduce_scatter x1, waiting for transfers between devices, body(): lax.psum_scatter(qkv_term.astype(jnp.bfloat16), 'dp', scatter_dimension=0...  135 us
    all_gather x1, waiting for transfers between devices, body(): lax.all_gather(wqkv, 'dp', axis=0, tiled=True)  90.7 us
    all_gather x1, waiting for transfers between devices, body(): lax.all_gather(wo, 'dp', axis=0, tiled=True)  79.3 us
  transfers between devices with their start and end apart: 14, of which 14 were waited for; matrix products, arithmetic and copies ran while one was open for 6% of the time, Pallas kernels for 0%

commit v1 on v0

v1 whole, which is shorter than its diff:
```python
import functools

import jax
import jax.numpy as jnp
from jax import lax
from jax.experimental import pallas as pl
from jax.experimental.pallas import tpu as pltpu
from jax.sharding import PartitionSpec as P

D = 2048
HEAD_DIM = 64
TOK = 128
RING = 4
QDIM = 2048
KVDIM = 256
GROUP = 8
QZ = 512
MZ = 640
FZ = 1408
SPLIT = 2048
EPS = 1e-05
THETA = 10000.0
MESH = pl.DeviceIdType.MESH
VMEM_LIMIT = 56 << 20
BF = jnp.bfloat16
F32 = jnp.float32
ANY = pl.BlockSpec(memory_space=pl.ANY)
VMEM = pl.BlockSpec(memory_space=pltpu.VMEM)


def coords():
    dp, ctx = lax.axis_index("dp"), lax.axis_index("ctx")
    y, xh = dp // 2, dp % 2
    xl, z, c = ctx // 8, (ctx // 2) % 4, ctx % 2
    return dict(y=y, x=xh * 2 + xl, xh=xh, xl=xl, z=z, c=c)


def device(q, **change):
    r = {k: change.get(k, q[k]) for k in ("y", "x", "z", "c")}
    return (r["y"] * 2 + r["x"] // 2, (r["x"] % 2) * 8 + r["z"] * 2 + r["c"])


def ring(q, axis):
    return [device(q, **{axis: (q[axis] + s) % 4}) for s in (1, 3, 2)]


def shift_pairs(axis, by):
    size = 2 if axis == "c" else 4
    pairs = []
    for y in range(4):
        for x in range(4):
            for z in range(4):
                for c in range(2):
                    q = dict(y=y, x=x, z=z, c=c)
                    pairs.append((device(q), device(q, **{axis: (q[axis] + by) % size})))
    return [(a[0] * 16 + a[1], b[0] * 16 + b[1]) for a, b in pairs]


def swap_pairs():
    pairs = []
    for y in range(4):
        for x in range(4):
            for z in range(4):
                for c in range(2):
                    q = dict(y=y, x=x, z=z, c=c)
                    pairs.append((device(q), device(q, y=z, z=y)))
    return [(a[0] * 16 + a[1], b[0] * 16 + b[1]) for a, b in pairs]


def move(v, axis, by):
    return lax.ppermute(v, ("dp", "ctx"), shift_pairs(axis, by))


class Copies:
    def __init__(self, send_sems, recv_sems):
        self.send_sems, self.recv_sems, self.n, self.open = send_sems, recv_sems, 0, []

    def send(self, src, dst, to):
        cp = pltpu.make_async_remote_copy(
            src_ref=src,
            dst_ref=dst,
            send_sem=self.send_sems.at[self.n],
            recv_sem=self.recv_sems.at[self.n],
            device_id=to,
            device_id_type=MESH,
        )
        cp.start()
        self.n += 1
        self.open.append(cp.wait_send)
        return cp

    def local(self, src, dst):
        cp = pltpu.make_async_copy(src, dst, self.send_sems.at[self.n])
        cp.start()
        self.n += 1
        return cp

    def close(self):
        for wait in self.open:
            wait()


def greet(targets):
    barrier = pltpu.get_barrier_semaphore()
    for to in targets:
        pl.semaphore_signal(barrier, inc=1, device_id=to, device_id_type=MESH)
    pl.semaphore_wait(barrier, len(targets))


def cost(us):
    return pl.CostEstimate(flops=int(us * 1e9), bytes_accessed=0, transcendentals=0)


def talk(kernel, name, cid, us, copies, ins, outs, scratch=(), near=()):
    return pl.pallas_call(
        kernel,
        name=name,
        out_shape=[jax.ShapeDtypeStruct(s, t) for s, t in outs],
        in_specs=[VMEM if i in near else ANY for i in range(len(ins))],
        out_specs=[ANY] * len(outs),
        scratch_shapes=[
            *scratch,
            pltpu.SemaphoreType.DMA((copies,)),
            pltpu.SemaphoreType.DMA((copies,)),
        ],
        cost_estimate=cost(us),
        compiler_params=pltpu.CompilerParams(
            collective_id=cid, has_side_effects=True, vmem_limit_bytes=VMEM_LIMIT
        ),
    )(*ins)


def fetch_kernel(
    x, seg, gn, wq, wo, w1, w3, w2, X, SEG, GN, WQ, WO, A1, A3, AX, AY, T2, TO, QP, P1, P3, ss, rs
):
    q = coords()
    y, xx, xh, xl, z, c = q["y"], q["x"], q["xh"], q["xl"], q["z"], q["c"]
    zs, ys, xs = ring(q, "z"), ring(q, "y"), ring(q, "x")
    mate = device(q, c=1 - c)
    other = device(q, x=xx ^ 1)
    other_mate = device(q, x=xx ^ 1, c=1 - c)
    swap = device(q, y=z, z=y)
    k = Copies(ss, rs)
    rows = pl.ds(pl.multiple_of(128 * c + 64 * xl, 64), 64)
    qcols = pl.ds(pl.multiple_of(MZ * z, 128), MZ)
    fcols = pl.ds(pl.multiple_of(FZ * z, 128), FZ)
    loads = [
        k.local(wq.at[rows, qcols], QP),
        k.local(w1.at[rows, fcols], P1),
        k.local(w3.at[rows, fcols], P3),
    ]
    barrier = pltpu.get_barrier_semaphore()
    greeted = zs + ys + xs + [mate, other_mate]
    for to in greeted:
        pl.semaphore_signal(barrier, inc=1, device_id=to, device_id_type=MESH)

    @pl.when(y != z)
    def _():
        pl.semaphore_signal(barrier, inc=1, device_id=swap, device_id_type=MESH)

    pl.semaphore_wait(barrier, len(greeted) + (y != z).astype(jnp.int32))
    piece = pl.ds(pl.multiple_of(128 * (c * 8 + z * 2 + xl), 128), 128)
    turned = []
    for src, dst in ((wo, TO), (w2, T2)):
        n = k.n
        k.n += 1
        remote = pltpu.make_async_remote_copy(
            src_ref=src.at[:, piece],
            dst_ref=dst,
            send_sem=ss.at[n],
            recv_sem=rs.at[n],
            device_id=swap,
            device_id_type=MESH,
        )
        here = pltpu.make_async_copy(src.at[:, piece], dst, ss.at[n])

        @pl.when(y != z)
        def _(remote=remote):
            remote.start()

        @pl.when(y == z)
        def _(here=here):
            here.start()

        turned.append((remote, here))
    for cp in loads:
        cp.wait()
    top, low = pl.ds(0, 32), pl.ds(32, 32)
    q_top = [k.send(QP.at[top], WQ.at[c, y, xh, xl, top], to) for to in xs]
    q_low = [k.send(QP.at[low], WQ.at[c, y, xh, xl, low], to) for to in ys]
    q_here = k.local(QP, WQ.at[c, y, xh, xl])
    seg_z = [k.send(seg, SEG.at[xl, z, c], to) for to in zs]
    seg_here = k.local(seg, SEG.at[xl, z, c])
    gn_y = [k.send(gn, GN.at[y, xh], to) for to in ys]
    gn_here = k.local(gn, GN.at[y, xh])
    x_z = [k.send(x, X.at[z], to) for to in zs]
    x_here = k.local(x, X.at[z])
    q_here.wait()
    for cp in q_top:
        cp.wait_recv()
    part = WQ.at[c, y, :, :, top]
    q2 = [k.send(part, part, to) for to in ys]
    for cp in q_low:
        cp.wait_recv()
    part = WQ.at[c, :, xh, xl, low]
    q2 += [k.send(part, part, to) for to in xs]
    for remote, here in turned:

        @pl.when(y != z)
        def _(remote=remote):
            remote.wait_recv()
            remote.wait_send()

        @pl.when(y == z)
        def _(here=here):
            here.wait()

    ocol = pl.ds(pl.multiple_of(128 * (c * 8 + y * 2 + xl), 128), 128)
    o1 = [k.send(TO, WO.at[xh, :, ocol], to) for to in xs]
    o1_here = k.local(TO, WO.at[xh, :, ocol])
    a1 = [k.send(P1, A1.at[xh, xl], to) for to in xs]
    a1_here = k.local(P1, A1.at[xh, xl])
    a3 = [k.send(P3, A3.at[y], to) for to in ys]
    a3_here = k.local(P3, A3.at[y])
    t_top, t_low = pl.ds(0, 352), pl.ds(352, 352)
    ax = [k.send(T2.at[t_top], AX.at[xh, xl], to) for to in xs]
    ax_here = k.local(T2.at[t_top], AX.at[xh, xl])
    ay = [k.send(T2.at[t_low], AY.at[y], to) for to in ys]
    ay_here = k.local(T2.at[t_low], AY.at[y])
    for cp in seg_z:
        cp.wait_recv()
    seg_here.wait()
    part = SEG.at[xl, :, c]
    seg2 = [k.send(part, part, to) for to in (mate, other, other_mate)]
    for cp in gn_y:
        cp.wait_recv()
    gn_here.wait()
    gn2 = k.send(GN.at[:, xh], GN.at[:, xh], device(q, x=3 - xx))
    for cp in o1:
        cp.wait_recv()
    o1_here.wait()
    part = WO.at[:, :, pl.ds(pl.multiple_of(128 * (c * 8 + y * 2), 256), 256)]
    o2 = [k.send(part, part, to) for to in ys]
    for cp in q2:
        cp.wait_recv()
    q3 = k.send(WQ.at[c], WQ.at[c], mate)
    for cp in o2:
        cp.wait_recv()
    part = WO.at[:, :, pl.ds(pl.multiple_of(1024 * c, 1024), 1024)]
    o3 = k.send(part, part, mate)
    for cp in x_z + a1 + a3 + ax + ay + seg2 + [gn2, q3, o3]:
        cp.wait_recv()
    for cp in (x_here, a1_here, a3_here, ax_here, ay_here):
        cp.wait()
    k.close()


def kv_kernel(kv, KV, ss, rs):
    q = coords()
    xx, xl, c = q["x"], q["xl"], q["c"]
    mate = device(q, c=1 - c)
    other = device(q, x=xx ^ 1)
    greet([mate, other])
    k = Copies(ss, rs)
    here = k.local(kv, KV.at[xl, :, c])
    near = k.send(kv, KV.at[xl, :, c], mate)
    far = pltpu.make_async_remote_copy(
        src_ref=kv,
        dst_ref=KV.at[0, :, c],
        send_sem=ss.at[2],
        recv_sem=rs.at[2],
        device_id=other,
        device_id_type=MESH,
    )
    on = pltpu.make_async_remote_copy(
        src_ref=KV.at[0, :, c],
        dst_ref=KV.at[0, :, c],
        send_sem=ss.at[3],
        recv_sem=rs.at[3],
        device_id=mate,
        device_id_type=MESH,
    )

    @pl.when(xl == 0)
    def _():
        far.start()
        far.wait_send()

    @pl.when(xl == 1)
    def _():
        far.wait_recv()
        on.start()
        on.wait_recv()
        on.wait_send()

    here.wait()
    near.wait_recv()
    k.close()


def gather_kernel(v, V, ss, rs):
    q = coords()
    zs = ring(q, "z")
    greet(zs)
    k = Copies(ss, rs)
    sent = [k.send(v, V.at[q["z"]], to) for to in zs]
    here = k.local(v, V.at[q["z"]])
    for cp in sent:
        cp.wait_recv()
    here.wait()
    k.close()


def assemble_kernel(*refs):
    n2, g = refs[0], refs[1:5]
    a1, a3, ax, ay = refs[5:9], refs[9:13], refs[13:17], refs[17:21]
    N2, G, W13, W2, gb, b1, b3, bx, by, ss, rs = refs[21:]
    q = coords()
    y, xx, z, c = q["y"], q["x"], q["z"], q["c"]
    zs = ring(q, "z")
    mate = device(q, c=1 - c)
    k = Copies(ss, rs)
    bufs = ((a1, b1), (a3, b3), (ax, bx), (ay, by), (g, gb))
    loads = [[k.local(refs[j], buf.at[j]) for refs, buf in bufs] for j in range(4)]
    greet(zs + [mate])
    sent = [k.send(n2, N2.at[z], to) for to in zs]
    heres = [k.local(n2, N2.at[z])]
    for j, step in enumerate((0, 3, 1, 2)):
        yy, x2 = (y + step) % 4, (xx + step) % 4
        xh, xl = x2 // 2, x2 % 2
        for cp in loads[j]:
            cp.wait()
        heres.append(k.local(gb.at[j], G.at[(z + step) % 4]))
        places = [
            (b1.at[j], W13.at[c, yy, :, :, :, pl.ds(0, FZ)]),
            (b3.at[j], W13.at[c, :, xh, xl, :, pl.ds(FZ, FZ)]),
        ]
        for b in range(2):
            cols = pl.ds(pl.multiple_of(128 * (c * 8 + yy * 2 + b), 128), 128)
            places.append((bx.at[j, :, b], W2.at[:, pl.ds(0, 352), cols]))
        for b in range(4):
            cols = pl.ds(pl.multiple_of(128 * (c * 8 + b * 2 + xl), 128), 128)
            places.append((by.at[j, b], W2.at[xh, pl.ds(352, 352), cols]))
        for src, dst in places:
            sent.append(k.send(src, dst, mate))
            heres.append(k.local(src, dst))
    for cp in sent:
        cp.wait_recv()
    for cp in heres:
        cp.wait()
    k.close()


def dkv_kernel(dkv, R, ss, rs):
    q = coords()
    xx, xl, c = q["x"], q["xl"], q["c"]
    mate = device(q, c=1 - c)
    other = device(q, x=xx ^ 1)
    other_mate = device(q, x=xx ^ 1, c=1 - c)
    greet([mate, other, other_mate])
    k = Copies(ss, rs)
    near = k.send(dkv.at[xl, :, 1 - c], R.at[0], mate)
    far = [
        pltpu.make_async_remote_copy(
            src_ref=dkv.at[0, :, cc],
            dst_ref=R.at[1 + i],
            send_sem=ss.at[1 + i],
            recv_sem=rs.at[1 + i],
            device_id=to,
            device_id_type=MESH,
        )
        for i, (to, cc) in enumerate(((other, c), (other_mate, 1 - c)))
    ]

    @pl.when(xl == 1)
    def _():
        for cp in far:
            cp.start()
        for cp in far:
            cp.wait_send()

    @pl.when(xl == 0)
    def _():
        for cp in far:
            cp.wait_recv()

    near.wait_recv()
    k.close()


def spread_kernel(
    fa, fb, f2, fo, fq, gain, G1, G3, G2, GO, GQ, gain_out, s0, s1, s2, s3, s4, total, ss, rs
):
    q = coords()
    y, xx, xh, xl, z, c = q["y"], q["x"], q["xh"], q["xl"], q["z"], q["c"]
    zs, ys = ring(q, "z"), ring(q, "y")
    mate, other, cross = device(q, c=1 - c), device(q, x=xx ^ 1), device(q, x=3 - xx)
    greet(zs + ys + [mate, other, cross])
    k = Copies(ss, rs)
    gain_y = [k.send(gain.at[(y + s) % 4], s0.at[y], to) for s, to in zip((1, 3, 2), ys)]
    gain_here = k.local(gain.at[y], s0.at[y])
    rows = pl.ds(pl.multiple_of(128 * c + 64 * xl, 64), 64)
    pair = pl.ds(pl.multiple_of(128 * c, 128), 128)
    fz = FZ * z
    rest = SPLIT - FZ
    wide = [
        (fa.at[:, pl.ds(0, FZ)], G1.at[rows, pl.ds(pl.multiple_of(fz, 128), FZ)]),
        (fa.at[:, pl.ds(FZ, rest)], G3.at[rows, pl.ds(pl.multiple_of(fz, 128), rest)]),
        (fb, G3.at[rows, pl.ds(pl.multiple_of(fz + rest, 128), FZ - rest)]),
    ]
    leg_z = [k.send(src, dst, to) for src, dst in wide for to in zs]
    heres = [k.local(src, dst) for src, dst in wide]
    col = pl.ds(pl.multiple_of(128 * (c * 8 + z * 2 + xl), 128), 128)
    cols = pl.ds(pl.multiple_of(128 * (c * 8 + z * 2), 256), 256)
    half = pl.ds(pl.multiple_of(1024 * c, 1024), 1024)
    mq = pl.ds(pl.multiple_of(MZ * z, 128), MZ)
    tall = [(f2, G2.at[:, col]), (fo, GO.at[:, col]), (fq, GQ.at[rows, mq])]
    leg_x = [k.send(src, dst, other) for src, dst in tall]
    tall_here = [k.local(src, dst) for src, dst in tall]
    for cp in leg_x:
        cp.wait_recv()
    for cp in tall_here:
        cp.wait()
    parts = [G2.at[:, cols], GO.at[:, cols], GQ.at[pair, mq]]
    leg_xz = [k.send(part, part, to) for part in parts for to in zs]
    for cp in gain_y:
        cp.wait_recv()
    gain_here.wait()
    s1[0] = s0[0] + s0[1] + s0[2] + s0[3]
    cp = k.send(s1.at[0, 1 - xh], s1.at[1, 0], cross)
    cp.wait_recv()
    s2[z] = s1[0, xh] + s1[1, 0]
    gain_z = [k.send(s2.at[z], s2.at[z], to) for to in zs]
    for cp in gain_z:
        cp.wait_recv()
    s3[0] = s2[0] + s2[1] + s2[2] + s2[3]
    cp = k.send(s3.at[0], s3.at[1], other)
    cp.wait_recv()
    s4[0] = s3[0] + s3[1]
    cp = k.send(s4.at[0], s4.at[1], mate)
    cp.wait_recv()
    total[...] = s4[0] + s4[1]
    gain_done = k.local(total, gain_out)
    for cp in leg_z:
        cp.wait_recv()
    for cp in heres:
        cp.wait()
    leg_zx = [k.send(ref.at[rows], ref.at[rows], other) for ref in (G1, G3)]
    for cp in leg_xz:
        cp.wait_recv()
    parts = [G2.at[:, half], GO.at[:, half], GQ.at[pair]]
    last = [k.send(part, part, mate) for part in parts]
    for cp in leg_zx:
        cp.wait_recv()
    last += [k.send(ref.at[pair], ref.at[pair], mate) for ref in (G1, G3)]
    for cp in last:
        cp.wait_recv()
    gain_done.wait()
    k.close()


PARAMS = pltpu.CompilerParams(vmem_limit_bytes=VMEM_LIMIT)


def to_pieces(v):
    return jnp.concatenate(
        [v[:, 256 * d + 128 * c : 256 * d + 128 * c + 128] for c in range(2) for d in range(8)],
        axis=1,
    )


def from_pieces(v):
    return jnp.concatenate(
        [v[:, 1024 * c + 128 * d : 1024 * c + 128 * d + 128] for d in range(8) for c in range(2)],
        axis=1,
    )


def swapped(u):
    lane = lax.broadcasted_iota(jnp.int32, u.shape, 1)
    return jnp.where(lane % 64 < 32, pltpu.roll(u, 96, 1), pltpu.roll(u, 32, 1))


def project_kernel(x, gain, w, cosine, sine, n1, query, kv):
    xv = x[0].astype(F32)
    scale = lax.rsqrt(jnp.mean(xv * xv, axis=-1, keepdims=True) + EPS)
    normed = to_pieces((xv * scale * gain[...]).astype(BF))
    n1[0] = normed
    cos, sin = cosine[0], sine[0]
    for j in range(5):
        u = jnp.dot(normed, w[:, 128 * j : 128 * j + 128], preferred_element_type=F32)
        turned = u * cos + swapped(u) * sin
        if j < 4:
            query[0, :, 128 * j : 128 * j + 128] = turned.astype(BF)
        else:
            lane = lax.broadcasted_iota(jnp.int32, u.shape, 1)
            kv[0] = jnp.where(lane < HEAD_DIM, turned, u).astype(BF)


def project(x, gain, w, cosine, sine):
    chunk = lambda cols: pl.BlockSpec((1, TOK, cols), lambda i: (i, 0, 0))
    whole = lambda shape: pl.BlockSpec(shape, lambda i: (0,) * len(shape))
    return pl.pallas_call(
        project_kernel,
        name="project",
        cost_estimate=cost(7),
        grid=(RING,),
        in_specs=[chunk(D), whole((1, D)), whole((D, MZ)), chunk(128), chunk(128)],
        out_specs=[chunk(D), chunk(QZ), chunk(128)],
        out_shape=[
            jax.ShapeDtypeStruct((RING, TOK, D), BF),
            jax.ShapeDtypeStruct((RING, TOK, QZ), BF),
            jax.ShapeDtypeStruct((RING, TOK, 128), BF),
        ],
        compiler_params=PARAMS,
    )(x, gain, w, cosine, sine)


def stacked_low(tiles):
    out = []
    for pair in range(4):
        tile = tiles[:, 128 * pair : 128 * pair + 128].astype(F32)
        lane = lax.broadcasted_iota(jnp.int32, tile.shape, 1)
        out.append(jnp.where(lane < HEAD_DIM, tile, 0.0))
        out.append(jnp.where(lane < HEAD_DIM, pltpu.roll(tile, 64, 1), 0.0))
    return jnp.concatenate(out, axis=0)


def stacked_high(tiles):
    out = []
    for pair in range(4):
        tile = tiles[:, 128 * pair : 128 * pair + 128].astype(F32)
        lane = lax.broadcasted_iota(jnp.int32, tile.shape, 1)
        out.append(jnp.where(lane >= HEAD_DIM, pltpu.roll(tile, 64, 1), 0.0))
        out.append(jnp.where(lane >= HEAD_DIM, tile, 0.0))
    return jnp.concatenate(out, axis=0)


def unstacked(v):
    tiles = []
    for pair in range(4):
        both = jnp.concatenate(
            [v[:, 256 * pair : 256 * pair + 128], v[:, 256 * pair + 128 : 256 * pair + 256]],
            axis=0,
        )
        tiles.append(both.T)
    return tiles


def nt(a, b):
    return lax.dot_general(a, b, (((1,), (1,)), ((), ())), preferred_element_type=F32)


def tn(a, b):
    return lax.dot_general(a, b, (((0,), (0,)), ((), ())), preferred_element_type=F32)


def chunk_scores(keys, stacked, kc, chunk, start):
    raw = nt(keys, stacked)
    key = kc * TOK + lax.broadcasted_iota(jnp.int32, raw.shape, 0)
    query = chunk * TOK + lax.broadcasted_iota(jnp.int32, raw.shape, 1) % TOK
    return jnp.where((key <= query) & (key >= start), raw, -1e30)


def attend_kernel(info, query, kv, start, out, logsum):
    i = pl.program_id(0)
    low, chunk = info[0, i], info[1, i]
    stacked = (stacked_low(query[0]) * (1.0 / HEAD_DIM**0.5)).astype(BF)
    starts = jnp.concatenate([start[0]] * GROUP, axis=1)

    def step(kc, carry):
        top, summed, total = carry
        keys = kv[kc]
        scores = chunk_scores(keys, stacked, kc, chunk, starts)
        new_top = jnp.maximum(top, jnp.max(scores, axis=0, keepdims=True))
        weights = jnp.exp(scores - new_top)
        fade = jnp.exp(top - new_top)
        summed = summed * fade + jnp.sum(weights, axis=0, keepdims=True)
        part = tn(keys, weights.astype(BF))
        return new_top, summed, total * fade + part[HEAD_DIM:]

    rows = GROUP * TOK
    carry = (jnp.full((1, rows), -1e30, F32), jnp.zeros((1, rows), F32), jnp.zeros((64, rows), F32))
    top, summed, total = lax.fori_loop(low, chunk + 1, step, carry)
    for pair, tile in enumerate(unstacked(total / summed)):
        out[0, :, 128 * pair : 128 * pair + 128] = tile.astype(BF)
    logsum[0] = top + jnp.log(summed)


def attend(info, query, kv, start):
    chunk = lambda r, cols: pl.BlockSpec((1, r, cols), lambda i, s: (i, 0, 0))
    return pl.pallas_call(
        attend_kernel,
        name="attend",
        cost_estimate=cost(12),
        grid_spec=pltpu.PrefetchScalarGridSpec(
            num_scalar_prefetch=1,
            grid=(RING,),
            in_specs=[
                chunk(TOK, QZ),
                pl.BlockSpec((16, TOK, 128), lambda i, s: (0, 0, 0)),
                chunk(1, TOK),
            ],
            out_specs=[chunk(TOK, QZ), chunk(1, GROUP * TOK)],
        ),
        out_shape=[
            jax.ShapeDtypeStruct((RING, TOK, QZ), BF),
            jax.ShapeDtypeStruct((RING, 1, GROUP * TOK), F32),
        ],
        compiler_params=PARAMS,
    )(info, query, kv, start)


def attend_back_kernel(
    info, query, kv, start, out, grad_out, logsum, cosine, sine, dquery, dkv, total
):
    i = pl.program_id(0)
    low, chunk = info[0, i], info[1, i]
    stacked = (stacked_low(query[0]) * (1.0 / HEAD_DIM**0.5)).astype(BF)
    grads = stacked_high(grad_out[0]).astype(BF)
    starts = jnp.concatenate([start[0]] * GROUP, axis=1)
    lse = logsum[0]
    deltas = []
    for pair in range(4):
        cols = slice(128 * pair, 128 * pair + 128)
        prod = (out[0, :, cols].astype(F32) * grad_out[0, :, cols].astype(F32)).T
        deltas.append(jnp.sum(prod[:HEAD_DIM], axis=0, keepdims=True))
        deltas.append(jnp.sum(prod[HEAD_DIM:], axis=0, keepdims=True))
    delta = jnp.concatenate(deltas, axis=1)

    @pl.when(i == 0)
    def _():
        total[...] = jnp.zeros_like(total)

    def step(kc, dq):
        keys = kv[kc]
        scores = chunk_scores(keys, stacked, kc, chunk, starts)
        probs = jnp.exp(scores - lse)
        grad_probs = nt(keys, grads)
        grad_scores = (probs * (grad_probs - delta)).astype(BF)
        total[kc] += jnp.dot(grad_scores, stacked, preferred_element_type=F32) + jnp.dot(
            probs.astype(BF), grads, preferred_element_type=F32
        )
        return dq + tn(keys, grad_scores)[:HEAD_DIM]

    dq = lax.fori_loop(low, chunk + 1, step, jnp.zeros((64, GROUP * TOK), F32))
    cos, sin = cosine[0], sine[0]
    for pair, tile in enumerate(unstacked(dq)):
        tile = tile * (1.0 / HEAD_DIM**0.5)
        dquery[0, :, 128 * pair : 128 * pair + 128] = (tile * cos - swapped(tile) * sin).astype(BF)

    @pl.when(i == RING - 1)
    def _():
        dkv[...] = total[...].astype(BF)


def attend_back(info, query, kv, start, out, grad_out, logsum, cosine, sine):
    chunk = lambda r, cols: pl.BlockSpec((1, r, cols), lambda i, s: (i, 0, 0))
    whole = pl.BlockSpec((16, TOK, 128), lambda i, s: (0, 0, 0))
    return pl.pallas_call(
        attend_back_kernel,
        name="attend_back",
        cost_estimate=cost(15),
        grid_spec=pltpu.PrefetchScalarGridSpec(
            num_scalar_prefetch=1,
            grid=(RING,),
            in_specs=[
                chunk(TOK, QZ),
                whole,
                chunk(1, TOK),
                chunk(TOK, QZ),
                chunk(TOK, QZ),
                chunk(1, GROUP * TOK),
                chunk(TOK, 128),
                chunk(TOK, 128),
            ],
            out_specs=[chunk(TOK, QZ), whole],
            scratch_shapes=[pltpu.VMEM((16, TOK, 128), F32)],
        ),
        out_shape=[
            jax.ShapeDtypeStruct((RING, TOK, QZ), BF),
            jax.ShapeDtypeStruct((16, TOK, 128), BF),
        ],
        compiler_params=PARAMS,
    )(info, query, kv, start, out, grad_out, logsum, cosine, sine)


def dmixed_kernel(xl, dkv, received, cosine, sine, out):
    t = dkv[...].astype(F32) + received[0].astype(F32)
    far = received[1].astype(F32) + received[2].astype(F32)
    t = jnp.where(xl[0] == 0, t + far, t)
    for i in range(RING):
        w = t[i]
        lane = lax.broadcasted_iota(jnp.int32, w.shape, 1)
        out[i] = jnp.where(lane < HEAD_DIM, w * cosine[i] - swapped(w) * sine[i], w).astype(BF)


def dmixed_kv(xl, dkv, received, cosine, sine):
    vmem = pl.BlockSpec(memory_space=pltpu.VMEM)
    return pl.pallas_call(
        dmixed_kernel,
        name="dmixed_kv",
        cost_estimate=cost(2),
        in_specs=[pl.BlockSpec(memory_space=pltpu.SMEM)] + [vmem] * 4,
        out_specs=vmem,
        out_shape=jax.ShapeDtypeStruct((RING, TOK, 128), BF),
        compiler_params=PARAMS,
    )(xl, dkv, received, cosine, sine)


def resid_kernel(x, a, b, c, d, gain, h, n2):
    total = x[...].astype(F32) + (
        (a[...].astype(F32) + b[...].astype(F32)) + (c[...].astype(F32) + d[...].astype(F32))
    )
    h[...] = total
    scale = lax.rsqrt(jnp.mean(total * total, axis=-1, keepdims=True) + EPS)
    n2[...] = to_pieces((total * scale * gain[...]).astype(BF))


def resid(x, parts, gain):
    return pl.pallas_call(
        resid_kernel,
        name="resid",
        cost_estimate=cost(3),
        out_shape=[jax.ShapeDtypeStruct((TOK, D), F32), jax.ShapeDtypeStruct((TOK, D), BF)],
        compiler_params=PARAMS,
    )(x, *parts, gain)


def rms_back(v, gain, grad):
    scale = lax.rsqrt(jnp.mean(v * v, axis=-1, keepdims=True) + EPS)
    unit = v * scale
    gain_grad = jnp.sum(grad * unit, axis=0, keepdims=True)
    inner = grad * gain
    return scale * (inner - unit * jnp.mean(inner * unit, axis=-1, keepdims=True)), gain_grad


def norm_back_kernel(v, base, a, b, c, d, gain, grad, *outs):
    dn = from_pieces(
        (a[...].astype(F32) + b[...].astype(F32)) + (c[...].astype(F32) + d[...].astype(F32))
    )
    back, gain_grad = rms_back(v[...].astype(F32), gain[...], dn)
    total = base[...].astype(F32) + back
    grad[...] = total
    outs[-1][...] = gain_grad
    if len(outs) == 2:
        outs[0][...] = total.astype(BF)


def norm_back(v, base, parts, gain, rounded):
    shapes = [jax.ShapeDtypeStruct((TOK, D), F32)]
    if rounded:
        shapes.append(jax.ShapeDtypeStruct((TOK, D), BF))
    shapes.append(jax.ShapeDtypeStruct((1, D), F32))
    return pl.pallas_call(
        norm_back_kernel,
        name="norm_back",
        cost_estimate=cost(4),
        out_shape=shapes,
        compiler_params=PARAMS,
    )(v, base, *parts, gain)


def pick(v, index, axis=0):
    return lax.dynamic_index_in_dim(v, index, axis, keepdims=False)


def scatter(v, q, axis, dim):
    at = q[axis]
    got = [move(pick(v, (at + s) % 4, dim), axis, s) for s in (1, 3, 2)]
    return [pick(v, at, dim)] + got


def add(parts):
    a, b, c, d = (p.astype(F32) for p in parts)
    return ((a + b) + (c + d)).astype(BF)


def scatter_cols(v, q, axis, width):
    at = q[axis]
    cut = lambda j: lax.dynamic_slice_in_dim(v, j * width, width, 1)
    return [cut(at)] + [move(cut((at + s) % 4), axis, s) for s in (1, 3, 2)]


def scatter_quarters(v, q, rows):
    cut = lambda j: lax.dynamic_slice(v, ((j // 2) * rows, (j % 2) * 128), (rows, 128))
    at = q["x"]
    return [cut(at)] + [move(cut((at + s) % 4), "x", s) for s in (1, 3, 2)]


def dot(a, b):
    return jnp.dot(a, b, preferred_element_type=F32)


def body(tokens, segments, cotangent, norm_attn, norm_ffn, wqkv, wo, w1, w3, w2):
    q = coords()
    y, xx, xl, z, c = q["y"], q["x"], q["xl"], q["z"], q["c"]
    x = tokens[0]
    g = cotangent[0]
    seg = jnp.broadcast_to(segments, (8, TOK))
    gn = jnp.concatenate(
        [jnp.broadcast_to(v[None], (16, 256)) for v in (norm_attn, norm_ffn)], axis=0
    )
    heads = wqkv[:, :QDIM].reshape(256, 4, QZ)
    kz = wqkv[:, QDIM : QDIM + KVDIM].reshape(256, 4, HEAD_DIM)
    vz = wqkv[:, QDIM + KVDIM :].reshape(256, 4, HEAD_DIM)
    wq = jnp.concatenate([heads, kz, vz], axis=2).reshape(256, 4 * MZ)

    X, SEG, GN, WQ, WO, A1, A3, AX, AY = talk(
        fetch_kernel,
        "fetch",
        1,
        30,
        80,
        (x, seg, gn, wq, wo, w1, w3, w2),
        [
            ((RING, TOK, D), BF),
            ((2, 4, 2, 8, TOK), jnp.int32),
            ((4, 2, 32, 256), BF),
            ((2, 4, 2, 2, 64, MZ), BF),
            ((2, 256, D), BF),
            ((2, 2, 64, FZ), BF),
            ((4, 64, FZ), BF),
            ((2, 2, 352, 128), BF),
            ((4, 352, 128), BF),
        ],
        scratch=[
            pltpu.VMEM((704, 128), BF),
            pltpu.VMEM((256, 128), BF),
            pltpu.VMEM((64, MZ), BF),
            pltpu.VMEM((64, FZ), BF),
            pltpu.VMEM((64, FZ), BF),
        ],
        near=(0, 1, 2),
    )
    legs = lambda v, axis: [v] + [move(v, axis, s) for s in (1, 3, 2)]
    a1, a3 = legs(A1, "y"), legs(A3, "x")
    ax, ay = legs(AX, "y"), legs(AY, "x")
    gs = legs(g, "z")

    docs = SEG[:, :, :, 0, :].reshape(16 * TOK)
    mine = pick(pick(SEG[:, :, :, 0, :], xl, 0), c, 1)
    chunks = xl * 8 + 2 * jnp.arange(4, dtype=jnp.int32) + c
    start = jnp.sum((docs[None, None, :] < mine[:, :, None]).astype(jnp.int32), axis=2)
    index = chunks[:, None] * TOK + jnp.arange(TOK, dtype=jnp.int32)[None]
    place = (index - start).astype(F32)
    lane = jnp.arange(128)
    freq = THETA ** (-(lane % 32).astype(F32) * 2.0 / HEAD_DIM)
    angle = place[:, :, None] * freq[None, None, :]
    cosine = jnp.cos(angle)
    sine = jnp.sin(angle) * jnp.where(lane % 64 < 32, -1.0, 1.0)
    info = jnp.stack([jnp.min(start, axis=1) // TOK, chunks])
    start = start[:, None, :]
    gain_attn = GN[:, :, 0, :].reshape(1, D).astype(F32)
    gain_ffn = GN[:, :, 16, :].reshape(1, D).astype(F32)

    WQ = WQ.reshape(D, MZ)
    WO = WO.reshape(QZ, D)
    n1, query, kv = project(X, gain_attn, WQ, cosine, sine)
    (KV,) = talk(
        kv_kernel, "kv", 2, 7, 4, (kv,), [((2, 4, 2, TOK, 128), BF)], near=(0,)
    )
    KV = KV.reshape(16, TOK, 128)
    heads_out, logsum = attend(info, query, KV, start)
    o = heads_out.reshape(RING * TOK, QZ)
    part = dot(o, WO).astype(BF).reshape(RING, TOK, D)
    h, n2 = resid(x, scatter(part, q, "z", 0), gain_ffn)

    N2, G, W13, W2 = talk(
        assemble_kernel,
        "assemble",
        3,
        27,
        110,
        (n2, *gs, *a1, *a3, *ax, *ay),
        [
            ((RING, TOK, D), BF),
            ((RING, TOK, D), BF),
            ((2, 4, 2, 2, 64, 2 * FZ), BF),
            ((2, 704, D), BF),
        ],
        scratch=[
            pltpu.VMEM((4, TOK, D), BF),
            pltpu.VMEM((4, 2, 2, 64, FZ), BF),
            pltpu.VMEM((4, 4, 64, FZ), BF),
            pltpu.VMEM((4, 2, 2, 352, 128), BF),
            pltpu.VMEM((4, 4, 352, 128), BF),
        ],
        near=(0,),
    )
    N2, G = N2.reshape(RING * TOK, D), G.reshape(RING * TOK, D)
    W13, W2 = W13.reshape(D, 2 * FZ), W2.reshape(FZ, D)
    gate, up = dot(N2, W13[:, :FZ]), dot(N2, W13[:, FZ:])
    hidden = (jax.nn.silu(gate) * up).astype(BF)
    out_part = dot(hidden, W2).astype(BF).reshape(RING, TOK, D)
    dhid = jnp.einsum("td,fd->tf", G, W2, preferred_element_type=F32)
    sigma = jax.nn.sigmoid(gate)
    dgate = (dhid * up * sigma * (1.0 + gate * (1.0 - sigma))).astype(BF)
    dup = (dhid * gate * sigma).astype(BF)
    both = jnp.concatenate([dgate, dup], axis=1)
    dn2 = jnp.einsum("tf,df->td", both, W13, preferred_element_type=F32)
    dn2 = dn2.astype(BF).reshape(RING, TOK, D)
    dn2_parts = scatter(dn2, q, "z", 0)

    half = lambda v, j: lax.dynamic_slice_in_dim(v, 1024 * j, 1024, 1)
    outer = lambda a, b: jnp.einsum("ta,tb->ab", a, b, preferred_element_type=F32)
    other13 = move(outer(half(N2, 1 - c), both).astype(BF), "c", 1)
    other2 = move(outer(hidden, half(G, 1 - c)).astype(BF), "c", 1)
    sum13 = (outer(half(N2, c), both) + other13.astype(F32)).astype(BF)
    sum2 = (outer(hidden, half(G, c)) + other2.astype(F32)).astype(BF)
    sum13 = sum13.reshape(4, 4, 64, 2 * FZ)
    fa = add(scatter(sum13[..., :SPLIT], q, "x", 1))
    fa = add(scatter(fa, q, "y", 0))
    fb = add(scatter(sum13[..., SPLIT:], q, "y", 0))
    fb = add(scatter(fb, q, "x", 0))
    f2 = add(scatter_cols(sum2, q, "y", 256))
    f2 = add(scatter_quarters(f2, q, 704))
    f2 = lax.ppermute(f2, ("dp", "ctx"), swap_pairs())

    dh, dhb, gain2 = norm_back(h, g, dn2_parts, gain_ffn, True)
    (DH,) = talk(
        gather_kernel, "gather", 4, 27, 4, (dhb,), [((RING, TOK, D), BF)], near=(0,)
    )
    DH = DH.reshape(RING * TOK, D)
    dheads = jnp.einsum("td,qd->tq", DH, WO, preferred_element_type=F32).astype(BF)
    dquery, dkv = attend_back(
        info, query, KV, start, heads_out, dheads.reshape(RING, TOK, QZ), logsum, cosine, sine
    )
    dkv = dkv.reshape(2, 4, 2, TOK, 128)
    (received,) = talk(
        dkv_kernel, "dkv", 5, 8, 4, (dkv,), [((3, 4, TOK, 128), BF)]
    )
    own_dkv = pick(pick(dkv, xl, 0), c, 1)
    dkv_rot = dmixed_kv(xl[None], own_dkv, received, cosine, sine)
    dmixed = jnp.concatenate([dquery, dkv_rot], axis=2).reshape(RING * TOK, MZ)
    dn1 = jnp.einsum("tc,dc->td", dmixed, WQ, preferred_element_type=F32)
    dn1 = dn1.astype(BF).reshape(RING, TOK, D)
    input_grad, gain1 = norm_back(x, dh, scatter(dn1, q, "z", 0), gain_attn, False)

    n1 = n1.reshape(RING * TOK, D)
    other_q = move(outer(half(n1, 1 - c), dmixed).astype(BF), "c", 1)
    other_o = move(outer(o, half(DH, 1 - c)).astype(BF), "c", 1)
    sum_q = (outer(half(n1, c), dmixed) + other_q.astype(F32)).astype(BF)
    sum_o = (outer(o, half(DH, c)) + other_o.astype(F32)).astype(BF)
    fq = add(scatter(sum_q.reshape(4, 4, 64, MZ), q, "x", 1))
    fq = add(scatter(fq, q, "y", 0))
    fo = add(scatter_cols(sum_o, q, "y", 256))
    fo = add(scatter_quarters(fo, q, 256))
    fo = lax.ppermute(fo, ("dp", "ctx"), swap_pairs())

    gains = jnp.concatenate([gain1, gain2], axis=0).reshape(2, 8, 256).transpose(1, 0, 2)
    gains = jnp.pad(gains, ((0, 0), (0, 6), (0, 0))).reshape(4, 2, 8, 256)
    small = (8, 256)
    G1, G3, G2, GO, GQ, gain_out = talk(
        spread_kernel,
        "spread",
        6,
        50,
        60,
        (fa, fb, f2, fo, fq, gains),
        [
            ((256, 4 * FZ), BF),
            ((256, 4 * FZ), BF),
            ((704, D), BF),
            ((256, D), BF),
            ((256, 4 * MZ), BF),
            (small, F32),
        ],
        scratch=[
            pltpu.VMEM((4, 2) + small, F32),
            pltpu.VMEM((2, 2) + small, F32),
            pltpu.VMEM((4,) + small, F32),
            pltpu.VMEM((2,) + small, F32),
            pltpu.VMEM((2,) + small, F32),
            pltpu.VMEM(small, F32),
        ],
        near=(0, 1, 2, 3, 4, 5),
    )
    GQ = GQ.astype(F32).reshape(256, 4, MZ)
    flat = lambda v: v.reshape(256, -1)
    grad_qkv = jnp.concatenate(
        [flat(GQ[:, :, :QZ]), flat(GQ[:, :, QZ : QZ + 64]), flat(GQ[:, :, QZ + 64 :])], axis=1
    )
    out_parts = [p.astype(F32) for p in scatter(out_part, q, "z", 0)]
    output = h + ((out_parts[0] + out_parts[1]) + (out_parts[2] + out_parts[3]))
    return (
        output[None],
        input_grad[None],
        gain_out[0],
        gain_out[1],
        grad_qkv,
        GO.astype(F32),
        G1.astype(F32),
        G3.astype(F32),
        G2.astype(F32),
    )


def solution(mesh):
    rows = P("dp", None)
    acts = P("dp", "ctx", None)
    return jax.shard_map(
        body,
        mesh=mesh,
        in_specs=(acts, P("dp", "ctx"), acts, P("dp"), P("dp"), rows, rows, rows, rows, rows),
        out_specs=(acts, acts, P("dp"), P("dp"), rows, rows, rows, rows, rows),
        check_vma=False,
    )
```

time: 2420 us -> 674 us (0.28)
  waiting for transfers between devices: 2000 us -> 174 us
  Pallas kernels: 0 us -> 300 us
  matrix products: 222 us -> 64.3 us
  blocking collectives: 104 us -> 0 us
  starting transfers between devices: 0.81 us -> 73.8 us
    all_gather x7 -> x0, waiting for transfers between devices: 902 us -> none  [the longest x1 235 us: body(): lax.all_gather(w1, 'dp', axis=0, tiled=True)]
    unnamed x17 -> x0, waiting for transfers between devices: 565 us -> none
    reduce_scatter x3 -> x0, waiting for transfers between devices: 457 us -> none  [the longest x1 246 us: body(): lax.psum_scatter(jnp.einsum('tr,td->rd', rows, grad_out, preferred_elemen...]
    pallas_call x0 -> x13, Pallas kernels: none -> 300 us  [the longest x6 247 us: talk(): pl.pallas_call(kernel, name=name, out_shape=[jax.ShapeDtypeStruct(s, t) f...]
    ppermute x0 -> x63, waiting for transfers between devices: none -> 174 us  [the longest x61 174 us: move(): return lax.ppermute(v, ('dp', 'ctx'), shift_pairs(axis, by))]
    dot_general x42 -> x16, matrix products: 222 us -> 64.3 us  [the longest x8 24.3 us: body(): jnp.einsum('ta,tb->ab', a, b, preferred_element_type=F32)]
    psum x1 -> x0, waiting for transfers between devices: 78.2 us -> none  [body(): lax.psum(qkv_piece.astype(jnp.bfloat16), 'ctx').astype(jnp.float32)]
    ppermute x0 -> x63, starting transfers between devices: none -> 73.8 us  [the longest x61 72.4 us: move(): return lax.ppermute(v, ('dp', 'ctx'), shift_pairs(axis, by))]
  transfers between devices with their start and end apart: 14 -> 63, of which waited for: 14 -> 28; matrix products, arithmetic and copies ran while one was open for 6% -> 9% of each run, Pallas kernels for 0% -> 15%
where the time goes in v1:
time: 674 us; the launch traced here: 664 us
  Pallas kernels  300 us (45%)
  waiting for transfers between devices  174 us (26%)
  starting transfers between devices  73.8 us (11%)
  matrix products  64.3 us (10%)
  local copies, waits for them, and re-layouts  26 us (4%)
  other arithmetic  25.1 us (4%)
    pallas_call x6, Pallas kernels, talk(): pl.pallas_call(kernel, name=name, out_shape=[jax.ShapeDtypeStruct(s, t) f...  247 us
    ppermute x61, waiting for transfers between devices, move(): return lax.ppermute(v, ('dp', 'ctx'), shift_pairs(axis, by))  174 us
    ppermute x61, starting transfers between devices, move(): return lax.ppermute(v, ('dp', 'ctx'), shift_pairs(axis, by))  72.4 us
    dot_general x8, matrix products, body(): jnp.einsum('ta,tb->ab', a, b, preferred_element_type=F32)  24.3 us
    dot_general x4, matrix products, dot(): return jnp.dot(a, b, preferred_element_type=F32)  17.7 us
    pallas_call x1, Pallas kernels, attend_back(): pl.pallas_call(attend_back_kernel, name='attend_back', cost_estimate=cost...  17.4 us
    pallas_call x1, Pallas kernels, attend(): pl.pallas_call(attend_kernel, name='attend', cost_estimate=cost(12), grid...  14.5 us
  transfers between devices with their start and end apart: 63, of which 28 were waited for; matrix products, arithmetic and copies ran while one was open for 9% of the time, Pallas kernels for 15%

profile of v1, /device:TPU:1, one launch (start us, length us, event | category | flops | bytes accessed | tf_op | source)
XLA Modules:
  0.0 664.4 jit_solution(9305796401767778770)
XLA Ops:
  6.5 57.2 %fetch.1 = (bf16[4,128,2048]{2,1,0:T(8,128)(2,1)}, s32[2,4,2,8,128]{4,3,2,1,0:T(8,128)}, bf16[4,2,32,256]{3,2,1,0:T(8,128)(2,1)}, bf16[2,4,2,2,64,640]{5,4,3,2,1...) custom-call(bf16[128,2048]{1,0:T(8,128)(2,1)} %bitcast.203, ...), custom_call_target="tpu_custom_call" | custom-call | flops 30000001024 | tf_op jit(solution)/shard_map/fetch/pallas_call | solution.py:115
  72.4 7.2 %project.1 = (bf16[4,128,2048]{2,1,0:T(8,128)(2,1)}, bf16[4,128,512]{2,1,0:T(8,128)(2,1)}, bf16[4,128,128]{2,1,0:T(8,128)(2,1)}) custom-call(bf16[4,128,2048]{2,1,0:T(8,128)(2,1)} %get-tuple-element.43.x, f32[1,2048]{1,0:T(1,128)} %convert.11.gain, bf16[2048,640]{1,0:T(8,128)(2,1)} %bitcast.213, f32[4,128,128]{2,1,0:T(8,128)} %get-tuple-element.132.cosine, ...), custom_call_target="tpu_custom_call" | custom-call | flops 7000000000 | tf_op jit(solution)/shard_map/project/pallas_call | solution.py:503
  84.7 14.5 %attend.1 = (bf16[4,128,512]{2,1,0:T(8,128)(2,1)}, f32[4,1,1024]{2,1,0:T(1,128)}) custom-call(s32[2,4]{1,0:T(2,128)} %pad_add_fusion.info, bf16[4,128,512]{2,1,0:T(8,128)(2,1)} %get-tuple-element.46.query, bf16[16,128,128]{2,1,0:T(8,128)(2,1)} %bitcast.233, s32[4,1,128]{2,1,0:T(1,128)} %bitcast.192), custom_call_target="tpu_custom_call" | custom-call | flops 12000000000 | tf_op jit(solution)/shard_map/attend/pallas_call | solution.py:592
  108.6 5.2 collective-permute-done.16.refs_19_
  117.8 7.2 %collective-permute-done.1.c = bf16[128,2048]{1,0:T(8,128)(2,1)S(1)} collective-permute-done((bf16[128,2048]{1,0:T(8,128)(2,1)S(1)}, bf16[128,2048]{1,0:T(8,128)(2,1)S(1)}, u32[]{:S(2)}, u32[]{:S(2)}) %collective-permute-start.1) | collective-permute-done | bytes 524320 | tf_op jit(solution)/shard_map/ppermute | solution.py:71
  127.4 17.5 %collective-permute-done.3.refs_2_ = bf16[128,2048]{1,0:T(8,128)(2,1)S(1)} collective-permute-done((bf16[128,2048]{1,0:T(8,128)(2,1)S(1)}, bf16[128,2048]{1,0:T(8,128)(2,1)S(1)}, u32[]{:S(2)}, u32[]{:S(2)}) %collective-permute-start.3) | collective-permute-done | bytes 524320 | tf_op jit(solution)/shard_map/ppermute | solution.py:71
  158.5 5.6 collective-permute-done.8.refs_8_
  166.6 12.3 %collective-permute-done.11.refs_12_ = bf16[4,64,1408]{2,1,0:T(8,128)(2,1)} collective-permute-done((bf16[4,64,1408]{2,1,0:T(8,128)(2,1)S(1)}, bf16[4,64,1408]{2,1,0:T(8,128)(2,1)}, u32[]{:S(2)}, u32[]{:S(2)}) %collective-permute-start.11) | collective-permute-done | bytes 720928 | tf_op jit(solution)/shard_map/ppermute | solution.py:71
  178.9 37.4 %assemble.1 = (bf16[4,128,2048]{2,1,0:T(8,128)(2,1)}, bf16[4,128,2048]{2,1,0:T(8,128)(2,1)}, bf16[2,4,2,2,64,2816]{5,4,3,2,1,0:T(8,128)(2,1)}, bf16[2,704,2048]{2,1,0:T(8,128)(2,1)}) custom-call(bf16[128,2048]{1,0:T(8,128)(2,1)} %get-tuple-element.51.refs_0_, bf16[128,2048]{1,0:T(8,128)(2,1)} %bitcast.198, bf16[128,2048]{1,0:T(8,128)(2,1)} %copy-done.20, ...), custom_call_target="tpu_custom_call" | custom-call | flops 27000000512 | tf_op jit(solution)/shard_map/assemble/pallas_call | solution.py:115
  216.4 8.4 %fusion.55 = f32[512,1408]{1,0:T(8,128)} fusion(bf16[512,2048]{1,0:T(8,128)(2,1)} %bitcast.223, bf16[1408,2048]{1,0:T(8,128)(2,1)} %bitcast.209), kind=kOutput, calls=%fused_computation.141 | convolution fusion | flops 2952790016 | bytes 10747904 | tf_op jit(solution)/shard_map/td,fd->tf/dot_general | solution.py:896
  229.9 6.7 %multiply_convert_fusion.1 = (bf16[512,1408]{1,0:T(8,128)(2,1)S(1)}, bf16[512,1408]{1,0:T(8,128)(2,1)S(1)}, bf16[512,1408]{1,0:T(8,128)(2,1)S(1)}) fusion(f32[512,1408]{1,0:T(8,128)} %fusion.55, f32[512,1408]{1,0:T(8,128)} %fusion, bf16[512,2048]{1,0:T(8,128)(2,1)S(1)} %bitcast.220, bf16[2048,2816]{1,0:T(8,128)(2,1)S(1)} %bitcast.207), kind=kOutput, calls=%fused_computation.15 | convolution fusion | flops 2964324352 | bytes 17956864 | tf_op jit(solution)/shard_map/dot_general | solution.py:792
  243.7 6.4 convolution_convert_fusion.2
  266.6 9.0 %collective-permute-done.22.c = bf16[128,2048]{1,0:T(8,128)(2,1)S(1)} collective-permute-done((bf16[128,2048]{1,0:T(8,128)(2,1)S(1)}, bf16[128,2048]{1,0:T(8,128)(2,1)S(1)}, u32[]{:S(2)}, u32[]{:S(2)}) %collective-permute-start.22) | collective-permute-done | bytes 524320 | tf_op jit(solution)/shard_map/ppermute | solution.py:71
  282.5 36.5 %gather.1 = bf16[4,128,2048]{2,1,0:T(8,128)(2,1)} custom-call(bf16[128,2048]{1,0:T(8,128)(2,1)} %get-tuple-element.61.v), custom_call_target="tpu_custom_call" | custom-call | flops 27000000512 | tf_op jit(solution)/shard_map/gather/pallas_call | solution.py:115
  324.6 17.4 %attend_back.1 = (bf16[4,128,512]{2,1,0:T(8,128)(2,1)}, bf16[16,128,128]{2,1,0:T(8,128)(2,1)}) custom-call(s32[2,4]{1,0:T(2,128)} %pad_add_fusion.info, bf16[4,128,512]{2,1,0:T(8,128)(2,1)} %get-tuple-element.46.query, bf16[16,128,128]{2,1,0:T(8,128)(2,1)} %bitcast.234, s32[4,1,128]{2,1,0:T(1,128)} %bitcast.193, bf16[4,128,512]{2,1,0:T(8,128)(2,1)} %get-tuple-element.48.out, ...), custom_call_target="tpu_custom_call" | custom-call | flops 15000000512 | tf_op jit(solution)/shard_map/attend_back/pallas_call | solution.py:660
  344.3 8.5 %dkv.1.received = bf16[3,4,128,128]{3,2,1,0:T(8,128)(2,1)} custom-call(bf16[2,4,2,128,128]{4,3,2,1,0:T(8,128)(2,1)} %bitcast.189), custom_call_target="tpu_custom_call" | custom-call | flops 8000000000 | tf_op jit(solution)/shard_map/dkv/pallas_call | solution.py:115
  367.3 7.7 %collective-permute-done.24.b = bf16[128,2048]{1,0:T(8,128)(2,1)S(1)} collective-permute-done((bf16[128,2048]{1,0:T(8,128)(2,1)S(1)}, bf16[128,2048]{1,0:T(8,128)(2,1)S(1)}, u32[]{:S(2)}, u32[]{:S(2)}) %collective-permute-start.24) | collective-permute-done | bytes 524320 | tf_op jit(solution)/shard_map/ppermute | solution.py:71
  380.7 8.2 %collective-permute-done.26.d = bf16[128,2048]{1,0:T(8,128)(2,1)S(1)} collective-permute-done((bf16[128,2048]{1,0:T(8,128)(2,1)S(1)}, bf16[128,2048]{1,0:T(8,128)(2,1)S(1)}, u32[]{:S(2)}, u32[]{:S(2)}) %collective-permute-start.26) | collective-permute-done | bytes 524320 | tf_op jit(solution)/shard_map/ppermute | solution.py:71
  428.3 5.4 add_convert_fusion
  437.0 28.4 %collective-permute-done.60 = bf16[64,640]{1,0:T(8,128)(2,1)S(1)} collective-permute-done((bf16[64,640]{1,0:T(8,128)(2,1)S(1)}, bf16[64,640]{1,0:T(8,128)(2,1)S(1)}, u32[]{:S(2)}, u32[]{:S(2)}) %collective-permute-start.60) | collective-permute-done | bytes 81952 | tf_op jit(solution)/shard_map/ppermute | solution.py:71
  472.6 7.6 %collective-permute-done.35 = bf16[4,64,768]{2,1,0:T(8,128)(2,1)S(1)} collective-permute-done((bf16[4,64,768]{2,1,0:T(8,128)(2,1)S(1)}, bf16[4,64,768]{2,1,0:T(8,128)(2,1)S(1)}, u32[]{:S(2)}, u32[]{:S(2)}) %collective-permute-start.35) | collective-permute-done | bytes 393248 | tf_op jit(solution)/shard_map/ppermute | solution.py:71
  483.5 8.9 %collective-permute-done.30 = bf16[4,64,2048]{2,1,0:T(8,128)(2,1)S(1)} collective-permute-done((bf16[4,64,2048]{2,1,0:T(8,128)(2,1)S(1)}, bf16[4,64,2048]{2,1,0:T(8,128)(2,1)S(1)}, u32[]{:S(2)}, u32[]{:S(2)}) %collective-permute-start.30) | collective-permute-done | bytes 1048608 | tf_op jit(solution)/shard_map/ppermute | solution.py:71
  493.9 19.7 %collective-permute-done.29 = bf16[4,64,2048]{2,1,0:T(8,128)(2,1)S(1)} collective-permute-done((bf16[4,64,2048]{2,1,0:T(8,128)(2,1)S(1)}, bf16[4,64,2048]{2,1,0:T(8,128)(2,1)S(1)}, u32[]{:S(2)}, u32[]{:S(2)}) %collective-permute-start.29) | collective-permute-done | bytes 1048608 | tf_op jit(solution)/shard_map/ppermute | solution.py:71
  538.5 103.2 %spread.1 = (bf16[256,5632]{1,0:T(8,128)(2,1)}, bf16[256,5632]{1,0:T(8,128)(2,1)}, bf16[704,2048]{1,0:T(8,128)(2,1)}, bf16[256,2048]{1,0:T(8,128)(2,1)}, bf16[256,2560]{1,0:T(8,128)(2,1)}, /*index=5*/f32[8,256]{1,0:T(8,128)}) custom-call(bf16[64,2048]{1,0:T(8,128)(2,1)} %fusion.28.fa, bf16[64,768]{1,0:T(8,128)(2,1)} %fusion.31.fb, ...), custom_call_target="tpu_custom_call" | custom-call | flops 49999998976 | tf_op jit(solution)/shard_map/spread/pallas_call | solution.py:115
  (324 shorter events, 216.3 us)
Async XLA Ops:
  63.7 38.9 %collective-permute-start.12 = (bf16[2,2,352,128]{3,2,1,0:T(8,128)(2,1)}, bf16[2,2,352,128]{3,2,1,0:T(8,128)(2,1)}, u32[]{:S(2)}, u32[]{:S(2)}) collective-permute-start(bf16[2,2,352,128]{3,2,1,0:T(8,128)(2,1)} %get-tuple-element.54.refs_13_), channel_id=1, source_target_pairs={{0,32},{1,33},{2,34},{3,35},{4,36},{5,37},{6,38},{7,39},{8,40},{9,... | collective-permute-start | bytes 1081352 | tf_op jit(solution)/shard_map/ppermute | solution.py:71
  63.7 41.5 %collective-permute-start.13 = (bf16[2,2,352,128]{3,2,1,0:T(8,128)(2,1)}, bf16[2,2,352,128]{3,2,1,0:T(8,128)(2,1)}, u32[]{:S(2)}, u32[]{:S(2)}) collective-permute-start(bf16[2,2,352,128]{3,2,1,0:T(8,128)(2,1)} %get-tuple-element.54.refs_13_), channel_id=1, source_target_pairs={{0,96},{1,97},{2,98},{3,99},{4,100},{5,101},{6,102},{7,103},{8,104... | collective-permute-start | bytes 1081352 | tf_op jit(solution)/shard_map/ppermute | solution.py:71
  66.4 38.9 %collective-permute-start.14 = (bf16[2,2,352,128]{3,2,1,0:T(8,128)(2,1)}, bf16[2,2,352,128]{3,2,1,0:T(8,128)(2,1)}, u32[]{:S(2)}, u32[]{:S(2)}) collective-permute-start(bf16[2,2,352,128]{3,2,1,0:T(8,128)(2,1)} %get-tuple-element.54.refs_13_), channel_id=1, source_target_pairs={{0,64},{1,65},{2,66},{3,67},{4,68},{5,69},{6,70},{7,71},{8,72},{9,... | collective-permute-start | bytes 1081352 | tf_op jit(solution)/shard_map/ppermute | solution.py:71
  66.4 41.7 %collective-permute-start.15 = (bf16[4,352,128]{2,1,0:T(8,128)(2,1)}, bf16[4,352,128]{2,1,0:T(8,128)(2,1)}, u32[]{:S(2)}, u32[]{:S(2)}) collective-permute-start(bf16[4,352,128]{2,1,0:T(8,128)(2,1)} %get-tuple-element.55.refs_17_), channel_id=1, source_target_pairs={{0,8},{1,9},{2,10},{3,11},{4,12},{5,13},{6,14},{7,15},{8,16},{9,17... | collective-permute-start | bytes 1081352 | tf_op jit(solution)/shard_map/ppermute | solution.py:71
  108.1 45.0 %collective-permute-start.6 = (bf16[2,2,64,1408]{3,2,1,0:T(8,128)(2,1)S(1)}, bf16[2,2,64,1408]{3,2,1,0:T(8,128)(2,1)S(1)}, u32[]{:S(2)}, u32[]{:S(2)}) collective-permute-start(bf16[2,2,64,1408]{3,2,1,0:T(8,128)(2,1)S(1)} %copy-done.13), channel_id=1, source_target_pairs={{0,32},{1,33},{2,34},{3,35},{4,36},{5,37},{6,38},{7,39},{8,40},{9,... | collective-permute-start | bytes 2162696 | tf_op jit(solution)/shard_map/ppermute | solution.py:71
  114.6 30.3 %collective-permute-start.3 = (bf16[128,2048]{1,0:T(8,128)(2,1)S(1)}, bf16[128,2048]{1,0:T(8,128)(2,1)S(1)}, u32[]{:S(2)}, u32[]{:S(2)}) collective-permute-start(bf16[128,2048]{1,0:T(8,128)(2,1)S(1)} %bitcast.200), channel_id=1, source_target_pairs={{0,2},{1,3},{2,4},{3,5},{4,6},{5,7},{6,0},{7,1},{8,10},{9,11},{10,... | collective-permute-start | bytes 1572872 | tf_op jit(solution)/shard_map/ppermute | solution.py:71
  117.6 32.8 %collective-permute-start.4 = (bf16[128,2048]{1,0:T(8,128)(2,1)S(1)}, bf16[128,2048]{1,0:T(8,128)(2,1)S(1)}, u32[]{:S(2)}, u32[]{:S(2)}) collective-permute-start(bf16[128,2048]{1,0:T(8,128)(2,1)S(1)} %bitcast.201), channel_id=1, source_target_pairs={{0,6},{1,7},{2,0},{3,1},{4,2},{5,3},{6,4},{7,5},{8,14},{9,15},{10,... | collective-permute-start | bytes 1572872 | tf_op jit(solution)/shard_map/ppermute | solution.py:71
  125.8 32.6 %collective-permute-start.7 = (bf16[2,2,64,1408]{3,2,1,0:T(8,128)(2,1)S(1)}, bf16[2,2,64,1408]{3,2,1,0:T(8,128)(2,1)S(1)}, u32[]{:S(2)}, u32[]{:S(2)}) collective-permute-start(bf16[2,2,64,1408]{3,2,1,0:T(8,128)(2,1)S(1)} %copy-done.13), channel_id=1, source_target_pairs={{0,96},{1,97},{2,98},{3,99},{4,100},{5,101},{6,102},{7,103},{8,104... | collective-permute-start | bytes 2162696 | tf_op jit(solution)/shard_map/ppermute | solution.py:71
  240.5 120.0 %collective-permute-start.20 = (bf16[128,2048]{1,0:T(8,128)(2,1)S(1)}, bf16[128,2048]{1,0:T(8,128)(2,1)S(1)}, u32[]{:S(2)}, u32[]{:S(2)}) collective-permute-start(bf16[128,2048]{1,0:T(8,128)(2,1)S(1)} %get-tuple-element.95), channel_id=1, source_target_pairs={{0,4},{1,5},{2,6},{3,7},{4,0},{5,1},{6,2},{7,3},{8,12},{9,13},{10,... | collective-permute-start | bytes 1572872 | tf_op jit(solution)/shard_map/ppermute | solution.py:71
  240.6 120.9 %collective-permute-start.19 = (bf16[128,2048]{1,0:T(8,128)(2,1)S(1)}, bf16[128,2048]{1,0:T(8,128)(2,1)S(1)}, u32[]{:S(2)}, u32[]{:S(2)}) collective-permute-start(bf16[128,2048]{1,0:T(8,128)(2,1)S(1)} %get-tuple-element.96), channel_id=1, source_target_pairs={{0,6},{1,7},{2,0},{3,1},{4,2},{5,3},{6,4},{7,5},{8,14},{9,15},{10,... | collective-permute-start | bytes 1572872 | tf_op jit(solution)/shard_map/ppermute | solution.py:71
  266.6 100.4 %collective-permute-start.18 = (bf16[128,2048]{1,0:T(8,128)(2,1)S(1)}, bf16[128,2048]{1,0:T(8,128)(2,1)S(1)}, u32[]{:S(2)}, u32[]{:S(2)}) collective-permute-start(bf16[128,2048]{1,0:T(8,128)(2,1)S(1)} %get-tuple-element.94), channel_id=1, source_target_pairs={{0,2},{1,3},{2,4},{3,5},{4,6},{5,7},{6,0},{7,1},{8,10},{9,11},{10,... | collective-permute-start | bytes 1572872 | tf_op jit(solution)/shard_map/ppermute | solution.py:71
  275.6 151.9 %collective-permute-start.27 = (bf16[1024,2816]{1,0:T(8,128)(2,1)}, bf16[1024,2816]{1,0:T(8,128)(2,1)}, u32[]{:S(2)}, u32[]{:S(2)}) collective-permute-start(bf16[1024,2816]{1,0:T(8,128)(2,1)} %convolution_convert_fusion), channel_id=1, source_target_pairs={{0,1},{1,0},{2,3},{3,2},{4,5},{5,4},{6,7},{7,6},{8,9},{9,8},{10,11... | collective-permute-start | bytes 17301512 | tf_op jit(solution)/shard_map/ppermute | solution.py:71
  364.2 56.3 %collective-permute-start.40 = (bf16[1408,1024]{1,0:T(8,128)(2,1)}, bf16[1408,1024]{1,0:T(8,128)(2,1)}, u32[]{:S(2)}, u32[]{:S(2)}) collective-permute-start(bf16[1408,1024]{1,0:T(8,128)(2,1)} %convolution_convert_fusion.1), channel_id=1, source_target_pairs={{0,1},{1,0},{2,3},{3,2},{4,5},{5,4},{6,7},{7,6},{8,9},{9,8},{10,11... | collective-permute-start | bytes 8650760 | tf_op jit(solution)/shard_map/ppermute | solution.py:71
  367.0 32.1 %collective-permute-start.56 = (bf16[1024,640]{1,0:T(8,128)(2,1)S(1)}, bf16[1024,640]{1,0:T(8,128)(2,1)}, u32[]{:S(2)}, u32[]{:S(2)}) collective-permute-start(bf16[1024,640]{1,0:T(8,128)(2,1)S(1)} %convolution_convert_fusion.6), channel_id=1, source_target_pairs={{0,1},{1,0},{2,3},{3,2},{4,5},{5,4},{6,7},{7,6},{8,9},{9,8},{10,11... | collective-permute-start | bytes 3932168 | tf_op jit(solution)/shard_map/ppermute | solution.py:71
  424.5 42.8 %collective-permute-start.43 = (bf16[1408,256]{1,0:T(8,128)(2,1)S(1)}, bf16[1408,256]{1,0:T(8,128)(2,1)S(1)}, u32[]{:S(2)}, u32[]{:S(2)}) collective-permute-start(bf16[1408,256]{1,0:T(8,128)(2,1)S(1)} %get-tuple-element.82), channel_id=1, source_target_pairs={{0,64},{1,65},{2,66},{3,67},{4,68},{5,69},{6,70},{7,71},{8,72},{9,... | collective-permute-start | bytes 2162696 | tf_op jit(solution)/shard_map/ppermute | solution.py:71
  426.8 43.8 %collective-permute-start.42 = (bf16[1408,256]{1,0:T(8,128)(2,1)S(1)}, bf16[1408,256]{1,0:T(8,128)(2,1)S(1)}, u32[]{:S(2)}, u32[]{:S(2)}) collective-permute-start(bf16[1408,256]{1,0:T(8,128)(2,1)S(1)} %get-tuple-element.83), channel_id=1, source_target_pairs={{0,96},{1,97},{2,98},{3,99},{4,100},{5,101},{6,102},{7,103},{8,104... | collective-permute-start | bytes 2162696 | tf_op jit(solution)/shard_map/ppermute | solution.py:71
  427.4 43.1 %collective-permute-start.41 = (bf16[1408,256]{1,0:T(8,128)(2,1)S(1)}, bf16[1408,256]{1,0:T(8,128)(2,1)S(1)}, u32[]{:S(2)}, u32[]{:S(2)}) collective-permute-start(bf16[1408,256]{1,0:T(8,128)(2,1)S(1)} %get-tuple-element.81), channel_id=1, source_target_pairs={{0,32},{1,33},{2,34},{3,35},{4,36},{5,37},{6,38},{7,39},{8,40},{9,... | collective-permute-start | bytes 2162696 | tf_op jit(solution)/shard_map/ppermute | solution.py:71
  433.8 31.7 %collective-permute-start.60 = (bf16[64,640]{1,0:T(8,128)(2,1)S(1)}, bf16[64,640]{1,0:T(8,128)(2,1)S(1)}, u32[]{:S(2)}, u32[]{:S(2)}) collective-permute-start(bf16[64,640]{1,0:T(8,128)(2,1)S(1)} %get-tuple-element.121), channel_id=1, source_target_pairs={{0,32},{1,33},{2,34},{3,35},{4,36},{5,37},{6,38},{7,39},{8,40},{9,... | collective-permute-start | bytes 245768 | tf_op jit(solution)/shard_map/ppermute | solution.py:71
  434.0 36.7 %collective-permute-start.36 = (bf16[4,64,768]{2,1,0:T(8,128)(2,1)S(1)}, bf16[4,64,768]{2,1,0:T(8,128)(2,1)S(1)}, u32[]{:S(2)}, u32[]{:S(2)}) collective-permute-start(bf16[4,64,768]{2,1,0:T(8,128)(2,1)S(1)} %get-tuple-element.102), channel_id=1, source_target_pairs={{0,64},{1,65},{2,66},{3,67},{4,68},{5,69},{6,70},{7,71},{8,72},{9,... | collective-permute-start | bytes 1179656 | tf_op jit(solution)/shard_map/ppermute | solution.py:71
  467.3 46.4 %collective-permute-start.29 = (bf16[4,64,2048]{2,1,0:T(8,128)(2,1)S(1)}, bf16[4,64,2048]{2,1,0:T(8,128)(2,1)S(1)}, u32[]{:S(2)}, u32[]{:S(2)}) collective-permute-start(bf16[4,64,2048]{2,1,0:T(8,128)(2,1)S(1)} %get-tuple-element.80), channel_id=1, source_target_pairs={{0,24},{1,25},{2,26},{3,27},{4,28},{5,29},{6,30},{7,31},{8,0},{9,1... | collective-permute-start | bytes 3145736 | tf_op jit(solution)/shard_map/ppermute | solution.py:71
  470.6 47.2 %collective-permute-start.28 = (bf16[4,64,2048]{2,1,0:T(8,128)(2,1)S(1)}, bf16[4,64,2048]{2,1,0:T(8,128)(2,1)S(1)}, u32[]{:S(2)}, u32[]{:S(2)}) collective-permute-start(bf16[4,64,2048]{2,1,0:T(8,128)(2,1)S(1)} %get-tuple-element.78), channel_id=1, source_target_pairs={{0,8},{1,9},{2,10},{3,11},{4,12},{5,13},{6,14},{7,15},{8,16},{9,17... | collective-permute-start | bytes 3145736 | tf_op jit(solution)/shard_map/ppermute | solution.py:71
  480.2 38.5 %collective-permute-start.46 = (bf16[704,128]{1,0:T(8,128)(2,1)S(1)}, bf16[704,128]{1,0:T(8,128)(2,1)S(1)}, u32[]{:S(2)}, u32[]{:S(2)}) collective-permute-start(bf16[704,128]{1,0:T(8,128)(2,1)S(1)} %get-tuple-element.116), channel_id=1, source_target_pairs={{0,16},{1,17},{2,18},{3,19},{4,20},{5,21},{6,22},{7,23},{8,24},{9,... | collective-permute-start | bytes 540680 | tf_op jit(solution)/shard_map/ppermute | solution.py:71
  481.0 40.5 %collective-permute-start.45 = (bf16[704,128]{1,0:T(8,128)(2,1)S(1)}, bf16[704,128]{1,0:T(8,128)(2,1)S(1)}, u32[]{:S(2)}, u32[]{:S(2)}) collective-permute-start(bf16[704,128]{1,0:T(8,128)(2,1)S(1)} %get-tuple-element.117), channel_id=1, source_target_pairs={{0,24},{1,25},{2,26},{3,27},{4,28},{5,29},{6,30},{7,31},{8,0},{9,1... | collective-permute-start | bytes 540680 | tf_op jit(solution)/shard_map/ppermute | solution.py:71
  492.4 32.7 %collective-permute-start.44 = (bf16[704,128]{1,0:T(8,128)(2,1)S(1)}, bf16[704,128]{1,0:T(8,128)(2,1)S(1)}, u32[]{:S(2)}, u32[]{:S(2)}) collective-permute-start(bf16[704,128]{1,0:T(8,128)(2,1)S(1)} %get-tuple-element.115), channel_id=1, source_target_pairs={{0,8},{1,9},{2,10},{3,11},{4,12},{5,13},{6,14},{7,15},{8,16},{9,17... | collective-permute-start | bytes 540680 | tf_op jit(solution)/shard_map/ppermute | solution.py:71
  (101 other events, 1049.5 us)

commit v2 on v1

--- a/solution.py
+++ b/solution.py
@@ -100,24 +100,141 @@
             wait()
 
 
-def greet(targets):
+def greet(targets, q=None):
     barrier = pltpu.get_barrier_semaphore()
     for to in targets:
         pl.semaphore_signal(barrier, inc=1, device_id=to, device_id_type=MESH)
-    pl.semaphore_wait(barrier, len(targets))
+    if q is None:
+        pl.semaphore_wait(barrier, len(targets))
+    else:
+        y, z = q["y"], q["z"]
+
+        @pl.when(y != z)
+        def _():
+            to = device(q, y=z, z=y)
+            pl.semaphore_signal(barrier, inc=1, device_id=to, device_id_type=MESH)
+
+        pl.semaphore_wait(barrier, len(targets) + (y != z).astype(jnp.int32))
+
+
+TOP, LOW = pl.ds(0, TOK // 2), pl.ds(TOK // 2, TOK // 2)
+
+
+def gather_start(k, q, src, dst):
+    z = q["z"]
+    up, down = device(q, z=(z + 1) % 4), device(q, z=(z + 3) % 4)
+    first = k.send(src.at[TOP], dst.at[z, TOP], up)
+    second = k.send(src.at[LOW], dst.at[z, LOW], down)
+    rest = [
+        k.send(src.at[LOW], dst.at[z, LOW], up),
+        k.send(src.at[TOP], dst.at[z, TOP], down),
+    ]
+    return first, second, rest, k.local(src, dst.at[z])
+
+
+def gather_pass(k, q, dst, state):
+    z = q["z"]
+    below, above = (z + 3) % 4, (z + 1) % 4
+    first, second, rest, here = state
+    first.wait_recv()
+    rest.append(k.send(dst.at[below, TOP], dst.at[below, TOP], device(q, z=above)))
+    second.wait_recv()
+    rest.append(k.send(dst.at[above, LOW], dst.at[above, LOW], device(q, z=below)))
+
+
+def gather_end(state):
+    for cp in state[2]:
+        cp.wait_recv()
+    state[3].wait()
+
+
+def sum_start(k, q, part, pass_top, pass_low, below, above):
+    z = q["z"]
+    up, down = device(q, z=(z + 1) % 4), device(q, z=(z + 3) % 4)
+    far = (z + 2) % 4
+    return (
+        k.send(part.at[far, TOP], pass_top, up),
+        k.send(part.at[far, LOW], pass_low, down),
+        [
+            k.send(part.at[(z + 1) % 4, LOW], below.at[LOW], up),
+            k.send(part.at[(z + 3) % 4, TOP], above.at[TOP], down),
+        ],
+    )
+
+
+def sum_pass(k, q, part, pass_top, pass_low, send_top, send_low, below, above, state):
+    z = q["z"]
+    up, down = device(q, z=(z + 1) % 4), device(q, z=(z + 3) % 4)
+    first, second, rest = state
+    first.wait_recv()
+    send_top[...] = (pass_top[...].astype(F32) + part[(z + 1) % 4, TOP].astype(F32)).astype(BF)
+    rest.append(k.send(send_top, below.at[TOP], up))
+    second.wait_recv()
+    send_low[...] = (pass_low[...].astype(F32) + part[(z + 3) % 4, LOW].astype(F32)).astype(BF)
+    rest.append(k.send(send_low, above.at[LOW], down))
+
+
+def sum_end(state):
+    for cp in state[2]:
+        cp.wait_recv()
+
+
+HALF = (TOK // 2, D)
+
+
+def turn(k, q, moves):
+    y, z = q["y"], q["z"]
+    swap = device(q, y=z, z=y)
+    pairs = []
+    for src, dst in moves:
+        n = k.n
+        k.n += 1
+        remote = pltpu.make_async_remote_copy(
+            src_ref=src,
+            dst_ref=dst,
+            send_sem=k.send_sems.at[n],
+            recv_sem=k.recv_sems.at[n],
+            device_id=swap,
+            device_id_type=MESH,
+        )
+        pairs.append((remote, pltpu.make_async_copy(src, dst, k.send_sems.at[n])))
+
+    @pl.when(y != z)
+    def _():
+        for remote, _ in pairs:
+            remote.start()
+
+    @pl.when(y == z)
+    def _():
+        for _, here in pairs:
+            here.start()
+
+    def wait():
+        @pl.when(y != z)
+        def _():
+            for remote, _ in pairs:
+                remote.wait_recv()
+                remote.wait_send()
+
+        @pl.when(y == z)
+        def _():
+            for _, here in pairs:
+                here.wait()
+
+    return wait
 
 
 def cost(us):
     return pl.CostEstimate(flops=int(us * 1e9), bytes_accessed=0, transcendentals=0)
 
 
-def talk(kernel, name, cid, us, copies, ins, outs, scratch=(), near=()):
+def talk(kernel, name, cid, us, copies, ins, outs, scratch=(), near=(), near_out=()):
     return pl.pallas_call(
         kernel,
         name=name,
         out_shape=[jax.ShapeDtypeStruct(s, t) for s, t in outs],
         in_specs=[VMEM if i in near else ANY for i in range(len(ins))],
-        out_specs=[ANY] * len(outs),
+        out_specs=[VMEM if i in near_out else ANY for i in range(len(outs))],
         scratch_shapes=[
             *scratch,
             pltpu.SemaphoreType.DMA((copies,)),
@@ -131,7 +248,7 @@
 
 
 def fetch_kernel(
-    x, seg, gn, wq, wo, w1, w3, w2, X, SEG, GN, WQ, WO, A1, A3, AX, AY, T2, TO, QP, P1, P3, ss, rs
+    x, seg, gn, wq, wo, w1, w3, X, SEG, GN, WQ, WO, A1, A3, TO, QP, P1, P3, ss, rs
 ):
     q = coords()
     y, xx, xh, xl, z, c = q["y"], q["x"], q["xh"], q["xl"], q["z"], q["c"]
@@ -139,7 +256,6 @@
     mate = device(q, c=1 - c)
     other = device(q, x=xx ^ 1)
     other_mate = device(q, x=xx ^ 1, c=1 - c)
-    swap = device(q, y=z, z=y)
     k = Copies(ss, rs)
     rows = pl.ds(pl.multiple_of(128 * c + 64 * xl, 64), 64)
     qcols = pl.ds(pl.multiple_of(MZ * z, 128), MZ)
@@ -149,40 +265,9 @@
         k.local(w1.at[rows, fcols], P1),
         k.local(w3.at[rows, fcols], P3),
     ]
-    barrier = pltpu.get_barrier_semaphore()
-    greeted = zs + ys + xs + [mate, other_mate]
-    for to in greeted:
-        pl.semaphore_signal(barrier, inc=1, device_id=to, device_id_type=MESH)
-
-    @pl.when(y != z)
-    def _():
-        pl.semaphore_signal(barrier, inc=1, device_id=swap, device_id_type=MESH)
-
-    pl.semaphore_wait(barrier, len(greeted) + (y != z).astype(jnp.int32))
+    greet(zs + ys + xs + [mate, other_mate], q)
     piece = pl.ds(pl.multiple_of(128 * (c * 8 + z * 2 + xl), 128), 128)
-    turned = []
-    for src, dst in ((wo, TO), (w2, T2)):
-        n = k.n
-        k.n += 1
-        remote = pltpu.make_async_remote_copy(
-            src_ref=src.at[:, piece],
-            dst_ref=dst,
-            send_sem=ss.at[n],
-            recv_sem=rs.at[n],
-            device_id=swap,
-            device_id_type=MESH,
-        )
-        here = pltpu.make_async_copy(src.at[:, piece], dst, ss.at[n])
-
-        @pl.when(y != z)
-        def _(remote=remote):
-            remote.start()
-
-        @pl.when(y == z)
-        def _(here=here):
-            here.start()
-
-        turned.append((remote, here))
+    turned = turn(k, q, [(wo.at[:, piece], TO)])
     for cp in loads:
         cp.wait()
     top, low = pl.ds(0, 32), pl.ds(32, 32)
@@ -193,8 +278,11 @@
     seg_here = k.local(seg, SEG.at[xl, z, c])
     gn_y = [k.send(gn, GN.at[y, xh], to) for to in ys]
     gn_here = k.local(gn, GN.at[y, xh])
-    x_z = [k.send(x, X.at[z], to) for to in zs]
-    x_here = k.local(x, X.at[z])
+    x_state = gather_start(k, q, x, X)
+    turned()
+    ocol = pl.ds(pl.multiple_of(128 * (c * 8 + y * 2 + xl), 128), 128)
+    o1 = [k.send(TO, WO.at[xh, :, ocol], to) for to in xs]
+    o1_here = k.local(TO, WO.at[xh, :, ocol])
     q_here.wait()
     for cp in q_top:
         cp.wait_recv()
@@ -204,29 +292,15 @@
         cp.wait_recv()
     part = WQ.at[c, :, xh, xl, low]
     q2 += [k.send(part, part, to) for to in xs]
-    for remote, here in turned:
-
-        @pl.when(y != z)
-        def _(remote=remote):
-            remote.wait_recv()
-            remote.wait_send()
-
-        @pl.when(y == z)
-        def _(here=here):
-            here.wait()
-
-    ocol = pl.ds(pl.multiple_of(128 * (c * 8 + y * 2 + xl), 128), 128)
-    o1 = [k.send(TO, WO.at[xh, :, ocol], to) for to in xs]
-    o1_here = k.local(TO, WO.at[xh, :, ocol])
+    for cp in o1:
+        cp.wait_recv()
+    o1_here.wait()
+    part = WO.at[:, :, pl.ds(pl.multiple_of(128 * (c * 8 + y * 2), 256), 256)]
+    o2 = [k.send(part, part, to) for to in ys]
     a1 = [k.send(P1, A1.at[xh, xl], to) for to in xs]
-    a1_here = k.local(P1, A1.at[xh, xl])
     a3 = [k.send(P3, A3.at[y], to) for to in ys]
-    a3_here = k.local(P3, A3.at[y])
-    t_top, t_low = pl.ds(0, 352), pl.ds(352, 352)
-    ax = [k.send(T2.at[t_top], AX.at[xh, xl], to) for to in xs]
-    ax_here = k.local(T2.at[t_top], AX.at[xh, xl])
-    ay = [k.send(T2.at[t_low], AY.at[y], to) for to in ys]
-    ay_here = k.local(T2.at[t_low], AY.at[y])
+    heres = [k.local(P1, A1.at[xh, xl]), k.local(P3, A3.at[y])]
+    gather_pass(k, q, X, x_state)
     for cp in seg_z:
         cp.wait_recv()
     seg_here.wait()
@@ -236,11 +310,6 @@
         cp.wait_recv()
     gn_here.wait()
     gn2 = k.send(GN.at[:, xh], GN.at[:, xh], device(q, x=3 - xx))
-    for cp in o1:
-        cp.wait_recv()
-    o1_here.wait()
-    part = WO.at[:, :, pl.ds(pl.multiple_of(128 * (c * 8 + y * 2), 256), 256)]
-    o2 = [k.send(part, part, to) for to in ys]
     for cp in q2:
         cp.wait_recv()
     q3 = k.send(WQ.at[c], WQ.at[c], mate)
@@ -248,10 +317,11 @@
         cp.wait_recv()
     part = WO.at[:, :, pl.ds(pl.multiple_of(1024 * c, 1024), 1024)]
     o3 = k.send(part, part, mate)
-    for cp in x_z + a1 + a3 + ax + ay + seg2 + [gn2, q3, o3]:
-        cp.wait_recv()
-    for cp in (x_here, a1_here, a3_here, ax_here, ay_here):
+    for cp in a1 + a3 + seg2 + [gn2, q3, o3]:
+        cp.wait_recv()
+    for cp in heres:
         cp.wait()
+    gather_end(x_state)
     k.close()
 
 
@@ -298,56 +368,107 @@
     k.close()
 
 
-def gather_kernel(v, V, ss, rs):
+def middle_kernel(*refs):
+    part, x, gain, t2 = refs[:4]
+    a1, a3, gs = refs[4:7], refs[7:10], refs[10:14]
+    N2, H, G, W13, W2 = refs[14:19]
+    pass_top, pass_low, send_top, send_low, below, above, n2, b1, b3, gb, ss, rs = refs[19:]
     q = coords()
-    zs = ring(q, "z")
-    greet(zs)
-    k = Copies(ss, rs)
-    sent = [k.send(v, V.at[q["z"]], to) for to in zs]
-    here = k.local(v, V.at[q["z"]])
-    for cp in sent:
-        cp.wait_recv()
-    here.wait()
-    k.close()
-
-
-def assemble_kernel(*refs):
-    n2, g = refs[0], refs[1:5]
-    a1, a3, ax, ay = refs[5:9], refs[9:13], refs[13:17], refs[17:21]
-    N2, G, W13, W2, gb, b1, b3, bx, by, ss, rs = refs[21:]
-    q = coords()
-    y, xx, z, c = q["y"], q["x"], q["z"], q["c"]
-    zs = ring(q, "z")
+    y, xx, xh, xl, z, c = q["y"], q["x"], q["xh"], q["xl"], q["z"], q["c"]
+    ys, xs = ring(q, "y"), ring(q, "x")
+    up, down = device(q, z=(z + 1) % 4), device(q, z=(z + 3) % 4)
     mate = device(q, c=1 - c)
     k = Copies(ss, rs)
-    bufs = ((a1, b1), (a3, b3), (ax, bx), (ay, by), (g, gb))
-    loads = [[k.local(refs[j], buf.at[j]) for refs, buf in bufs] for j in range(4)]
-    greet(zs + [mate])
-    sent = [k.send(n2, N2.at[z], to) for to in zs]
-    heres = [k.local(n2, N2.at[z])]
-    for j, step in enumerate((0, 3, 1, 2)):
+    loads = [
+        [k.local(a1[j], b1.at[j]), k.local(a3[j], b3.at[j])] for j in range(3)
+    ] + [[k.local(gs[j], gb.at[j]) for j in range(4)]]
+    greet(ys + xs + [up, down, mate])
+    state = sum_start(k, q, part, pass_top, pass_low, below, above)
+    col = pl.ds(pl.multiple_of(128 * (c * 8 + y * 2 + xl), 128), 128)
+    t_top, t_low = pl.ds(0, 352), pl.ds(352, 352)
+    w2x = [k.send(t2.at[t_top], W2.at[xh, t_top, col], to) for to in xs]
+    w2y = [k.send(t2.at[t_low], W2.at[xh, t_low, col], to) for to in ys]
+    w2_here = k.local(t2, W2.at[xh, :, col])
+    f1, f3 = pl.ds(0, FZ), pl.ds(FZ, FZ)
+    for cp in loads[0]:
+        cp.wait()
+    far = [
+        k.send(b1.at[0], W13.at[c, y, :, :, :, f1], ys[2]),
+        k.send(b3.at[0], W13.at[c, :, xh, xl, :, f3], xs[2]),
+    ]
+    sent, heres = [], []
+    for j, step in enumerate((0, 3, 1)):
         yy, x2 = (y + step) % 4, (xx + step) % 4
-        xh, xl = x2 // 2, x2 % 2
-        for cp in loads[j]:
-            cp.wait()
-        heres.append(k.local(gb.at[j], G.at[(z + step) % 4]))
-        places = [
-            (b1.at[j], W13.at[c, yy, :, :, :, pl.ds(0, FZ)]),
-            (b3.at[j], W13.at[c, :, xh, xl, :, pl.ds(FZ, FZ)]),
-        ]
-        for b in range(2):
-            cols = pl.ds(pl.multiple_of(128 * (c * 8 + yy * 2 + b), 128), 128)
-            places.append((bx.at[j, :, b], W2.at[:, pl.ds(0, 352), cols]))
-        for b in range(4):
-            cols = pl.ds(pl.multiple_of(128 * (c * 8 + b * 2 + xl), 128), 128)
-            places.append((by.at[j, b], W2.at[xh, pl.ds(352, 352), cols]))
-        for src, dst in places:
+        if j:
+            for cp in loads[j]:
+                cp.wait()
+        for src, dst in (
+            (b1.at[j], W13.at[c, yy, :, :, :, f1]),
+            (b3.at[j], W13.at[c, :, x2 // 2, x2 % 2, :, f3]),
+        ):
             sent.append(k.send(src, dst, mate))
             heres.append(k.local(src, dst))
+    sum_pass(k, q, part, pass_top, pass_low, send_top, send_low, below, above, state)
+    for j, step in enumerate((0, 3, 1, 2)):
+        loads[3][j].wait()
+        heres.append(k.local(gb.at[j], G.at[(z + step) % 4]))
+    w2_here.wait()
+    for cp in w2x:
+        cp.wait_recv()
+    ref = W2.at[:, t_top, pl.ds(pl.multiple_of(128 * (c * 8 + y * 2), 256), 256)]
+    legs = [k.send(ref, ref, to) for to in ys]
+    for cp in w2y:
+        cp.wait_recv()
+    for b in range(4):
+        ref = W2.at[xh, t_low, pl.ds(pl.multiple_of(128 * (c * 8 + b * 2 + xl), 128), 128)]
+        legs += [k.send(ref, ref, to) for to in xs]
+    sum_end(state)
+    total = x[...].astype(F32) + (
+        part[z].astype(F32) + (below[...].astype(F32) + above[...].astype(F32))
+    )
+    H[...] = total
+    scale = lax.rsqrt(jnp.mean(total * total, axis=-1, keepdims=True) + EPS)
+    n2[...] = to_pieces((total * scale * gain[...]).astype(BF))
+    state = gather_start(k, q, n2, N2)
+    for cp in far:
+        cp.wait_recv()
+    x2 = (xx + 2) % 4
+    for ref in (
+        W13.at[c, (y + 2) % 4, :, :, :, f1],
+        W13.at[c, :, x2 // 2, x2 % 2, :, f3],
+    ):
+        sent.append(k.send(ref, ref, mate))
+    gather_pass(k, q, N2, state)
+    for cp in legs:
+        cp.wait_recv()
+    ref = W2.at[:, :, pl.ds(pl.multiple_of(1024 * c, 1024), 1024)]
+    sent.append(k.send(ref, ref, mate))
     for cp in sent:
         cp.wait_recv()
     for cp in heres:
         cp.wait()
+    gather_end(state)
+    k.close()
+
+
+def gather_kernel(v, sa, sb, s2, V, Ra, Rb, R2, ss, rs):
+    q = coords()
+    y, xx, z = q["y"], q["x"], q["z"]
+    up, down = device(q, z=(z + 1) % 4), device(q, z=(z + 3) % 4)
+    ys, xs = ring(q, "y")[:2], ring(q, "x")[:2]
+    greet([up, down] + ys + xs)
+    k = Copies(ss, rs)
+    state = gather_start(k, q, v, V)
+    legs = []
+    for i, step in enumerate((1, 3)):
+        yy, x2 = (y + step) % 4, (xx + step) % 4
+        legs.append(k.send(sa.at[:, x2], Ra.at[i], xs[i]))
+        legs.append(k.send(s2.at[:, pl.ds(pl.multiple_of(256 * yy, 256), 256)], R2.at[i], ys[i]))
+        legs.append(k.send(sb.at[yy], Rb.at[i], ys[i]))
+    gather_pass(k, q, V, state)
+    gather_end(state)
+    for cp in legs:
+        cp.wait_recv()
     k.close()
 
 
@@ -388,78 +509,165 @@
     k.close()
 
 
-def spread_kernel(
-    fa, fb, f2, fo, fq, gain, G1, G3, G2, GO, GQ, gain_out, s0, s1, s2, s3, s4, total, ss, rs
+def quarter(xt, rows):
+    return (
+        pl.ds(pl.multiple_of((xt // 2) * rows, rows), rows),
+        pl.ds(pl.multiple_of((xt % 2) * 128, 128), 128),
+    )
+
+
+def wide_kernel(
+    dn, fa, fb, f2, sq, so, D2, G1, G3, G2, Rq, Ro,
+    pass_top, pass_low, send_top, send_low, la, lb, l2, pa, pb, p2, t2, ss, rs,
 ):
     q = coords()
     y, xx, xh, xl, z, c = q["y"], q["x"], q["xh"], q["xl"], q["z"], q["c"]
-    zs, ys = ring(q, "z"), ring(q, "y")
+    zs, ys, xs = ring(q, "z"), ring(q, "y"), ring(q, "x")
+    mate, other = device(q, c=1 - c), device(q, x=xx ^ 1)
+    greet(zs + ys + xs + [mate], q)
+    k = Copies(ss, rs)
+    steps = (1, 3, 2)
+    state = sum_start(k, q, dn, pass_top, pass_low, D2.at[0], D2.at[1])
+    leg_a = [k.send(fa.at[(y + s) % 4], la.at[i], ys[i]) for i, s in enumerate(steps)]
+    leg_b = [k.send(fb.at[(xx + s) % 4], lb.at[i], xs[i]) for i, s in enumerate(steps)]
+    leg_2 = []
+    for i, s in enumerate(steps):
+        r, cc = quarter((xx + s) % 4, 704)
+        leg_2.append(k.send(f2.at[r, cc], l2.at[i], xs[i]))
+    heavy = []
+    for i, s in enumerate(steps):
+        heavy.append(k.send(sq.at[:, (xx + s) % 4], Rq.at[i], xs[i]))
+        cols = pl.ds(pl.multiple_of(256 * ((y + s) % 4), 256), 256)
+        heavy.append(k.send(so.at[:, cols], Ro.at[i], ys[i]))
+    sum_pass(k, q, dn, pass_top, pass_low, send_top, send_low, D2.at[0], D2.at[1], state)
+    for cp in leg_2:
+        cp.wait_recv()
+    r, cc = quarter(xx, 704)
+    p2[...] = add4(f2[r, cc], l2[0], l2[1], l2[2])
+    turned = turn(k, q, [(p2, t2)])
+    for cp in leg_b:
+        cp.wait_recv()
+    pb[...] = add4(fb[xx], lb[0], lb[1], lb[2])
+    for cp in leg_a:
+        cp.wait_recv()
+    pa[...] = add4(fa[y], la[0], la[1], la[2])
+    rows = pl.ds(pl.multiple_of(128 * c + 64 * xl, 64), 64)
+    rest = SPLIT - FZ
+
+    def blocks(zz):
+        at = lambda off, n: pl.ds(pl.multiple_of(FZ * zz + off, 128), n)
+        return [G1.at[rows, at(0, FZ)], G3.at[rows, at(0, rest)], G3.at[rows, at(rest, FZ - rest)]]
+
+    own = [pa.at[:, pl.ds(0, FZ)], pa.at[:, pl.ds(FZ, rest)], pb]
+    leg_z = [[k.send(src, dst, to) for src, dst in zip(own, blocks(z))] for to in zs]
+    heres = [k.local(src, dst) for src, dst in zip(own, blocks(z))]
+    leg_zx = [k.send(src, dst, other) for src, dst in zip(own, blocks(z))]
+    turned()
+    col = pl.ds(pl.multiple_of(128 * (c * 8 + z * 2 + xl), 128), 128)
+    leg_x = k.send(t2, G2.at[:, col], other)
+    heres.append(k.local(t2, G2.at[:, col]))
+    leg_x.wait_recv()
+    heres[-1].wait()
+    ref = G2.at[:, pl.ds(pl.multiple_of(128 * (c * 8 + z * 2), 256), 256)]
+    leg_xz = [k.send(ref, ref, to) for to in zs]
+    for i, s in enumerate(steps):
+        for cp in leg_z[i]:
+            cp.wait_recv()
+        leg_zx += [k.send(ref, ref, other) for ref in blocks((z - s + 4) % 4)]
+    for cp in leg_xz:
+        cp.wait_recv()
+    ref = G2.at[:, pl.ds(pl.multiple_of(1024 * c, 1024), 1024)]
+    last = [k.send(ref, ref, mate)]
+    for cp in heres[:-1]:
+        cp.wait()
+    for cp in leg_zx:
+        cp.wait_recv()
+    pair = pl.ds(pl.multiple_of(128 * c, 128), 128)
+    last += [k.send(ref.at[pair], ref.at[pair], mate) for ref in (G1, G3)]
+    for cp in heavy + last:
+        cp.wait_recv()
+    sum_end(state)
+    k.close()
+
+
+def last_kernel(
+    part, fq, fo, gain, D2, GO, GQ, gain_out,
+    pass_top, pass_low, send_top, send_low, lq, lo, pq, po, to_, s0, s1, s2, s3, s4, total, ss, rs,
+):
+    q = coords()
+    y, xx, xh, xl, z, c = q["y"], q["x"], q["xh"], q["xl"], q["z"], q["c"]
+    zs, ys, xs = ring(q, "z"), ring(q, "y"), ring(q, "x")
     mate, other, cross = device(q, c=1 - c), device(q, x=xx ^ 1), device(q, x=3 - xx)
-    greet(zs + ys + [mate, other, cross])
+    greet(zs + ys + xs + [mate], q)
     k = Copies(ss, rs)
-    gain_y = [k.send(gain.at[(y + s) % 4], s0.at[y], to) for s, to in zip((1, 3, 2), ys)]
+    steps = (1, 3, 2)
+    gain_y = [k.send(gain.at[(y + s) % 4], s0.at[y], ys[i]) for i, s in enumerate(steps)]
     gain_here = k.local(gain.at[y], s0.at[y])
+    leg_o = []
+    for i, s in enumerate(steps):
+        r, cc = quarter((xx + s) % 4, 256)
+        leg_o.append(k.send(fo.at[r, cc], lo.at[i], xs[i]))
+    leg_q = [k.send(fq.at[(y + s) % 4], lq.at[i], ys[i]) for i, s in enumerate(steps)]
+    for cp in gain_y:
+        cp.wait_recv()
+    gain_here.wait()
+    s1[0] = (s0[0] + s0[1]) + (s0[2] + s0[3])
+    gain_x = k.send(s1.at[0, 1 - xh], s1.at[1, 0], cross)
+    for cp in leg_o:
+        cp.wait_recv()
+    r, cc = quarter(xx, 256)
+    po[...] = add4(fo[r, cc], lo[0], lo[1], lo[2])
+    turned = turn(k, q, [(po, to_)])
+    gain_x.wait_recv()
+    s2[z] = s1[0, xh] + s1[1, 0]
+    gain_z = [k.send(s2.at[z], s2.at[z], to) for to in zs]
+    for cp in leg_q:
+        cp.wait_recv()
+    pq[...] = add4(fq[y], lq[0], lq[1], lq[2])
     rows = pl.ds(pl.multiple_of(128 * c + 64 * xl, 64), 64)
     pair = pl.ds(pl.multiple_of(128 * c, 128), 128)
-    fz = FZ * z
-    rest = SPLIT - FZ
-    wide = [
-        (fa.at[:, pl.ds(0, FZ)], G1.at[rows, pl.ds(pl.multiple_of(fz, 128), FZ)]),
-        (fa.at[:, pl.ds(FZ, rest)], G3.at[rows, pl.ds(pl.multiple_of(fz, 128), rest)]),
-        (fb, G3.at[rows, pl.ds(pl.multiple_of(fz + rest, 128), FZ - rest)]),
-    ]
-    leg_z = [k.send(src, dst, to) for src, dst in wide for to in zs]
-    heres = [k.local(src, dst) for src, dst in wide]
+    mq = pl.ds(pl.multiple_of(MZ * z, 128), MZ)
+    leg_x = [k.send(pq, GQ.at[rows, mq], other)]
+    heres = [k.local(pq, GQ.at[rows, mq])]
+    turned()
     col = pl.ds(pl.multiple_of(128 * (c * 8 + z * 2 + xl), 128), 128)
-    cols = pl.ds(pl.multiple_of(128 * (c * 8 + z * 2), 256), 256)
-    half = pl.ds(pl.multiple_of(1024 * c, 1024), 1024)
-    mq = pl.ds(pl.multiple_of(MZ * z, 128), MZ)
-    tall = [(f2, G2.at[:, col]), (fo, GO.at[:, col]), (fq, GQ.at[rows, mq])]
-    leg_x = [k.send(src, dst, other) for src, dst in tall]
-    tall_here = [k.local(src, dst) for src, dst in tall]
+    leg_x.append(k.send(to_, GO.at[:, col], other))
+    heres.append(k.local(to_, GO.at[:, col]))
+    for cp in gain_z:
+        cp.wait_recv()
+    s3[0] = (s2[0] + s2[1]) + (s2[2] + s2[3])
+    gain_x = k.send(s3.at[0], s3.at[1], other)
     for cp in leg_x:
         cp.wait_recv()
-    for cp in tall_here:
+    for cp in heres:
         cp.wait()
-    parts = [G2.at[:, cols], GO.at[:, cols], GQ.at[pair, mq]]
-    leg_xz = [k.send(part, part, to) for part in parts for to in zs]
-    for cp in gain_y:
-        cp.wait_recv()
-    gain_here.wait()
-    s1[0] = s0[0] + s0[1] + s0[2] + s0[3]
-    cp = k.send(s1.at[0, 1 - xh], s1.at[1, 0], cross)
-    cp.wait_recv()
-    s2[z] = s1[0, xh] + s1[1, 0]
-    gain_z = [k.send(s2.at[z], s2.at[z], to) for to in zs]
-    for cp in gain_z:
-        cp.wait_recv()
-    s3[0] = s2[0] + s2[1] + s2[2] + s2[3]
-    cp = k.send(s3.at[0], s3.at[1], other)
-    cp.wait_recv()
+    refs = [GQ.at[pair, mq], GO.at[:, pl.ds(pl.multiple_of(128 * (c * 8 + z * 2), 256), 256)]]
+    leg_xz = [k.send(ref, ref, to) for ref in refs for to in zs]
+    state = sum_start(k, q, part, pass_top, pass_low, D2.at[0], D2.at[1])
+    gain_x.wait_recv()
     s4[0] = s3[0] + s3[1]
-    cp = k.send(s4.at[0], s4.at[1], mate)
-    cp.wait_recv()
+    gain_c = k.send(s4.at[0], s4.at[1], mate)
+    sum_pass(k, q, part, pass_top, pass_low, send_top, send_low, D2.at[0], D2.at[1], state)
+    gain_c.wait_recv()
     total[...] = s4[0] + s4[1]
     gain_done = k.local(total, gain_out)
-    for cp in leg_z:
-        cp.wait_recv()
-    for cp in heres:
-        cp.wait()
-    leg_zx = [k.send(ref.at[rows], ref.at[rows], other) for ref in (G1, G3)]
     for cp in leg_xz:
         cp.wait_recv()
-    parts = [G2.at[:, half], GO.at[:, half], GQ.at[pair]]
-    last = [k.send(part, part, mate) for part in parts]
-    for cp in leg_zx:
-        cp.wait_recv()
-    last += [k.send(ref.at[pair], ref.at[pair], mate) for ref in (G1, G3)]
+    refs = [GQ.at[pair], GO.at[:, pl.ds(pl.multiple_of(1024 * c, 1024), 1024)]]
+    last = [k.send(ref, ref, mate) for ref in refs]
     for cp in last:
         cp.wait_recv()
+    sum_end(state)
     gain_done.wait()
     k.close()
 
 
 PARAMS = pltpu.CompilerParams(vmem_limit_bytes=VMEM_LIMIT)
+
+
+def add4(a, b, c, d):
+    a, b, c, d = (v.astype(F32) for v in (a, b, c, d))
+    return ((a + b) + (c + d)).astype(BF)
 
 
 def to_pieces(v):
@@ -708,25 +916,6 @@
     )(xl, dkv, received, cosine, sine)
 
 
-def resid_kernel(x, a, b, c, d, gain, h, n2):
-    total = x[...].astype(F32) + (
-        (a[...].astype(F32) + b[...].astype(F32)) + (c[...].astype(F32) + d[...].astype(F32))
-    )
-    h[...] = total
-    scale = lax.rsqrt(jnp.mean(total * total, axis=-1, keepdims=True) + EPS)
-    n2[...] = to_pieces((total * scale * gain[...]).astype(BF))
-
-
-def resid(x, parts, gain):
-    return pl.pallas_call(
-        resid_kernel,
-        name="resid",
-        cost_estimate=cost(3),
-        out_shape=[jax.ShapeDtypeStruct((TOK, D), F32), jax.ShapeDtypeStruct((TOK, D), BF)],
-        compiler_params=PARAMS,
-    )(x, *parts, gain)
-
-
 def rms_back(v, gain, grad):
     scale = lax.rsqrt(jnp.mean(v * v, axis=-1, keepdims=True) + EPS)
     unit = v * scale
@@ -735,10 +924,9 @@
     return scale * (inner - unit * jnp.mean(inner * unit, axis=-1, keepdims=True)), gain_grad
 
 
-def norm_back_kernel(v, base, a, b, c, d, gain, grad, *outs):
-    dn = from_pieces(
-        (a[...].astype(F32) + b[...].astype(F32)) + (c[...].astype(F32) + d[...].astype(F32))
-    )
+def norm_back_kernel(n, v, base, *refs):
+    parts, gain, grad, outs = refs[:n], refs[n], refs[n + 1], refs[n + 2 :]
+    dn = from_pieces(functools.reduce(jnp.add, [p[...].astype(F32) for p in parts]))
     back, gain_grad = rms_back(v[...].astype(F32), gain[...], dn)
     total = base[...].astype(F32) + back
     grad[...] = total
@@ -753,7 +941,7 @@
         shapes.append(jax.ShapeDtypeStruct((TOK, D), BF))
     shapes.append(jax.ShapeDtypeStruct((1, D), F32))
     return pl.pallas_call(
-        norm_back_kernel,
+        functools.partial(norm_back_kernel, len(parts)),
         name="norm_back",
         cost_estimate=cost(4),
         out_shape=shapes,
@@ -771,21 +959,12 @@
     return [pick(v, at, dim)] + got
 
 
-def add(parts):
-    a, b, c, d = (p.astype(F32) for p in parts)
-    return ((a + b) + (c + d)).astype(BF)
-
-
-def scatter_cols(v, q, axis, width):
-    at = q[axis]
-    cut = lambda j: lax.dynamic_slice_in_dim(v, j * width, width, 1)
-    return [cut(at)] + [move(cut((at + s) % 4), axis, s) for s in (1, 3, 2)]
-
-
-def scatter_quarters(v, q, rows):
-    cut = lambda j: lax.dynamic_slice(v, ((j // 2) * rows, (j % 2) * 128), (rows, 128))
-    at = q["x"]
-    return [cut(at)] + [move(cut((at + s) % 4), "x", s) for s in (1, 3, 2)]
+def add(*parts):
+    return functools.reduce(jnp.add, [p.astype(F32) for p in parts]).astype(BF)
+
+
+def cut(v, j, width):
+    return lax.dynamic_slice_in_dim(v, j * width, width, 1)
 
 
 def dot(a, b):
@@ -806,13 +985,13 @@
     vz = wqkv[:, QDIM + KVDIM :].reshape(256, 4, HEAD_DIM)
     wq = jnp.concatenate([heads, kz, vz], axis=2).reshape(256, 4 * MZ)
 
-    X, SEG, GN, WQ, WO, A1, A3, AX, AY = talk(
+    X, SEG, GN, WQ, WO, A1, A3 = talk(
         fetch_kernel,
         "fetch",
         1,
         30,
         80,
-        (x, seg, gn, wq, wo, w1, w3, w2),
+        (x, seg, gn, wq, wo, w1, w3),
         [
             ((RING, TOK, D), BF),
             ((2, 4, 2, 8, TOK), jnp.int32),
@@ -821,11 +1000,8 @@
             ((2, 256, D), BF),
             ((2, 2, 64, FZ), BF),
             ((4, 64, FZ), BF),
-            ((2, 2, 352, 128), BF),
-            ((4, 352, 128), BF),
         ],
         scratch=[
-            pltpu.VMEM((704, 128), BF),
             pltpu.VMEM((256, 128), BF),
             pltpu.VMEM((64, MZ), BF),
             pltpu.VMEM((64, FZ), BF),
@@ -833,10 +1009,10 @@
         ],
         near=(0, 1, 2),
     )
-    legs = lambda v, axis: [v] + [move(v, axis, s) for s in (1, 3, 2)]
-    a1, a3 = legs(A1, "y"), legs(A3, "x")
-    ax, ay = legs(AX, "y"), legs(AY, "x")
-    gs = legs(g, "z")
+    a1 = [A1] + [move(A1, "y", s) for s in (1, 3)]
+    a3 = [A3] + [move(A3, "x", s) for s in (1, 3)]
+    t2 = lax.dynamic_slice_in_dim(w2, 128 * (c * 8 + z * 2 + xl), 128, 1)
+    t2 = lax.ppermute(t2, ("dp", "ctx"), swap_pairs())
 
     docs = SEG[:, :, :, 0, :].reshape(16 * TOK)
     mine = pick(pick(SEG[:, :, :, 0, :], xl, 0), c, 1)
@@ -861,32 +1037,34 @@
         kv_kernel, "kv", 2, 7, 4, (kv,), [((2, 4, 2, TOK, 128), BF)], near=(0,)
     )
     KV = KV.reshape(16, TOK, 128)
+    KV, t2, a1, a3, g = lax.optimization_barrier((KV, t2, a1, a3, g))
+    gs = [g] + [move(g, "z", s) for s in (1, 3, 2)]
     heads_out, logsum = attend(info, query, KV, start)
     o = heads_out.reshape(RING * TOK, QZ)
     part = dot(o, WO).astype(BF).reshape(RING, TOK, D)
-    h, n2 = resid(x, scatter(part, q, "z", 0), gain_ffn)
-
-    N2, G, W13, W2 = talk(
-        assemble_kernel,
-        "assemble",
+    N2, h, G, W13, W2 = talk(
+        middle_kernel,
+        "middle",
         3,
-        27,
+        45,
         110,
-        (n2, *gs, *a1, *a3, *ax, *ay),
+        (part, x, gain_ffn, t2, *a1, *a3, *gs),
         [
             ((RING, TOK, D), BF),
+            ((TOK, D), F32),
             ((RING, TOK, D), BF),
             ((2, 4, 2, 2, 64, 2 * FZ), BF),
             ((2, 704, D), BF),
         ],
         scratch=[
+            *[pltpu.VMEM(HALF, BF)] * 4,
+            *[pltpu.VMEM((TOK, D), BF)] * 3,
+            pltpu.VMEM((3, 2, 2, 64, FZ), BF),
+            pltpu.VMEM((3, 4, 64, FZ), BF),
             pltpu.VMEM((4, TOK, D), BF),
-            pltpu.VMEM((4, 2, 2, 64, FZ), BF),
-            pltpu.VMEM((4, 4, 64, FZ), BF),
-            pltpu.VMEM((4, 2, 2, 352, 128), BF),
-            pltpu.VMEM((4, 4, 352, 128), BF),
-        ],
-        near=(0,),
+        ],
+        near=(0, 1, 2, 3),
+        near_out=(1,),
     )
     N2, G = N2.reshape(RING * TOK, D), G.reshape(RING * TOK, D)
     W13, W2 = W13.reshape(D, 2 * FZ), W2.reshape(FZ, D)
@@ -909,18 +1087,28 @@
     sum13 = (outer(half(N2, c), both) + other13.astype(F32)).astype(BF)
     sum2 = (outer(hidden, half(G, c)) + other2.astype(F32)).astype(BF)
     sum13 = sum13.reshape(4, 4, 64, 2 * FZ)
-    fa = add(scatter(sum13[..., :SPLIT], q, "x", 1))
-    fa = add(scatter(fa, q, "y", 0))
-    fb = add(scatter(sum13[..., SPLIT:], q, "y", 0))
-    fb = add(scatter(fb, q, "x", 0))
-    f2 = add(scatter_cols(sum2, q, "y", 256))
-    f2 = add(scatter_quarters(f2, q, 704))
-    f2 = lax.ppermute(f2, ("dp", "ctx"), swap_pairs())
+    sum_a, sum_b = sum13[..., :SPLIT], sum13[..., SPLIT:]
 
     dh, dhb, gain2 = norm_back(h, g, dn2_parts, gain_ffn, True)
-    (DH,) = talk(
-        gather_kernel, "gather", 4, 27, 4, (dhb,), [((RING, TOK, D), BF)], near=(0,)
-    )
+    DH, Ra, Rb, R2 = talk(
+        gather_kernel,
+        "gather",
+        4,
+        30,
+        20,
+        (dhb, sum_a, sum_b, sum2),
+        [
+            ((RING, TOK, D), BF),
+            ((2, 4, 64, SPLIT), BF),
+            ((2, 4, 64, 2 * FZ - SPLIT), BF),
+            ((2, 1408, 256), BF),
+        ],
+        near=(0,),
+    )
+    DH, sum_a, sum_b, sum2 = lax.optimization_barrier((DH, sum_a, sum_b, sum2))
+    far_a = move(pick(sum_a, (xx + 2) % 4, 1), "x", 2)
+    far_b = move(pick(sum_b, (y + 2) % 4), "y", 2)
+    far_2 = move(cut(sum2, (y + 2) % 4, 256), "y", 2)
     DH = DH.reshape(RING * TOK, D)
     dheads = jnp.einsum("td,qd->tq", DH, WO, preferred_element_type=F32).astype(BF)
     dquery, dkv = attend_back(
@@ -935,38 +1123,71 @@
     dmixed = jnp.concatenate([dquery, dkv_rot], axis=2).reshape(RING * TOK, MZ)
     dn1 = jnp.einsum("tc,dc->td", dmixed, WQ, preferred_element_type=F32)
     dn1 = dn1.astype(BF).reshape(RING, TOK, D)
-    input_grad, gain1 = norm_back(x, dh, scatter(dn1, q, "z", 0), gain_attn, False)
-
+
+    fa = add(pick(sum_a, xx, 1), Ra[0], Ra[1], far_a)
+    fb = add(pick(sum_b, y), Rb[0], Rb[1], far_b)
+    f2 = add(cut(sum2, y, 256), R2[0], R2[1], far_2)
     n1 = n1.reshape(RING * TOK, D)
+    other_o = move(outer(o, half(DH, 1 - c)).astype(BF), "c", 1)
+    sum_o = (outer(o, half(DH, c)) + other_o.astype(F32)).astype(BF)
     other_q = move(outer(half(n1, 1 - c), dmixed).astype(BF), "c", 1)
-    other_o = move(outer(o, half(DH, 1 - c)).astype(BF), "c", 1)
     sum_q = (outer(half(n1, c), dmixed) + other_q.astype(F32)).astype(BF)
-    sum_o = (outer(o, half(DH, c)) + other_o.astype(F32)).astype(BF)
-    fq = add(scatter(sum_q.reshape(4, 4, 64, MZ), q, "x", 1))
-    fq = add(scatter(fq, q, "y", 0))
-    fo = add(scatter_cols(sum_o, q, "y", 256))
-    fo = add(scatter_quarters(fo, q, 256))
-    fo = lax.ppermute(fo, ("dp", "ctx"), swap_pairs())
+    sum_q = sum_q.reshape(4, 4, 64, MZ)
+    rest = 2 * FZ - SPLIT
+    D1, G1, G3, G2, Rq, Ro = talk(
+        wide_kernel,
+        "wide",
+        6,
+        50,
+        90,
+        (dn1, fa, fb, f2, sum_q, sum_o),
+        [
+            ((2, TOK, D), BF),
+            ((256, 4 * FZ), BF),
+            ((256, 4 * FZ), BF),
+            ((704, D), BF),
+            ((3, 4, 64, MZ), BF),
+            ((3, 512, 256), BF),
+        ],
+        scratch=[
+            *[pltpu.VMEM(HALF, BF)] * 4,
+            pltpu.VMEM((3, 64, SPLIT), BF),
+            pltpu.VMEM((3, 64, rest), BF),
+            pltpu.VMEM((3, 704, 128), BF),
+            pltpu.VMEM((64, SPLIT), BF),
+            pltpu.VMEM((64, rest), BF),
+            pltpu.VMEM((704, 128), BF),
+            pltpu.VMEM((704, 128), BF),
+        ],
+        near=(0, 1, 2, 3),
+    )
+    input_grad, gain1 = norm_back(x, dh, (pick(dn1, z), D1[0], D1[1]), gain_attn, False)
+    fq = add(pick(sum_q, xx, 1), Rq[0], Rq[1], Rq[2])
+    fo = add(cut(sum_o, y, 256), Ro[0], Ro[1], Ro[2])
 
     gains = jnp.concatenate([gain1, gain2], axis=0).reshape(2, 8, 256).transpose(1, 0, 2)
     gains = jnp.pad(gains, ((0, 0), (0, 6), (0, 0))).reshape(4, 2, 8, 256)
     small = (8, 256)
-    G1, G3, G2, GO, GQ, gain_out = talk(
-        spread_kernel,
-        "spread",
-        6,
-        50,
+    D3, GO, GQ, gain_out = talk(
+        last_kernel,
+        "last",
+        7,
+        30,
         60,
-        (fa, fb, f2, fo, fq, gains),
+        (out_part, fq, fo, gains),
         [
-            ((256, 4 * FZ), BF),
-            ((256, 4 * FZ), BF),
-            ((704, D), BF),
+            ((2, TOK, D), BF),
             ((256, D), BF),
             ((256, 4 * MZ), BF),
             (small, F32),
         ],
         scratch=[
+            *[pltpu.VMEM(HALF, BF)] * 4,
+            pltpu.VMEM((3, 64, MZ), BF),
+            pltpu.VMEM((3, 256, 128), BF),
+            pltpu.VMEM((64, MZ), BF),
+            pltpu.VMEM((256, 128), BF),
+            pltpu.VMEM((256, 128), BF),
             pltpu.VMEM((4, 2) + small, F32),
             pltpu.VMEM((2, 2) + small, F32),
             pltpu.VMEM((4,) + small, F32),
@@ -974,15 +1195,15 @@
             pltpu.VMEM((2,) + small, F32),
             pltpu.VMEM(small, F32),
         ],
-        near=(0, 1, 2, 3, 4, 5),
+        near=(0, 1, 2, 3),
     )
     GQ = GQ.astype(F32).reshape(256, 4, MZ)
     flat = lambda v: v.reshape(256, -1)
     grad_qkv = jnp.concatenate(
         [flat(GQ[:, :, :QZ]), flat(GQ[:, :, QZ : QZ + 64]), flat(GQ[:, :, QZ + 64 :])], axis=1
     )
-    out_parts = [p.astype(F32) for p in scatter(out_part, q, "z", 0)]
-    output = h + ((out_parts[0] + out_parts[1]) + (out_parts[2] + out_parts[3]))
+    own = pick(out_part, z).astype(F32)
+    output = h + (own + (D3[0].astype(F32) + D3[1].astype(F32)))
     return (
         output[None],
         input_grad[None],

time: 674 us -> 519 us (0.77)
  waiting for transfers between devices: 174 us -> 36.9 us
  starting transfers between devices: 73.8 us -> 35.4 us
  local copies, waits for them, and re-layouts: 26 us -> 34.6 us
  other arithmetic: 25.1 us -> 32.3 us
    ppermute x61 -> x17, waiting for transfers between devices: 174 us -> 36.9 us  [move(): return lax.ppermute(v, ('dp', 'ctx'), shift_pairs(axis, by))]
    ppermute x61 -> x17, starting transfers between devices: 72.4 us -> 34.8 us  [move(): return lax.ppermute(v, ('dp', 'ctx'), shift_pairs(axis, by))]
    pallas_call x6 -> x7, Pallas kernels: 247 us -> 257 us  [talk(): pl.pallas_call(kernel, name=name, out_shape=[jax.ShapeDtypeStruct(s, t) f...]
  transfers between devices with their start and end apart: 63 -> 18, of which waited for: 28 -> 4; matrix products, arithmetic and copies ran while one was open for 9% -> 8% of each run, Pallas kernels for 15% -> 6%
where the time goes in v2:
time: 519 us; the launch traced here: 509 us
  Pallas kernels  306 us (59%)
  matrix products  62.8 us (12%)
  waiting for transfers between devices  36.9 us (7%)
  starting transfers between devices  35.4 us (7%)
  local copies, waits for them, and re-layouts  34.6 us (7%)
  other arithmetic  32.3 us (6%)
    pallas_call x7, Pallas kernels, talk(): pl.pallas_call(kernel, name=name, out_shape=[jax.ShapeDtypeStruct(s, t) f...  257 us
    ppermute x17, waiting for transfers between devices, move(): return lax.ppermute(v, ('dp', 'ctx'), shift_pairs(axis, by))  36.9 us
    ppermute x17, starting transfers between devices, move(): return lax.ppermute(v, ('dp', 'ctx'), shift_pairs(axis, by))  34.8 us
    dot_general x8, matrix products, body(): jnp.einsum('ta,tb->ab', a, b, preferred_element_type=F32)  24.3 us
    pallas_call x1, Pallas kernels, attend_back(): pl.pallas_call(attend_back_kernel, name='attend_back', cost_estimate=cost...  17.4 us
    dot_general x4, matrix products, dot(): return jnp.dot(a, b, preferred_element_type=F32)  17.3 us
    pallas_call x1, Pallas kernels, attend(): pl.pallas_call(attend_kernel, name='attend', cost_estimate=cost(12), grid...  14.5 us
  transfers between devices with their start and end apart: 18, of which 4 were waited for; matrix products, arithmetic and copies ran while one was open for 8% of the time, Pallas kernels for 6%

profile of v2, /device:TPU:1, one launch (start us, length us, event | category | flops | bytes accessed | tf_op | source)
XLA Modules:
  0.0 509.3 jit_solution(7518187716561151779)
XLA Ops:
  11.9 42.3 %fetch.1 = (bf16[4,128,2048]{2,1,0:T(8,128)(2,1)}, s32[2,4,2,8,128]{4,3,2,1,0:T(8,128)}, bf16[4,2,32,256]{3,2,1,0:T(8,128)(2,1)}, bf16[2,4,2,2,64,640]{5,4,3,2,1...) custom-call(bf16[128,2048]{1,0:T(8,128)(2,1)} %bitcast.178, ...), custom_call_target="tpu_custom_call" | custom-call | flops 30000001024 | tf_op jit(solution)/shard_map/fetch/pallas_call | solution.py:232
  65.6 7.2 %project.1 = (bf16[4,128,2048]{2,1,0:T(8,128)(2,1)}, bf16[4,128,512]{2,1,0:T(8,128)(2,1)}, bf16[4,128,128]{2,1,0:T(8,128)(2,1)}) custom-call(bf16[4,128,2048]{2,1,0:T(8,128)(2,1)} %get-tuple-element.61.x, f32[1,2048]{1,0:T(1,128)} %convert.16.gain.refs_3_, bf16[2048,640]{1,0:T(8,128)(2,1)} %bitcast.188, f32[4,128,128]{2,1,0:T(8,128)} %get-tuple-element.129.cosine, ...), custom_call_target="tpu_custom_call" | custom-call | flops 7000000000 | tf_op jit(solution)/shard_map/project/pallas_call | solution.py:711
  72.9 5.8 %kv.1 = bf16[2,4,2,128,128]{4,3,2,1,0:T(8,128)(2,1)} custom-call(bf16[4,128,128]{2,1,0:T(8,128)(2,1)} %get-tuple-element.65.kv), custom_call_target="tpu_custom_call" | custom-call | flops 7000000000 | tf_op jit(solution)/shard_map/kv/pallas_call | solution.py:232
  83.7 13.2 %collective-permute-start.7 = (bf16[128,2048]{1,0:T(8,128)(2,1)S(1)}, bf16[128,2048]{1,0:T(8,128)(2,1)S(1)}, u32[]{:S(2)}, u32[]{:S(2)}) collective-permute-start(bf16[128,2048]{1,0:T(8,128)(2,1)S(1)} %bitcast.177), channel_id=1, source_target_pairs={{0,4},{1,5},{2,6},{3,7},{4,0},{5,1},{6,2},{7,3},{8,12},{9,13},{10,... | collective-permute-start | bytes 1572872 | tf_op jit(solution)/shard_map/ppermute | solution.py:71
  96.9 14.5 %attend.1 = (bf16[4,128,512]{2,1,0:T(8,128)(2,1)}, f32[4,1,1024]{2,1,0:T(1,128)}) custom-call(s32[2,4]{1,0:T(2,128)} %pad_add_fusion.info, bf16[4,128,512]{2,1,0:T(8,128)(2,1)} %get-tuple-element.64.query, bf16[16,128,128]{2,1,0:T(8,128)(2,1)} %bitcast.209, s32[4,1,128]{2,1,0:T(1,128)} %bitcast.167), custom_call_target="tpu_custom_call" | custom-call | flops 12000000000 | tf_op jit(solution)/shard_map/attend/pallas_call | solution.py:800
  116.2 50.4 %middle.1 = (bf16[4,128,2048]{2,1,0:T(8,128)(2,1)}, f32[128,2048]{1,0:T(8,128)}, bf16[4,128,2048]{2,1,0:T(8,128)(2,1)}, bf16[2,4,2,2,64,2816]{5,4,3,2,1,0:T(8,128)(2,1)}, bf16[2,704,2048]{2,1,0:T(8,128)(2,1)}) custom-call(bf16[4,128,2048]{2,1,0:T(8,128)(2,1)} %bitcast.204, bf16[128,2048]{1,0:T(8,128)(2,1)} %bitcast.179, f32[1,2048]{1,0:T(1,128)} %convert.15.refs_2_.refs_4_, ...), custom_call_target="tpu_custom_call" | custom-call | flops 44999999488 | tf_op jit(solution)/shard_map/middle/pallas_call | solution.py:232
  166.6 6.6 %fusion.46 = f32[512,1408]{1,0:T(8,128)S(1)} fusion(bf16[512,2048]{1,0:T(8,128)(2,1)} %bitcast.198, bf16[1408,2048]{1,0:T(8,128)(2,1)} %bitcast.184), kind=kOutput, calls=%fused_computation.105 | convolution fusion | flops 2952790016 | bytes 10747904 | tf_op jit(solution)/shard_map/td,fd->tf/dot_general | solution.py:1074
  177.1 5.6 %multiply_convert_fusion.1 = (bf16[512,1408]{1,0:T(8,128)(2,1)S(1)}, bf16[512,1408]{1,0:T(8,128)(2,1)}, bf16[512,1408]{1,0:T(8,128)(2,1)S(1)}) fusion(f32[512,1408]{1,0:T(8,128)S(1)} %fusion.46, f32[512,1408]{1,0:T(8,128)S(1)} %fusion, bf16[512,2048]{1,0:T(8,128)(2,1)S(1)} %bitcast.195, bf16[2048,2816]{1,0:T(8,128)(2,1)S(1)} %bitcast.183), kind=kOutput, calls=%fused_computation.15 | convolution fusion | flops 2964324352 | bytes 17956864 | tf_op jit(solution)/shard_map/dot_general | solution.py:971
  182.8 5.1 convolution_convert_fusion
  191.7 9.1 %convolution_convert_fusion.2 = bf16[512,2048]{1,0:T(8,128)(2,1)S(1)} fusion(bf16[2048,2816]{1,0:T(8,128)(2,1)} %bitcast.181, bf16[512,1408]{1,0:T(8,128)(2,1)S(1)} %copy-done.48, bf16[512,1408]{1,0:T(8,128)(2,1)S(1)} %copy-done.45), kind=kOutput, calls=%fused_computation.9 | convolution fusion | flops 5912395776 | bytes 16515072 | tf_op jit(solution)/shard_map/tf,df->td/dot_general | solution.py:1079
  206.3 4.6 convolution_convert_fusion.5
  210.9 5.3 %collective-permute-done.8.refs_1_ = bf16[128,2048]{1,0:T(8,128)(2,1)S(1)} collective-permute-done((bf16[128,2048]{1,0:T(8,128)(2,1)S(1)}, bf16[128,2048]{1,0:T(8,128)(2,1)S(1)}, u32[]{:S(2)}, u32[]{:S(2)}) %collective-permute-start.8) | collective-permute-done | bytes 524320 | tf_op jit(solution)/shard_map/ppermute | solution.py:71
  216.2 11.6 %collective-permute-done.10.refs_3_ = bf16[128,2048]{1,0:T(8,128)(2,1)S(1)} collective-permute-done((bf16[128,2048]{1,0:T(8,128)(2,1)S(1)}, bf16[128,2048]{1,0:T(8,128)(2,1)S(1)}, u32[]{:S(2)}, u32[]{:S(2)}) %collective-permute-start.10) | collective-permute-done | bytes 524320 | tf_op jit(solution)/shard_map/ppermute | solution.py:71
  228.6 4.0 norm_back.2
  232.6 5.1 add_convert_fusion.1.s2
  237.7 5.4 %add_convert_fusion = bf16[1024,2816]{1,0:T(8,128)(2,1)S(1)} fusion(bf16[1024,2816]{1,0:T(8,128)(2,1)} %collective-permute-done.11, bf16[512,2048]{1,0:T(8,128)(2,1)S(1)} %bitcast.197, s32[]{:T(128)S(6)} %select_n.168, bf16[512,1408]{1,0:T(8,128)(2,1)S(1)} %copy-done.49, bf16[512,1408]{1,0:T(8,128)(2,1)S(1)} %copy-done.46), kind=kOutput, calls=%fused_computation | convolution fusion | flops 2967207936 | bytes 15466500 | tf_op jit(solution)/shard_map/ta,tb->ab/dot_general | solution.py:1084
  247.0 29.0 %gather.1 = (bf16[4,128,2048]{2,1,0:T(8,128)(2,1)}, bf16[2,4,64,2048]{3,2,1,0:T(8,128)(2,1)}, bf16[2,4,64,768]{3,2,1,0:T(8,128)(2,1)}, bf16[2,1408,256]{2,1,0:T(8,128)(2,1)}) custom-call(bf16[128,2048]{1,0:T(8,128)(2,1)} %get-tuple-element.85.v, bf16[4,4,64,2048]{3,2,1,0:T(8,128)(2,1)} %slice.127.sa, bf16[4,4,64,768]{3,2,1,0:T(8,128)(2,1)} %slice.128.sb, ...), custom_call_target="tpu_custom_call" | custom-call | flops 30000001024 | tf_op jit(solution)/shard_map/gather/pallas_call | solution.py:232
  279.7 17.4 %attend_back.1 = (bf16[4,128,512]{2,1,0:T(8,128)(2,1)}, bf16[16,128,128]{2,1,0:T(8,128)(2,1)}) custom-call(s32[2,4]{1,0:T(2,128)} %pad_add_fusion.info, bf16[4,128,512]{2,1,0:T(8,128)(2,1)} %get-tuple-element.64.query, bf16[16,128,128]{2,1,0:T(8,128)(2,1)} %bitcast.210, s32[4,1,128]{2,1,0:T(1,128)} %bitcast.168, bf16[4,128,512]{2,1,0:T(8,128)(2,1)} %get-tuple-element.69.out, ...), custom_call_target="tpu_custom_call" | custom-call | flops 15000000512 | tf_op jit(solution)/shard_map/attend_back/pallas_call | solution.py:868
  298.7 8.5 %dkv.1.received = bf16[3,4,128,128]{3,2,1,0:T(8,128)(2,1)} custom-call(bf16[2,4,2,128,128]{4,3,2,1,0:T(8,128)(2,1)} %bitcast.164), custom_call_target="tpu_custom_call" | custom-call | flops 8000000000 | tf_op jit(solution)/shard_map/dkv/pallas_call | solution.py:232
  322.5 5.4 %collective-permute-done.15 = bf16[4,64,768]{2,1,0:T(8,128)(2,1)S(1)} collective-permute-done((bf16[4,64,768]{2,1,0:T(8,128)(2,1)S(1)}, bf16[4,64,768]{2,1,0:T(8,128)(2,1)S(1)}, u32[]{:S(2)}, u32[]{:S(2)}) %collective-permute-start.15) | collective-permute-done | bytes 393248 | tf_op jit(solution)/shard_map/ppermute | solution.py:71
  328.9 14.5 %collective-permute-done.16 = bf16[1408,256]{1,0:T(8,128)(2,1)S(1)} collective-permute-done((bf16[1408,256]{1,0:T(8,128)(2,1)S(1)}, bf16[1408,256]{1,0:T(8,128)(2,1)S(1)}, u32[]{:S(2)}, u32[]{:S(2)}) %collective-permute-start.16) | collective-permute-done | bytes 720928 | tf_op jit(solution)/shard_map/ppermute | solution.py:71
  350.2 75.4 %wide.1 = (bf16[2,128,2048]{2,1,0:T(8,128)(2,1)}, bf16[256,5632]{1,0:T(8,128)(2,1)}, bf16[256,5632]{1,0:T(8,128)(2,1)}, bf16[704,2048]{1,0:T(8,128)(2,1)}, bf16[...) custom-call(bf16[4,128,2048]{2,1,0:T(8,128)(2,1)} %bitcast.155, bf16[4,64,2048]{2,1,0:T(8,128)(2,1)} %fusion.5.fa, ...), custom_call_target="tpu_custom_call" | custom-call | flops 49999998976 | tf_op jit(solution)/shard_map/wide/pallas_call | solution.py:232
  430.9 3.7 norm_back.3
  436.0 45.3 %last.1 = (bf16[2,128,2048]{2,1,0:T(8,128)(2,1)}, bf16[256,2048]{1,0:T(8,128)(2,1)}, bf16[256,2560]{1,0:T(8,128)(2,1)}, f32[8,256]{1,0:T(8,128)}) custom-call(bf16[4,128,2048]{2,1,0:T(8,128)(2,1)} %bitcast.156, bf16[4,64,640]{2,1,0:T(8,128)(2,1)} %fusion.24.fq, bf16[512,256]{1,0:T(8,128)(2,1)} %fusion.25.fo, f32[4,2,8,256]{3,2,1,0:T(8,128)} %bitcast.160), custom_call_target="tpu_custom_call" | custom-call | flops 30000001024 | tf_op jit(solution)/shard_map/last/pallas_call | solution.py:232
  (205 shorter events, 112.7 us)
Async XLA Ops:
  0.6 59.4 %copy-start = (bf16[704,2048]{1,0:T(8,128)(2,1)S(1)}, bf16[704,2048]{1,0:T(8,128)(2,1)}, u32[]{:S(2)}) copy-start(bf16[704,2048]{1,0:T(8,128)(2,1)} %param.19) | copy-start | bytes 8650756
  54.2 25.7 %collective-permute-start.1 = (bf16[2,2,64,1408]{3,2,1,0:T(8,128)(2,1)}, bf16[2,2,64,1408]{3,2,1,0:T(8,128)(2,1)}, u32[]{:S(2)}, u32[]{:S(2)}) collective-permute-start(bf16[2,2,64,1408]{3,2,1,0:T(8,128)(2,1)} %get-tuple-element.72.refs_4_), channel_id=1, source_target_pairs={{0,32},{1,33},{2,34},{3,35},{4,36},{5,37},{6,38},{7,39},{8,40},{9,... | collective-permute-start | bytes 2162696 | tf_op jit(solution)/shard_map/ppermute | solution.py:71
  54.8 25.1 %collective-permute-start.2 = (bf16[2,2,64,1408]{3,2,1,0:T(8,128)(2,1)}, bf16[2,2,64,1408]{3,2,1,0:T(8,128)(2,1)}, u32[]{:S(2)}, u32[]{:S(2)}) collective-permute-start(bf16[2,2,64,1408]{3,2,1,0:T(8,128)(2,1)} %get-tuple-element.72.refs_4_), channel_id=1, source_target_pairs={{0,96},{1,97},{2,98},{3,99},{4,100},{5,101},{6,102},{7,103},{8,104... | collective-permute-start | bytes 2162696 | tf_op jit(solution)/shard_map/ppermute | solution.py:71
  56.9 23.0 %collective-permute-start.3 = (bf16[4,64,1408]{2,1,0:T(8,128)(2,1)}, bf16[4,64,1408]{2,1,0:T(8,128)(2,1)}, u32[]{:S(2)}, u32[]{:S(2)}) collective-permute-start(bf16[4,64,1408]{2,1,0:T(8,128)(2,1)} %get-tuple-element.75.refs_7_), channel_id=1, source_target_pairs={{0,8},{1,9},{2,10},{3,11},{4,12},{5,13},{6,14},{7,15},{8,16},{9,17... | collective-permute-start | bytes 2162696 | tf_op jit(solution)/shard_map/ppermute | solution.py:71
  59.1 20.8 %collective-permute-start.4 = (bf16[4,64,1408]{2,1,0:T(8,128)(2,1)}, bf16[4,64,1408]{2,1,0:T(8,128)(2,1)}, u32[]{:S(2)}, u32[]{:S(2)}) collective-permute-start(bf16[4,64,1408]{2,1,0:T(8,128)(2,1)} %get-tuple-element.75.refs_7_), channel_id=1, source_target_pairs={{0,24},{1,25},{2,26},{3,27},{4,28},{5,29},{6,30},{7,31},{8,0},{9,1... | collective-permute-start | bytes 2162696 | tf_op jit(solution)/shard_map/ppermute | solution.py:71
  60.1 19.8 %collective-permute-start = (bf16[704,128]{1,0:T(8,128)(2,1)S(1)}, bf16[704,128]{1,0:T(8,128)(2,1)S(1)}, u32[]{:S(2)}, u32[]{:S(2)}) collective-permute-start(bf16[704,128]{1,0:T(8,128)(2,1)S(1)} %constant_dynamic-slice_fusion.1), channel_id=1, source_target_pairs={{0,0},{1,1},{2,32},{3,33},{4,64},{5,65},{6,96},{7,97},{8,8},{9,9},... | collective-permute-start | bytes 540680 | tf_op jit(solution)/shard_map/ppermute | solution.py:1015
  79.9 31.5 %copy-start.31 = (bf16[704,128]{1,0:T(8,128)(2,1)}, bf16[704,128]{1,0:T(8,128)(2,1)S(1)}, u32[]{:S(2)}) copy-start(bf16[704,128]{1,0:T(8,128)(2,1)S(1)} %collective-permute-done.refs_3_) | copy-start | bytes 540676
  80.0 35.1 %collective-permute-start.5 = (bf16[128,2048]{1,0:T(8,128)(2,1)S(1)}, bf16[128,2048]{1,0:T(8,128)(2,1)S(1)}, u32[]{:S(2)}, u32[]{:S(2)}) collective-permute-start(bf16[128,2048]{1,0:T(8,128)(2,1)S(1)} %bitcast.175), channel_id=1, source_target_pairs={{0,2},{1,3},{2,4},{3,5},{4,6},{5,7},{6,0},{7,1},{8,10},{9,11},{10,... | collective-permute-start | bytes 1572872 | tf_op jit(solution)/shard_map/ppermute | solution.py:71
  82.6 32.4 %collective-permute-start.6 = (bf16[128,2048]{1,0:T(8,128)(2,1)S(1)}, bf16[128,2048]{1,0:T(8,128)(2,1)S(1)}, u32[]{:S(2)}, u32[]{:S(2)}) collective-permute-start(bf16[128,2048]{1,0:T(8,128)(2,1)S(1)} %bitcast.176), channel_id=1, source_target_pairs={{0,6},{1,7},{2,0},{3,1},{4,2},{5,3},{6,4},{7,5},{8,14},{9,15},{10,... | collective-permute-start | bytes 1572872 | tf_op jit(solution)/shard_map/ppermute | solution.py:71
  83.7 31.3 %collective-permute-start.7 = (bf16[128,2048]{1,0:T(8,128)(2,1)S(1)}, bf16[128,2048]{1,0:T(8,128)(2,1)S(1)}, u32[]{:S(2)}, u32[]{:S(2)}) collective-permute-start(bf16[128,2048]{1,0:T(8,128)(2,1)S(1)} %bitcast.177), channel_id=1, source_target_pairs={{0,4},{1,5},{2,6},{3,7},{4,0},{5,1},{6,2},{7,3},{8,12},{9,13},{10,... | collective-permute-start | bytes 1572872 | tf_op jit(solution)/shard_map/ppermute | solution.py:71
  187.8 49.9 %collective-permute-start.11 = (bf16[1024,2816]{1,0:T(8,128)(2,1)}, bf16[1024,2816]{1,0:T(8,128)(2,1)}, u32[]{:S(2)}, u32[]{:S(2)}) collective-permute-start(bf16[1024,2816]{1,0:T(8,128)(2,1)} %convolution_convert_fusion), channel_id=1, source_target_pairs={{0,1},{1,0},{2,3},{3,2},{4,5},{5,4},{6,7},{7,6},{8,9},{9,8},{10,11... | collective-permute-start | bytes 17301512 | tf_op jit(solution)/shard_map/ppermute | solution.py:71
  188.0 18.3 %slice-start.1 = ((s8[5767168]{0:T(1024)(128)(4,1)}), s8[4194304]{0:T(1024)(128)(4,1)S(1)}, s32[]{:S(2)}) async-start(s8[5767168]{0:T(1024)(128)(4,1)} %bitcast.185), calls=%async_computation.1 | async-start | bytes 8388608
  191.3 41.4 %collective-permute-start.12 = (bf16[1408,1024]{1,0:T(8,128)(2,1)S(1)}, bf16[1408,1024]{1,0:T(8,128)(2,1)S(1)}, u32[]{:S(2)}, u32[]{:S(2)}) collective-permute-start(bf16[1408,1024]{1,0:T(8,128)(2,1)S(1)} %convolution_convert_fusion.1), channel_id=1, source_target_pairs={{0,1},{1,0},{2,3},{3,2},{4,5},{5,4},{6,7},{7,6},{8,9},{9,8},{10,11... | collective-permute-start | bytes 8650760 | tf_op jit(solution)/shard_map/ppermute | solution.py:71
  201.7 14.4 %collective-permute-start.8 = (bf16[128,2048]{1,0:T(8,128)(2,1)S(1)}, bf16[128,2048]{1,0:T(8,128)(2,1)S(1)}, u32[]{:S(2)}, u32[]{:S(2)}) collective-permute-start(bf16[128,2048]{1,0:T(8,128)(2,1)S(1)} %get-tuple-element.118), channel_id=1, source_target_pairs={{0,2},{1,3},{2,4},{3,5},{4,6},{5,7},{6,0},{7,1},{8,10},{9,11},{10,... | collective-permute-start | bytes 1572872 | tf_op jit(solution)/shard_map/ppermute | solution.py:71
  202.7 13.4 %collective-permute-start.9 = (bf16[128,2048]{1,0:T(8,128)(2,1)S(1)}, bf16[128,2048]{1,0:T(8,128)(2,1)S(1)}, u32[]{:S(2)}, u32[]{:S(2)}) collective-permute-start(bf16[128,2048]{1,0:T(8,128)(2,1)S(1)} %get-tuple-element.117), channel_id=1, source_target_pairs={{0,6},{1,7},{2,0},{3,1},{4,2},{5,3},{6,4},{7,5},{8,14},{9,15},{10,... | collective-permute-start | bytes 1572872 | tf_op jit(solution)/shard_map/ppermute | solution.py:71
  204.4 23.4 %collective-permute-start.10 = (bf16[128,2048]{1,0:T(8,128)(2,1)S(1)}, bf16[128,2048]{1,0:T(8,128)(2,1)S(1)}, u32[]{:S(2)}, u32[]{:S(2)}) collective-permute-start(bf16[128,2048]{1,0:T(8,128)(2,1)S(1)} %get-tuple-element.116), channel_id=1, source_target_pairs={{0,4},{1,5},{2,6},{3,7},{4,0},{5,1},{6,2},{7,3},{8,12},{9,13},{10,... | collective-permute-start | bytes 1572872 | tf_op jit(solution)/shard_map/ppermute | solution.py:71
  247.0 29.0 %copy-start.35 = (bf16[2,256,2048]{2,1,0:T(8,128)(2,1)S(1)}, bf16[2,256,2048]{2,1,0:T(8,128)(2,1)}, u32[]{:S(2)}) copy-start(bf16[2,256,2048]{2,1,0:T(8,128)(2,1)} %get-tuple-element.70) | copy-start | bytes 6291460
  313.5 32.9 %collective-permute-start.14 = (bf16[4,64,2048]{2,1,0:T(8,128)(2,1)S(1)}, bf16[4,64,2048]{2,1,0:T(8,128)(2,1)S(1)}, u32[]{:S(2)}, u32[]{:S(2)}) collective-permute-start(bf16[4,64,2048]{2,1,0:T(8,128)(2,1)S(1)} %dynamic-slice_bitcast_fusion), channel_id=1, source_target_pairs={{0,16},{1,17},{2,18},{3,19},{4,20},{5,21},{6,22},{7,23},{8,24},{9,... | collective-permute-start | bytes 3145736 | tf_op jit(solution)/shard_map/ppermute | solution.py:71
  316.1 11.8 %collective-permute-start.15 = (bf16[4,64,768]{2,1,0:T(8,128)(2,1)S(1)}, bf16[4,64,768]{2,1,0:T(8,128)(2,1)S(1)}, u32[]{:S(2)}, u32[]{:S(2)}) collective-permute-start(bf16[4,64,768]{2,1,0:T(8,128)(2,1)S(1)} %dynamic-slice_bitcast_fusion.6), channel_id=1, source_target_pairs={{0,64},{1,65},{2,66},{3,67},{4,68},{5,69},{6,70},{7,71},{8,72},{9,... | collective-permute-start | bytes 1179656 | tf_op jit(solution)/shard_map/ppermute | solution.py:71
  317.4 25.9 %collective-permute-start.16 = (bf16[1408,256]{1,0:T(8,128)(2,1)S(1)}, bf16[1408,256]{1,0:T(8,128)(2,1)S(1)}, u32[]{:S(2)}, u32[]{:S(2)}) collective-permute-start(bf16[1408,256]{1,0:T(8,128)(2,1)S(1)} %constant_dynamic-slice_fusion), channel_id=1, source_target_pairs={{0,64},{1,65},{2,66},{3,67},{4,68},{5,69},{6,70},{7,71},{8,72},{9,... | collective-permute-start | bytes 2162696 | tf_op jit(solution)/shard_map/ppermute | solution.py:71
  319.3 25.4 %collective-permute-start.17 = (bf16[512,1024]{1,0:T(8,128)(2,1)S(1)}, bf16[512,1024]{1,0:T(8,128)(2,1)S(1)}, u32[]{:S(2)}, u32[]{:S(2)}) collective-permute-start(bf16[512,1024]{1,0:T(8,128)(2,1)S(1)} %convolution_convert_fusion.7), channel_id=1, source_target_pairs={{0,1},{1,0},{2,3},{3,2},{4,5},{5,4},{6,7},{7,6},{8,9},{9,8},{10,11... | collective-permute-start | bytes 3145736 | tf_op jit(solution)/shard_map/ppermute | solution.py:71
  321.5 21.9 %copy-start.10 = (bf16[2,1408,256]{2,1,0:T(8,128)(2,1)S(1)}, bf16[2,1408,256]{2,1,0:T(8,128)(2,1)}, u32[]{:S(2)}) copy-start(bf16[2,1408,256]{2,1,0:T(8,128)(2,1)} %get-tuple-element.96) | copy-start | bytes 4325380
  321.5 26.6 %collective-permute-start.13 = (bf16[1024,640]{1,0:T(8,128)(2,1)S(1)}, bf16[1024,640]{1,0:T(8,128)(2,1)S(1)}, u32[]{:S(2)}, u32[]{:S(2)}) collective-permute-start(bf16[1024,640]{1,0:T(8,128)(2,1)S(1)} %convolution_convert_fusion.6), channel_id=1, source_target_pairs={{0,1},{1,0},{2,3},{3,2},{4,5},{5,4},{6,7},{7,6},{8,9},{9,8},{10,11... | collective-permute-start | bytes 3932168 | tf_op jit(solution)/shard_map/ppermute | solution.py:71
  328.9 15.8 %copy-start.42 = (bf16[4,128,512]{2,1,0:T(8,128)(2,1)S(1)}, bf16[4,128,512]{2,1,0:T(8,128)(2,1)}, u32[]{:S(2)}) copy-start(bf16[4,128,512]{2,1,0:T(8,128)(2,1)} %get-tuple-element.69.out) | copy-start | bytes 1572868
  (47 other events, 231.7 us)

commit v3 on v2

v3 whole, which is shorter than its diff:
```python
import functools

import jax
import jax.numpy as jnp
from jax import lax
from jax.experimental import pallas as pl
from jax.experimental.pallas import tpu as pltpu
from jax.sharding import PartitionSpec as P

D = 2048
HEAD_DIM = 64
TOK = 128
RING = 4
QDIM = 2048
KVDIM = 256
GROUP = 8
QZ = 512
MZ = 640
FZ = 1408
SPLIT = 2048
EPS = 1e-05
THETA = 10000.0
MESH = pl.DeviceIdType.MESH
VMEM_LIMIT = 56 << 20
BF = jnp.bfloat16
F32 = jnp.float32
ANY = pl.BlockSpec(memory_space=pl.ANY)
VMEM = pl.BlockSpec(memory_space=pltpu.VMEM)


def coords():
    dp, ctx = lax.axis_index("dp"), lax.axis_index("ctx")
    y, xh = dp // 2, dp % 2
    xl, z, c = ctx // 8, (ctx // 2) % 4, ctx % 2
    return dict(y=y, x=xh * 2 + xl, xh=xh, xl=xl, z=z, c=c)


def device(q, **change):
    r = {k: change.get(k, q[k]) for k in ("y", "x", "z", "c")}
    return (r["y"] * 2 + r["x"] // 2, (r["x"] % 2) * 8 + r["z"] * 2 + r["c"])


def ring(q, axis):
    return [device(q, **{axis: (q[axis] + s) % 4}) for s in (1, 3, 2)]


def shift_pairs(axis, by):
    size = 2 if axis == "c" else 4
    pairs = []
    for y in range(4):
        for x in range(4):
            for z in range(4):
                for c in range(2):
                    q = dict(y=y, x=x, z=z, c=c)
                    pairs.append((device(q), device(q, **{axis: (q[axis] + by) % size})))
    return [(a[0] * 16 + a[1], b[0] * 16 + b[1]) for a, b in pairs]


def swap_pairs():
    pairs = []
    for y in range(4):
        for x in range(4):
            for z in range(4):
                for c in range(2):
                    q = dict(y=y, x=x, z=z, c=c)
                    pairs.append((device(q), device(q, y=z, z=y)))
    return [(a[0] * 16 + a[1], b[0] * 16 + b[1]) for a, b in pairs]


def move(v, axis, by):
    return lax.ppermute(v, ("dp", "ctx"), shift_pairs(axis, by))


class Copies:
    def __init__(self, send_sems, recv_sems):
        self.send_sems, self.recv_sems, self.n, self.open = send_sems, recv_sems, 0, []

    def send(self, src, dst, to):
        cp = pltpu.make_async_remote_copy(
            src_ref=src,
            dst_ref=dst,
            send_sem=self.send_sems.at[self.n],
            recv_sem=self.recv_sems.at[self.n],
            device_id=to,
            device_id_type=MESH,
        )
        cp.start()
        self.n += 1
        self.open.append(cp)
        return cp

    def local(self, src, dst):
        cp = pltpu.make_async_copy(src, dst, self.send_sems.at[self.n])
        cp.start()
        self.n += 1
        return cp

    def close(self):
        for cp in self.open:
            cp.wait_send()


def deal(k, q, src, col, dst):
    y, z = q["y"], q["z"]
    n = k.n
    k.n += 4
    copies = [
        pltpu.make_async_remote_copy(
            src_ref=src.at[:, col((y + s) % 4)],
            dst_ref=dst,
            send_sem=k.send_sems.at[n + i],
            recv_sem=k.recv_sems.at[n],
            device_id=to,
            device_id_type=MESH,
        )
        for i, (s, to) in enumerate(zip((1, 3, 2), ring(q, "y")))
    ]
    here = pltpu.make_async_copy(src.at[:, col(y)], dst, k.send_sems.at[n + 3])

    @pl.when(y == z)
    def _():
        for cp in copies:
            cp.start()
        here.start()

    def wait():
        @pl.when(y == z)
        def _():
            for cp in copies:
                cp.wait_send()
            here.wait()

        @pl.when(y != z)
        def _():
            copies[0].wait_recv()

    return wait


def greet(targets, q=None):
    barrier = pltpu.get_barrier_semaphore()
    for to in targets:
        pl.semaphore_signal(barrier, inc=1, device_id=to, device_id_type=MESH)
    if q is None:
        pl.semaphore_wait(barrier, len(targets))
    else:
        y, z = q["y"], q["z"]

        @pl.when(y != z)
        def _():
            to = device(q, y=z, z=y)
            pl.semaphore_signal(barrier, inc=1, device_id=to, device_id_type=MESH)

        pl.semaphore_wait(barrier, len(targets) + (y != z).astype(jnp.int32))


TOP, LOW = pl.ds(0, TOK // 2), pl.ds(TOK // 2, TOK // 2)
HALF = (TOK // 2, D)


class Gather:
    def __init__(self, k, q, axis, src, dst):
        at = q[axis]
        self.k, self.dst = k, dst
        self.above, self.below, self.far = (at + 1) % 4, (at + 3) % 4, (at + 2) % 4
        self.up, self.down = device(q, **{axis: self.above}), device(q, **{axis: self.below})
        self.low0 = k.send(src(0), dst(at, 0), self.up)
        self.top1 = k.send(src(1), dst(at, 1), self.down)
        self.low1 = k.send(src(1), dst(at, 1), self.up)
        self.top0 = k.send(src(0), dst(at, 0), self.down)

    def relay(self):
        self.low0.wait_recv()
        ref = self.dst(self.below, 0)
        self.far0 = self.k.send(ref, ref, self.up)
        self.top1.wait_recv()
        ref = self.dst(self.above, 1)
        self.far1 = self.k.send(ref, ref, self.down)

    def near(self):
        self.low1.wait_recv()
        self.top0.wait_recv()

    def end(self):
        self.far0.wait_recv()
        self.far1.wait_recv()


class Sum:
    def __init__(self, k, q, axis, block, below, above, passed):
        at = q[axis]
        self.k, self.below, self.above, self.passed = k, below, above, passed
        up, down, far = (at + 1) % 4, (at + 3) % 4, (at + 2) % 4
        self.up, self.down = device(q, **{axis: up}), device(q, **{axis: down})
        self.first = k.send(block(far, 0), passed[0], self.up)
        self.second = k.send(block(far, 1), passed[1], self.down)
        self.rest = [
            k.send(block(up, 1), below(1), self.up),
            k.send(block(down, 0), above(0), self.down),
        ]

    def relay(self, own0, own1, sent):
        self.first.wait_recv()
        sent[0][...] = (self.passed[0][...].astype(F32) + own0[...].astype(F32)).astype(BF)
        self.rest.append(self.k.send(sent[0], self.below(0), self.up))
        self.second.wait_recv()
        sent[1][...] = (self.passed[1][...].astype(F32) + own1[...].astype(F32)).astype(BF)
        self.rest.append(self.k.send(sent[1], self.above(1), self.down))

    def end(self):
        for cp in self.rest:
            cp.wait_recv()

    def sent(self):
        for cp in self.rest[2:]:
            cp.wait_send()
            self.k.open = [o for o in self.k.open if o is not cp]


def halves(ref):
    return lambda h: ref.at[(TOP, LOW)[h]]


def ring_halves(ref):
    return lambda j, h: ref.at[j, (TOP, LOW)[h]]


def turn(k, q, moves):
    y, z = q["y"], q["z"]
    swap = device(q, y=z, z=y)
    pairs = []
    for src, dst in moves:
        n = k.n
        k.n += 1
        remote = pltpu.make_async_remote_copy(
            src_ref=src,
            dst_ref=dst,
            send_sem=k.send_sems.at[n],
            recv_sem=k.recv_sems.at[n],
            device_id=swap,
            device_id_type=MESH,
        )
        pairs.append((remote, pltpu.make_async_copy(src, dst, k.send_sems.at[n])))

    @pl.when(y != z)
    def _():
        for remote, _ in pairs:
            remote.start()

    @pl.when(y == z)
    def _():
        for _, here in pairs:
            here.start()

    def wait():
        @pl.when(y != z)
        def _():
            for remote, _ in pairs:
                remote.wait_recv()
                remote.wait_send()

        @pl.when(y == z)
        def _():
            for _, here in pairs:
                here.wait()

    return wait


def cost(us):
    return pl.CostEstimate(flops=int(us * 1e9), bytes_accessed=0, transcendentals=0)


def talk(kernel, name, cid, us, copies, ins, outs, scratch=(), near=(), near_out=(), alias={}):
    return pl.pallas_call(
        kernel,
        name=name,
        out_shape=[jax.ShapeDtypeStruct(s, t) for s, t in outs],
        in_specs=[VMEM if i in near else ANY for i in range(len(ins))],
        out_specs=[VMEM if i in near_out else ANY for i in range(len(outs))],
        scratch_shapes=[
            *scratch,
            pltpu.SemaphoreType.DMA((copies,)),
            pltpu.SemaphoreType.DMA((copies,)),
        ],
        cost_estimate=cost(us),
        input_output_aliases=alias,
        compiler_params=pltpu.CompilerParams(
            collective_id=cid, has_side_effects=True, vmem_limit_bytes=VMEM_LIMIT
        ),
    )(*ins)


def fetch_kernel(
    x, g, seg, na, nf, wq, wo, w1, w3, w2, X, G, SEG, GN, WQ, WO, W13, T2,
    TO, TV, QP, KT, VT, P1, P3, SG, NG, ss, rs,
):
    q = coords()
    y, xx, xh, xl, z, c = q["y"], q["x"], q["xh"], q["xl"], q["z"], q["c"]
    zs, ys, xs = ring(q, "z"), ring(q, "y"), ring(q, "x")
    mate = device(q, c=1 - c)
    other = device(q, x=xx ^ 1)
    other_mate = device(q, x=xx ^ 1, c=1 - c)
    k = Copies(ss, rs)
    rows = pl.ds(pl.multiple_of(128 * c + 64 * xl, 64), 64)
    qcols = pl.ds(pl.multiple_of(QZ * z, 128), QZ)
    tile = 128 * (z // 2)
    kcols = pl.ds(pl.multiple_of(QDIM + tile, 128), 128)
    vcols = pl.ds(pl.multiple_of(QDIM + KVDIM + tile, 128), 128)
    fcols = pl.ds(pl.multiple_of(FZ * z, 128), FZ)
    loads = [
        k.local(wq.at[rows, qcols], QP.at[:, pl.ds(0, QZ)]),
        k.local(wq.at[rows, kcols], KT),
        k.local(wq.at[rows, vcols], VT),
        k.local(w1.at[rows, fcols], P1),
        k.local(w3.at[rows, fcols], P3),
    ]
    SG[...] = jnp.broadcast_to(seg[...], (8, TOK))
    NG[0:16] = jnp.broadcast_to(na[...].astype(F32), (16, 256)).astype(BF)
    NG[16:32] = jnp.broadcast_to(nf[...].astype(F32), (16, 256)).astype(BF)
    greet(zs + ys + xs + [mate, other_mate])
    lanes = lambda j, n=1: pl.ds(pl.multiple_of(128 * j, 128 * n), 128 * n)
    dealt = deal(k, q, wo, lambda j: lanes(c * 8 + j * 2 + xl), TO)
    x_ring = Gather(k, q, "z", halves(x), ring_halves(X))
    for cp in loads:
        cp.wait()
    odd = z % 2 == 1
    kt, vt = KT[...].astype(F32), VT[...].astype(F32)
    lane = lax.broadcasted_iota(jnp.int32, kt.shape, 1)
    kt = jnp.where(odd, pltpu.roll(kt, 64, 1), kt)
    vt = jnp.where(odd, vt, pltpu.roll(vt, 64, 1))
    QP[:, QZ:] = jnp.where(lane < HEAD_DIM, kt, vt).astype(BF)
    f1, f3 = pl.ds(0, FZ), pl.ds(FZ, FZ)
    top, low = pl.ds(0, 32), pl.ds(32, 32)
    q_top = [k.send(QP.at[top], WQ.at[c, y, xh, xl, top], to) for to in xs]
    q_low = [k.send(QP.at[low], WQ.at[c, y, xh, xl, low], to) for to in ys]
    seg_z = [k.send(SG, SEG.at[xl, z, c], to) for to in zs]
    gn_y = [k.send(NG, GN.at[y, xh], to) for to in ys]
    q_here = k.local(QP, WQ.at[c, y, xh, xl])
    seg_here = k.local(SG, SEG.at[xl, z, c])
    gn_here = k.local(NG, GN.at[y, xh])
    a3_here = k.local(P3, W13.at[c, y, xh, xl, :, f3])
    heres = [
        k.local(P1, W13.at[c, y, xh, xl, :, f1]),
        k.local(x, X.at[z]),
        k.local(g, G.at[z]),
    ]
    dealt()
    o1 = [k.send(TO, WO.at[xh, :, lanes(c * 8 + y * 2 + xl)], to) for to in xs]
    o1_here = k.local(TO, WO.at[xh, :, lanes(c * 8 + y * 2 + xl)])
    thirty = lambda h: pl.ds(32 * h, 32)
    up_y = Gather(
        k, q, "y", lambda h: P3.at[thirty(h)], lambda j, h: W13.at[c, j, xh, xl, thirty(h), f3]
    )
    gate_x = Gather(
        k, q, "x", lambda h: P1.at[thirty(h)],
        lambda j, h: W13.at[c, y, j // 2, j % 2, thirty(h), f1],
    )
    q_here.wait()
    for cp in q_top:
        cp.wait_recv()
    q_y = Gather(k, q, "y", lambda h: WQ.at[c, y, h, :, top], lambda j, h: WQ.at[c, j, h, :, top])
    for cp in q_low:
        cp.wait_recv()
    q_half = lambda j, h: WQ.at[c, pl.ds(2 * h, 2), j // 2, j % 2, low]
    q_x = Gather(k, q, "x", lambda h: q_half(xx, h), q_half)
    for cp in seg_z:
        cp.wait_recv()
    seg_here.wait()
    part = SEG.at[xl, :, c]
    seg2 = [k.send(part, part, to) for to in (mate, other, other_mate)]
    for cp in gn_y:
        cp.wait_recv()
    gn_here.wait()
    gn2 = k.send(GN.at[:, xh], GN.at[:, xh], device(q, x=3 - xx))
    x_ring.relay()
    g_ring = Gather(k, q, "z", halves(g), ring_halves(G))
    up_y.relay()
    gate_x.relay()
    for cp in o1:
        cp.wait_recv()
    o1_here.wait()
    o_half = lambda j, h: WO.at[h, :, lanes(c * 8 + j * 2, 2)]
    o_y = Gather(k, q, "y", lambda h: o_half(y, h), o_half)
    w2_dealt = deal(k, q, w2, lambda j: lanes(c * 8 + xl * 4 + j), TV)
    q_y.relay()
    q_x.relay()
    up_y.near()
    up_y.end()
    a3_here.wait()
    part = W13.at[c, :, xh, xl, :, f3]
    a3 = [k.send(part, part, to) for to in xs[:2]]
    o_y.relay()
    g_ring.relay()
    for r in (q_y, q_x):
        r.near()
        r.end()
    q3 = k.send(WQ.at[c], WQ.at[c], mate)
    o_y.near()
    o_y.end()
    part = WO.at[:, :, pl.ds(pl.multiple_of(1024 * c, 1024), 1024)]
    o3 = k.send(part, part, mate)
    w2_dealt()
    heres.append(k.local(TV, T2))
    for cp in a3 + seg2 + [gn2, q3, o3]:
        cp.wait_recv()
    for cp in heres:
        cp.wait()
    for r in (gate_x, x_ring, g_ring):
        r.near()
        r.end()
    k.close()


def kv_kernel(kv, KV, ss, rs):
    q = coords()
    xx, xl, c = q["x"], q["xl"], q["c"]
    mate = device(q, c=1 - c)
    other = device(q, x=xx ^ 1)
    greet([mate, other])
    k = Copies(ss, rs)
    here = k.local(kv, KV.at[xl, :, c])
    near = k.send(kv, KV.at[xl, :, c], mate)
    far = pltpu.make_async_remote_copy(
        src_ref=kv,
        dst_ref=KV.at[0, :, c],
        send_sem=ss.at[2],
        recv_sem=rs.at[2],
        device_id=other,
        device_id_type=MESH,
    )
    on = pltpu.make_async_remote_copy(
        src_ref=KV.at[0, :, c],
        dst_ref=KV.at[0, :, c],
        send_sem=ss.at[3],
        recv_sem=rs.at[3],
        device_id=mate,
        device_id_type=MESH,
    )

    @pl.when(xl == 0)
    def _():
        far.start()
        far.wait_send()

    @pl.when(xl == 1)
    def _():
        far.wait_recv()
        on.start()
        on.wait_recv()
        on.wait_send()

    here.wait()
    near.wait_recv()
    k.close()


def middle_kernel(
    part, x, gain, t2, _, N2, H, W13, W2, p0, p1, v0, v1, below, above, n2, ss, rs
):
    q = coords()
    y, xx, xh, xl, z, c = q["y"], q["x"], q["xh"], q["xl"], q["z"], q["c"]
    ys, xs = ring(q, "y"), ring(q, "x")
    up, down = device(q, z=(z + 1) % 4), device(q, z=(z + 3) % 4)
    mate = device(q, c=1 - c)
    k = Copies(ss, rs)
    greet(ys + xs + [up, down, mate])
    z_sum = Sum(k, q, "z", ring_halves(part), halves(below), halves(above), (p0, p1))
    f1, f3 = pl.ds(0, FZ), pl.ds(FZ, FZ)
    up1 = lambda j: W13.at[c, :, j // 2, j % 2, :, f3]
    up_half = lambda j, h: W13.at[c, pl.ds(2 * h, 2), j // 2, j % 2, :, f3]
    cols = lambda cc, j, n: pl.ds(pl.multiple_of(128 * (cc * 8 + j), 128 * n), 128 * n)
    w2_here = k.local(t2, W2.at[xh, :, cols(c, xl * 4 + y, 1)])
    w2y = Gather(
        k, q, "y", lambda h: t2.at[pl.ds(352 * h, 352)],
        lambda j, h: W2.at[xh, pl.ds(352 * h, 352), cols(c, xl * 4 + j, 1)],
    )
    lower, higher = (xx + 3) % 4, (xx + 1) % 4
    far = [
        k.send(up_half(lower, 0), up_half(lower, 0), xs[0]),
        k.send(up_half(higher, 1), up_half(higher, 1), xs[1]),
    ]
    sent = [k.send(up1(j), up1(j), mate) for j in (xx, lower, higher)]
    w2y.relay()
    block = lambda j: W13.at[c, j, :, :, :, f1]
    gate = Gather(
        k, q, "y", lambda h: W13.at[c, y, h, :, :, f1], lambda j, h: W13.at[c, j, h, :, :, f1]
    )
    sent.append(k.send(block(y), block(y), mate))
    z_sum.relay(part.at[(z + 1) % 4, TOP], part.at[(z + 3) % 4, LOW], (v0, v1))
    w2_here.wait()
    w2y.near()
    w2y.end()
    down2 = lambda j: W2.at[j // 2, :, cols(c, (j % 2) * 4, 4)]
    down_half = lambda j, h: W2.at[j // 2, pl.ds(352 * h, 352), cols(c, (j % 2) * 4, 4)]
    down_ring = Gather(k, q, "x", lambda h: down_half(xx, h), down_half)
    sent.append(k.send(down2(xx), down2(xx), mate))
    z_sum.end()
    total = x[...].astype(F32) + (
        part[z].astype(F32) + (below[...].astype(F32) + above[...].astype(F32))
    )
    H[...] = total
    scale = lax.rsqrt(jnp.mean(total * total, axis=-1, keepdims=True) + EPS)
    n2[...] = to_pieces((total * scale * gain[...]).astype(BF))
    n2_ring = Gather(k, q, "z", halves(n2), ring_halves(N2))
    n2_here = k.local(n2, N2.at[z])
    gate.relay()
    down_ring.relay()
    for cp in far:
        cp.wait_recv()
    ref = up1((xx + 2) % 4)
    sent.append(k.send(ref, ref, mate))
    gate.near()
    for j in (gate.below, gate.above):
        sent.append(k.send(block(j), block(j), mate))
    n2_ring.relay()
    gate.end()
    sent.append(k.send(block(gate.far), block(gate.far), mate))
    down_ring.near()
    for j in (down_ring.below, down_ring.above):
        sent.append(k.send(down2(j), down2(j), mate))
    down_ring.end()
    sent.append(k.send(down2(down_ring.far), down2(down_ring.far), mate))
    for cp in sent:
        cp.wait_recv()
    n2_here.wait()
    n2_ring.near()
    n2_ring.end()
    k.close()


def back_kernel(
    dn2, out_part, hidden, G, N2, both, h, gain, V, D3, FA, FB, F2, DH, GAIN, *scratch
):
    (
        p0, p1, p2, p3, v0, v1, below, above, near0, near1, mine, dhb, hv, gv, nv, bv, hT,
        mate2, mate13, sum2, sum13, *bufs, ss, rs,
    ) = scratch
    q = coords()
    y, xx, z, c = q["y"], q["x"], q["z"], q["c"]
    mate = device(q, c=1 - c)
    k = Copies(ss, rs)
    get_h, get_g = k.local(hidden, hv), k.local(G, gv)
    get_n, get_b = k.local(N2, nv), k.local(both, bv)
    get_part = [
        k.local(dn2.at[(z + 1) % 4, TOP], near0),
        k.local(dn2.at[(z + 3) % 4, LOW], near1),
        k.local(dn2.at[z], mine),
    ]
    targets = [mate]
    for axis in ("x", "y", "z"):
        targets += ring(q, axis)[:2]
    greet(targets)
    z_sum = Sum(k, q, "z", ring_halves(dn2), halves(below), halves(above), (p0, p1))
    get_h.wait()
    get_g.wait()
    hT[...] = hv[...].T
    lanes = lambda cc, j: pl.ds(pl.multiple_of(1024 * cc + 256 * j, 256), 256)
    sent2, sent13 = [], []
    for j in range(4):
        mate2[j] = dot(hT[...], gv[:, lanes(1 - c, j)]).astype(BF)
        sent2.append(k.send(mate2.at[j], sum2.at[j], mate))
    get_n.wait()
    get_b.wait()
    for j in range(4):
        mate13[j] = tn(nv[:, lanes(1 - c, j)], bv[...]).astype(BF).reshape(4, 64, 2 * FZ)
        sent13.append(k.send(mate13.at[j], sum13.at[j], mate))
        if j == 0:
            for cp in get_part:
                cp.wait()
            z_sum.relay(near0, near1, (v0, v1))
    z_sum.end()
    dn = from_pieces(
        mine[...].astype(F32) + (below[...].astype(F32) + above[...].astype(F32))
    )
    back, gain_grad = rms_back(h[...], gain[...], dn)
    total = gv[pl.ds(pl.multiple_of(TOK * z, TOK), TOK)].astype(F32) + back
    DH[...] = total
    GAIN[...] = gain_grad
    dhb[...] = total.astype(BF)
    v_ring = Gather(k, q, "z", halves(dhb), ring_halves(V))
    here = k.local(dhb, V.at[z])
    for j in range(4):
        sent2[j].wait_recv()
        sum2[j] = (dot(hT[...], gv[:, lanes(c, j)]) + sum2[j].astype(F32)).astype(BF)
    half = lambda ref: lambda i: ref.at[i]
    rest = 2 * FZ - SPLIT
    jobs = [
        ("y", lambda j, i: sum2.at[j, pl.ds(704 * i, 704)], F2),
        ("x", lambda j, i: sum13.at[pl.ds(2 * i, 2), j, :, pl.ds(0, SPLIT)], FA),
        ("y", lambda j, i: sum13.at[j, pl.ds(2 * i, 2), :, pl.ds(SPLIT, rest)], FB),
    ]
    sums = []

    def start(n):
        axis, block, _ = jobs[n]
        b = bufs[4 * n : 4 * n + 4]
        sums.append(Sum(k, q, axis, block, half(b[2]), half(b[3]), (b[0].at[0], b[0].at[1])))

    def relay(n):
        axis, block, _ = jobs[n]
        b = bufs[4 * n : 4 * n + 4]
        at = q[axis]
        sums[n].relay(block((at + 1) % 4, 0), block((at + 3) % 4, 1), (b[1].at[0], b[1].at[1]))

    start(0)
    for j in range(4):
        sent13[j].wait_recv()
        own = tn(nv[:, lanes(c, j)], bv[...]).reshape(4, 64, 2 * FZ)
        sum13[j] = (own + sum13[j].astype(F32)).astype(BF)
        if j == 1:
            v_ring.relay()
    start(1)
    start(2)
    out_sum = Sum(
        k, q, "z", ring_halves(out_part), halves(D3.at[0]), halves(D3.at[1]), (p2, p3)
    )
    get_part = [
        k.local(out_part.at[(z + 1) % 4, TOP], near0),
        k.local(out_part.at[(z + 3) % 4, LOW], near1),
    ]
    relay(0)
    relay(1)
    relay(2)
    for cp in get_part:
        cp.wait()
    z_sum.sent()
    out_sum.relay(near0, near1, (v0, v1))
    done = []
    for n in range(3):
        axis, block, out = jobs[n]
        b = bufs[4 * n : 4 * n + 4]
        sums[n].end()
        for i in range(2):
            total = block(q[axis], i)[...].astype(F32) + (
                b[2][i].astype(F32) + b[3][i].astype(F32)
            )
            b[2][i] = total.astype(BF)
        done.append(k.local(b[2], out))
    v_ring.near()
    v_ring.end()
    here.wait()
    out_sum.end()
    for cp in done:
        cp.wait()
    k.close()


def dkv_kernel(dkv, cosine, sine, out, R, ss, rs):
    q = coords()
    xx, xl, c = q["x"], q["xl"], q["c"]
    mate = device(q, c=1 - c)
    other = device(q, x=xx ^ 1)
    other_mate = device(q, x=xx ^ 1, c=1 - c)
    greet([mate, other, other_mate])
    k = Copies(ss, rs)
    near = k.send(dkv.at[xl, :, 1 - c], R.at[0], mate)
    far = [
        pltpu.make_async_remote_copy(
            src_ref=dkv.at[0, :, cc],
            dst_ref=R.at[1 + i],
            send_sem=ss.at[1 + i],
            recv_sem=rs.at[1 + i],
            device_id=to,
            device_id_type=MESH,
        )
        for i, (to, cc) in enumerate(((other, c), (other_mate, 1 - c)))
    ]

    @pl.when(xl == 1)
    def _():
        R[1] = jnp.zeros(R.shape[1:], BF)
        R[2] = jnp.zeros(R.shape[1:], BF)
        for cp in far:
            cp.start()
        for cp in far:
            cp.wait_send()

    @pl.when(xl == 0)
    def _():
        for cp in far:
            cp.wait_recv()

    near.wait_recv()
    for i in range(RING):
        w = dkv[xl, i, c].astype(F32) + R[0, i].astype(F32)
        w = w + (R[1, i].astype(F32) + R[2, i].astype(F32))
        lane = lax.broadcasted_iota(jnp.int32, w.shape, 1)
        out[i] = jnp.where(lane < HEAD_DIM, w * cosine[i] - swapped(w) * sine[i], w).astype(BF)
    k.close()


def quarter(xt, rows):
    return (
        pl.ds(pl.multiple_of((xt // 2) * rows, rows), rows),
        pl.ds(pl.multiple_of((xt % 2) * 128, 128), 128),
    )


def wide_kernel(
    dn, fa, fb, f2, sq, so, D2, G1, G3, G2, FQ, FO,
    p0, p1, v0, v1, la, lb, l2, pa, pb, p2, t2, rq, ro, ss, rs,
):
    q = coords()
    y, xx, xh, xl, z, c = q["y"], q["x"], q["xh"], q["xl"], q["z"], q["c"]
    zs, ys, xs = ring(q, "z"), ring(q, "y"), ring(q, "x")
    mate, other = device(q, c=1 - c), device(q, x=xx ^ 1)
    greet(zs + ys + xs + [mate], q)
    k = Copies(ss, rs)
    steps = (1, 3, 2)
    z_sum = Sum(k, q, "z", ring_halves(dn), halves(D2.at[0]), halves(D2.at[1]), (p0, p1))
    leg_2 = []
    for i, s in enumerate(steps):
        r, cc = quarter((xx + s) % 4, 704)
        leg_2.append(k.send(f2.at[r, cc], l2.at[i], xs[i]))
    leg_a = [k.send(fa.at[(y + s) % 4], la.at[i], ys[i]) for i, s in enumerate(steps)]
    leg_b = [k.send(fb.at[(xx + s) % 4], lb.at[i], xs[i]) for i, s in enumerate(steps)]
    z_sum.relay(dn.at[(z + 1) % 4, TOP], dn.at[(z + 3) % 4, LOW], (v0, v1))
    for cp in leg_2:
        cp.wait_recv()
    r, cc = quarter(xx, 704)
    p2[...] = add4(f2[r, cc], l2[0], l2[1], l2[2])
    turned = turn(k, q, [(p2, t2)])
    heavy = []
    for i, s in enumerate(steps):
        cols = pl.ds(pl.multiple_of(256 * ((y + s) % 4), 256), 256)
        heavy.append(k.send(so.at[:, cols], ro.at[i], ys[i]))
        heavy.append(k.send(sq.at[(y + s) % 4], rq.at[i], ys[i]))
    for cp in leg_a:
        cp.wait_recv()
    pa[...] = add4(fa[y], la[0], la[1], la[2])
    for cp in leg_b:
        cp.wait_recv()
    pb[...] = add4(fb[xx], lb[0], lb[1], lb[2])
    at = lambda zz, off, n: pl.ds(pl.multiple_of(FZ * zz + off, 128), n)
    rows = pl.ds(pl.multiple_of(128 * c + 64 * xl, 64), 64)
    pair = pl.ds(pl.multiple_of(128 * c, 128), 128)
    f1 = pl.ds(0, FZ)
    rest = SPLIT - FZ
    own = [
        (pa.at[:, f1], G1.at[rows, at(z, 0, FZ)]),
        (pa.at[:, pl.ds(FZ, rest)], G3.at[rows, at(z, 0, rest)]),
        (pb, G3.at[rows, at(z, rest, FZ - rest)]),
    ]
    half_rows = lambda h: pl.ds(pl.multiple_of(128 * c + 64 * xl + 32 * h, 32), 32)

    def over_z(src, ref, off, n):
        return Gather(
            k, q, "z", lambda h: src.at[pl.ds(32 * h, 32)],
            lambda j, h: ref.at[half_rows(h), at(j, off, n)],
        )

    rings = [
        over_z(pa.at[:, f1], G1, 0, FZ),
        over_z(pa.at[:, pl.ds(FZ, rest)], G3, 0, rest),
        over_z(pb, G3, rest, FZ - rest),
    ]
    to_x = [k.send(src, dst, other) for src, dst in own]
    heres = [k.local(src, dst) for src, dst in own]
    for r in rings:
        r.relay()
    turned()
    col = pl.ds(pl.multiple_of(128 * (c * 8 + z * 2 + xl), 128), 128)
    down_x = k.send(t2, G2.at[:, col], other)
    down_here = k.local(t2, G2.at[:, col])
    blocks = lambda j: [G1.at[rows, at(j, 0, FZ)], G3.at[rows, at(j, 0, FZ)]]
    for r in rings:
        r.near()
    for j in (rings[0].below, rings[0].above):
        to_x += [k.send(ref, ref, other) for ref in blocks(j)]
    down_x.wait_recv()
    down_here.wait()
    down_half = lambda j, h: G2.at[
        pl.ds(352 * h, 352), pl.ds(pl.multiple_of(128 * (c * 8 + j * 2), 256), 256)
    ]
    down_ring = Gather(k, q, "z", lambda h: down_half(z, h), down_half)
    for r in rings:
        r.end()
    to_x += [k.send(ref, ref, other) for ref in blocks(rings[0].far)]
    down_ring.relay()
    for cp in heavy:
        cp.wait_recv()
    cols = pl.ds(pl.multiple_of(256 * y, 256), 256)
    ro[0] = add4(so[:, cols], ro[0], ro[1], ro[2])
    rq[0] = add4(sq[y], rq[0], rq[1], rq[2])
    done = [k.local(ro.at[0], FO), k.local(rq.at[0], FQ)]
    down_ring.near()
    down_ring.end()
    ref = G2.at[:, pl.ds(pl.multiple_of(1024 * c, 1024), 1024)]
    last = [k.send(ref, ref, mate)]
    for cp in to_x:
        cp.wait_recv()
    for cp in heres:
        cp.wait()
    last += [k.send(ref.at[pair], ref.at[pair], mate) for ref in (G1, G3)]
    for cp in last:
        cp.wait_recv()
    for cp in done:
        cp.wait()
    z_sum.end()
    k.close()


def last_kernel(
    fq, fo, gain1, gain2, GO, GQ, GKV, gain_out,
    lq, lo, pq, po, to_, gain, s0, s1, s2, s3, s4, total, ss, rs,
):
    q = coords()
    y, xx, xh, xl, z, c = q["y"], q["x"], q["xh"], q["xl"], q["z"], q["c"]
    zs, ys, xs = ring(q, "z"), ring(q, "y"), ring(q, "x")
    mate, other, cross = device(q, c=1 - c), device(q, x=xx ^ 1), device(q, x=3 - xx)
    gain[...] = jnp.zeros_like(gain)
    for d in range(8):
        gain[d // 2, d % 2, 0:1] = gain1[:, 256 * d : 256 * d + 256]
        gain[d // 2, d % 2, 1:2] = gain2[:, 256 * d : 256 * d + 256]
    greet(zs + ys + xs + [mate], q)
    k = Copies(ss, rs)
    steps = (1, 3, 2)
    leg_o, leg_q = [], []
    for i, s in enumerate(steps):
        r, cc = quarter((xx + s) % 4, 256)
        leg_o.append(k.send(fo.at[r, cc], lo.at[i], xs[i]))
    gain_y = [k.send(gain.at[(y + s) % 4], s0.at[y], ys[i]) for i, s in enumerate(steps)]
    gain_here = k.local(gain.at[y], s0.at[y])
    for i, s in enumerate(steps):
        leg_q.append(k.send(fq.at[(xx + s) % 4], lq.at[i], xs[i]))
    for cp in leg_o:
        cp.wait_recv()
    r, cc = quarter(xx, 256)
    po[...] = add4(fo[r, cc], lo[0], lo[1], lo[2])
    turned = turn(k, q, [(po, to_)])
    for cp in gain_y:
        cp.wait_recv()
    gain_here.wait()
    s1[0] = (s0[0] + s0[1]) + (s0[2] + s0[3])
    gain_x = k.send(s1.at[0, 1 - xh], s1.at[1, 0], cross)
    for cp in leg_q:
        cp.wait_recv()
    pq[...] = add4(fq[xx], lq[0], lq[1], lq[2])
    rows = pl.ds(pl.multiple_of(128 * c + 64 * xl, 64), 64)
    qc = lambda j: pl.ds(pl.multiple_of(QZ * j, 128), QZ)
    kc = lambda j: pl.ds(pl.multiple_of(128 * j, 128), 128)
    own = [
        (pq.at[:, pl.ds(0, QZ)], GQ.at[rows, qc(z)]),
        (pq.at[:, pl.ds(QZ, 128)], GKV.at[rows, kc(z)]),
    ]
    q_x = [k.send(src, dst, other) for src, dst in own]
    q_here = [k.local(src, dst) for src, dst in own]
    gain_x.wait_recv()
    s2[z] = s1[0, xh] + s1[1, 0]
    gain_z = [k.send(s2.at[z], s2.at[z], to) for to in zs]
    turned()
    col = pl.ds(pl.multiple_of(128 * (c * 8 + z * 2 + xl), 128), 128)
    o_x = k.send(to_, GO.at[:, col], other)
    o_here = k.local(to_, GO.at[:, col])
    for cp in q_x:
        cp.wait_recv()
    for cp in q_here:
        cp.wait()
    half_rows = lambda h: pl.ds(pl.multiple_of(128 * c + 64 * h, 64), 64)
    q_half = lambda j, h: GQ.at[half_rows(h), qc(j)]
    kv_half = lambda j, h: GKV.at[half_rows(h), kc(j)]
    rings = [Gather(k, q, "z", lambda h: f(z, h), f) for f in (q_half, kv_half)]
    o_x.wait_recv()
    o_here.wait()
    o_half = lambda j, h: GO.at[
        pl.ds(128 * h, 128), pl.ds(pl.multiple_of(128 * (c * 8 + j * 2), 256), 256)
    ]
    rings.append(Gather(k, q, "z", lambda h: o_half(z, h), o_half))
    for cp in gain_z:
        cp.wait_recv()
    s3[0] = (s2[0] + s2[1]) + (s2[2] + s2[3])
    gain_x = k.send(s3.at[0], s3.at[1], other)
    for r in rings:
        r.relay()
    gain_x.wait_recv()
    s4[0] = s3[0] + s3[1]
    gain_c = k.send(s4.at[0], s4.at[1], mate)
    for r in rings:
        r.near()
        r.end()
    pair = pl.ds(pl.multiple_of(128 * c, 128), 128)
    refs = [GQ.at[pair], GKV.at[pair], GO.at[:, pl.ds(pl.multiple_of(1024 * c, 1024), 1024)]]
    last = [k.send(ref, ref, mate) for ref in refs]
    gain_c.wait_recv()
    total[...] = s4[0] + s4[1]
    gain_done = k.local(total, gain_out)
    for cp in last:
        cp.wait_recv()
    gain_done.wait()
    k.close()


PARAMS = pltpu.CompilerParams(vmem_limit_bytes=VMEM_LIMIT)


def add4(a, b, c, d):
    a, b, c, d = (v.astype(F32) for v in (a, b, c, d))
    return ((a + b) + (c + d)).astype(BF)


def to_pieces(v):
    return jnp.concatenate(
        [v[:, 256 * d + 128 * c : 256 * d + 128 * c + 128] for c in range(2) for d in range(8)],
        axis=1,
    )


def from_pieces(v):
    return jnp.concatenate(
        [v[:, 1024 * c + 128 * d : 1024 * c + 128 * d + 128] for d in range(8) for c in range(2)],
        axis=1,
    )


def swapped(u):
    lane = lax.broadcasted_iota(jnp.int32, u.shape, 1)
    return jnp.where(lane % 64 < 32, pltpu.roll(u, 96, 1), pltpu.roll(u, 32, 1))


def project_kernel(x, gain, w, cosine, sine, n1, query, kv):
    two = 2 * TOK
    xv = x[...].reshape(two, D).astype(F32)
    scale = lax.rsqrt(jnp.mean(xv * xv, axis=-1, keepdims=True) + EPS)
    normed = to_pieces((xv * scale * gain[...]).astype(BF))
    n1[...] = normed.reshape(2, TOK, D)
    cos, sin = cosine[...].reshape(two, 128), sine[...].reshape(two, 128)
    mixed = jnp.dot(normed, w[...], preferred_element_type=F32)
    for j in range(5):
        u = mixed[:, 128 * j : 128 * j + 128]
        turned = u * cos + swapped(u) * sin
        if j < 4:
            query[:, :, 128 * j : 128 * j + 128] = turned.astype(BF).reshape(2, TOK, 128)
        else:
            lane = lax.broadcasted_iota(jnp.int32, u.shape, 1)
            kv[...] = jnp.where(lane < HEAD_DIM, turned, u).astype(BF).reshape(2, TOK, 128)


def project(x, gain, w, cosine, sine):
    chunk = lambda cols: pl.BlockSpec((2, TOK, cols), lambda i: (i, 0, 0))
    whole = lambda shape: pl.BlockSpec(shape, lambda i: (0,) * len(shape))
    return pl.pallas_call(
        project_kernel,
        name="project",
        cost_estimate=cost(7),
        grid=(2,),
        in_specs=[chunk(D), whole((1, D)), whole((D, MZ)), chunk(128), chunk(128)],
        out_specs=[chunk(D), chunk(QZ), chunk(128)],
        out_shape=[
            jax.ShapeDtypeStruct((RING, TOK, D), BF),
            jax.ShapeDtypeStruct((RING, TOK, QZ), BF),
            jax.ShapeDtypeStruct((RING, TOK, 128), BF),
        ],
        compiler_params=PARAMS,
    )(x, gain, w, cosine, sine)


def stacked_low(tiles):
    out = []
    for pair in range(4):
        tile = tiles[:, 128 * pair : 128 * pair + 128].astype(F32)
        lane = lax.broadcasted_iota(jnp.int32, tile.shape, 1)
        out.append(jnp.where(lane < HEAD_DIM, tile, 0.0))
        out.append(jnp.where(lane < HEAD_DIM, pltpu.roll(tile, 64, 1), 0.0))
    return jnp.concatenate(out, axis=0)


def stacked_high(tiles):
    out = []
    for pair in range(4):
        tile = tiles[:, 128 * pair : 128 * pair + 128].astype(F32)
        lane = lax.broadcasted_iota(jnp.int32, tile.shape, 1)
        out.append(jnp.where(lane >= HEAD_DIM, pltpu.roll(tile, 64, 1), 0.0))
        out.append(jnp.where(lane >= HEAD_DIM, tile, 0.0))
    return jnp.concatenate(out, axis=0)


def unstacked(v):
    tiles = []
    for pair in range(4):
        both = jnp.concatenate(
            [v[:, 256 * pair : 256 * pair + 128], v[:, 256 * pair + 128 : 256 * pair + 256]],
            axis=0,
        )
        tiles.append(both.T)
    return tiles


def nt(a, b):
    return lax.dot_general(a, b, (((1,), (1,)), ((), ())), preferred_element_type=F32)


def tn(a, b):
    return lax.dot_general(a, b, (((0,), (0,)), ((), ())), preferred_element_type=F32)


def chunk_scores(keys, stacked, kc, chunk, start):
    raw = nt(keys, stacked)
    key = kc * TOK + lax.broadcasted_iota(jnp.int32, raw.shape, 0)
    query = chunk * TOK + lax.broadcasted_iota(jnp.int32, raw.shape, 1) % TOK
    return jnp.where((key <= query) & (key >= start), raw, -1e30)


def attend_kernel(info, query, kv, start, out, logsum):
    i = pl.program_id(0)
    low, chunk = info[0, i], info[1, i]
    stacked = (stacked_low(query[0]) * (1.0 / HEAD_DIM**0.5)).astype(BF)
    starts = jnp.concatenate([start[0]] * GROUP, axis=1)

    def step(kc, carry):
        top, summed, total = carry
        keys = kv[kc]
        scores = chunk_scores(keys, stacked, kc, chunk, starts)
        new_top = jnp.maximum(top, jnp.max(scores, axis=0, keepdims=True))
        weights = jnp.exp(scores - new_top)
        fade = jnp.exp(top - new_top)
        summed = summed * fade + jnp.sum(weights, axis=0, keepdims=True)
        part = tn(keys, weights.astype(BF))
        return new_top, summed, total * fade + part[HEAD_DIM:]

    rows = GROUP * TOK
    carry = (jnp.full((1, rows), -1e30, F32), jnp.zeros((1, rows), F32), jnp.zeros((64, rows), F32))
    top, summed, total = lax.fori_loop(low, chunk + 1, step, carry)
    for pair, tile in enumerate(unstacked(total / summed)):
        out[0, :, 128 * pair : 128 * pair + 128] = tile.astype(BF)
    logsum[0] = top + jnp.log(summed)


def attend(info, query, kv, start):
    chunk = lambda r, cols: pl.BlockSpec((1, r, cols), lambda i, s: (i, 0, 0))
    return pl.pallas_call(
        attend_kernel,
        name="attend",
        cost_estimate=cost(12),
        grid_spec=pltpu.PrefetchScalarGridSpec(
            num_scalar_prefetch=1,
            grid=(RING,),
            in_specs=[
                chunk(TOK, QZ),
                pl.BlockSpec((16, TOK, 128), lambda i, s: (0, 0, 0)),
                chunk(1, TOK),
            ],
            out_specs=[chunk(TOK, QZ), chunk(1, GROUP * TOK)],
        ),
        out_shape=[
            jax.ShapeDtypeStruct((RING, TOK, QZ), BF),
            jax.ShapeDtypeStruct((RING, 1, GROUP * TOK), F32),
        ],
        compiler_params=PARAMS,
    )(info, query, kv, start)


def attend_back_kernel(
    info, query, kv, start, out, grad_out, logsum, cosine, sine, dquery, dkv, total
):
    i = pl.program_id(0)
    low, chunk = info[0, i], info[1, i]
    stacked = (stacked_low(query[0]) * (1.0 / HEAD_DIM**0.5)).astype(BF)
    grads = stacked_high(grad_out[0]).astype(BF)
    starts = jnp.concatenate([start[0]] * GROUP, axis=1)
    lse = logsum[0]
    deltas = []
    for pair in range(4):
        cols = slice(128 * pair, 128 * pair + 128)
        prod = (out[0, :, cols].astype(F32) * grad_out[0, :, cols].astype(F32)).T
        deltas.append(jnp.sum(prod[:HEAD_DIM], axis=0, keepdims=True))
        deltas.append(jnp.sum(prod[HEAD_DIM:], axis=0, keepdims=True))
    delta = jnp.concatenate(deltas, axis=1)

    @pl.when(i == 0)
    def _():
        total[...] = jnp.zeros_like(total)

    def step(kc, dq):
        keys = kv[kc]
        scores = chunk_scores(keys, stacked, kc, chunk, starts)
        probs = jnp.exp(scores - lse)
        grad_probs = nt(keys, grads)
        grad_scores = (probs * (grad_probs - delta)).astype(BF)
        total[kc] += jnp.dot(grad_scores, stacked, preferred_element_type=F32) + jnp.dot(
            probs.astype(BF), grads, preferred_element_type=F32
        )
        return dq + tn(keys, grad_scores)[:HEAD_DIM]

    dq = lax.fori_loop(low, chunk + 1, step, jnp.zeros((64, GROUP * TOK), F32))
    cos, sin = cosine[0], sine[0]
    for pair, tile in enumerate(unstacked(dq)):
        tile = tile * (1.0 / HEAD_DIM**0.5)
        dquery[0, :, 128 * pair : 128 * pair + 128] = (tile * cos - swapped(tile) * sin).astype(BF)

    @pl.when(i == RING - 1)
    def _():
        dkv[...] = total[...].astype(BF)


def attend_back(info, query, kv, start, out, grad_out, logsum, cosine, sine):
    chunk = lambda r, cols: pl.BlockSpec((1, r, cols), lambda i, s: (i, 0, 0))
    whole = pl.BlockSpec((16, TOK, 128), lambda i, s: (0, 0, 0))
    return pl.pallas_call(
        attend_back_kernel,
        name="attend_back",
        cost_estimate=cost(15),
        grid_spec=pltpu.PrefetchScalarGridSpec(
            num_scalar_prefetch=1,
            grid=(RING,),
            in_specs=[
                chunk(TOK, QZ),
                whole,
                chunk(1, TOK),
                chunk(TOK, QZ),
                chunk(TOK, QZ),
                chunk(1, GROUP * TOK),
                chunk(TOK, 128),
                chunk(TOK, 128),
            ],
            out_specs=[chunk(TOK, QZ), whole],
            scratch_shapes=[pltpu.VMEM((16, TOK, 128), F32)],
        ),
        out_shape=[
            jax.ShapeDtypeStruct((RING, TOK, QZ), BF),
            jax.ShapeDtypeStruct((16, TOK, 128), BF),
        ],
        compiler_params=PARAMS,
    )(info, query, kv, start, out, grad_out, logsum, cosine, sine)


def rms_back(v, gain, grad):
    scale = lax.rsqrt(jnp.mean(v * v, axis=-1, keepdims=True) + EPS)
    unit = v * scale
    gain_grad = jnp.sum(grad * unit, axis=0, keepdims=True)
    inner = grad * gain
    return scale * (inner - unit * jnp.mean(inner * unit, axis=-1, keepdims=True)), gain_grad


def norm_back_kernel(v, base, a, b, c, gain, grad, gain_out):
    dn = from_pieces(a[...].astype(F32) + (b[...].astype(F32) + c[...].astype(F32)))
    back, gain_grad = rms_back(v[...].astype(F32), gain[...], dn)
    grad[...] = base[...] + back
    gain_out[...] = gain_grad


def norm_back(v, base, parts, gain):
    return pl.pallas_call(
        norm_back_kernel,
        name="norm_back",
        cost_estimate=cost(4),
        out_shape=[jax.ShapeDtypeStruct((TOK, D), F32), jax.ShapeDtypeStruct((1, D), F32)],
        compiler_params=PARAMS,
    )(v, base, *parts, gain)


def pick(v, index, axis=0):
    return lax.dynamic_index_in_dim(v, index, axis, keepdims=False)


def dot(a, b):
    return jnp.dot(a, b, preferred_element_type=F32)


def body(tokens, segments, cotangent, norm_attn, norm_ffn, wqkv, wo, w1, w3, w2):
    q = coords()
    y, xx, xl, z, c = q["y"], q["x"], q["xl"], q["z"], q["c"]
    x = tokens[0]
    g = cotangent[0]
    X, G, SEG, GN, WQ, WO, W13, t2 = talk(
        fetch_kernel,
        "fetch",
        1,
        40,
        100,
        (x, g, segments, norm_attn[None], norm_ffn[None], wqkv, wo, w1, w3, w2),
        [
            ((RING, TOK, D), BF),
            ((RING, TOK, D), BF),
            ((2, 4, 2, 8, TOK), jnp.int32),
            ((4, 2, 32, 256), BF),
            ((2, 4, 2, 2, 64, MZ), BF),
            ((2, 256, D), BF),
            ((2, 4, 2, 2, 64, 2 * FZ), BF),
            ((704, 128), BF),
        ],
        scratch=[
            pltpu.VMEM((256, 128), BF),
            pltpu.VMEM((704, 128), BF),
            pltpu.VMEM((64, MZ), BF),
            pltpu.VMEM((64, 128), BF),
            pltpu.VMEM((64, 128), BF),
            pltpu.VMEM((64, FZ), BF),
            pltpu.VMEM((64, FZ), BF),
            pltpu.VMEM((8, TOK), jnp.int32),
            pltpu.VMEM((32, 256), BF),
        ],
        near=(0, 1, 2, 3, 4),
    )

    docs = SEG[:, :, :, 0, :].reshape(16 * TOK)
    mine = pick(pick(SEG[:, :, :, 0, :], xl, 0), c, 1)
    chunks = xl * 8 + 2 * jnp.arange(4, dtype=jnp.int32) + c
    start = jnp.sum((docs[None, None, :] < mine[:, :, None]).astype(jnp.int32), axis=2)
    index = chunks[:, None] * TOK + jnp.arange(TOK, dtype=jnp.int32)[None]
    place = (index - start).astype(F32)
    lane = jnp.arange(128)
    freq = THETA ** (-(lane % 32).astype(F32) * 2.0 / HEAD_DIM)
    angle = place[:, :, None] * freq[None, None, :]
    cosine = jnp.cos(angle)
    sine = jnp.sin(angle) * jnp.where(lane % 64 < 32, -1.0, 1.0)
    info = jnp.stack([jnp.min(start, axis=1) // TOK, chunks])
    start = start[:, None, :]
    gain_attn = GN[:, :, 0, :].reshape(1, D).astype(F32)
    gain_ffn = GN[:, :, 16, :].reshape(1, D).astype(F32)

    WQ = WQ.reshape(D, MZ)
    WO = WO.reshape(QZ, D)
    n1, query, kv = project(X, gain_attn, WQ, cosine, sine)
    (KV,) = talk(
        kv_kernel, "kv", 2, 7, 4, (kv,), [((2, 4, 2, TOK, 128), BF)], near=(0,)
    )
    KV = KV.reshape(16, TOK, 128)
    heads_out, logsum = attend(info, query, KV, start)
    o = heads_out.reshape(RING * TOK, QZ)
    part = dot(o, WO).astype(BF).reshape(RING, TOK, D)
    N2, h, W13, W2 = talk(
        middle_kernel,
        "middle",
        3,
        42,
        60,
        (part, x, gain_ffn, t2, W13),
        [
            ((RING, TOK, D), BF),
            ((TOK, D), F32),
            ((2, 4, 2, 2, 64, 2 * FZ), BF),
            ((2, 704, D), BF),
        ],
        scratch=[
            *[pltpu.VMEM(HALF, BF)] * 4,
            *[pltpu.VMEM((TOK, D), BF)] * 3,
        ],
        near=(0, 1, 2, 3),
        near_out=(1,),
        alias={4: 2},
    )
    N2, G = N2.reshape(RING * TOK, D), G.reshape(RING * TOK, D)
    W13, W2 = W13.reshape(D, 2 * FZ), W2.reshape(FZ, D)
    gate, up = dot(N2, W13[:, :FZ]), dot(N2, W13[:, FZ:])
    hidden = (jax.nn.silu(gate) * up).astype(BF)
    dhid = jnp.einsum("td,fd->tf", G, W2, preferred_element_type=F32)
    sigma = jax.nn.sigmoid(gate)
    dgate = (dhid * up * sigma * (1.0 + gate * (1.0 - sigma))).astype(BF)
    dup = (dhid * gate * sigma).astype(BF)
    both = jnp.concatenate([dgate, dup], axis=1)
    dn2 = jnp.einsum("tf,df->td", both, W13, preferred_element_type=F32)
    dn2 = dn2.astype(BF).reshape(RING, TOK, D)
    out_part = dot(hidden, W2).astype(BF).reshape(RING, TOK, D)
    half = lambda v, j: lax.dynamic_slice_in_dim(v, 1024 * j, 1024, 1)
    outer = lambda a, b: jnp.einsum("ta,tb->ab", a, b, preferred_element_type=F32)
    rest = 2 * FZ - SPLIT
    buffers = []
    for shape in ((704, 256), (2, 64, SPLIT), (2, 64, rest)):
        buffers += [pltpu.VMEM((2,) + shape, BF)] * 4
    DH, D3, fa, fb, f2, dh, gain2 = talk(
        back_kernel,
        "back",
        4,
        60,
        100,
        (dn2, out_part, hidden, G, N2, both, h, gain_ffn),
        [
            ((RING, TOK, D), BF),
            ((2, TOK, D), BF),
            ((2, 2, 64, SPLIT), BF),
            ((2, 2, 64, rest), BF),
            ((2, 704, 256), BF),
            ((TOK, D), F32),
            ((1, D), F32),
        ],
        scratch=[
            *[pltpu.VMEM(HALF, BF)] * 6,
            *[pltpu.VMEM((TOK, D), BF)] * 2,
            *[pltpu.VMEM(HALF, BF)] * 2,
            *[pltpu.VMEM((TOK, D), BF)] * 2,
            pltpu.VMEM((RING * TOK, FZ), BF),
            pltpu.VMEM((RING * TOK, D), BF),
            pltpu.VMEM((RING * TOK, D), BF),
            pltpu.VMEM((RING * TOK, 2 * FZ), BF),
            pltpu.VMEM((FZ, RING * TOK), BF),
            pltpu.VMEM((4, FZ, 256), BF),
            pltpu.VMEM((4, 4, 64, 2 * FZ), BF),
            pltpu.VMEM((4, FZ, 256), BF),
            pltpu.VMEM((4, 4, 64, 2 * FZ), BF),
            *buffers,
        ],
        near=(6, 7),
        near_out=(5, 6),
    )
    fa, fb = fa.reshape(4, 64, SPLIT), fb.reshape(4, 64, rest)
    f2 = f2.reshape(1408, 256)
    DH = DH.reshape(RING * TOK, D)
    dheads = jnp.einsum("td,qd->tq", DH, WO, preferred_element_type=F32).astype(BF)
    dquery, dkv = attend_back(
        info, query, KV, start, heads_out, dheads.reshape(RING, TOK, QZ), logsum, cosine, sine
    )
    dkv = dkv.reshape(2, 4, 2, TOK, 128)
    (dkv_rot,) = talk(
        dkv_kernel,
        "dkv",
        5,
        8,
        4,
        (dkv, cosine, sine),
        [((RING, TOK, 128), BF)],
        scratch=[pltpu.VMEM((3, RING, TOK, 128), BF)],
        near=(0, 1, 2),
        near_out=(0,),
    )
    dmixed = jnp.concatenate([dquery, dkv_rot], axis=2).reshape(RING * TOK, MZ)
    dn1 = jnp.einsum("tc,dc->td", dmixed, WQ, preferred_element_type=F32)
    dn1 = dn1.astype(BF).reshape(RING, TOK, D)

    n1 = n1.reshape(RING * TOK, D)
    other_o = move(outer(o, half(DH, 1 - c)).astype(BF), "c", 1)
    sum_o = (outer(o, half(DH, c)) + other_o.astype(F32)).astype(BF)
    other_q = move(outer(half(n1, 1 - c), dmixed).astype(BF), "c", 1)
    sum_q = (outer(half(n1, c), dmixed) + other_q.astype(F32)).astype(BF)
    sum_q = sum_q.reshape(4, 4, 64, MZ)
    D1, G1, G3, G2, fq, fo = talk(
        wide_kernel,
        "wide",
        6,
        55,
        90,
        (dn1, fa, fb, f2, sum_q, sum_o),
        [
            ((2, TOK, D), BF),
            ((256, 4 * FZ), BF),
            ((256, 4 * FZ), BF),
            ((704, D), BF),
            ((4, 64, MZ), BF),
            ((512, 256), BF),
        ],
        scratch=[
            *[pltpu.VMEM(HALF, BF)] * 4,
            pltpu.VMEM((3, 64, SPLIT), BF),
            pltpu.VMEM((3, 64, rest), BF),
            pltpu.VMEM((3, 704, 128), BF),
            pltpu.VMEM((64, SPLIT), BF),
            pltpu.VMEM((64, rest), BF),
            pltpu.VMEM((704, 128), BF),
            pltpu.VMEM((704, 128), BF),
            pltpu.VMEM((3, 4, 64, MZ), BF),
            pltpu.VMEM((3, 512, 256), BF),
        ],
        near=(0, 1, 2, 3, 4, 5),
    )
    input_grad, gain1 = norm_back(x, dh, (pick(dn1, z), D1[0], D1[1]), gain_attn)

    small = (8, 256)
    GO, GQ, GKV, gain_out = talk(
        last_kernel,
        "last",
        7,
        30,
        60,
        (fq, fo, gain1, gain2),
        [
            ((256, D), BF),
            ((256, QDIM), BF),
            ((256, 2 * KVDIM), BF),
            (small, F32),
        ],
        scratch=[
            pltpu.VMEM((3, 64, MZ), BF),
            pltpu.VMEM((3, 256, 128), BF),
            pltpu.VMEM((64, MZ), BF),
            pltpu.VMEM((256, 128), BF),
            pltpu.VMEM((256, 128), BF),
            pltpu.VMEM((4, 2) + small, F32),
            pltpu.VMEM((4, 2) + small, F32),
            pltpu.VMEM((2, 2) + small, F32),
            pltpu.VMEM((4,) + small, F32),
            pltpu.VMEM((2,) + small, F32),
            pltpu.VMEM((2,) + small, F32),
            pltpu.VMEM(small, F32),
        ],
        near=(0, 1, 2, 3),
    )
    pairs = GKV.reshape(256, 4, 2, HEAD_DIM)
    flat = lambda v: v.reshape(256, -1)
    grad_qkv = jnp.concatenate([GQ, flat(pairs[:, :, 0]), flat(pairs[:, :, 1])], axis=1)
    own = pick(out_part, z).astype(F32)
    output = h + (own + (D3[0].astype(F32) + D3[1].astype(F32)))
    return (
        output[None],
        input_grad[None],
        gain_out[0],
        gain_out[1],
        grad_qkv.astype(F32),
        GO.astype(F32),
        G1.astype(F32),
        G3.astype(F32),
        G2.astype(F32),
    )


def solution(mesh):
    rows = P("dp", None)
    acts = P("dp", "ctx", None)
    return jax.shard_map(
        body,
        mesh=mesh,
        in_specs=(acts, P("dp", "ctx"), acts, P("dp"), P("dp"), rows, rows, rows, rows, rows),
        out_specs=(acts, acts, P("dp"), P("dp"), rows, rows, rows, rows, rows),
        check_vma=False,
    )
```

time: 519 us -> 416 us (0.80); the launches traced: 509 us -> 413 us
  waiting for transfers between devices: 36.9 us -> 0.01 us
  starting transfers between devices: 35.4 us -> 4.88 us
  local copies, waits for them, and re-layouts: 34.6 us -> 10 us
  Pallas kernels: 306 us -> 321 us
  matrix products: 62.8 us -> 51.5 us
  other arithmetic: 32.3 us -> 24.7 us
    ppermute x17 -> x2, waiting for transfers between devices: 36.9 us -> 0.01 us  [move(): return lax.ppermute(v, ('dp', 'ctx'), shift_pairs(axis, by))]
    ppermute x17 -> x2, starting transfers between devices: 34.8 us -> 4.88 us  [move(): return lax.ppermute(v, ('dp', 'ctx'), shift_pairs(axis, by))]
    pallas_call x7, Pallas kernels: 257 us -> 279 us  [talk(): pl.pallas_call(kernel, name=name, out_shape=[jax.ShapeDtypeStruct(s, t) f...]
    dot_general x8 -> x4, matrix products: 24.3 us -> 9.27 us  [body(): jnp.einsum('ta,tb->ab', a, b, preferred_element_type=F32)]
    unnamed x110 -> x48, local copies, waits for them, and re-layouts: 9.92 us -> 0.1 us
    slice x7 -> x1, local copies, waits for them, and re-layouts: 8.74 us -> 0.02 us  [body(): pairs[:, :, 0]]
    dot_general x4, matrix products: 17.3 us -> 25.2 us  [dot(): return jnp.dot(a, b, preferred_element_type=F32)]
    reshape x6 -> x0, local copies, waits for them, and re-layouts: 6.89 us -> none  [the longest x1 2.7 us: body(): GQ = GQ.astype(F32).reshape(256, 4, MZ)]
  transfers between devices with their start and end apart: 18 -> 2, of which waited for: 4 -> 0; matrix products, arithmetic and copies ran while one was open for 8% -> 4% of each run, Pallas kernels for 6% -> 7%
where the time goes in v3:
time: 416 us; the launch traced here: 413 us
  Pallas kernels  321 us (77%)
  matrix products  51.5 us (12%)
  other arithmetic  24.7 us (6%)
  local copies, waits for them, and re-layouts  10 us (2%)
  starting transfers between devices  4.88 us (1%)
    pallas_call x7, Pallas kernels, talk(): pl.pallas_call(kernel, name=name, out_shape=[jax.ShapeDtypeStruct(s, t) f...  279 us
    dot_general x4, matrix products, dot(): return jnp.dot(a, b, preferred_element_type=F32)  25.2 us
    pallas_call x1, Pallas kernels, attend_back(): pl.pallas_call(attend_back_kernel, name='attend_back', cost_estimate=cost...  17.4 us
    pallas_call x1, Pallas kernels, attend(): pl.pallas_call(attend_kernel, name='attend', cost_estimate=cost(12), grid...  14.5 us
    dot_general x4, matrix products, body(): jnp.einsum('ta,tb->ab', a, b, preferred_element_type=F32)  9.27 us
  transfers between devices with their start and end apart: 2, of which 0 were waited for; matrix products, arithmetic and copies ran while one was open for 4% of the time, Pallas kernels for 7%

profile of v3, /device:TPU:1, one launch (start us, length us, event | category | flops | bytes accessed | tf_op | source)
XLA Modules:
  0.0 413.4 jit_solution(2202840160588441477)
XLA Ops:
  3.2 45.1 %fetch.1 = (bf16[4,128,2048]{2,1,0:T(8,128)(2,1)}, bf16[4,128,2048]{2,1,0:T(8,128)(2,1)}, s32[2,4,2,8,128]{4,3,2,1,0:T(8,128)}, bf16[4,2,32,256]{3,2,1,0:T(8,128...) custom-call(bf16[128,2048]{1,0:T(8,128)(2,1)} %bitcast.92, ...), custom_call_target="tpu_custom_call" | custom-call | flops 40000000000 | tf_op jit(solution)/shard_map/fetch/pallas_call | solution.py:275
  53.9 5.9 %project.1 = (bf16[4,128,2048]{2,1,0:T(8,128)(2,1)}, bf16[4,128,512]{2,1,0:T(8,128)(2,1)}, bf16[4,128,128]{2,1,0:T(8,128)(2,1)}) custom-call(bf16[4,128,2048]{2,1,0:T(8,128)(2,1)} %get-tuple-element.48.x, f32[1,2048]{1,0:T(1,128)} %convert.3.gain, bf16[2048,640]{1,0:T(8,128)(2,1)} %bitcast.102, f32[4,128,128]{2,1,0:T(8,128)} %get-tuple-element.97.cosine, ...), custom_call_target="tpu_custom_call" | custom-call | flops 7000000000 | tf_op jit(solution)/shard_map/project/pallas_call | solution.py:942
  59.8 5.7 %kv.1 = bf16[2,4,2,128,128]{4,3,2,1,0:T(8,128)(2,1)} custom-call(bf16[4,128,128]{2,1,0:T(8,128)(2,1)} %get-tuple-element.52.kv), custom_call_target="tpu_custom_call" | custom-call | flops 7000000000 | tf_op jit(solution)/shard_map/kv/pallas_call | solution.py:275
  66.0 14.5 %attend.1 = (bf16[4,128,512]{2,1,0:T(8,128)(2,1)}, f32[4,1,1024]{2,1,0:T(1,128)}) custom-call(s32[2,4]{1,0:T(2,128)} %pad_add_fusion.info, bf16[4,128,512]{2,1,0:T(8,128)(2,1)} %get-tuple-element.51.query, bf16[16,128,128]{2,1,0:T(8,128)(2,1)} %bitcast.125, s32[4,1,128]{2,1,0:T(1,128)} %bitcast.86), custom_call_target="tpu_custom_call" | custom-call | flops 12000000000 | tf_op jit(solution)/shard_map/attend/pallas_call | solution.py:1031
  80.5 3.6 convolution_convert_fusion.1
  84.1 45.1 %middle.1 = (bf16[4,128,2048]{2,1,0:T(8,128)(2,1)}, f32[128,2048]{1,0:T(8,128)}, bf16[2,4,2,2,64,2816]{5,4,3,2,1,0:T(8,128)(2,1)}, bf16[2,704,2048]{2,1,0:T(8,128)(2,1)}) custom-call(bf16[4,128,2048]{2,1,0:T(8,128)(2,1)} %bitcast.117, bf16[128,2048]{1,0:T(8,128)(2,1)} %bitcast.93, f32[1,2048]{1,0:T(1,128)} %convert.2.gain, ...), custom_call_target="tpu_custom_call", output_to_operand_aliasing={{2}: (4, {})} | custom-call | flops 41999998976 | tf_op jit(solution)/shard_map/middle/pallas_call | solution.py:275
  129.3 8.4 %fusion.2 = f32[512,1408]{1,0:T(8,128)} fusion(bf16[512,2048]{1,0:T(8,128)(2,1)} %bitcast.113, bf16[2048,2816]{1,0:T(8,128)(2,1)} %bitcast.95), kind=kOutput, calls=%fused_computation.2 | convolution fusion | flops 2952790016 | bytes 10747904 | tf_op jit(solution)/shard_map/dot_general | solution.py:1157
  137.7 3.5 fusion.27
  141.3 6.0 %multiply_convert_fusion.2 = (bf16[512,1408]{1,0:T(8,128)(2,1)S(1)}, bf16[512,1408]{1,0:T(8,128)(2,1)S(1)}, bf16[512,1408]{1,0:T(8,128)(2,1)S(1)}) fusion(f32[512,1408]{1,0:T(8,128)} %fusion.2, f32[512,1408]{1,0:T(8,128)S(1)} %fusion.27, bf16[512,2048]{1,0:T(8,128)(2,1)S(1)} %bitcast.115, bf16[2048,2816]{1,0:T(8,128)(2,1)S(1)} %bitcast.98), kind=kOutput, calls=%fused_computation.12 | convolution fusion | flops 2964324352 | bytes 17956864 | tf_op jit(solution)/shard_map/dot_general | solution.py:1157
  147.3 7.7 %convolution_convert_fusion = bf16[512,2048]{1,0:T(8,128)(2,1)} fusion(bf16[2048,2816]{1,0:T(8,128)(2,1)S(1)} %bitcast.99, bf16[512,1408]{1,0:T(8,128)(2,1)S(1)} %get-tuple-element.87, bf16[512,1408]{1,0:T(8,128)(2,1)S(1)} %get-tuple-element.86), kind=kOutput, calls=%fused_computation.5 | convolution fusion | flops 5912395776 | bytes 16515072 | tf_op jit(solution)/shard_map/tf,df->td/dot_general | solution.py:1252
  156.8 7.2 %convolution_convert_fusion.3 = bf16[512,2048]{1,0:T(8,128)(2,1)} fusion(bf16[512,1408]{1,0:T(8,128)(2,1)S(1)} %get-tuple-element.85.hidden, bf16[1408,2048]{1,0:T(8,128)(2,1)} %bitcast.100), kind=kOutput, calls=%fused_computation.8 | convolution fusion | flops 2953838592 | bytes 9306112 | tf_op jit(solution)/shard_map/dot_general | solution.py:1157
  164.0 68.1 %back.1 = (bf16[4,128,2048]{2,1,0:T(8,128)(2,1)}, bf16[2,128,2048]{2,1,0:T(8,128)(2,1)}, bf16[2,2,64,2048]{3,2,1,0:T(8,128)(2,1)}, bf16[2,2,64,768]{3,2,1,0:T(8,...) custom-call(bf16[4,128,2048]{2,1,0:T(8,128)(2,1)} %bitcast.116, ...), custom_call_target="tpu_custom_call" | custom-call | flops 60000002048 | tf_op jit(solution)/shard_map/back/pallas_call | solution.py:275
  232.2 3.1 convolution_convert_fusion.5
  235.2 4.7 %collective-permute-start.1 = (bf16[512,1024]{1,0:T(8,128)(2,1)}, bf16[512,1024]{1,0:T(8,128)(2,1)}, u32[]{:S(2)}, u32[]{:S(2)}) collective-permute-start(bf16[512,1024]{1,0:T(8,128)(2,1)} %convolution_convert_fusion.5), channel_id=1, source_target_pairs={{0,1},{1,0},{2,3},{3,2},{4,5},{5,4},{6,7},{7,6},{8,9},{9,8},{10,11... | collective-permute-start | bytes 3145736 | tf_op jit(solution)/shard_map/ppermute | solution.py:71
  242.0 17.4 %attend_back.1 = (bf16[4,128,512]{2,1,0:T(8,128)(2,1)}, bf16[16,128,128]{2,1,0:T(8,128)(2,1)}) custom-call(s32[2,4]{1,0:T(2,128)} %pad_add_fusion.info, bf16[4,128,512]{2,1,0:T(8,128)(2,1)} %get-tuple-element.51.query, bf16[16,128,128]{2,1,0:T(8,128)(2,1)} %bitcast.126, s32[4,1,128]{2,1,0:T(1,128)} %bitcast.87, bf16[4,128,512]{2,1,0:T(8,128)(2,1)} %get-tuple-element.53.out, ...), custom_call_target="tpu_custom_call" | custom-call | flops 15000000512 | tf_op jit(solution)/shard_map/attend_back/pallas_call | solution.py:1099
  259.4 10.4 %dkv.1 = bf16[4,128,128]{2,1,0:T(8,128)(2,1)} custom-call(bf16[2,4,2,128,128]{4,3,2,1,0:T(8,128)(2,1)} %bitcast.127, f32[4,128,128]{2,1,0:T(8,128)} %get-tuple-element.97.cosine, f32[4,128,128]{2,1,0:T(8,128)} %get-tuple-element.96.sine), custom_call_target="tpu_custom_call" | custom-call | flops 8000000000 | tf_op jit(solution)/shard_map/dkv/pallas_call | solution.py:275
  272.1 3.7 convolution_convert_fusion.2
  276.7 3.1 fusion.4
  285.0 67.9 %wide.1 = (bf16[2,128,2048]{2,1,0:T(8,128)(2,1)}, bf16[256,5632]{1,0:T(8,128)(2,1)}, bf16[256,5632]{1,0:T(8,128)(2,1)}, bf16[704,2048]{1,0:T(8,128)(2,1)}, bf16[...) custom-call(bf16[4,128,2048]{2,1,0:T(8,128)(2,1)} %bitcast.80, bf16[4,64,2048]{2,1,0:T(8,128)(2,1)} %bitcast.119, ...), custom_call_target="tpu_custom_call" | custom-call | flops 54999998464 | tf_op jit(solution)/shard_map/wide/pallas_call | solution.py:275
  355.2 3.7 norm_back.1
  358.9 37.2 %last.1 = (bf16[256,2048]{1,0:T(8,128)(2,1)}, bf16[256,2048]{1,0:T(8,128)(2,1)}, bf16[256,512]{1,0:T(8,128)(2,1)}, f32[8,256]{1,0:T(8,128)}) custom-call(bf16[4,64,640]{2,1,0:T(8,128)(2,1)} %get-tuple-element.74.fq, bf16[512,256]{1,0:T(8,128)(2,1)} %get-tuple-element.75.fo, f32[1,2048]{1,0:T(1,128)} %get-tuple-element.76.gain1, ...), custom_call_target="tpu_custom_call" | custom-call | flops 30000001024 | tf_op jit(solution)/shard_map/last/pallas_call | solution.py:275
  401.6 3.2 convert_element_type.122
  404.8 3.2 convert_element_type.123
  408.0 3.3 convert_element_type.124
  (81 shorter events, 30.3 us)
Async XLA Ops:
  49.8 10.0 %copy-start.8 = (s32[4,128]{1,0:T(4,128)}, s32[4,128]{1,0:T(4,128)S(1)}, u32[]{:S(2)}) copy-start(s32[4,128]{1,0:T(4,128)S(1)} %convert_reduce_fusion) | copy-start | bytes 6148
  66.0 14.5 %copy-start.14 = (bf16[2,256,2048]{2,1,0:T(8,128)(2,1)S(1)}, bf16[2,256,2048]{2,1,0:T(8,128)(2,1)}, u32[]{:S(2)}) copy-start(bf16[2,256,2048]{2,1,0:T(8,128)(2,1)} %get-tuple-element.54) | copy-start | bytes 6291460
  129.3 8.4 %copy-start.9 = (bf16[2,704,2048]{2,1,0:T(8,128)(2,1)S(1)}, bf16[2,704,2048]{2,1,0:T(8,128)(2,1)}, u32[]{:S(2)}) copy-start(bf16[2,704,2048]{2,1,0:T(8,128)(2,1)} %get-tuple-element.60) | copy-start | bytes 17301508
  129.3 8.4 %copy-start.16 = (bf16[4,128,2048]{2,1,0:T(8,128)(2,1)S(1)}, bf16[4,128,2048]{2,1,0:T(8,128)(2,1)}, u32[]{:S(2)}) copy-start(bf16[4,128,2048]{2,1,0:T(8,128)(2,1)} %get-tuple-element.61) | copy-start | bytes 6291460
  129.3 11.9 %slice-start = ((s8[11534336]{0:T(1024)(128)(4,1)}), s8[4194304]{0:T(1024)(128)(4,1)S(1)}, s32[]{:S(2)}) async-start(s8[11534336]{0:T(1024)(128)(4,1)} %bitcast.96), calls=%async_computation | async-start | bytes 8388608
  129.3 11.9 %slice-start.1 = ((s8[11534336]{0:T(1024)(128)(4,1)}), s8[4194304]{0:T(1024)(128)(4,1)S(1)}, s32[]{:S(2)}) async-start(s8[11534336]{0:T(1024)(128)(4,1)} %bitcast.96), calls=%async_computation.1 | async-start | bytes 8388608
  137.7 3.5 slice-start.2
  137.7 3.5 copy-start.17
  147.3 9.5 %copy-start.20 = (bf16[512,1408]{1,0:T(8,128)(2,1)}, bf16[512,1408]{1,0:T(8,128)(2,1)S(1)}, u32[]{:S(2)}) copy-start(bf16[512,1408]{1,0:T(8,128)(2,1)S(1)} %get-tuple-element.85.hidden) | copy-start | bytes 4325380
  164.0 68.1 %copy-start.18 = (bf16[4,128,512]{2,1,0:T(8,128)(2,1)S(1)}, bf16[4,128,512]{2,1,0:T(8,128)(2,1)}, u32[]{:S(2)}) copy-start(bf16[4,128,512]{2,1,0:T(8,128)(2,1)} %get-tuple-element.53.out) | copy-start | bytes 1572868
  232.1 7.8 %copy-start.12 = (bf16[4,128,2048]{2,1,0:T(8,128)(2,1)S(1)}, bf16[4,128,2048]{2,1,0:T(8,128)(2,1)}, u32[]{:S(2)}) copy-start(bf16[4,128,2048]{2,1,0:T(8,128)(2,1)} %get-tuple-element.64) | copy-start | bytes 6291460
  232.1 7.8 %copy-start.15 = (bf16[2,256,2048]{2,1,0:T(8,128)(2,1)S(1)}, bf16[2,256,2048]{2,1,0:T(8,128)(2,1)}, u32[]{:S(2)}) copy-start(bf16[2,256,2048]{2,1,0:T(8,128)(2,1)} %get-tuple-element.54) | copy-start | bytes 6291460
  235.2 44.6 %collective-permute-start.1 = (bf16[512,1024]{1,0:T(8,128)(2,1)}, bf16[512,1024]{1,0:T(8,128)(2,1)}, u32[]{:S(2)}, u32[]{:S(2)}) collective-permute-start(bf16[512,1024]{1,0:T(8,128)(2,1)} %convolution_convert_fusion.5), channel_id=1, source_target_pairs={{0,1},{1,0},{2,3},{3,2},{4,5},{5,4},{6,7},{7,6},{8,9},{9,8},{10,11... | collective-permute-start | bytes 3145736 | tf_op jit(solution)/shard_map/ppermute | solution.py:71
  259.4 10.4 %copy-start.6 = (bf16[4,128,512]{2,1,0:T(8,128)(2,1)S(1)}, bf16[4,128,512]{2,1,0:T(8,128)(2,1)}, u32[]{:S(2)}) copy-start(bf16[4,128,512]{2,1,0:T(8,128)(2,1)} %get-tuple-element.66) | copy-start | bytes 1572868
  259.4 11.4 %copy-start.10 = (bf16[4,128,2048]{2,1,0:T(8,128)(2,1)S(1)}, bf16[4,128,2048]{2,1,0:T(8,128)(2,1)}, u32[]{:S(2)}) copy-start(bf16[4,128,2048]{2,1,0:T(8,128)(2,1)} %get-tuple-element.71) | copy-start | bytes 6291460
  271.9 11.1 %collective-permute-start = (bf16[1024,640]{1,0:T(8,128)(2,1)S(1)}, bf16[1024,640]{1,0:T(8,128)(2,1)S(1)}, u32[]{:S(2)}, u32[]{:S(2)}) collective-permute-start(bf16[1024,640]{1,0:T(8,128)(2,1)S(1)} %convolution_convert_fusion.4), channel_id=1, source_target_pairs={{0,1},{1,0},{2,3},{3,2},{4,5},{5,4},{6,7},{7,6},{8,9},{9,8},{10,11... | collective-permute-start | bytes 3932168 | tf_op jit(solution)/shard_map/ppermute | solution.py:71
  272.1 4.6 %copy-start.3 = (f32[128,2048]{1,0:T(8,128)S(1)}, f32[128,2048]{1,0:T(8,128)}, u32[]{:S(2)}) copy-start(f32[128,2048]{1,0:T(8,128)} %get-tuple-element.57.h) | copy-start | bytes 3145732
  272.1 4.6 %copy-start.4 = (bf16[2,128,2048]{2,1,0:T(8,128)(2,1)S(1)}, bf16[2,128,2048]{2,1,0:T(8,128)(2,1)}, u32[]{:S(2)}) copy-start(bf16[2,128,2048]{2,1,0:T(8,128)(2,1)} %get-tuple-element.62) | copy-start | bytes 3145732
  275.8 7.1 %copy-start.7 = (bf16[512,2048]{1,0:T(8,128)(2,1)}, bf16[512,2048]{1,0:T(8,128)(2,1)S(1)}, u32[]{:S(2)}) copy-start(bf16[512,2048]{1,0:T(8,128)(2,1)S(1)} %convolution_convert_fusion.2) | copy-start | bytes 6291460
  275.8 4.0 copy-start.13
  275.8 4.0 copy-start.19
  396.1 5.6 %copy-start.2 = (bf16[256,5632]{1,0:T(8,128)(2,1)S(1)}, bf16[256,5632]{1,0:T(8,128)(2,1)}, u32[]{:S(2)}) copy-start(bf16[256,5632]{1,0:T(8,128)(2,1)} %get-tuple-element.82) | copy-start | bytes 8650756
  401.6 3.2 copy-start.1
  408.0 3.3 copy-start.5
  (2 other events, 6.3 us)

commit v4 on v3

--- a/solution.py
+++ b/solution.py
@@ -21,7 +21,7 @@
 EPS = 1e-05
 THETA = 10000.0
 MESH = pl.DeviceIdType.MESH
-VMEM_LIMIT = 56 << 20
+VMEM_LIMIT = 60 << 20
 BF = jnp.bfloat16
 F32 = jnp.float32
 ANY = pl.BlockSpec(memory_space=pl.ANY)
@@ -530,67 +530,56 @@
 
 
 def back_kernel(
-    dn2, out_part, hidden, G, N2, both, h, gain, V, D3, FA, FB, F2, DH, GAIN, *scratch
+    dn2, hidden, G, N2, both, W2, WO, h, gain, V, FA, FB, F2, DO, OUT, DH, GAIN, *scratch
 ):
     (
-        p0, p1, p2, p3, v0, v1, below, above, near0, near1, mine, dhb, hv, gv, nv, bv, hT,
-        mate2, mate13, sum2, sum13, *bufs, ss, rs,
+        p0, p1, p2, p3, v0, v1, below, above, out_below, out_above, near0, near1, mine, dhb,
+        vv, hv, gv, nv, bv, ov, wv, hT, outs, mate2, mate13, sum2, sum13, *bufs, ss, rs,
     ) = scratch
     q = coords()
     y, xx, z, c = q["y"], q["x"], q["z"], q["c"]
     mate = device(q, c=1 - c)
     k = Copies(ss, rs)
+    get_n, get_b = k.local(N2, nv), k.local(both, bv)
     get_h, get_g = k.local(hidden, hv), k.local(G, gv)
-    get_n, get_b = k.local(N2, nv), k.local(both, bv)
     get_part = [
         k.local(dn2.at[(z + 1) % 4, TOP], near0),
         k.local(dn2.at[(z + 3) % 4, LOW], near1),
         k.local(dn2.at[z], mine),
     ]
+    tile = lambda j: pl.ds(512 * j, 512)
+    get_w = [k.local(W2.at[:, tile(j)], wv.at[j]) for j in range(2)]
+    get_o = k.local(WO, ov)
     targets = [mate]
     for axis in ("x", "y", "z"):
         targets += ring(q, axis)[:2]
     greet(targets)
     z_sum = Sum(k, q, "z", ring_halves(dn2), halves(below), halves(above), (p0, p1))
-    get_h.wait()
-    get_g.wait()
-    hT[...] = hv[...].T
     lanes = lambda cc, j: pl.ds(pl.multiple_of(1024 * cc + 256 * j, 256), 256)
     sent2, sent13 = [], []
-    for j in range(4):
-        mate2[j] = dot(hT[...], gv[:, lanes(1 - c, j)]).astype(BF)
-        sent2.append(k.send(mate2.at[j], sum2.at[j], mate))
     get_n.wait()
     get_b.wait()
     for j in range(4):
         mate13[j] = tn(nv[:, lanes(1 - c, j)], bv[...]).astype(BF).reshape(4, 64, 2 * FZ)
         sent13.append(k.send(mate13.at[j], sum13.at[j], mate))
-        if j == 0:
-            for cp in get_part:
-                cp.wait()
+    get_h.wait()
+    get_g.wait()
+    hT[...] = hv[...].T
+    for cp in get_part:
+        cp.wait()
+    for j in range(4):
+        mate2[j] = dot(hT[...], gv[:, lanes(1 - c, j)]).astype(BF)
+        sent2.append(k.send(mate2.at[j], sum2.at[j], mate))
+        if j == 2:
             z_sum.relay(near0, near1, (v0, v1))
-    z_sum.end()
-    dn = from_pieces(
-        mine[...].astype(F32) + (below[...].astype(F32) + above[...].astype(F32))
-    )
-    back, gain_grad = rms_back(h[...], gain[...], dn)
-    total = gv[pl.ds(pl.multiple_of(TOK * z, TOK), TOK)].astype(F32) + back
-    DH[...] = total
-    GAIN[...] = gain_grad
-    dhb[...] = total.astype(BF)
-    v_ring = Gather(k, q, "z", halves(dhb), ring_halves(V))
-    here = k.local(dhb, V.at[z])
-    for j in range(4):
-        sent2[j].wait_recv()
-        sum2[j] = (dot(hT[...], gv[:, lanes(c, j)]) + sum2[j].astype(F32)).astype(BF)
     half = lambda ref: lambda i: ref.at[i]
     rest = 2 * FZ - SPLIT
     jobs = [
-        ("y", lambda j, i: sum2.at[j, pl.ds(704 * i, 704)], F2),
         ("x", lambda j, i: sum13.at[pl.ds(2 * i, 2), j, :, pl.ds(0, SPLIT)], FA),
         ("y", lambda j, i: sum13.at[j, pl.ds(2 * i, 2), :, pl.ds(SPLIT, rest)], FB),
+        ("y", lambda j, i: sum2.at[j, pl.ds(704 * i, 704)], F2),
     ]
-    sums = []
+    sums, done = [], []
 
     def start(n):
         axis, block, _ = jobs[n]
@@ -603,31 +592,7 @@
         at = q[axis]
         sums[n].relay(block((at + 1) % 4, 0), block((at + 3) % 4, 1), (b[1].at[0], b[1].at[1]))
 
-    start(0)
-    for j in range(4):
-        sent13[j].wait_recv()
-        own = tn(nv[:, lanes(c, j)], bv[...]).reshape(4, 64, 2 * FZ)
-        sum13[j] = (own + sum13[j].astype(F32)).astype(BF)
-        if j == 1:
-            v_ring.relay()
-    start(1)
-    start(2)
-    out_sum = Sum(
-        k, q, "z", ring_halves(out_part), halves(D3.at[0]), halves(D3.at[1]), (p2, p3)
-    )
-    get_part = [
-        k.local(out_part.at[(z + 1) % 4, TOP], near0),
-        k.local(out_part.at[(z + 3) % 4, LOW], near1),
-    ]
-    relay(0)
-    relay(1)
-    relay(2)
-    for cp in get_part:
-        cp.wait()
-    z_sum.sent()
-    out_sum.relay(near0, near1, (v0, v1))
-    done = []
-    for n in range(3):
+    def end(n):
         axis, block, out = jobs[n]
         b = bufs[4 * n : 4 * n + 4]
         sums[n].end()
@@ -637,56 +602,58 @@
             )
             b[2][i] = total.astype(BF)
         done.append(k.local(b[2], out))
+
+    for j in range(4):
+        sent13[j].wait_recv()
+        own = tn(nv[:, lanes(c, j)], bv[...]).reshape(4, 64, 2 * FZ)
+        sum13[j] = (own + sum13[j].astype(F32)).astype(BF)
+    start(0)
+    start(1)
+    for j in range(4):
+        sent2[j].wait_recv()
+        sum2[j] = (dot(hT[...], gv[:, lanes(c, j)]) + sum2[j].astype(F32)).astype(BF)
+    start(2)
+    z_sum.end()
+    dn = from_pieces(
+        mine[...].astype(F32) + (below[...].astype(F32) + above[...].astype(F32))
+    )
+    back, gain_grad = rms_back(h[...], gain[...], dn)
+    total = gv[pl.ds(pl.multiple_of(TOK * z, TOK), TOK)].astype(F32) + back
+    DH[...] = total
+    GAIN[...] = gain_grad
+    dhb[...] = total.astype(BF)
+    v_ring = Gather(k, q, "z", halves(dhb), ring_halves(vv))
+    here = k.local(dhb, vv.at[z])
+    for j in range(4):
+        get_w[j].wait()
+        part = dot(hv[...], wv[j % 2]).astype(BF)
+        outs[:, :, tile(j)] = part.reshape(RING, TOK, 512)
+        if j < 2:
+            get_w.append(k.local(W2.at[:, tile(j + 2)], wv.at[j]))
+    out_sum = Sum(
+        k, q, "z", ring_halves(outs), halves(out_below), halves(out_above), (p2, p3)
+    )
+    relay(1)
+    relay(0)
+    v_ring.relay()
+    relay(2)
+    z_sum.sent()
+    out_sum.relay(outs.at[(z + 1) % 4, TOP], outs.at[(z + 3) % 4, LOW], (v0, v1))
+    end(1)
+    end(0)
     v_ring.near()
     v_ring.end()
     here.wait()
+    get_o.wait()
+    done.append(k.local(vv, V))
+    DO[...] = nt(vv[...].reshape(RING * TOK, D), ov[...]).astype(BF)
+    end(2)
     out_sum.end()
+    OUT[...] = h[...] + (
+        outs[z].astype(F32) + (out_below[...].astype(F32) + out_above[...].astype(F32))
+    )
     for cp in done:
         cp.wait()
-    k.close()
-
-
-def dkv_kernel(dkv, cosine, sine, out, R, ss, rs):
-    q = coords()
-    xx, xl, c = q["x"], q["xl"], q["c"]
-    mate = device(q, c=1 - c)
-    other = device(q, x=xx ^ 1)
-    other_mate = device(q, x=xx ^ 1, c=1 - c)
-    greet([mate, other, other_mate])
-    k = Copies(ss, rs)
-    near = k.send(dkv.at[xl, :, 1 - c], R.at[0], mate)
-    far = [
-        pltpu.make_async_remote_copy(
-            src_ref=dkv.at[0, :, cc],
-            dst_ref=R.at[1 + i],
-            send_sem=ss.at[1 + i],
-            recv_sem=rs.at[1 + i],
-            device_id=to,
-            device_id_type=MESH,
-        )
-        for i, (to, cc) in enumerate(((other, c), (other_mate, 1 - c)))
-    ]
-
-    @pl.when(xl == 1)
-    def _():
-        R[1] = jnp.zeros(R.shape[1:], BF)
-        R[2] = jnp.zeros(R.shape[1:], BF)
-        for cp in far:
-            cp.start()
-        for cp in far:
-            cp.wait_send()
-
-    @pl.when(xl == 0)
-    def _():
-        for cp in far:
-            cp.wait_recv()
-
-    near.wait_recv()
-    for i in range(RING):
-        w = dkv[xl, i, c].astype(F32) + R[0, i].astype(F32)
-        w = w + (R[1, i].astype(F32) + R[2, i].astype(F32))
-        lane = lax.broadcasted_iota(jnp.int32, w.shape, 1)
-        out[i] = jnp.where(lane < HEAD_DIM, w * cosine[i] - swapped(w) * sine[i], w).astype(BF)
     k.close()
 
 
@@ -697,162 +664,227 @@
     )
 
 
-def wide_kernel(
-    dn, fa, fb, f2, sq, so, D2, G1, G3, G2, FQ, FO,
-    p0, p1, v0, v1, la, lb, l2, pa, pb, p2, t2, rq, ro, ss, rs,
+def tail_kernel(
+    dkv, dq, cosine, sine, x, dh, gain, gain2, fa, fb, f2, wq, n1, o, dho,
+    IG, G1, G3, G2, GO, GQ, GKV, gain_out, *scratch,
 ):
+    (
+        wv, nv, ov, gv, R, dm, dn, p0, p1, v0, v1, below, above, mate_o, sum_o, mate_q, sum_q,
+        ob0, ob1, ob2, ob3, qb0, qb1, qb2, qb3, la, lb, l2, pa, pb, p2, t2, lo, lq, fo, fq,
+        po, pq, to_, gains, s0, s1, s2, s3, s4, total, ss, rs,
+    ) = scratch
     q = coords()
     y, xx, xh, xl, z, c = q["y"], q["x"], q["xh"], q["xl"], q["z"], q["c"]
     zs, ys, xs = ring(q, "z"), ring(q, "y"), ring(q, "x")
-    mate, other = device(q, c=1 - c), device(q, x=xx ^ 1)
-    greet(zs + ys + xs + [mate], q)
+    mate, other, cross = device(q, c=1 - c), device(q, x=xx ^ 1), device(q, x=3 - xx)
+    other_mate = device(q, x=xx ^ 1, c=1 - c)
+    steps = (1, 3, 2)
     k = Copies(ss, rs)
-    steps = (1, 3, 2)
-    z_sum = Sum(k, q, "z", ring_halves(dn), halves(D2.at[0]), halves(D2.at[1]), (p0, p1))
+    get_o, get_g = k.local(o, ov), k.local(dho, gv)
+    get_w, get_n = k.local(wq, wv), k.local(n1, nv)
+    greet(zs + ys + xs + [mate, other_mate], q)
+    near = k.send(dkv.at[xl, :, 1 - c], R.at[0], mate)
+    n = k.n
+    k.n += 2
+    pre, far = [
+        pltpu.make_async_remote_copy(
+            src_ref=src,
+            dst_ref=dst,
+            send_sem=ss.at[n + i],
+            recv_sem=rs.at[n + i],
+            device_id=to,
+            device_id_type=MESH,
+        )
+        for i, (src, dst, to) in enumerate(
+            ((dkv.at[0, :, 1 - c], R.at[1], mate), (R.at[2], R.at[3], other))
+        )
+    ]
+
+    @pl.when(xl == 1)
+    def _():
+        pre.start()
+
     leg_2 = []
     for i, s in enumerate(steps):
         r, cc = quarter((xx + s) % 4, 704)
         leg_2.append(k.send(f2.at[r, cc], l2.at[i], xs[i]))
     leg_a = [k.send(fa.at[(y + s) % 4], la.at[i], ys[i]) for i, s in enumerate(steps)]
     leg_b = [k.send(fb.at[(xx + s) % 4], lb.at[i], xs[i]) for i, s in enumerate(steps)]
-    z_sum.relay(dn.at[(z + 1) % 4, TOP], dn.at[(z + 3) % 4, LOW], (v0, v1))
+    lanes = lambda cc, j: pl.ds(pl.multiple_of(1024 * cc + 256 * j, 256), 256)
+    get_o.wait()
+    get_g.wait()
+    swaps = []
+    for j in range(4):
+        mate_o[j] = tn(ov[...], gv[:, lanes(1 - c, j)]).astype(BF)
+        swaps.append(k.send(mate_o.at[j], sum_o.at[j], mate))
+
+    @pl.when(xl == 1)
+    def _():
+        R[3] = jnp.zeros(R.shape[1:], BF)
+        pre.wait()
+        for i in range(RING):
+            R[2, i] = (dkv[0, i, c].astype(F32) + R[1, i].astype(F32)).astype(BF)
+        far.start()
+
+    for j in range(4):
+        swaps[j].wait_recv()
+        sum_o[j] = (tn(ov[...], gv[:, lanes(c, j)]) + sum_o[j].astype(F32)).astype(BF)
+    half = lambda ref: lambda h: ref.at[h]
+    o_block = lambda j, h: sum_o.at[j, pl.ds(256 * h, 256)]
+    q_block = lambda j, h: sum_q.at[j, pl.ds(2 * h, 2)]
+    o_sum = Sum(k, q, "y", o_block, half(ob2), half(ob3), (ob0.at[0], ob0.at[1]))
     for cp in leg_2:
         cp.wait_recv()
     r, cc = quarter(xx, 704)
     p2[...] = add4(f2[r, cc], l2[0], l2[1], l2[2])
     turned = turn(k, q, [(p2, t2)])
-    heavy = []
-    for i, s in enumerate(steps):
-        cols = pl.ds(pl.multiple_of(256 * ((y + s) % 4), 256), 256)
-        heavy.append(k.send(so.at[:, cols], ro.at[i], ys[i]))
-        heavy.append(k.send(sq.at[(y + s) % 4], rq.at[i], ys[i]))
-    for cp in leg_a:
-        cp.wait_recv()
-    pa[...] = add4(fa[y], la[0], la[1], la[2])
-    for cp in leg_b:
-        cp.wait_recv()
-    pb[...] = add4(fb[xx], lb[0], lb[1], lb[2])
     at = lambda zz, off, n: pl.ds(pl.multiple_of(FZ * zz + off, 128), n)
     rows = pl.ds(pl.multiple_of(128 * c + 64 * xl, 64), 64)
     pair = pl.ds(pl.multiple_of(128 * c, 128), 128)
     f1 = pl.ds(0, FZ)
     rest = SPLIT - FZ
-    own = [
-        (pa.at[:, f1], G1.at[rows, at(z, 0, FZ)]),
-        (pa.at[:, pl.ds(FZ, rest)], G3.at[rows, at(z, 0, rest)]),
-        (pb, G3.at[rows, at(z, rest, FZ - rest)]),
-    ]
-    half_rows = lambda h: pl.ds(pl.multiple_of(128 * c + 64 * xl + 32 * h, 32), 32)
+    quarter_rows = lambda h: pl.ds(pl.multiple_of(128 * c + 64 * xl + 32 * h, 32), 32)
 
     def over_z(src, ref, off, n):
         return Gather(
             k, q, "z", lambda h: src.at[pl.ds(32 * h, 32)],
-            lambda j, h: ref.at[half_rows(h), at(j, off, n)],
+            lambda j, h: ref.at[quarter_rows(h), at(j, off, n)],
         )
 
-    rings = [
-        over_z(pa.at[:, f1], G1, 0, FZ),
-        over_z(pa.at[:, pl.ds(FZ, rest)], G3, 0, rest),
-        over_z(pb, G3, rest, FZ - rest),
-    ]
-    to_x = [k.send(src, dst, other) for src, dst in own]
-    heres = [k.local(src, dst) for src, dst in own]
-    for r in rings:
-        r.relay()
+    spans = [(G1, 0, FZ), (G3, 0, rest), (G3, rest, FZ - rest)]
+    pieces = [pa.at[:, f1], pa.at[:, pl.ds(FZ, rest)], pb]
+    block = lambda i, j: spans[i][0].at[rows, at(j, spans[i][1], spans[i][2])]
+    for cp in leg_a:
+        cp.wait_recv()
+    pa[...] = add4(fa[y], la[0], la[1], la[2])
+    rings = [over_z(pieces[i], *spans[i]) for i in range(2)]
+    to_x = [k.send(pieces[i], block(i, z), other) for i in range(2)]
+    for cp in leg_b:
+        cp.wait_recv()
+    pb[...] = add4(fb[xx], lb[0], lb[1], lb[2])
+    rings.append(over_z(pieces[2], *spans[2]))
+    to_x.append(k.send(pieces[2], block(2, z), other))
+    heres = [k.local(pieces[i], block(i, z)) for i in range(3)]
+    o_sum.relay(o_block((y + 1) % 4, 0), o_block((y + 3) % 4, 1), (ob1.at[0], ob1.at[1]))
+
+    @pl.when(xl == 1)
+    def _():
+        far.wait_send()
+
+    @pl.when(xl == 0)
+    def _():
+        far.wait_recv()
+
+    near.wait_recv()
+    for i in range(RING):
+        part = slice(TOK * i, TOK * i + TOK)
+        w = dkv[xl, i, c].astype(F32) + (R[0, i].astype(F32) + R[3, i].astype(F32))
+        lane = lax.broadcasted_iota(jnp.int32, w.shape, 1)
+        dm[part, :QZ] = dq[i]
+        dm[part, QZ:] = jnp.where(
+            lane < HEAD_DIM, w * cosine[i] - swapped(w) * sine[i], w
+        ).astype(BF)
+    get_w.wait()
+    dn[...] = nt(dm[...], wv[...]).astype(BF).reshape(RING, TOK, D)
+    z_sum = Sum(k, q, "z", ring_halves(dn), halves(below), halves(above), (p0, p1))
+    get_n.wait()
+    cols = lambda cc: pl.ds(pl.multiple_of(1024 * cc, 1024), 1024)
+    shape = (4, 4, 64, MZ)
+    mate_q[...] = tn(nv[:, cols(1 - c)], dm[...]).astype(BF).reshape(shape)
+    swap = k.send(mate_q, sum_q, mate)
+
+    def onward(i):
+        rings[i].near()
+        for j in (rings[i].below, rings[i].above):
+            to_x.append(k.send(block(i, j), block(i, j), other))
+
+    rings[0].relay()
+    onward(0)
+    rings[1].relay()
+    onward(1)
+    swap.wait_recv()
+    own = tn(nv[:, cols(c)], dm[...]).reshape(shape)
+    sum_q[...] = (own + sum_q[...].astype(F32)).astype(BF)
+    q_sum = Sum(k, q, "y", q_block, half(qb2), half(qb3), (qb0.at[0], qb0.at[1]))
+    rings[2].relay()
     turned()
     col = pl.ds(pl.multiple_of(128 * (c * 8 + z * 2 + xl), 128), 128)
     down_x = k.send(t2, G2.at[:, col], other)
     down_here = k.local(t2, G2.at[:, col])
-    blocks = lambda j: [G1.at[rows, at(j, 0, FZ)], G3.at[rows, at(j, 0, FZ)]]
-    for r in rings:
-        r.near()
-    for j in (rings[0].below, rings[0].above):
-        to_x += [k.send(ref, ref, other) for ref in blocks(j)]
+    onward(2)
+    o_sum.end()
+    for h in range(2):
+        part = o_block(y, h)[...].astype(F32) + (ob2[h].astype(F32) + ob3[h].astype(F32))
+        fo[pl.ds(256 * h, 256)] = part.astype(BF)
+    leg_o, leg_q = [], []
+    for i, s in enumerate(steps):
+        r, cc = quarter((xx + s) % 4, 256)
+        leg_o.append(k.send(fo.at[r, cc], lo.at[i], xs[i]))
+    q_sum.relay(q_block((y + 1) % 4, 0), q_block((y + 3) % 4, 1), (qb1.at[0], qb1.at[1]))
+    z_sum.relay(dn.at[(z + 1) % 4, TOP], dn.at[(z + 3) % 4, LOW], (v0, v1))
+    q_sum.end()
+    for h in range(2):
+        part = q_block(y, h)[...].astype(F32) + (qb2[h].astype(F32) + qb3[h].astype(F32))
+        fq[pl.ds(2 * h, 2)] = part.astype(BF)
+    for i, s in enumerate(steps):
+        leg_q.append(k.send(fq.at[(xx + s) % 4], lq.at[i], xs[i]))
+    rings[0].end()
+    to_x.append(k.send(block(0, rings[0].far), block(0, rings[0].far), other))
     down_x.wait_recv()
     down_here.wait()
     down_half = lambda j, h: G2.at[
         pl.ds(352 * h, 352), pl.ds(pl.multiple_of(128 * (c * 8 + j * 2), 256), 256)
     ]
     down_ring = Gather(k, q, "z", lambda h: down_half(z, h), down_half)
-    for r in rings:
-        r.end()
-    to_x += [k.send(ref, ref, other) for ref in blocks(rings[0].far)]
-    down_ring.relay()
-    for cp in heavy:
-        cp.wait_recv()
-    cols = pl.ds(pl.multiple_of(256 * y, 256), 256)
-    ro[0] = add4(so[:, cols], ro[0], ro[1], ro[2])
-    rq[0] = add4(sq[y], rq[0], rq[1], rq[2])
-    done = [k.local(ro.at[0], FO), k.local(rq.at[0], FQ)]
-    down_ring.near()
-    down_ring.end()
-    ref = G2.at[:, pl.ds(pl.multiple_of(1024 * c, 1024), 1024)]
-    last = [k.send(ref, ref, mate)]
-    for cp in to_x:
-        cp.wait_recv()
-    for cp in heres:
-        cp.wait()
-    last += [k.send(ref.at[pair], ref.at[pair], mate) for ref in (G1, G3)]
-    for cp in last:
-        cp.wait_recv()
-    for cp in done:
-        cp.wait()
+    for i in (1, 2):
+        rings[i].end()
+        to_x.append(k.send(block(i, rings[i].far), block(i, rings[i].far), other))
     z_sum.end()
-    k.close()
-
-
-def last_kernel(
-    fq, fo, gain1, gain2, GO, GQ, GKV, gain_out,
-    lq, lo, pq, po, to_, gain, s0, s1, s2, s3, s4, total, ss, rs,
-):
-    q = coords()
-    y, xx, xh, xl, z, c = q["y"], q["x"], q["xh"], q["xl"], q["z"], q["c"]
-    zs, ys, xs = ring(q, "z"), ring(q, "y"), ring(q, "x")
-    mate, other, cross = device(q, c=1 - c), device(q, x=xx ^ 1), device(q, x=3 - xx)
-    gain[...] = jnp.zeros_like(gain)
+    back, gain1 = rms_back(
+        x[...].astype(F32),
+        gain[...],
+        from_pieces(dn[z].astype(F32) + (below[...].astype(F32) + above[...].astype(F32))),
+    )
+    IG[...] = dh[...] + back
+    gains[...] = jnp.zeros_like(gains)
     for d in range(8):
-        gain[d // 2, d % 2, 0:1] = gain1[:, 256 * d : 256 * d + 256]
-        gain[d // 2, d % 2, 1:2] = gain2[:, 256 * d : 256 * d + 256]
-    greet(zs + ys + xs + [mate], q)
-    k = Copies(ss, rs)
-    steps = (1, 3, 2)
-    leg_o, leg_q = [], []
-    for i, s in enumerate(steps):
-        r, cc = quarter((xx + s) % 4, 256)
-        leg_o.append(k.send(fo.at[r, cc], lo.at[i], xs[i]))
-    gain_y = [k.send(gain.at[(y + s) % 4], s0.at[y], ys[i]) for i, s in enumerate(steps)]
-    gain_here = k.local(gain.at[y], s0.at[y])
-    for i, s in enumerate(steps):
-        leg_q.append(k.send(fq.at[(xx + s) % 4], lq.at[i], xs[i]))
+        gains[d // 2, d % 2, 0:1] = gain1[:, 256 * d : 256 * d + 256]
+        gains[d // 2, d % 2, 1:2] = gain2[:, 256 * d : 256 * d + 256]
+    gain_y = [k.send(gains.at[(y + s) % 4], s0.at[y], ys[i]) for i, s in enumerate(steps)]
+    gain_here = k.local(gains.at[y], s0.at[y])
     for cp in leg_o:
         cp.wait_recv()
     r, cc = quarter(xx, 256)
     po[...] = add4(fo[r, cc], lo[0], lo[1], lo[2])
-    turned = turn(k, q, [(po, to_)])
+    o_turned = turn(k, q, [(po, to_)])
+    down_ring.relay()
+    for cp in leg_q:
+        cp.wait_recv()
+    pq[...] = add4(fq[xx], lq[0], lq[1], lq[2])
+    qc = lambda j: pl.ds(pl.multiple_of(QZ * j, 128), QZ)
+    kc = lambda j: pl.ds(pl.multiple_of(128 * j, 128), 128)
+    q_pieces = [
+        (pq.at[:, pl.ds(0, QZ)], GQ.at[rows, qc(z)]),
+        (pq.at[:, pl.ds(QZ, 128)], GKV.at[rows, kc(z)]),
+    ]
+    q_x = [k.send(src, dst, other) for src, dst in q_pieces]
+    q_here = [k.local(src, dst) for src, dst in q_pieces]
     for cp in gain_y:
         cp.wait_recv()
     gain_here.wait()
     s1[0] = (s0[0] + s0[1]) + (s0[2] + s0[3])
     gain_x = k.send(s1.at[0, 1 - xh], s1.at[1, 0], cross)
-    for cp in leg_q:
-        cp.wait_recv()
-    pq[...] = add4(fq[xx], lq[0], lq[1], lq[2])
-    rows = pl.ds(pl.multiple_of(128 * c + 64 * xl, 64), 64)
-    qc = lambda j: pl.ds(pl.multiple_of(QZ * j, 128), QZ)
-    kc = lambda j: pl.ds(pl.multiple_of(128 * j, 128), 128)
-    own = [
-        (pq.at[:, pl.ds(0, QZ)], GQ.at[rows, qc(z)]),
-        (pq.at[:, pl.ds(QZ, 128)], GKV.at[rows, kc(z)]),
-    ]
-    q_x = [k.send(src, dst, other) for src, dst in own]
-    q_here = [k.local(src, dst) for src, dst in own]
     gain_x.wait_recv()
     s2[z] = s1[0, xh] + s1[1, 0]
     gain_z = [k.send(s2.at[z], s2.at[z], to) for to in zs]
-    turned()
-    col = pl.ds(pl.multiple_of(128 * (c * 8 + z * 2 + xl), 128), 128)
+    o_turned()
     o_x = k.send(to_, GO.at[:, col], other)
     o_here = k.local(to_, GO.at[:, col])
+    for cp in to_x:
+        cp.wait_recv()
+    for cp in heres:
+        cp.wait()
+    last = [k.send(ref.at[pair], ref.at[pair], mate) for ref in (G1, G3)]
     for cp in q_x:
         cp.wait_recv()
     for cp in q_here:
@@ -860,28 +892,34 @@
     half_rows = lambda h: pl.ds(pl.multiple_of(128 * c + 64 * h, 64), 64)
     q_half = lambda j, h: GQ.at[half_rows(h), qc(j)]
     kv_half = lambda j, h: GKV.at[half_rows(h), kc(j)]
-    rings = [Gather(k, q, "z", lambda h: f(z, h), f) for f in (q_half, kv_half)]
+    last_rings = [
+        Gather(k, q, "z", lambda h: q_half(z, h), q_half),
+        Gather(k, q, "z", lambda h: kv_half(z, h), kv_half),
+    ]
+    down_ring.near()
+    down_ring.end()
+    last.append(k.send(G2.at[:, cols(c)], G2.at[:, cols(c)], mate))
     o_x.wait_recv()
     o_here.wait()
     o_half = lambda j, h: GO.at[
         pl.ds(128 * h, 128), pl.ds(pl.multiple_of(128 * (c * 8 + j * 2), 256), 256)
     ]
-    rings.append(Gather(k, q, "z", lambda h: o_half(z, h), o_half))
+    last_rings.append(Gather(k, q, "z", lambda h: o_half(z, h), o_half))
     for cp in gain_z:
         cp.wait_recv()
     s3[0] = (s2[0] + s2[1]) + (s2[2] + s2[3])
     gain_x = k.send(s3.at[0], s3.at[1], other)
-    for r in rings:
-        r.relay()
+    last_rings[0].relay()
+    last_rings[1].relay()
     gain_x.wait_recv()
     s4[0] = s3[0] + s3[1]
     gain_c = k.send(s4.at[0], s4.at[1], mate)
-    for r in rings:
+    last_rings[2].relay()
+    for r in last_rings:
         r.near()
         r.end()
-    pair = pl.ds(pl.multiple_of(128 * c, 128), 128)
-    refs = [GQ.at[pair], GKV.at[pair], GO.at[:, pl.ds(pl.multiple_of(1024 * c, 1024), 1024)]]
-    last = [k.send(ref, ref, mate) for ref in refs]
+    refs = [GQ.at[pair], GKV.at[pair], GO.at[:, cols(c)]]
+    last += [k.send(ref, ref, mate) for ref in refs]
     gain_c.wait_recv()
     total[...] = s4[0] + s4[1]
     gain_done = k.local(total, gain_out)
@@ -1130,23 +1168,6 @@
     gain_grad = jnp.sum(grad * unit, axis=0, keepdims=True)
     inner = grad * gain
     return scale * (inner - unit * jnp.mean(inner * unit, axis=-1, keepdims=True)), gain_grad
-
-
-def norm_back_kernel(v, base, a, b, c, gain, grad, gain_out):
-    dn = from_pieces(a[...].astype(F32) + (b[...].astype(F32) + c[...].astype(F32)))
-    back, gain_grad = rms_back(v[...].astype(F32), gain[...], dn)
-    grad[...] = base[...] + back
-    gain_out[...] = gain_grad
-
-
-def norm_back(v, base, parts, gain):
-    return pl.pallas_call(
-        norm_back_kernel,
-        name="norm_back",
-        cost_estimate=cost(4),
-        out_shape=[jax.ShapeDtypeStruct((TOK, D), F32), jax.ShapeDtypeStruct((1, D), F32)],
-        compiler_params=PARAMS,
-    )(v, base, *parts, gain)
 
 
 def pick(v, index, axis=0):
@@ -1251,95 +1272,91 @@
     both = jnp.concatenate([dgate, dup], axis=1)
     dn2 = jnp.einsum("tf,df->td", both, W13, preferred_element_type=F32)
     dn2 = dn2.astype(BF).reshape(RING, TOK, D)
-    out_part = dot(hidden, W2).astype(BF).reshape(RING, TOK, D)
-    half = lambda v, j: lax.dynamic_slice_in_dim(v, 1024 * j, 1024, 1)
-    outer = lambda a, b: jnp.einsum("ta,tb->ab", a, b, preferred_element_type=F32)
     rest = 2 * FZ - SPLIT
     buffers = []
-    for shape in ((704, 256), (2, 64, SPLIT), (2, 64, rest)):
+    for shape in ((2, 64, SPLIT), (2, 64, rest), (704, 256)):
         buffers += [pltpu.VMEM((2,) + shape, BF)] * 4
-    DH, D3, fa, fb, f2, dh, gain2 = talk(
+    DH, fa, fb, f2, dheads, output, dh, gain2 = talk(
         back_kernel,
         "back",
         4,
         60,
         100,
-        (dn2, out_part, hidden, G, N2, both, h, gain_ffn),
+        (dn2, hidden, G, N2, both, W2, WO, h, gain_ffn),
         [
             ((RING, TOK, D), BF),
-            ((2, TOK, D), BF),
             ((2, 2, 64, SPLIT), BF),
             ((2, 2, 64, rest), BF),
             ((2, 704, 256), BF),
+            ((RING * TOK, QZ), BF),
+            ((TOK, D), F32),
             ((TOK, D), F32),
             ((1, D), F32),
         ],
         scratch=[
             *[pltpu.VMEM(HALF, BF)] * 6,
-            *[pltpu.VMEM((TOK, D), BF)] * 2,
+            *[pltpu.VMEM((TOK, D), BF)] * 4,
             *[pltpu.VMEM(HALF, BF)] * 2,
             *[pltpu.VMEM((TOK, D), BF)] * 2,
+            pltpu.VMEM((RING, TOK, D), BF),
             pltpu.VMEM((RING * TOK, FZ), BF),
             pltpu.VMEM((RING * TOK, D), BF),
             pltpu.VMEM((RING * TOK, D), BF),
             pltpu.VMEM((RING * TOK, 2 * FZ), BF),
+            pltpu.VMEM((QZ, D), BF),
+            pltpu.VMEM((2, FZ, 512), BF),
             pltpu.VMEM((FZ, RING * TOK), BF),
+            pltpu.VMEM((RING, TOK, D), BF),
             pltpu.VMEM((4, FZ, 256), BF),
             pltpu.VMEM((4, 4, 64, 2 * FZ), BF),
             pltpu.VMEM((4, FZ, 256), BF),
             pltpu.VMEM((4, 4, 64, 2 * FZ), BF),
             *buffers,
         ],
-        near=(6, 7),
-        near_out=(5, 6),
+        near=(7, 8),
+        near_out=(4, 5, 6, 7),
     )
     fa, fb = fa.reshape(4, 64, SPLIT), fb.reshape(4, 64, rest)
     f2 = f2.reshape(1408, 256)
     DH = DH.reshape(RING * TOK, D)
-    dheads = jnp.einsum("td,qd->tq", DH, WO, preferred_element_type=F32).astype(BF)
     dquery, dkv = attend_back(
         info, query, KV, start, heads_out, dheads.reshape(RING, TOK, QZ), logsum, cosine, sine
     )
-    dkv = dkv.reshape(2, 4, 2, TOK, 128)
-    (dkv_rot,) = talk(
-        dkv_kernel,
-        "dkv",
-        5,
-        8,
-        4,
-        (dkv, cosine, sine),
-        [((RING, TOK, 128), BF)],
-        scratch=[pltpu.VMEM((3, RING, TOK, 128), BF)],
-        near=(0, 1, 2),
-        near_out=(0,),
-    )
-    dmixed = jnp.concatenate([dquery, dkv_rot], axis=2).reshape(RING * TOK, MZ)
-    dn1 = jnp.einsum("tc,dc->td", dmixed, WQ, preferred_element_type=F32)
-    dn1 = dn1.astype(BF).reshape(RING, TOK, D)
-
-    n1 = n1.reshape(RING * TOK, D)
-    other_o = move(outer(o, half(DH, 1 - c)).astype(BF), "c", 1)
-    sum_o = (outer(o, half(DH, c)) + other_o.astype(F32)).astype(BF)
-    other_q = move(outer(half(n1, 1 - c), dmixed).astype(BF), "c", 1)
-    sum_q = (outer(half(n1, c), dmixed) + other_q.astype(F32)).astype(BF)
-    sum_q = sum_q.reshape(4, 4, 64, MZ)
-    D1, G1, G3, G2, fq, fo = talk(
-        wide_kernel,
-        "wide",
+    small = (8, 256)
+    input_grad, G1, G3, G2, GO, GQ, GKV, gain_out = talk(
+        tail_kernel,
+        "tail",
         6,
-        55,
-        90,
-        (dn1, fa, fb, f2, sum_q, sum_o),
+        75,
+        170,
+        (
+            dkv.reshape(2, 4, 2, TOK, 128), dquery, cosine, sine, x, dh, gain_attn, gain2,
+            fa, fb, f2, WQ, n1.reshape(RING * TOK, D), o, DH,
+        ),
         [
-            ((2, TOK, D), BF),
+            ((TOK, D), F32),
             ((256, 4 * FZ), BF),
             ((256, 4 * FZ), BF),
             ((704, D), BF),
-            ((4, 64, MZ), BF),
-            ((512, 256), BF),
+            ((256, D), BF),
+            ((256, QDIM), BF),
+            ((256, 2 * KVDIM), BF),
+            (small, F32),
         ],
         scratch=[
+            pltpu.VMEM((D, MZ), BF),
+            pltpu.VMEM((RING * TOK, D), BF),
+            pltpu.VMEM((RING * TOK, QZ), BF),
+            pltpu.VMEM((RING * TOK, D), BF),
+            pltpu.VMEM((4, RING, TOK, 128), BF),
+            pltpu.VMEM((RING * TOK, MZ), BF),
+            pltpu.VMEM((RING, TOK, D), BF),
             *[pltpu.VMEM(HALF, BF)] * 4,
+            *[pltpu.VMEM((TOK, D), BF)] * 2,
+            *[pltpu.VMEM((4, QZ, 256), BF)] * 2,
+            *[pltpu.VMEM((4, 4, 64, MZ), BF)] * 2,
+            *[pltpu.VMEM((2, 256, 256), BF)] * 4,
+            *[pltpu.VMEM((2, 2, 64, MZ), BF)] * 4,
             pltpu.VMEM((3, 64, SPLIT), BF),
             pltpu.VMEM((3, 64, rest), BF),
             pltpu.VMEM((3, 704, 128), BF),
@@ -1347,32 +1364,12 @@
             pltpu.VMEM((64, rest), BF),
             pltpu.VMEM((704, 128), BF),
             pltpu.VMEM((704, 128), BF),
-            pltpu.VMEM((3, 4, 64, MZ), BF),
-            pltpu.VMEM((3, 512, 256), BF),
-        ],
-        near=(0, 1, 2, 3, 4, 5),
-    )
-    input_grad, gain1 = norm_back(x, dh, (pick(dn1, z), D1[0], D1[1]), gain_attn)
-
-    small = (8, 256)
-    GO, GQ, GKV, gain_out = talk(
-        last_kernel,
-        "last",
-        7,
-        30,
-        60,
-        (fq, fo, gain1, gain2),
-        [
-            ((256, D), BF),
-            ((256, QDIM), BF),
-            ((256, 2 * KVDIM), BF),
-            (small, F32),
-        ],
-        scratch=[
+            pltpu.VMEM((3, 256, 128), BF),
             pltpu.VMEM((3, 64, MZ), BF),
-            pltpu.VMEM((3, 256, 128), BF),
+            pltpu.VMEM((512, 256), BF),
+            pltpu.VMEM((4, 64, MZ), BF),
+            pltpu.VMEM((256, 128), BF),
             pltpu.VMEM((64, MZ), BF),
-            pltpu.VMEM((256, 128), BF),
             pltpu.VMEM((256, 128), BF),
             pltpu.VMEM((4, 2) + small, F32),
             pltpu.VMEM((4, 2) + small, F32),
@@ -1382,13 +1379,12 @@
             pltpu.VMEM((2,) + small, F32),
             pltpu.VMEM(small, F32),
         ],
-        near=(0, 1, 2, 3),
+        near=tuple(range(11)),
+        near_out=(0,),
     )
     pairs = GKV.reshape(256, 4, 2, HEAD_DIM)
     flat = lambda v: v.reshape(256, -1)
     grad_qkv = jnp.concatenate([GQ, flat(pairs[:, :, 0]), flat(pairs[:, :, 1])], axis=1)
-    own = pick(out_part, z).astype(F32)
-    output = h + (own + (D3[0].astype(F32) + D3[1].astype(F32)))
     return (
         output[None],
         input_grad[None],

time: 416 us -> 345 us (0.83)
  Pallas kernels: 321 us -> 285 us
  matrix products: 51.5 us -> 26 us
  starting transfers between devices: 4.88 us -> 0 us
    pallas_call x7 -> x5, Pallas kernels: 279 us -> 247 us  [talk(): pl.pallas_call(kernel, name=name, out_shape=[jax.ShapeDtypeStruct(s, t) f...]
    dot_general x6 -> x0, matrix products: 15.1 us -> none  [the longest x4 9.27 us: body(): jnp.einsum('ta,tb->ab', a, b, preferred_element_type=F32)]
    dot_general x4 -> x3, matrix products: 25.2 us -> 12.5 us  [dot(): return jnp.dot(a, b, preferred_element_type=F32)]
    ppermute x2 -> x0, starting transfers between devices: 4.88 us -> none  [move(): return lax.ppermute(v, ('dp', 'ctx'), shift_pairs(axis, by))]
  transfers between devices with their start and end apart: 2 -> 0, of which waited for: 0 -> 0; matrix products, arithmetic and copies ran while one was open for 4% -> 0% of each run, Pallas kernels for 7% -> 0%
where the time goes in v4:
time: 345 us; the launch traced here: 342 us
  Pallas kernels  285 us (83%)
  matrix products  26 us (8%)
  other arithmetic  20.7 us (6%)
  local copies, waits for them, and re-layouts  9.28 us (3%)
    pallas_call x5, Pallas kernels, talk(): pl.pallas_call(kernel, name=name, out_shape=[jax.ShapeDtypeStruct(s, t) f...  247 us
    pallas_call x1, Pallas kernels, attend_back(): pl.pallas_call(attend_back_kernel, name='attend_back', cost_estimate=cost...  17.4 us
    pallas_call x1, Pallas kernels, attend(): pl.pallas_call(attend_kernel, name='attend', cost_estimate=cost(12), grid...  14.5 us
    dot_general x3, matrix products, dot(): return jnp.dot(a, b, preferred_element_type=F32)  12.5 us
    dot_general x1, matrix products, body(): dn2 = jnp.einsum('tf,df->td', both, W13, preferred_element_type=F32)  7.5 us

profile of v4, /device:TPU:1, one launch (start us, length us, event | category | flops | bytes accessed | tf_op | source)
XLA Modules:
  0.0 341.9 jit_solution(12469306619681334648)
XLA Ops:
  0.7 1.2 broadcast_in_dim.29.na
  1.9 1.2 broadcast_in_dim.30.nf
  3.1 45.1 %fetch.1 = (bf16[4,128,2048]{2,1,0:T(8,128)(2,1)}, bf16[4,128,2048]{2,1,0:T(8,128)(2,1)}, s32[2,4,2,8,128]{4,3,2,1,0:T(8,128)}, bf16[4,2,32,256]{3,2,1,0:T(8,128...) custom-call(bf16[128,2048]{1,0:T(8,128)(2,1)} %bitcast.62, ...), custom_call_target="tpu_custom_call" | custom-call | flops 40000000000 | tf_op jit(solution)/shard_map/fetch/pallas_call | solution.py:275
  52.5 2.0 fusion.4
  54.4 5.9 %project.1 = (bf16[4,128,2048]{2,1,0:T(8,128)(2,1)}, bf16[4,128,512]{2,1,0:T(8,128)(2,1)}, bf16[4,128,128]{2,1,0:T(8,128)(2,1)}) custom-call(bf16[4,128,2048]{2,1,0:T(8,128)(2,1)} %get-tuple-element.46.x, f32[1,2048]{1,0:T(1,128)} %convert.2.gain, bf16[2048,640]{1,0:T(8,128)(2,1)} %bitcast.70, f32[4,128,128]{2,1,0:T(8,128)} %get-tuple-element.89.cosine, ...), custom_call_target="tpu_custom_call" | custom-call | flops 7000000000 | tf_op jit(solution)/shard_map/project/pallas_call | solution.py:980
  60.3 5.7 %kv.1 = bf16[2,4,2,128,128]{4,3,2,1,0:T(8,128)(2,1)} custom-call(bf16[4,128,128]{2,1,0:T(8,128)(2,1)} %get-tuple-element.50.kv), custom_call_target="tpu_custom_call" | custom-call | flops 7000000000 | tf_op jit(solution)/shard_map/kv/pallas_call | solution.py:275
  66.0 14.5 %attend.1 = (bf16[4,128,512]{2,1,0:T(8,128)(2,1)}, f32[4,1,1024]{2,1,0:T(1,128)}) custom-call(s32[2,4]{1,0:T(2,128)} %pad_add_fusion.info, bf16[4,128,512]{2,1,0:T(8,128)(2,1)} %get-tuple-element.49.query, bf16[16,128,128]{2,1,0:T(8,128)(2,1)} %bitcast.87, s32[4,1,128]{2,1,0:T(1,128)} %bitcast.56), custom_call_target="tpu_custom_call" | custom-call | flops 12000000000 | tf_op jit(solution)/shard_map/attend/pallas_call | solution.py:1069
  80.5 3.6 %convolution_convert_fusion.1 = bf16[512,2048]{1,0:T(8,128)(2,1)} fusion(bf16[512,512]{1,0:T(8,128)(2,1)} %bitcast.85, bf16[512,2048]{1,0:T(8,128)(2,1)S(1)} %bitcast.75), kind=kOutput, calls=%fused_computation.6 | convolution fusion | flops 1074790400 | bytes 4718592 | tf_op jit(solution)/shard_map/dot_general | solution.py:1178
  84.2 45.3 %middle.1 = (bf16[4,128,2048]{2,1,0:T(8,128)(2,1)}, f32[128,2048]{1,0:T(8,128)}, bf16[2,4,2,2,64,2816]{5,4,3,2,1,0:T(8,128)(2,1)}, bf16[2,704,2048]{2,1,0:T(8,128)(2,1)}) custom-call(bf16[4,128,2048]{2,1,0:T(8,128)(2,1)} %bitcast.82, bf16[128,2048]{1,0:T(8,128)(2,1)} %bitcast.63, f32[1,2048]{1,0:T(1,128)} %convert.3.gain, ...), custom_call_target="tpu_custom_call", output_to_operand_aliasing={{2}: (4, {})} | custom-call | flops 41999998976 | tf_op jit(solution)/shard_map/middle/pallas_call | solution.py:275
  129.5 6.0 %fusion.12 = f32[512,1408]{1,0:T(8,128)S(1)} fusion(bf16[512,2048]{1,0:T(8,128)(2,1)S(1)} %bitcast.73, bf16[1408,2048]{1,0:T(8,128)(2,1)} %bitcast.68), kind=kOutput, calls=%fused_computation.36 | convolution fusion | flops 2952790016 | bytes 10747904 | tf_op jit(solution)/shard_map/td,fd->tf/dot_general | solution.py:1268
  136.1 3.4 %fusion = f32[512,1408]{1,0:T(8,128)S(1)} fusion(bf16[512,2048]{1,0:T(8,128)(2,1)S(1)} %bitcast.79, bf16[2048,2816]{1,0:T(8,128)(2,1)S(1)} %bitcast.65), kind=kOutput, calls=%fused_computation | convolution fusion | flops 2952790016 | bytes 10747904 | tf_op jit(solution)/shard_map/dot_general | solution.py:1178
  139.5 5.5 %multiply_convert_fusion = (bf16[512,1408]{1,0:T(8,128)(2,1)}, bf16[512,1408]{1,0:T(8,128)(2,1)S(1)}, bf16[512,1408]{1,0:T(8,128)(2,1)S(1)}) fusion(f32[512,1408]{1,0:T(8,128)S(1)} %fusion, f32[512,1408]{1,0:T(8,128)S(1)} %fusion.12, bf16[512,2048]{1,0:T(8,128)(2,1)S(1)} %bitcast.80, bf16[2048,2816]{1,0:T(8,128)(2,1)S(1)} %bitcast.66), kind=kOutput, calls=%fused_computation.8 | convolution fusion | flops 2964324352 | bytes 17956864 | tf_op jit(solution)/shard_map/dot_general | solution.py:1178
  145.0 7.5 %convolution_convert_fusion = bf16[512,2048]{1,0:T(8,128)(2,1)} fusion(bf16[2048,2816]{1,0:T(8,128)(2,1)S(1)} %bitcast.67, bf16[512,1408]{1,0:T(8,128)(2,1)S(1)} %get-tuple-element.81, bf16[512,1408]{1,0:T(8,128)(2,1)S(1)} %get-tuple-element.80), kind=kOutput, calls=%fused_computation.5 | convolution fusion | flops 5912395776 | bytes 16515072 | tf_op jit(solution)/shard_map/tf,df->td/dot_general | solution.py:1273
  152.5 1.8 pad_maximum_fusion.both
  154.3 60.2 %back.1 = (bf16[4,128,2048]{2,1,0:T(8,128)(2,1)}, bf16[2,2,64,2048]{3,2,1,0:T(8,128)(2,1)}, bf16[2,2,64,768]{3,2,1,0:T(8,128)(2,1)}, bf16[2,704,256]{2,1,0:T(8,1...) custom-call(bf16[4,128,2048]{2,1,0:T(8,128)(2,1)} %bitcast.81, ...), custom_call_target="tpu_custom_call" | custom-call | flops 60000002048 | tf_op jit(solution)/shard_map/back/pallas_call | solution.py:275
  214.5 17.4 %attend_back.1 = (bf16[4,128,512]{2,1,0:T(8,128)(2,1)}, bf16[16,128,128]{2,1,0:T(8,128)(2,1)}) custom-call(s32[2,4]{1,0:T(2,128)} %pad_add_fusion.info, bf16[4,128,512]{2,1,0:T(8,128)(2,1)} %get-tuple-element.49.query, bf16[16,128,128]{2,1,0:T(8,128)(2,1)} %bitcast.88, s32[4,1,128]{2,1,0:T(1,128)} %bitcast.57, bf16[4,128,512]{2,1,0:T(8,128)(2,1)} %get-tuple-element.51.out, ...), custom_call_target="tpu_custom_call" | custom-call | flops 15000000512 | tf_op jit(solution)/shard_map/attend_back/pallas_call | solution.py:1137
  231.9 90.7 %tail.1 = (f32[128,2048]{1,0:T(8,128)}, bf16[256,5632]{1,0:T(8,128)(2,1)}, bf16[256,5632]{1,0:T(8,128)(2,1)}, bf16[704,2048]{1,0:T(8,128)(2,1)}, bf16[256,2048]{...) custom-call(bf16[2,4,2,128,128]{4,3,2,1,0:T(8,128)(2,1)} %bitcast.89, ...), custom_call_target="tpu_custom_call" | custom-call | flops 74999996416 | tf_op jit(solution)/shard_map/tail/pallas_call | solution.py:275
  322.6 1.4 fusion.11
  324.0 1.1 copy.23
  325.3 3.2 maximum_convert_fusion
  328.5 1.6 convert_element_type.70
  330.1 3.2 convert_element_type.71
  333.3 3.2 convert_element_type.72
  336.5 3.3 convert_element_type.73
  (38 shorter events, 6.9 us)
Async XLA Ops:
  49.7 10.6 %copy-start.6 = (s32[4,128]{1,0:T(4,128)}, s32[4,128]{1,0:T(4,128)S(1)}, u32[]{:S(2)}) copy-start(s32[4,128]{1,0:T(4,128)S(1)} %convert_reduce_fusion) | copy-start | bytes 6148
  66.0 14.5 %copy-start.9 = (bf16[2,256,2048]{2,1,0:T(8,128)(2,1)S(1)}, bf16[2,256,2048]{2,1,0:T(8,128)(2,1)}, u32[]{:S(2)}) copy-start(bf16[2,256,2048]{2,1,0:T(8,128)(2,1)} %get-tuple-element.52) | copy-start | bytes 6291460
  84.1 45.3 %copy-start.8 = (bf16[4,128,2048]{2,1,0:T(8,128)(2,1)S(1)}, bf16[4,128,2048]{2,1,0:T(8,128)(2,1)}, u32[]{:S(2)}) copy-start(bf16[4,128,2048]{2,1,0:T(8,128)(2,1)} %get-tuple-element.44) | copy-start | bytes 6291460
  129.5 6.0 %copy-start.7 = (bf16[2,4,2,2,64,2816]{5,4,3,2,1,0:T(8,128)(2,1)S(1)}, bf16[2,4,2,2,64,2816]{5,4,3,2,1,0:T(8,128)(2,1)}, u32[]{:S(2)}) copy-start(bf16[2,4,2,2,64,2816]{5,4,3,2,1,0:T(8,128)(2,1)} %get-tuple-element.57) | copy-start | bytes 34603012
  129.5 6.6 %copy-start.10 = (bf16[4,128,2048]{2,1,0:T(8,128)(2,1)S(1)}, bf16[4,128,2048]{2,1,0:T(8,128)(2,1)}, u32[]{:S(2)}) copy-start(bf16[4,128,2048]{2,1,0:T(8,128)(2,1)} %get-tuple-element.56) | copy-start | bytes 6291460
  322.6 5.9 %copy-start.3 = (bf16[256,2048]{1,0:T(8,128)(2,1)S(1)}, bf16[256,2048]{1,0:T(8,128)(2,1)}, u32[]{:S(2)}) copy-start(bf16[256,2048]{1,0:T(8,128)(2,1)} %get-tuple-element.75) | copy-start | bytes 3145732
  325.3 4.7 %copy-start.2 = (bf16[256,5632]{1,0:T(8,128)(2,1)S(1)}, bf16[256,5632]{1,0:T(8,128)(2,1)}, u32[]{:S(2)}) copy-start(bf16[256,5632]{1,0:T(8,128)(2,1)} %get-tuple-element.76) | copy-start | bytes 8650756
  330.1 3.2 copy-start.1
  333.3 3.2 copy-start
  336.5 3.3 copy-start.4
  336.5 4.3 %copy-start.5 = (f32[128,2048]{1,0:T(8,128)S(1)}, f32[128,2048]{1,0:T(8,128)}, u32[]{:S(2)}) copy-start(f32[128,2048]{1,0:T(8,128)} %get-tuple-element.71) | copy-start | bytes 3145732

commit v5 on v4

--- a/solution.py
+++ b/solution.py
@@ -291,9 +291,10 @@
     )(*ins)
 
 
-def fetch_kernel(
-    x, g, seg, na, nf, wq, wo, w1, w3, w2, X, G, SEG, GN, WQ, WO, W13, T2,
-    TO, TV, QP, KT, VT, P1, P3, SG, NG, ss, rs,
+def front_kernel(
+    x, g, seg, na, nf, freq, wq, wo, w1, w3, w2,
+    G, WQ, WO, W13, T2, N1, Q, KV, COS, SIN, START, GA, GF,
+    TO, TV, QP, KT, VT, P1, P3, SG, NG, SEGS, GN, XV, WV, NV, QV, KVV, ss, rs,
 ):
     q = coords()
     y, xx, xh, xl, z, c = q["y"], q["x"], q["xh"], q["xl"], q["z"], q["c"]
@@ -319,9 +320,10 @@
     NG[0:16] = jnp.broadcast_to(na[...].astype(F32), (16, 256)).astype(BF)
     NG[16:32] = jnp.broadcast_to(nf[...].astype(F32), (16, 256)).astype(BF)
     greet(zs + ys + xs + [mate, other_mate])
+    seg_z = [k.send(SG, SEGS.at[xl, z, c], to) for to in zs]
+    x_ring = Gather(k, q, "z", halves(x), ring_halves(XV))
     lanes = lambda j, n=1: pl.ds(pl.multiple_of(128 * j, 128 * n), 128 * n)
     dealt = deal(k, q, wo, lambda j: lanes(c * 8 + j * 2 + xl), TO)
-    x_ring = Gather(k, q, "z", halves(x), ring_halves(X))
     for cp in loads:
         cp.wait()
     odd = z % 2 == 1
@@ -332,115 +334,141 @@
     QP[:, QZ:] = jnp.where(lane < HEAD_DIM, kt, vt).astype(BF)
     f1, f3 = pl.ds(0, FZ), pl.ds(FZ, FZ)
     top, low = pl.ds(0, 32), pl.ds(32, 32)
-    q_top = [k.send(QP.at[top], WQ.at[c, y, xh, xl, top], to) for to in xs]
-    q_low = [k.send(QP.at[low], WQ.at[c, y, xh, xl, low], to) for to in ys]
-    seg_z = [k.send(SG, SEG.at[xl, z, c], to) for to in zs]
+    thirty = lambda h: pl.ds(32 * h, 32)
+    q_top = [k.send(QP.at[top], WV.at[c, y, xh, xl, top], to) for to in xs]
+    q_low = [k.send(QP.at[low], WV.at[c, y, xh, xl, low], to) for to in ys]
     gn_y = [k.send(NG, GN.at[y, xh], to) for to in ys]
-    q_here = k.local(QP, WQ.at[c, y, xh, xl])
-    seg_here = k.local(SG, SEG.at[xl, z, c])
+    up_y = Gather(
+        k, q, "y", lambda h: P3.at[thirty(h)], lambda j, h: W13.at[c, j, xh, xl, thirty(h), f3]
+    )
+    gate_x = Gather(
+        k, q, "x", lambda h: P1.at[thirty(h)],
+        lambda j, h: W13.at[c, y, j // 2, j % 2, thirty(h), f1],
+    )
+    q_here = k.local(QP, WV.at[c, y, xh, xl])
+    seg_here = k.local(SG, SEGS.at[xl, z, c])
     gn_here = k.local(NG, GN.at[y, xh])
-    a3_here = k.local(P3, W13.at[c, y, xh, xl, :, f3])
-    heres = [
-        k.local(P1, W13.at[c, y, xh, xl, :, f1]),
-        k.local(x, X.at[z]),
-        k.local(g, G.at[z]),
-    ]
+    x_here = k.local(x, XV.at[z])
+    up_here = k.local(P3, W13.at[c, y, xh, xl, :, f3])
+    heres = [k.local(P1, W13.at[c, y, xh, xl, :, f1]), k.local(g, G.at[z])]
     dealt()
     o1 = [k.send(TO, WO.at[xh, :, lanes(c * 8 + y * 2 + xl)], to) for to in xs]
     o1_here = k.local(TO, WO.at[xh, :, lanes(c * 8 + y * 2 + xl)])
-    thirty = lambda h: pl.ds(32 * h, 32)
-    up_y = Gather(
-        k, q, "y", lambda h: P3.at[thirty(h)], lambda j, h: W13.at[c, j, xh, xl, thirty(h), f3]
-    )
-    gate_x = Gather(
-        k, q, "x", lambda h: P1.at[thirty(h)],
-        lambda j, h: W13.at[c, y, j // 2, j % 2, thirty(h), f1],
-    )
+    for cp in seg_z:
+        cp.wait_recv()
+    seg_here.wait()
+    part = SEGS.at[xl, :, c]
+    seg2 = [k.send(part, part, to) for to in (mate, other, other_mate)]
     q_here.wait()
     for cp in q_top:
         cp.wait_recv()
-    q_y = Gather(k, q, "y", lambda h: WQ.at[c, y, h, :, top], lambda j, h: WQ.at[c, j, h, :, top])
-    for cp in q_low:
-        cp.wait_recv()
-    q_half = lambda j, h: WQ.at[c, pl.ds(2 * h, 2), j // 2, j % 2, low]
-    q_x = Gather(k, q, "x", lambda h: q_half(xx, h), q_half)
-    for cp in seg_z:
-        cp.wait_recv()
-    seg_here.wait()
-    part = SEG.at[xl, :, c]
-    seg2 = [k.send(part, part, to) for to in (mate, other, other_mate)]
+    q_y = Gather(k, q, "y", lambda h: WV.at[c, y, h, :, top], lambda j, h: WV.at[c, j, h, :, top])
     for cp in gn_y:
         cp.wait_recv()
     gn_here.wait()
     gn2 = k.send(GN.at[:, xh], GN.at[:, xh], device(q, x=3 - xx))
+    gate_x.relay()
+    for cp in q_low:
+        cp.wait_recv()
+    q_half = lambda j, h: WV.at[c, pl.ds(2 * h, 2), j // 2, j % 2, low]
+    q_x = Gather(k, q, "x", lambda h: q_half(xx, h), q_half)
     x_ring.relay()
     g_ring = Gather(k, q, "z", halves(g), ring_halves(G))
     up_y.relay()
-    gate_x.relay()
     for cp in o1:
         cp.wait_recv()
     o1_here.wait()
     o_half = lambda j, h: WO.at[h, :, lanes(c * 8 + j * 2, 2)]
     o_y = Gather(k, q, "y", lambda h: o_half(y, h), o_half)
+    for cp in seg2:
+        cp.wait_recv()
+    docs = [SEGS[i // 8, (i // 2) % 4, i % 2, 0:1].astype(F32) for i in range(16)]
+    columns = jnp.concatenate(docs + [jnp.zeros((TOK - 16, TOK), F32)], axis=0).T
+    for i in range(RING):
+        mine = SEGS[xl, i, c, 0:1].astype(F32)
+        count = jnp.zeros((TOK, TOK), F32)
+        for j in range(16):
+            count = count + jnp.where(columns[:, j : j + 1] < mine, 1.0, 0.0)
+        first = jnp.sum(count, axis=0, keepdims=True)
+        START[i] = first.astype(jnp.int32)
+        index = TOK * (8 * xl + 2 * i + c) + lax.broadcasted_iota(jnp.int32, (1, TOK), 1)
+        place = index.astype(F32) - first
+        angle = jnp.broadcast_to(place, (TOK, TOK)).T * freq[...]
+        COS[i] = jnp.cos(angle)
+        sine = jnp.sin(angle)
+        lane = lax.broadcasted_iota(jnp.int32, sine.shape, 1)
+        SIN[i] = jnp.where(lane % 64 < 32, -sine, sine)
+    q_y.relay()
     w2_dealt = deal(k, q, w2, lambda j: lanes(c * 8 + xl * 4 + j), TV)
-    q_y.relay()
     q_x.relay()
     up_y.near()
     up_y.end()
-    a3_here.wait()
+    up_here.wait()
     part = W13.at[c, :, xh, xl, :, f3]
     a3 = [k.send(part, part, to) for to in xs[:2]]
     o_y.relay()
-    g_ring.relay()
+    gn2.wait_recv()
+    whole = lambda r: jnp.concatenate(
+        [GN[d // 2, d % 2, r : r + 1].astype(F32) for d in range(8)], axis=1
+    )
+    gain = whole(0)
+    GA[...] = gain
+    GF[...] = whole(16)
+    x_ring.near()
+    x_ring.end()
+    x_here.wait()
+    for i in range(RING):
+        xv = XV[i].astype(F32)
+        scale = lax.rsqrt(jnp.mean(xv * xv, axis=-1, keepdims=True) + EPS)
+        NV[i] = to_pieces((xv * scale * gain).astype(BF))
+    done = [k.local(NV, N1)]
     for r in (q_y, q_x):
         r.near()
         r.end()
-    q3 = k.send(WQ.at[c], WQ.at[c], mate)
+    q3 = k.send(WV.at[c], WV.at[c], mate)
+    g_ring.relay()
+    q3.wait_recv()
+    done.append(k.local(WV, WQ))
+    mixed = dot(NV[...].reshape(RING * TOK, D), WV[...].reshape(D, MZ))
+    for i in range(RING):
+        cos, sin = COS[i], SIN[i]
+        for j in range(5):
+            u = mixed[TOK * i : TOK * i + TOK, 128 * j : 128 * j + 128]
+            turned = u * cos + swapped(u) * sin
+            if j < 4:
+                QV[i, :, 128 * j : 128 * j + 128] = turned.astype(BF)
+            else:
+                lane = lax.broadcasted_iota(jnp.int32, u.shape, 1)
+                KVV[i] = jnp.where(lane < HEAD_DIM, turned, u).astype(BF)
+    near = k.send(KVV, KV.at[xl, :, c], mate)
+    n = k.n
+    k.n += 2
+    far, on = [
+        pltpu.make_async_remote_copy(
+            src_ref=src,
+            dst_ref=KV.at[0, :, c],
+            send_sem=ss.at[n + i],
+            recv_sem=rs.at[n + i],
+            device_id=to,
+            device_id_type=MESH,
+        )
+        for i, (src, to) in enumerate(((KVV, other), (KV.at[0, :, c], mate)))
+    ]
+
+    @pl.when(xl == 0)
+    def _():
+        far.start()
+
+    done += [k.local(KVV, KV.at[xl, :, c]), k.local(QV, Q)]
     o_y.near()
     o_y.end()
     part = WO.at[:, :, pl.ds(pl.multiple_of(1024 * c, 1024), 1024)]
     o3 = k.send(part, part, mate)
     w2_dealt()
-    heres.append(k.local(TV, T2))
-    for cp in a3 + seg2 + [gn2, q3, o3]:
-        cp.wait_recv()
-    for cp in heres:
-        cp.wait()
-    for r in (gate_x, x_ring, g_ring):
-        r.near()
-        r.end()
-    k.close()
-
-
-def kv_kernel(kv, KV, ss, rs):
-    q = coords()
-    xx, xl, c = q["x"], q["xl"], q["c"]
-    mate = device(q, c=1 - c)
-    other = device(q, x=xx ^ 1)
-    greet([mate, other])
-    k = Copies(ss, rs)
-    here = k.local(kv, KV.at[xl, :, c])
-    near = k.send(kv, KV.at[xl, :, c], mate)
-    far = pltpu.make_async_remote_copy(
-        src_ref=kv,
-        dst_ref=KV.at[0, :, c],
-        send_sem=ss.at[2],
-        recv_sem=rs.at[2],
-        device_id=other,
-        device_id_type=MESH,
-    )
-    on = pltpu.make_async_remote_copy(
-        src_ref=KV.at[0, :, c],
-        dst_ref=KV.at[0, :, c],
-        send_sem=ss.at[3],
-        recv_sem=rs.at[3],
-        device_id=mate,
-        device_id_type=MESH,
-    )
+    done.append(k.local(TV, T2))
 
     @pl.when(xl == 0)
     def _():
-        far.start()
         far.wait_send()
 
     @pl.when(xl == 1)
@@ -450,8 +478,14 @@
         on.wait_recv()
         on.wait_send()
 
-    here.wait()
     near.wait_recv()
+    for cp in a3 + [o3]:
+        cp.wait_recv()
+    for cp in heres + done:
+        cp.wait()
+    for r in (gate_x, g_ring):
+        r.near()
+        r.end()
     k.close()
 
 
@@ -956,43 +990,6 @@
     return jnp.where(lane % 64 < 32, pltpu.roll(u, 96, 1), pltpu.roll(u, 32, 1))
 
 
-def project_kernel(x, gain, w, cosine, sine, n1, query, kv):
-    two = 2 * TOK
-    xv = x[...].reshape(two, D).astype(F32)
-    scale = lax.rsqrt(jnp.mean(xv * xv, axis=-1, keepdims=True) + EPS)
-    normed = to_pieces((xv * scale * gain[...]).astype(BF))
-    n1[...] = normed.reshape(2, TOK, D)
-    cos, sin = cosine[...].reshape(two, 128), sine[...].reshape(two, 128)
-    mixed = jnp.dot(normed, w[...], preferred_element_type=F32)
-    for j in range(5):
-        u = mixed[:, 128 * j : 128 * j + 128]
-        turned = u * cos + swapped(u) * sin
-        if j < 4:
-            query[:, :, 128 * j : 128 * j + 128] = turned.astype(BF).reshape(2, TOK, 128)
-        else:
-            lane = lax.broadcasted_iota(jnp.int32, u.shape, 1)
-            kv[...] = jnp.where(lane < HEAD_DIM, turned, u).astype(BF).reshape(2, TOK, 128)
-
-
-def project(x, gain, w, cosine, sine):
-    chunk = lambda cols: pl.BlockSpec((2, TOK, cols), lambda i: (i, 0, 0))
-    whole = lambda shape: pl.BlockSpec(shape, lambda i: (0,) * len(shape))
-    return pl.pallas_call(
-        project_kernel,
-        name="project",
-        cost_estimate=cost(7),
-        grid=(2,),
-        in_specs=[chunk(D), whole((1, D)), whole((D, MZ)), chunk(128), chunk(128)],
-        out_specs=[chunk(D), chunk(QZ), chunk(128)],
-        out_shape=[
-            jax.ShapeDtypeStruct((RING, TOK, D), BF),
-            jax.ShapeDtypeStruct((RING, TOK, QZ), BF),
-            jax.ShapeDtypeStruct((RING, TOK, 128), BF),
-        ],
-        compiler_params=PARAMS,
-    )(x, gain, w, cosine, sine)
-
-
 def stacked_low(tiles):
     out = []
     for pair in range(4):
@@ -1032,23 +1029,42 @@
     return lax.dot_general(a, b, (((0,), (0,)), ((), ())), preferred_element_type=F32)
 
 
-def chunk_scores(keys, stacked, kc, chunk, start):
+def own_chunk(i):
+    ctx = lax.axis_index("ctx")
+    return (ctx // 8) * 8 + 2 * i + ctx % 2
+
+
+def over_chunks(start, chunk, step, carry):
+    first = start.astype(F32)
+    low = jnp.min(first).astype(jnp.int32) // TOK
+    high = jnp.minimum((jnp.max(first).astype(jnp.int32) + TOK - 1) // TOK, chunk)
+    carry = lax.fori_loop(low, high, lambda kc, cr: step(kc, 1, True, cr), carry)
+    pairs = (chunk - high) // 2
+    carry = lax.fori_loop(0, pairs, lambda n, cr: step(high + 2 * n, 2, False, cr), carry)
+    carry = lax.fori_loop(
+        high + 2 * pairs, chunk, lambda kc, cr: step(kc, 1, False, cr), carry
+    )
+    return step(chunk, 1, True, carry)
+
+
+def chunk_scores(keys, stacked, kc, chunk, starts, masked):
     raw = nt(keys, stacked)
+    if not masked:
+        return raw
     key = kc * TOK + lax.broadcasted_iota(jnp.int32, raw.shape, 0)
     query = chunk * TOK + lax.broadcasted_iota(jnp.int32, raw.shape, 1) % TOK
-    return jnp.where((key <= query) & (key >= start), raw, -1e30)
-
-
-def attend_kernel(info, query, kv, start, out, logsum):
-    i = pl.program_id(0)
-    low, chunk = info[0, i], info[1, i]
+    return jnp.where((key <= query) & (key >= starts), raw, -1e30)
+
+
+def attend_kernel(query, kv, start, out, logsum):
+    chunk = own_chunk(pl.program_id(0))
     stacked = (stacked_low(query[0]) * (1.0 / HEAD_DIM**0.5)).astype(BF)
     starts = jnp.concatenate([start[0]] * GROUP, axis=1)
 
-    def step(kc, carry):
+    def step(kc, size, masked, carry):
         top, summed, total = carry
-        keys = kv[kc]
-        scores = chunk_scores(keys, stacked, kc, chunk, starts)
+        keys = kv[pl.ds(kc, size)].reshape(size * TOK, 128)
+        scores = chunk_scores(keys, stacked, kc, chunk, starts, masked)
         new_top = jnp.maximum(top, jnp.max(scores, axis=0, keepdims=True))
         weights = jnp.exp(scores - new_top)
         fade = jnp.exp(top - new_top)
@@ -1058,41 +1074,38 @@
 
     rows = GROUP * TOK
     carry = (jnp.full((1, rows), -1e30, F32), jnp.zeros((1, rows), F32), jnp.zeros((64, rows), F32))
-    top, summed, total = lax.fori_loop(low, chunk + 1, step, carry)
+    top, summed, total = over_chunks(start[0], chunk, step, carry)
     for pair, tile in enumerate(unstacked(total / summed)):
         out[0, :, 128 * pair : 128 * pair + 128] = tile.astype(BF)
     logsum[0] = top + jnp.log(summed)
 
 
-def attend(info, query, kv, start):
-    chunk = lambda r, cols: pl.BlockSpec((1, r, cols), lambda i, s: (i, 0, 0))
+def attend(query, kv, start):
+    chunk = lambda r, cols: pl.BlockSpec((1, r, cols), lambda i: (i, 0, 0))
     return pl.pallas_call(
         attend_kernel,
         name="attend",
         cost_estimate=cost(12),
-        grid_spec=pltpu.PrefetchScalarGridSpec(
-            num_scalar_prefetch=1,
-            grid=(RING,),
-            in_specs=[
-                chunk(TOK, QZ),
-                pl.BlockSpec((16, TOK, 128), lambda i, s: (0, 0, 0)),
-                chunk(1, TOK),
-            ],
-            out_specs=[chunk(TOK, QZ), chunk(1, GROUP * TOK)],
-        ),
+        grid=(RING,),
+        in_specs=[
+            chunk(TOK, QZ),
+            pl.BlockSpec((16, TOK, 128), lambda i: (0, 0, 0)),
+            chunk(1, TOK),
+        ],
+        out_specs=[chunk(TOK, QZ), chunk(1, GROUP * TOK)],
         out_shape=[
             jax.ShapeDtypeStruct((RING, TOK, QZ), BF),
             jax.ShapeDtypeStruct((RING, 1, GROUP * TOK), F32),
         ],
         compiler_params=PARAMS,
-    )(info, query, kv, start)
+    )(query, kv, start)
 
 
 def attend_back_kernel(
-    info, query, kv, start, out, grad_out, logsum, cosine, sine, dquery, dkv, total
+    query, kv, start, out, grad_out, logsum, cosine, sine, dquery, dkv, total
 ):
     i = pl.program_id(0)
-    low, chunk = info[0, i], info[1, i]
+    chunk = own_chunk(i)
     stacked = (stacked_low(query[0]) * (1.0 / HEAD_DIM**0.5)).astype(BF)
     grads = stacked_high(grad_out[0]).astype(BF)
     starts = jnp.concatenate([start[0]] * GROUP, axis=1)
@@ -1109,18 +1122,17 @@
     def _():
         total[...] = jnp.zeros_like(total)
 
-    def step(kc, dq):
-        keys = kv[kc]
-        scores = chunk_scores(keys, stacked, kc, chunk, starts)
+    def step(kc, size, masked, dq):
+        keys = kv[pl.ds(kc, size)].reshape(size * TOK, 128)
+        scores = chunk_scores(keys, stacked, kc, chunk, starts, masked)
         probs = jnp.exp(scores - lse)
         grad_probs = nt(keys, grads)
         grad_scores = (probs * (grad_probs - delta)).astype(BF)
-        total[kc] += jnp.dot(grad_scores, stacked, preferred_element_type=F32) + jnp.dot(
-            probs.astype(BF), grads, preferred_element_type=F32
-        )
+        part = dot(grad_scores, stacked) + dot(probs.astype(BF), grads)
+        total[pl.ds(kc, size)] += part.reshape(size, TOK, 128)
         return dq + tn(keys, grad_scores)[:HEAD_DIM]
 
-    dq = lax.fori_loop(low, chunk + 1, step, jnp.zeros((64, GROUP * TOK), F32))
+    dq = over_chunks(start[0], chunk, step, jnp.zeros((64, GROUP * TOK), F32))
     cos, sin = cosine[0], sine[0]
     for pair, tile in enumerate(unstacked(dq)):
         tile = tile * (1.0 / HEAD_DIM**0.5)
@@ -1131,35 +1143,32 @@
         dkv[...] = total[...].astype(BF)
 
 
-def attend_back(info, query, kv, start, out, grad_out, logsum, cosine, sine):
-    chunk = lambda r, cols: pl.BlockSpec((1, r, cols), lambda i, s: (i, 0, 0))
-    whole = pl.BlockSpec((16, TOK, 128), lambda i, s: (0, 0, 0))
+def attend_back(query, kv, start, out, grad_out, logsum, cosine, sine):
+    chunk = lambda r, cols: pl.BlockSpec((1, r, cols), lambda i: (i, 0, 0))
+    whole = pl.BlockSpec((16, TOK, 128), lambda i: (0, 0, 0))
     return pl.pallas_call(
         attend_back_kernel,
         name="attend_back",
         cost_estimate=cost(15),
-        grid_spec=pltpu.PrefetchScalarGridSpec(
-            num_scalar_prefetch=1,
-            grid=(RING,),
-            in_specs=[
-                chunk(TOK, QZ),
-                whole,
-                chunk(1, TOK),
-                chunk(TOK, QZ),
-                chunk(TOK, QZ),
-                chunk(1, GROUP * TOK),
-                chunk(TOK, 128),
-                chunk(TOK, 128),
-            ],
-            out_specs=[chunk(TOK, QZ), whole],
-            scratch_shapes=[pltpu.VMEM((16, TOK, 128), F32)],
-        ),
+        grid=(RING,),
+        in_specs=[
+            chunk(TOK, QZ),
+            whole,
+            chunk(1, TOK),
+            chunk(TOK, QZ),
+            chunk(TOK, QZ),
+            chunk(1, GROUP * TOK),
+            chunk(TOK, 128),
+            chunk(TOK, 128),
+        ],
+        out_specs=[chunk(TOK, QZ), whole],
+        scratch_shapes=[pltpu.VMEM((16, TOK, 128), F32)],
         out_shape=[
             jax.ShapeDtypeStruct((RING, TOK, QZ), BF),
             jax.ShapeDtypeStruct((16, TOK, 128), BF),
         ],
         compiler_params=PARAMS,
-    )(info, query, kv, start, out, grad_out, logsum, cosine, sine)
+    )(query, kv, start, out, grad_out, logsum, cosine, sine)
 
 
 def rms_back(v, gain, grad):
@@ -1170,6 +1179,40 @@
     return scale * (inner - unit * jnp.mean(inner * unit, axis=-1, keepdims=True)), gain_grad
 
 
+def finish_kernel(a, b, g1, g3, g2, go, gq, gkv, out, grad, gate, up, down, proj, qkv):
+    out[...] = a[...]
+    grad[...] = b[...]
+    for src, dst in ((g1, gate), (g3, up), (g2, down), (go, proj)):
+        dst[...] = src[...].astype(F32)
+    qkv[:, :QDIM] = gq[...].astype(F32)
+    kv = gkv[...].astype(F32)
+    tiles = [kv[:, 128 * j : 128 * j + 128] for j in range(4)]
+    lane = lax.broadcasted_iota(jnp.int32, tiles[0].shape, 1)
+    for j in range(2):
+        one, two = tiles[2 * j], tiles[2 * j + 1]
+        keys = jnp.where(lane < HEAD_DIM, one, pltpu.roll(two, 64, 1))
+        values = jnp.where(lane < HEAD_DIM, pltpu.roll(one, 64, 1), two)
+        qkv[:, QDIM + 128 * j : QDIM + 128 * j + 128] = keys
+        qkv[:, QDIM + KVDIM + 128 * j : QDIM + KVDIM + 128 * j + 128] = values
+
+
+def finish(*arrays):
+    steps = 4
+    spec = lambda v: pl.BlockSpec((v.shape[0] // steps, v.shape[1]), lambda i: (i, 0))
+    outs = [jax.ShapeDtypeStruct(v.shape, F32) for v in arrays[:-2]]
+    outs.append(jax.ShapeDtypeStruct((256, QDIM + 2 * KVDIM), F32))
+    return pl.pallas_call(
+        finish_kernel,
+        name="finish",
+        cost_estimate=cost(12),
+        grid=(steps,),
+        in_specs=[spec(v) for v in arrays],
+        out_specs=[spec(v) for v in outs],
+        out_shape=outs,
+        compiler_params=PARAMS,
+    )(*arrays)
+
+
 def pick(v, index, axis=0):
     return lax.dynamic_index_in_dim(v, index, axis, keepdims=False)
 
@@ -1183,22 +1226,33 @@
     y, xx, xl, z, c = q["y"], q["x"], q["xl"], q["z"], q["c"]
     x = tokens[0]
     g = cotangent[0]
-    X, G, SEG, GN, WQ, WO, W13, t2 = talk(
-        fetch_kernel,
-        "fetch",
+    lane = jnp.arange(128)
+    freq = THETA ** (-(lane % 32).astype(F32) * 2.0 / HEAD_DIM)
+    table = ((RING, TOK, 128), F32)
+    G, WQ, WO, W13, t2, n1, query, KV, cosine, sine, start, gain_attn, gain_ffn = talk(
+        front_kernel,
+        "front",
         1,
-        40,
-        100,
-        (x, g, segments, norm_attn[None], norm_ffn[None], wqkv, wo, w1, w3, w2),
+        46,
+        120,
+        (
+            x, g, segments, norm_attn[None], norm_ffn[None], freq[None],
+            wqkv, wo, w1, w3, w2,
+        ),
         [
             ((RING, TOK, D), BF),
-            ((RING, TOK, D), BF),
-            ((2, 4, 2, 8, TOK), jnp.int32),
-            ((4, 2, 32, 256), BF),
             ((2, 4, 2, 2, 64, MZ), BF),
             ((2, 256, D), BF),
             ((2, 4, 2, 2, 64, 2 * FZ), BF),
             ((704, 128), BF),
+            ((RING, TOK, D), BF),
+            ((RING, TOK, QZ), BF),
+            ((2, 4, 2, TOK, 128), BF),
+            table,
+            table,
+            ((RING, 1, TOK), jnp.int32),
+            ((1, D), F32),
+            ((1, D), F32),
         ],
         scratch=[
             pltpu.VMEM((256, 128), BF),
@@ -1210,34 +1264,21 @@
             pltpu.VMEM((64, FZ), BF),
             pltpu.VMEM((8, TOK), jnp.int32),
             pltpu.VMEM((32, 256), BF),
+            pltpu.VMEM((2, 4, 2, 8, TOK), jnp.int32),
+            pltpu.VMEM((4, 2, 32, 256), BF),
+            pltpu.VMEM((RING, TOK, D), BF),
+            pltpu.VMEM((2, 4, 2, 2, 64, MZ), BF),
+            pltpu.VMEM((RING, TOK, D), BF),
+            pltpu.VMEM((RING, TOK, QZ), BF),
+            pltpu.VMEM((RING, TOK, 128), BF),
         ],
-        near=(0, 1, 2, 3, 4),
-    )
-
-    docs = SEG[:, :, :, 0, :].reshape(16 * TOK)
-    mine = pick(pick(SEG[:, :, :, 0, :], xl, 0), c, 1)
-    chunks = xl * 8 + 2 * jnp.arange(4, dtype=jnp.int32) + c
-    start = jnp.sum((docs[None, None, :] < mine[:, :, None]).astype(jnp.int32), axis=2)
-    index = chunks[:, None] * TOK + jnp.arange(TOK, dtype=jnp.int32)[None]
-    place = (index - start).astype(F32)
-    lane = jnp.arange(128)
-    freq = THETA ** (-(lane % 32).astype(F32) * 2.0 / HEAD_DIM)
-    angle = place[:, :, None] * freq[None, None, :]
-    cosine = jnp.cos(angle)
-    sine = jnp.sin(angle) * jnp.where(lane % 64 < 32, -1.0, 1.0)
-    info = jnp.stack([jnp.min(start, axis=1) // TOK, chunks])
-    start = start[:, None, :]
-    gain_attn = GN[:, :, 0, :].reshape(1, D).astype(F32)
-    gain_ffn = GN[:, :, 16, :].reshape(1, D).astype(F32)
-
+        near=tuple(range(6)),
+        near_out=(8, 9, 10, 11, 12),
+    )
     WQ = WQ.reshape(D, MZ)
     WO = WO.reshape(QZ, D)
-    n1, query, kv = project(X, gain_attn, WQ, cosine, sine)
-    (KV,) = talk(
-        kv_kernel, "kv", 2, 7, 4, (kv,), [((2, 4, 2, TOK, 128), BF)], near=(0,)
-    )
     KV = KV.reshape(16, TOK, 128)
-    heads_out, logsum = attend(info, query, KV, start)
+    heads_out, logsum = attend(query, KV, start)
     o = heads_out.reshape(RING * TOK, QZ)
     part = dot(o, WO).astype(BF).reshape(RING, TOK, D)
     N2, h, W13, W2 = talk(
@@ -1320,7 +1361,7 @@
     f2 = f2.reshape(1408, 256)
     DH = DH.reshape(RING * TOK, D)
     dquery, dkv = attend_back(
-        info, query, KV, start, heads_out, dheads.reshape(RING, TOK, QZ), logsum, cosine, sine
+        query, KV, start, heads_out, dheads.reshape(RING, TOK, QZ), logsum, cosine, sine
     )
     small = (8, 256)
     input_grad, G1, G3, G2, GO, GQ, GKV, gain_out = talk(
@@ -1382,19 +1423,19 @@
         near=tuple(range(11)),
         near_out=(0,),
     )
-    pairs = GKV.reshape(256, 4, 2, HEAD_DIM)
-    flat = lambda v: v.reshape(256, -1)
-    grad_qkv = jnp.concatenate([GQ, flat(pairs[:, :, 0]), flat(pairs[:, :, 1])], axis=1)
+    output, input_grad, gate_grad, up_grad, down_grad, out_grad, qkv_grad = finish(
+        output, input_grad, G1, G3, G2, GO, GQ, GKV
+    )
     return (
         output[None],
         input_grad[None],
         gain_out[0],
         gain_out[1],
-        grad_qkv.astype(F32),
-        GO.astype(F32),
-        G1.astype(F32),
-        G3.astype(F32),
-        G2.astype(F32),
+        qkv_grad,
+        out_grad,
+        gate_grad,
+        up_grad,
+        down_grad,
     )
 
 

time: 345 us -> 330 us (0.957)
  other arithmetic: 20.7 us -> 2.3 us
  matrix products: 26 us -> 38.5 us
  local copies, waits for them, and re-layouts: 9.28 us -> 3.8 us
    convert_element_type x8 -> x0, other arithmetic: 15.8 us -> none  [the longest x1 3.3 us: body(): G2.astype(F32)]
    dot_general x1, matrix products: 5.99 us -> 18.6 us  [body(): dhid = jnp.einsum('td,fd->tf', G, W2, preferred_element_type=F32)]
    pallas_call x1, Pallas kernels: 5.9 us -> 12.3 us  [finish(): pl.pallas_call(finish_kernel, name='finish', cost_estimate=cost(12), grid...]
    pallas_call x5 -> x4, Pallas kernels: 247 us -> 243 us  [talk(): pl.pallas_call(kernel, name=name, out_shape=[jax.ShapeDtypeStruct(s, t) f...]
where the time goes in v5:
time: 330 us; the launch traced here: 327 us
  Pallas kernels  282 us (85%)
  matrix products  38.5 us (12%)
  local copies, waits for them, and re-layouts  3.8 us (1%)
    pallas_call x4, Pallas kernels, talk(): pl.pallas_call(kernel, name=name, out_shape=[jax.ShapeDtypeStruct(s, t) f...  243 us
    dot_general x1, matrix products, body(): dhid = jnp.einsum('td,fd->tf', G, W2, preferred_element_type=F32)  18.6 us
    pallas_call x1, Pallas kernels, attend_back(): pl.pallas_call(attend_back_kernel, name='attend_back', cost_estimate=cost...  14.5 us
    dot_general x3, matrix products, dot(): return jnp.dot(a, b, preferred_element_type=F32)  12.5 us
    pallas_call x1, Pallas kernels, finish(): pl.pallas_call(finish_kernel, name='finish', cost_estimate=cost(12), grid...  12.3 us
    pallas_call x1, Pallas kernels, attend(): pl.pallas_call(attend_kernel, name='attend', cost_estimate=cost(12), grid...  11.6 us
    dot_general x1, matrix products, body(): dn2 = jnp.einsum('tf,df->td', both, W13, preferred_element_type=F32)  7.32 us

profile of v5, /device:TPU:1, one launch (start us, length us, event | category | flops | bytes accessed | tf_op | source)
XLA Modules:
  0.0 327.1 jit_solution(11701623591780217524)
XLA Ops:
  0.6 0.5 fusion.7.freq
  1.2 1.2 broadcast_in_dim.13.na
  2.4 1.2 broadcast_in_dim.14.nf
  3.6 45.9 %front.1 = (bf16[4,128,2048]{2,1,0:T(8,128)(2,1)}, bf16[2,4,2,2,64,640]{5,4,3,2,1,0:T(8,128)(2,1)}, bf16[2,256,2048]{2,1,0:T(8,128)(2,1)}, bf16[2,4,2,2,64,2816]...) custom-call(bf16[128,2048]{1,0:T(8,128)(2,1)} %bitcast.33, ...), custom_call_target="tpu_custom_call" | custom-call | flops 46000001024 | tf_op jit(solution)/shard_map/front/pallas_call | solution.py:275
  49.5 0.0 copy-start.2
  49.5 11.6 %attend.1 = (bf16[4,128,512]{2,1,0:T(8,128)(2,1)}, f32[4,1,1024]{2,1,0:T(1,128)}) custom-call(bf16[4,128,512]{2,1,0:T(8,128)(2,1)} %get-tuple-element.54.query, bf16[16,128,128]{2,1,0:T(8,128)(2,1)} %bitcast.59, s32[4,1,128]{2,1,0:T(1,128)} %get-tuple-element.56.start), custom_call_target="tpu_custom_call" | custom-call | flops 12000000000 | tf_op jit(solution)/shard_map/attend/pallas_call | solution.py:1085
  61.1 0.0 copy-done.2
  61.1 3.6 %convolution_convert_fusion.1 = bf16[512,2048]{1,0:T(8,128)(2,1)} fusion(bf16[512,512]{1,0:T(8,128)(2,1)} %bitcast.57, bf16[512,2048]{1,0:T(8,128)(2,1)S(1)} %bitcast.46), kind=kOutput, calls=%fused_computation.5 | convolution fusion | flops 1074790400 | bytes 4718592 | tf_op jit(solution)/shard_map/dot_general | solution.py:1221
  64.8 46.1 %middle.1 = (bf16[4,128,2048]{2,1,0:T(8,128)(2,1)}, f32[128,2048]{1,0:T(8,128)}, bf16[2,4,2,2,64,2816]{5,4,3,2,1,0:T(8,128)(2,1)}, bf16[2,704,2048]{2,1,0:T(8,128)(2,1)}) custom-call(bf16[4,128,2048]{2,1,0:T(8,128)(2,1)} %bitcast.52, bf16[128,2048]{1,0:T(8,128)(2,1)} %bitcast.34, f32[1,2048]{1,0:T(1,128)} %get-tuple-element.59.gain, ...), custom_call_target="tpu_custom_call", output_to_operand_aliasing={{2}: (4, {})} | custom-call | flops 41999998976 | tf_op jit(solution)/shard_map/middle/pallas_call | solution.py:275
  110.9 0.0 copy-done.1
  110.9 0.0 copy-start
  110.9 0.0 copy-start.3
  110.9 18.6 %fusion.9 = f32[512,1408]{1,0:T(8,128)S(1)} fusion(bf16[512,2048]{1,0:T(8,128)(2,1)S(1)} %bitcast.44, bf16[1408,2048]{1,0:T(8,128)(2,1)} %bitcast.39), kind=kOutput, calls=%fused_computation.17 | convolution fusion | flops 2952790016 | bytes 10747904 | tf_op jit(solution)/shard_map/td,fd->tf/dot_general | solution.py:1309
  129.6 0.0 copy-done
  129.6 0.0 copy-done.3
  129.6 3.4 %fusion = f32[512,1408]{1,0:T(8,128)S(1)} fusion(bf16[512,2048]{1,0:T(8,128)(2,1)S(1)} %bitcast.49, bf16[2048,2816]{1,0:T(8,128)(2,1)S(1)} %bitcast.36), kind=kOutput, calls=%fused_computation | convolution fusion | flops 2952790016 | bytes 10747904 | tf_op jit(solution)/shard_map/dot_general | solution.py:1221
  133.0 5.5 %multiply_convert_fusion = (bf16[512,1408]{1,0:T(8,128)(2,1)}, bf16[512,1408]{1,0:T(8,128)(2,1)S(1)}, bf16[512,1408]{1,0:T(8,128)(2,1)S(1)}) fusion(f32[512,1408]{1,0:T(8,128)S(1)} %fusion, f32[512,1408]{1,0:T(8,128)S(1)} %fusion.9, bf16[512,2048]{1,0:T(8,128)(2,1)S(1)} %bitcast.50, bf16[2048,2816]{1,0:T(8,128)(2,1)S(1)} %bitcast.37), kind=kOutput, calls=%fused_computation.7 | convolution fusion | flops 2964324352 | bytes 17956864 | tf_op jit(solution)/shard_map/dot_general | solution.py:1221
  138.5 7.3 %convolution_convert_fusion = bf16[512,2048]{1,0:T(8,128)(2,1)} fusion(bf16[2048,2816]{1,0:T(8,128)(2,1)S(1)} %bitcast.38, bf16[512,1408]{1,0:T(8,128)(2,1)S(1)} %get-tuple-element.99, bf16[512,1408]{1,0:T(8,128)(2,1)S(1)} %get-tuple-element.98), kind=kOutput, calls=%fused_computation.4 | convolution fusion | flops 5912395776 | bytes 16515072 | tf_op jit(solution)/shard_map/tf,df->td/dot_general | solution.py:1314
  145.8 1.8 pad_maximum_fusion.both
  147.6 60.9 %back.1 = (bf16[4,128,2048]{2,1,0:T(8,128)(2,1)}, bf16[2,2,64,2048]{3,2,1,0:T(8,128)(2,1)}, bf16[2,2,64,768]{3,2,1,0:T(8,128)(2,1)}, bf16[2,704,256]{2,1,0:T(8,1...) custom-call(bf16[4,128,2048]{2,1,0:T(8,128)(2,1)} %bitcast.51, ...), custom_call_target="tpu_custom_call" | custom-call | flops 60000002048 | tf_op jit(solution)/shard_map/back/pallas_call | solution.py:275
  208.5 14.5 %attend_back.1 = (bf16[4,128,512]{2,1,0:T(8,128)(2,1)}, bf16[16,128,128]{2,1,0:T(8,128)(2,1)}) custom-call(bf16[4,128,512]{2,1,0:T(8,128)(2,1)} %get-tuple-element.54.query, bf16[16,128,128]{2,1,0:T(8,128)(2,1)} %bitcast.60, s32[4,1,128]{2,1,0:T(1,128)} %get-tuple-element.56.start, bf16[4,128,512]{2,1,0:T(8,128)(2,1)} %get-tuple-element.57.out, ...), custom_call_target="tpu_custom_call" | custom-call | flops 15000000512 | tf_op jit(solution)/shard_map/attend_back/pallas_call | solution.py:1149
  223.0 90.3 %tail.1 = (f32[128,2048]{1,0:T(8,128)}, bf16[256,5632]{1,0:T(8,128)(2,1)}, bf16[256,5632]{1,0:T(8,128)(2,1)}, bf16[704,2048]{1,0:T(8,128)(2,1)}, bf16[256,2048]{...) custom-call(bf16[2,4,2,128,128]{4,3,2,1,0:T(8,128)(2,1)} %bitcast.61, ...), custom_call_target="tpu_custom_call" | custom-call | flops 74999996416 | tf_op jit(solution)/shard_map/tail/pallas_call | solution.py:275
  313.3 1.3 fusion.8
  314.6 12.3 %finish.1 = (f32[128,2048]{1,0:T(8,128)}, f32[128,2048]{1,0:T(8,128)}, f32[256,5632]{1,0:T(8,128)}, f32[256,5632]{1,0:T(8,128)}, f32[704,2048]{1,0:T(8,128)}, /*index=5*/f32[256,2048]{1,0:T(8,128)}, f32[256,2560]{1,0:T(8,128)}) custom-call(f32[128,2048]{1,0:T(8,128)} %get-tuple-element.66.a, f32[128,2048]{1,0:T(8,128)} %get-tuple-element.82.b, ...), custom_call_target="tpu_custom_call" | custom-call | flops 12000000000 | tf_op jit(solution)/shard_map/finish/pallas_call | solution.py:1204
  (1 shorter events, 0.0 us)
Async XLA Ops:
  49.5 11.6 %copy-start.2 = (bf16[2,256,2048]{2,1,0:T(8,128)(2,1)S(1)}, bf16[2,256,2048]{2,1,0:T(8,128)(2,1)}, u32[]{:S(2)}) copy-start(bf16[2,256,2048]{2,1,0:T(8,128)(2,1)} %get-tuple-element.58) | copy-start | bytes 6291460
  64.8 46.1 %copy-start.1 = (bf16[4,128,2048]{2,1,0:T(8,128)(2,1)S(1)}, bf16[4,128,2048]{2,1,0:T(8,128)(2,1)}, u32[]{:S(2)}) copy-start(bf16[4,128,2048]{2,1,0:T(8,128)(2,1)} %get-tuple-element.53) | copy-start | bytes 6291460
  110.9 18.7 %copy-start = (bf16[2,4,2,2,64,2816]{5,4,3,2,1,0:T(8,128)(2,1)S(1)}, bf16[2,4,2,2,64,2816]{5,4,3,2,1,0:T(8,128)(2,1)}, u32[]{:S(2)}) copy-start(bf16[2,4,2,2,64,2816]{5,4,3,2,1,0:T(8,128)(2,1)} %get-tuple-element.64) | copy-start | bytes 34603012
  110.9 18.7 %copy-start.3 = (bf16[4,128,2048]{2,1,0:T(8,128)(2,1)S(1)}, bf16[4,128,2048]{2,1,0:T(8,128)(2,1)}, u32[]{:S(2)}) copy-start(bf16[4,128,2048]{2,1,0:T(8,128)(2,1)} %get-tuple-element.63) | copy-start | bytes 6291460

commit v6 on v5

--- a/solution.py
+++ b/solution.py
@@ -17,7 +17,7 @@
 QZ = 512
 MZ = 640
 FZ = 1408
-SPLIT = 2048
+SPLIT = 1536
 EPS = 1e-05
 THETA = 10000.0
 MESH = pl.DeviceIdType.MESH
@@ -98,6 +98,7 @@
     def close(self):
         for cp in self.open:
             cp.wait_send()
+        self.open = []
 
 
 def deal(k, q, src, col, dst):
@@ -210,11 +211,6 @@
     def end(self):
         for cp in self.rest:
             cp.wait_recv()
-
-    def sent(self):
-        for cp in self.rest[2:]:
-            cp.wait_send()
-            self.k.open = [o for o in self.k.open if o is not cp]
 
 
 def halves(ref):
@@ -489,131 +485,126 @@
     k.close()
 
 
-def middle_kernel(
-    part, x, gain, t2, _, N2, H, W13, W2, p0, p1, v0, v1, below, above, n2, ss, rs
+def core_kernel(
+    o, x, gain, t2, w13, wo_in, G, V, FA, FB, F2, DO, OUT, DH, GAIN, *scratch
 ):
+    (
+        W, W2, N2, gv, hv, hT, bv, part, outs, wo, ov, vv, hf, xb,
+        p0, p1, p2, p3, v0, v1, v2, v3, below, above, out_below, out_above, *rest_of,
+    ) = scratch
+    bufs, (used, ss, rs) = rest_of[:-3], rest_of[-3:]
     q = coords()
     y, xx, xh, xl, z, c = q["y"], q["x"], q["xh"], q["xl"], q["z"], q["c"]
     ys, xs = ring(q, "y"), ring(q, "x")
     up, down = device(q, z=(z + 1) % 4), device(q, z=(z + 3) % 4)
     mate = device(q, c=1 - c)
     k = Copies(ss, rs)
+    f1, f3 = pl.ds(0, FZ), pl.ds(FZ, FZ)
+    lower, higher = (xx + 3) % 4, (xx + 1) % 4
+    gate_at = lambda ref, j: ref.at[c, j, :, :, :, f1]
+    gate_half = lambda ref, j, h: ref.at[c, j, h, :, :, f1]
+    up_at = lambda ref, j: ref.at[c, :, j // 2, j % 2, :, f3]
+    up_half = lambda ref, j, h: ref.at[c, pl.ds(2 * h, 2), j // 2, j % 2, :, f3]
+    get_wo, get_o = k.local(wo_in, wo), k.local(o, ov)
+    loads = [k.local(x, xb), k.local(gate_at(w13, y), gate_at(W, y))]
+    loads += [k.local(up_at(w13, j), up_at(W, j)) for j in (xx, lower, higher)]
+    get_g = k.local(G, gv)
     greet(ys + xs + [up, down, mate])
-    z_sum = Sum(k, q, "z", ring_halves(part), halves(below), halves(above), (p0, p1))
-    f1, f3 = pl.ds(0, FZ), pl.ds(FZ, FZ)
-    up1 = lambda j: W13.at[c, :, j // 2, j % 2, :, f3]
-    up_half = lambda j, h: W13.at[c, pl.ds(2 * h, 2), j // 2, j % 2, :, f3]
-    cols = lambda cc, j, n: pl.ds(pl.multiple_of(128 * (cc * 8 + j), 128 * n), 128 * n)
-    w2_here = k.local(t2, W2.at[xh, :, cols(c, xl * 4 + y, 1)])
+    cols = lambda j, n: pl.ds(pl.multiple_of(128 * (8 * c + j), 128 * n), 128 * n)
+    frows = lambda j, h: pl.ds(pl.multiple_of(704 * (j // 2) + 352 * h, 32), 352)
+    w2_here = k.local(t2, W2.at[pl.ds(pl.multiple_of(704 * xh, 64), 704), cols(xl * 4 + y, 1)])
     w2y = Gather(
         k, q, "y", lambda h: t2.at[pl.ds(352 * h, 352)],
-        lambda j, h: W2.at[xh, pl.ds(352 * h, 352), cols(c, xl * 4 + j, 1)],
-    )
-    lower, higher = (xx + 3) % 4, (xx + 1) % 4
+        lambda j, h: W2.at[frows(xx, h), cols(xl * 4 + j, 1)],
+    )
     far = [
-        k.send(up_half(lower, 0), up_half(lower, 0), xs[0]),
-        k.send(up_half(higher, 1), up_half(higher, 1), xs[1]),
+        k.send(up_half(w13, lower, 0), up_half(W, lower, 0), xs[0]),
+        k.send(up_half(w13, higher, 1), up_half(W, higher, 1), xs[1]),
     ]
-    sent = [k.send(up1(j), up1(j), mate) for j in (xx, lower, higher)]
+    sent = [k.send(up_at(w13, j), up_at(W, j), mate) for j in (xx, lower, higher)]
+    get_wo.wait()
+    get_o.wait()
+    rows = RING * TOK
+    part[...] = dot(ov[...].reshape(rows, QZ), wo[...]).astype(BF).reshape(RING, TOK, D)
+    z_sum = Sum(k, q, "z", ring_halves(part), halves(below), halves(above), (p0, p1))
     w2y.relay()
-    block = lambda j: W13.at[c, j, :, :, :, f1]
     gate = Gather(
-        k, q, "y", lambda h: W13.at[c, y, h, :, :, f1], lambda j, h: W13.at[c, j, h, :, :, f1]
-    )
-    sent.append(k.send(block(y), block(y), mate))
-    z_sum.relay(part.at[(z + 1) % 4, TOP], part.at[(z + 3) % 4, LOW], (v0, v1))
+        k, q, "y", lambda h: gate_half(w13, y, h), lambda j, h: gate_half(W, j, h)
+    )
+    sent.append(k.send(gate_at(w13, y), gate_at(W, y), mate))
     w2_here.wait()
     w2y.near()
     w2y.end()
-    down2 = lambda j: W2.at[j // 2, :, cols(c, (j % 2) * 4, 4)]
-    down_half = lambda j, h: W2.at[j // 2, pl.ds(352 * h, 352), cols(c, (j % 2) * 4, 4)]
+    down2 = lambda j: W2.at[
+        pl.ds(pl.multiple_of(704 * (j // 2), 64), 704), cols((j % 2) * 4, 4)
+    ]
+    down_half = lambda j, h: W2.at[frows(j, h), cols((j % 2) * 4, 4)]
     down_ring = Gather(k, q, "x", lambda h: down_half(xx, h), down_half)
     sent.append(k.send(down2(xx), down2(xx), mate))
+    z_sum.relay(part.at[(z + 1) % 4, TOP], part.at[(z + 3) % 4, LOW], (v0, v1))
     z_sum.end()
-    total = x[...].astype(F32) + (
+    for cp in loads:
+        cp.wait()
+    total = xb[...].astype(F32) + (
         part[z].astype(F32) + (below[...].astype(F32) + above[...].astype(F32))
     )
-    H[...] = total
+    hf[...] = total
     scale = lax.rsqrt(jnp.mean(total * total, axis=-1, keepdims=True) + EPS)
-    n2[...] = to_pieces((total * scale * gain[...]).astype(BF))
-    n2_ring = Gather(k, q, "z", halves(n2), ring_halves(N2))
-    n2_here = k.local(n2, N2.at[z])
+    N2[z] = to_pieces((total * scale * gain[...]).astype(BF))
+    n2_ring = Gather(k, q, "z", halves(N2.at[z]), ring_halves(N2))
     gate.relay()
     down_ring.relay()
     for cp in far:
         cp.wait_recv()
-    ref = up1((xx + 2) % 4)
+    ref = up_at(W, (xx + 2) % 4)
     sent.append(k.send(ref, ref, mate))
     gate.near()
     for j in (gate.below, gate.above):
-        sent.append(k.send(block(j), block(j), mate))
-    n2_ring.relay()
-    gate.end()
-    sent.append(k.send(block(gate.far), block(gate.far), mate))
+        sent.append(k.send(gate_at(W, j), gate_at(W, j), mate))
     down_ring.near()
     for j in (down_ring.below, down_ring.above):
         sent.append(k.send(down2(j), down2(j), mate))
+    n2_ring.relay()
+    gate.end()
+    sent.append(k.send(gate_at(W, gate.far), gate_at(W, gate.far), mate))
     down_ring.end()
     sent.append(k.send(down2(down_ring.far), down2(down_ring.far), mate))
+    get_g.wait()
     for cp in sent:
         cp.wait_recv()
-    n2_here.wait()
+    tiles = [(256 * i, min(256 * i + 256, FZ)) for i in range(6)]
+    gs = gv[...].reshape(rows, D)
+    for a, b in tiles:
+        bv[:, a:b] = nt(gs, W2[a:b]).astype(BF)
     n2_ring.near()
     n2_ring.end()
     k.close()
-
-
-def back_kernel(
-    dn2, hidden, G, N2, both, W2, WO, h, gain, V, FA, FB, F2, DO, OUT, DH, GAIN, *scratch
-):
-    (
-        p0, p1, p2, p3, v0, v1, below, above, out_below, out_above, near0, near1, mine, dhb,
-        vv, hv, gv, nv, bv, ov, wv, hT, outs, mate2, mate13, sum2, sum13, *bufs, ss, rs,
-    ) = scratch
-    q = coords()
-    y, xx, z, c = q["y"], q["x"], q["z"], q["c"]
-    mate = device(q, c=1 - c)
-    k = Copies(ss, rs)
-    get_n, get_b = k.local(N2, nv), k.local(both, bv)
-    get_h, get_g = k.local(hidden, hv), k.local(G, gv)
-    get_part = [
-        k.local(dn2.at[(z + 1) % 4, TOP], near0),
-        k.local(dn2.at[(z + 3) % 4, LOW], near1),
-        k.local(dn2.at[z], mine),
-    ]
-    tile = lambda j: pl.ds(512 * j, 512)
-    get_w = [k.local(W2.at[:, tile(j)], wv.at[j]) for j in range(2)]
-    get_o = k.local(WO, ov)
-    targets = [mate]
-    for axis in ("x", "y", "z"):
-        targets += ring(q, axis)[:2]
-    greet(targets)
-    z_sum = Sum(k, q, "z", ring_halves(dn2), halves(below), halves(above), (p0, p1))
-    lanes = lambda cc, j: pl.ds(pl.multiple_of(1024 * cc + 256 * j, 256), 256)
-    sent2, sent13 = [], []
-    get_n.wait()
-    get_b.wait()
+    n2 = N2[...].reshape(rows, D)
+    for a, b in tiles:
+        gates = dot(n2, W[:, :, :, :, :, a:b].reshape(D, b - a))
+        ups = dot(n2, W[:, :, :, :, :, FZ + a : FZ + b].reshape(D, b - a))
+        sigma = jax.nn.sigmoid(gates)
+        silu = gates * sigma
+        hv[:, a:b] = (silu * ups).astype(BF)
+        dhid = bv[:, a:b].astype(F32)
+        bv[:, a:b] = (dhid * ups * sigma * (1.0 + gates * (1.0 - sigma))).astype(BF)
+        bv[:, FZ + a : FZ + b] = (dhid * silu).astype(BF)
     for j in range(4):
-        mate13[j] = tn(nv[:, lanes(1 - c, j)], bv[...]).astype(BF).reshape(4, 64, 2 * FZ)
-        sent13.append(k.send(mate13.at[j], sum13.at[j], mate))
-    get_h.wait()
-    get_g.wait()
-    hT[...] = hv[...].T
-    for cp in get_part:
-        cp.wait()
-    for j in range(4):
-        mate2[j] = dot(hT[...], gv[:, lanes(1 - c, j)]).astype(BF)
-        sent2.append(k.send(mate2.at[j], sum2.at[j], mate))
-        if j == 2:
-            z_sum.relay(near0, near1, (v0, v1))
+        at = slice(512 * j, 512 * j + 512)
+        outs[:, :, at] = dot(hv[...], W2[:, at]).astype(BF).reshape(RING, TOK, 512)
+    out_sum = Sum(
+        k, q, "z", ring_halves(outs), halves(out_below), halves(out_above), (p2, p3)
+    )
+    pl.semaphore_signal(used.at[0], inc=1, device_id=mate, device_id_type=MESH)
     half = lambda ref: lambda i: ref.at[i]
     rest = 2 * FZ - SPLIT
     jobs = [
-        ("x", lambda j, i: sum13.at[pl.ds(2 * i, 2), j, :, pl.ds(0, SPLIT)], FA),
-        ("y", lambda j, i: sum13.at[j, pl.ds(2 * i, 2), :, pl.ds(SPLIT, rest)], FB),
-        ("y", lambda j, i: sum2.at[j, pl.ds(704 * i, 704)], F2),
+        ("y", lambda j, i: W2.at[pl.ds(704 * i, 704), lanes(0, j)], F2),
+        ("x", lambda j, i: W.at[0, pl.ds(2 * i, 2), j // 2, j % 2, :, pl.ds(0, SPLIT)], FA),
+        ("y", lambda j, i: W.at[0, j, i, :, :, pl.ds(SPLIT, rest)], FB),
     ]
     sums, done = [], []
+    lanes = lambda cc, j: pl.ds(pl.multiple_of(1024 * cc + 256 * j, 256), 256)
 
     def start(n):
         axis, block, _ = jobs[n]
@@ -637,55 +628,66 @@
             b[2][i] = total.astype(BF)
         done.append(k.local(b[2], out))
 
+    hT[...] = hv[...].T
+    pl.semaphore_wait(used.at[0], 1)
+    sent2, sent13 = [], []
+    for j in range(4):
+        W2[:, 1024 + 256 * j : 1280 + 256 * j] = dot(
+            hT[...], gv[:, :, lanes(1 - c, j)].reshape(rows, 256)
+        ).astype(BF)
+        sent2.append(k.send(W2.at[:, lanes(1, j)], W2.at[:, lanes(0, j)], mate))
+    for j in range(4):
+        sent2[j].wait_recv()
+        at = slice(256 * j, 256 * j + 256)
+        own = dot(hT[...], gv[:, :, lanes(c, j)].reshape(rows, 256))
+        W2[:, at] = (own + W2[:, at].astype(F32)).astype(BF)
+    start(0)
+    out_sum.relay(outs.at[(z + 1) % 4, TOP], outs.at[(z + 3) % 4, LOW], (v2, v3))
+    for j in range(2):
+        at = slice(1024 * j, 1024 * j + 1024)
+        dn = nt(bv[...], W[j].reshape(1024, 2 * FZ))
+        part[:, :, at] = dn.astype(BF).reshape(RING, TOK, 1024)
+    z_sum = Sum(k, q, "z", ring_halves(part), halves(below), halves(above), (p0, p1))
+    pl.semaphore_signal(used.at[1], inc=1, device_id=mate, device_id_type=MESH)
+    pl.semaphore_wait(used.at[1], 1)
+    shape = (2, 2, 64, 2 * FZ)
+    for j in range(4):
+        W[1, j] = tn(N2[:, :, lanes(1 - c, j)].reshape(rows, 256), bv[...]).astype(BF).reshape(shape)
+        sent13.append(k.send(W.at[1, j], W.at[0, j], mate))
+        if j == 0:
+            relay(0)
     for j in range(4):
         sent13[j].wait_recv()
-        own = tn(nv[:, lanes(c, j)], bv[...]).reshape(4, 64, 2 * FZ)
-        sum13[j] = (own + sum13[j].astype(F32)).astype(BF)
-    start(0)
+        own = tn(N2[:, :, lanes(c, j)].reshape(rows, 256), bv[...]).reshape(shape)
+        W[0, j] = (own + W[0, j].astype(F32)).astype(BF)
+        if j == 1:
+            z_sum.relay(part.at[(z + 1) % 4, TOP], part.at[(z + 3) % 4, LOW], (v0, v1))
     start(1)
-    for j in range(4):
-        sent2[j].wait_recv()
-        sum2[j] = (dot(hT[...], gv[:, lanes(c, j)]) + sum2[j].astype(F32)).astype(BF)
     start(2)
+    end(0)
     z_sum.end()
     dn = from_pieces(
-        mine[...].astype(F32) + (below[...].astype(F32) + above[...].astype(F32))
-    )
-    back, gain_grad = rms_back(h[...], gain[...], dn)
-    total = gv[pl.ds(pl.multiple_of(TOK * z, TOK), TOK)].astype(F32) + back
+        part[z].astype(F32) + (below[...].astype(F32) + above[...].astype(F32))
+    )
+    back, gain_grad = rms_back(hf[...], gain[...], dn)
+    total = gv[z].astype(F32) + back
     DH[...] = total
     GAIN[...] = gain_grad
-    dhb[...] = total.astype(BF)
-    v_ring = Gather(k, q, "z", halves(dhb), ring_halves(vv))
-    here = k.local(dhb, vv.at[z])
-    for j in range(4):
-        get_w[j].wait()
-        part = dot(hv[...], wv[j % 2]).astype(BF)
-        outs[:, :, tile(j)] = part.reshape(RING, TOK, 512)
-        if j < 2:
-            get_w.append(k.local(W2.at[:, tile(j + 2)], wv.at[j]))
-    out_sum = Sum(
-        k, q, "z", ring_halves(outs), halves(out_below), halves(out_above), (p2, p3)
+    vv[z] = total.astype(BF)
+    v_ring = Gather(k, q, "z", halves(vv.at[z]), ring_halves(vv))
+    out_sum.end()
+    OUT[...] = hf[...] + (
+        outs[z].astype(F32) + (out_below[...].astype(F32) + out_above[...].astype(F32))
     )
     relay(1)
-    relay(0)
+    relay(2)
     v_ring.relay()
-    relay(2)
-    z_sum.sent()
-    out_sum.relay(outs.at[(z + 1) % 4, TOP], outs.at[(z + 3) % 4, LOW], (v0, v1))
-    end(1)
-    end(0)
+    end(2)
     v_ring.near()
     v_ring.end()
-    here.wait()
-    get_o.wait()
     done.append(k.local(vv, V))
-    DO[...] = nt(vv[...].reshape(RING * TOK, D), ov[...]).astype(BF)
-    end(2)
-    out_sum.end()
-    OUT[...] = h[...] + (
-        outs[z].astype(F32) + (out_below[...].astype(F32) + out_above[...].astype(F32))
-    )
+    DO[...] = nt(vv[...].reshape(rows, D), wo[...]).astype(BF)
+    end(1)
     for cp in done:
         cp.wait()
     k.close()
@@ -1280,50 +1282,18 @@
     KV = KV.reshape(16, TOK, 128)
     heads_out, logsum = attend(query, KV, start)
     o = heads_out.reshape(RING * TOK, QZ)
-    part = dot(o, WO).astype(BF).reshape(RING, TOK, D)
-    N2, h, W13, W2 = talk(
-        middle_kernel,
-        "middle",
-        3,
-        42,
-        60,
-        (part, x, gain_ffn, t2, W13),
-        [
-            ((RING, TOK, D), BF),
-            ((TOK, D), F32),
-            ((2, 4, 2, 2, 64, 2 * FZ), BF),
-            ((2, 704, D), BF),
-        ],
-        scratch=[
-            *[pltpu.VMEM(HALF, BF)] * 4,
-            *[pltpu.VMEM((TOK, D), BF)] * 3,
-        ],
-        near=(0, 1, 2, 3),
-        near_out=(1,),
-        alias={4: 2},
-    )
-    N2, G = N2.reshape(RING * TOK, D), G.reshape(RING * TOK, D)
-    W13, W2 = W13.reshape(D, 2 * FZ), W2.reshape(FZ, D)
-    gate, up = dot(N2, W13[:, :FZ]), dot(N2, W13[:, FZ:])
-    hidden = (jax.nn.silu(gate) * up).astype(BF)
-    dhid = jnp.einsum("td,fd->tf", G, W2, preferred_element_type=F32)
-    sigma = jax.nn.sigmoid(gate)
-    dgate = (dhid * up * sigma * (1.0 + gate * (1.0 - sigma))).astype(BF)
-    dup = (dhid * gate * sigma).astype(BF)
-    both = jnp.concatenate([dgate, dup], axis=1)
-    dn2 = jnp.einsum("tf,df->td", both, W13, preferred_element_type=F32)
-    dn2 = dn2.astype(BF).reshape(RING, TOK, D)
     rest = 2 * FZ - SPLIT
     buffers = []
-    for shape in ((2, 64, SPLIT), (2, 64, rest), (704, 256)):
+    for shape in ((704, 256), (2, 64, SPLIT), (2, 64, rest)):
         buffers += [pltpu.VMEM((2,) + shape, BF)] * 4
+    chunks = pltpu.VMEM((RING, TOK, D), BF)
     DH, fa, fb, f2, dheads, output, dh, gain2 = talk(
-        back_kernel,
-        "back",
-        4,
-        60,
-        100,
-        (dn2, hidden, G, N2, both, W2, WO, h, gain_ffn),
+        core_kernel,
+        "core",
+        3,
+        120,
+        150,
+        (heads_out, x, gain_ffn, t2, W13, WO, G),
         [
             ((RING, TOK, D), BF),
             ((2, 2, 64, SPLIT), BF),
@@ -1335,26 +1305,26 @@
             ((1, D), F32),
         ],
         scratch=[
-            *[pltpu.VMEM(HALF, BF)] * 6,
+            pltpu.VMEM((2, 4, 2, 2, 64, 2 * FZ), BF),
+            pltpu.VMEM((FZ, D), BF),
+            chunks,
+            chunks,
+            pltpu.VMEM((RING * TOK, FZ), BF),
+            pltpu.VMEM((FZ, RING * TOK), BF),
+            pltpu.VMEM((RING * TOK, 2 * FZ), BF),
+            chunks,
+            chunks,
+            pltpu.VMEM((QZ, D), BF),
+            pltpu.VMEM((RING, TOK, QZ), BF),
+            chunks,
+            pltpu.VMEM((TOK, D), F32),
+            pltpu.VMEM((TOK, D), BF),
+            *[pltpu.VMEM(HALF, BF)] * 8,
             *[pltpu.VMEM((TOK, D), BF)] * 4,
-            *[pltpu.VMEM(HALF, BF)] * 2,
-            *[pltpu.VMEM((TOK, D), BF)] * 2,
-            pltpu.VMEM((RING, TOK, D), BF),
-            pltpu.VMEM((RING * TOK, FZ), BF),
-            pltpu.VMEM((RING * TOK, D), BF),
-            pltpu.VMEM((RING * TOK, D), BF),
-            pltpu.VMEM((RING * TOK, 2 * FZ), BF),
-            pltpu.VMEM((QZ, D), BF),
-            pltpu.VMEM((2, FZ, 512), BF),
-            pltpu.VMEM((FZ, RING * TOK), BF),
-            pltpu.VMEM((RING, TOK, D), BF),
-            pltpu.VMEM((4, FZ, 256), BF),
-            pltpu.VMEM((4, 4, 64, 2 * FZ), BF),
-            pltpu.VMEM((4, FZ, 256), BF),
-            pltpu.VMEM((4, 4, 64, 2 * FZ), BF),
             *buffers,
+            pltpu.SemaphoreType.REGULAR((2,)),
         ],
-        near=(7, 8),
+        near=(2,),
         near_out=(4, 5, 6, 7),
     )
     fa, fb = fa.reshape(4, 64, SPLIT), fb.reshape(4, 64, rest)

time: 330 us -> 298 us (0.903)
  matrix products: 38.5 us -> 0 us
  Pallas kernels: 282 us -> 287 us
    dot_general x5 -> x0, matrix products: 38.5 us -> none  [the longest x1 18.6 us: body(): dhid = jnp.einsum('td,fd->tf', G, W2, preferred_element_type=F32)]
    pallas_call x4 -> x3, Pallas kernels: 243 us -> 248 us  [talk(): pl.pallas_call(kernel, name=name, out_shape=[jax.ShapeDtypeStruct(s, t) f...]
where the time goes in v6:
time: 298 us; the launch traced here: 292 us
  Pallas kernels  287 us (96%)
  local copies, waits for them, and re-layouts  3.78 us (1%)
    pallas_call x3, Pallas kernels, talk(): pl.pallas_call(kernel, name=name, out_shape=[jax.ShapeDtypeStruct(s, t) f...  248 us
    pallas_call x1, Pallas kernels, attend_back(): pl.pallas_call(attend_back_kernel, name='attend_back', cost_estimate=cost...  14.5 us
    pallas_call x1, Pallas kernels, finish(): pl.pallas_call(finish_kernel, name='finish', cost_estimate=cost(12), grid...  12.3 us
    pallas_call x1, Pallas kernels, attend(): pl.pallas_call(attend_kernel, name='attend', cost_estimate=cost(12), grid...  11.9 us

profile of v6, /device:TPU:1, one launch (start us, length us, event | category | flops | bytes accessed | tf_op | source)
XLA Modules:
  0.0 292.2 jit_solution(5469815492008579754)
XLA Ops:
  0.6 0.5 fusion.3.freq
  1.2 1.2 broadcast_in_dim.13.na
  2.4 1.2 broadcast_in_dim.14.nf
  3.6 45.9 %front.1 = (bf16[4,128,2048]{2,1,0:T(8,128)(2,1)}, bf16[2,4,2,2,64,640]{5,4,3,2,1,0:T(8,128)(2,1)}, bf16[2,256,2048]{2,1,0:T(8,128)(2,1)}, bf16[2,4,2,2,64,2816]...) custom-call(bf16[128,2048]{1,0:T(8,128)(2,1)} %bitcast.20, ...), custom_call_target="tpu_custom_call" | custom-call | flops 46000001024 | tf_op jit(solution)/shard_map/front/pallas_call | solution.py:271
  49.5 11.9 %attend.1 = (bf16[4,128,512]{2,1,0:T(8,128)(2,1)}, f32[4,1,1024]{2,1,0:T(1,128)}) custom-call(bf16[4,128,512]{2,1,0:T(8,128)(2,1)} %get-tuple-element.49.query, bf16[16,128,128]{2,1,0:T(8,128)(2,1)} %bitcast.33, s32[4,1,128]{2,1,0:T(1,128)} %get-tuple-element.51.start), custom_call_target="tpu_custom_call" | custom-call | flops 12000000000 | tf_op jit(solution)/shard_map/attend/pallas_call | solution.py:1087
  61.5 115.4 %core.1 = (bf16[4,128,2048]{2,1,0:T(8,128)(2,1)}, bf16[2,2,64,1536]{3,2,1,0:T(8,128)(2,1)}, bf16[2,2,64,1280]{3,2,1,0:T(8,128)(2,1)}, bf16[2,704,256]{2,1,0:T(8,...) custom-call(bf16[4,128,512]{2,1,0:T(8,128)(2,1)} %get-tuple-element.52.o.ou, ...), custom_call_target="tpu_custom_call" | custom-call | flops 120000004096 | tf_op jit(solution)/shard_map/core/pallas_call | solution.py:271
  176.9 14.5 %attend_back.1 = (bf16[4,128,512]{2,1,0:T(8,128)(2,1)}, bf16[16,128,128]{2,1,0:T(8,128)(2,1)}) custom-call(bf16[4,128,512]{2,1,0:T(8,128)(2,1)} %get-tuple-element.49.query, bf16[16,128,128]{2,1,0:T(8,128)(2,1)} %bitcast.34, s32[4,1,128]{2,1,0:T(1,128)} %get-tuple-element.51.start, bf16[4,128,512]{2,1,0:T(8,128)(2,1)} %get-tuple-element.52.o.out, ...), custom_call_target="tpu_custom_call" | custom-call | flops 15000000512 | tf_op jit(solution)/shard_map/attend_back/pallas_call | solution.py:1151
  191.4 86.8 %tail.1 = (f32[128,2048]{1,0:T(8,128)}, bf16[256,5632]{1,0:T(8,128)(2,1)}, bf16[256,5632]{1,0:T(8,128)(2,1)}, bf16[704,2048]{1,0:T(8,128)(2,1)}, bf16[256,2048]{...) custom-call(bf16[2,4,2,128,128]{4,3,2,1,0:T(8,128)(2,1)} %bitcast.35, ...), custom_call_target="tpu_custom_call" | custom-call | flops 74999996416 | tf_op jit(solution)/shard_map/tail/pallas_call | solution.py:271
  278.2 1.3 fusion.4
  279.5 12.3 %finish.1 = (f32[128,2048]{1,0:T(8,128)}, f32[128,2048]{1,0:T(8,128)}, f32[256,5632]{1,0:T(8,128)}, f32[256,5632]{1,0:T(8,128)}, f32[704,2048]{1,0:T(8,128)}, /*index=5*/f32[256,2048]{1,0:T(8,128)}, f32[256,2560]{1,0:T(8,128)}) custom-call(f32[128,2048]{1,0:T(8,128)} %get-tuple-element.58.a, f32[128,2048]{1,0:T(8,128)} %get-tuple-element.74.b, ...), custom_call_target="tpu_custom_call" | custom-call | flops 12000000000 | tf_op jit(solution)/shard_map/finish/pallas_call | solution.py:1206

commit v7 on v6

--- a/solution.py
+++ b/solution.py
@@ -2,6 +2,7 @@
 
 import jax
 import jax.numpy as jnp
+import numpy as np
 from jax import lax
 from jax.experimental import pallas as pl
 from jax.experimental.pallas import tpu as pltpu
@@ -170,15 +171,24 @@
         self.low1 = k.send(src(1), dst(at, 1), self.up)
         self.top0 = k.send(src(0), dst(at, 0), self.down)
 
+        self.waiting = {0: self.low0, 1: self.top1}
+
+    def arrived(self, half):
+        cp = self.waiting.pop(half, None)
+        if cp is not None:
+            cp.wait_recv()
+
     def relay(self):
-        self.low0.wait_recv()
+        self.arrived(0)
         ref = self.dst(self.below, 0)
         self.far0 = self.k.send(ref, ref, self.up)
-        self.top1.wait_recv()
+        self.arrived(1)
         ref = self.dst(self.above, 1)
         self.far1 = self.k.send(ref, ref, self.down)
 
     def near(self):
+        self.arrived(0)
+        self.arrived(1)
         self.low1.wait_recv()
         self.top0.wait_recv()
 
@@ -313,8 +323,8 @@
         k.local(w3.at[rows, fcols], P3),
     ]
     SG[...] = jnp.broadcast_to(seg[...], (8, TOK))
-    NG[0:16] = jnp.broadcast_to(na[...].astype(F32), (16, 256)).astype(BF)
-    NG[16:32] = jnp.broadcast_to(nf[...].astype(F32), (16, 256)).astype(BF)
+    NG[0:16] = jnp.broadcast_to(na[...].astype(F32)[None], (16, 256)).astype(BF)
+    NG[16:32] = jnp.broadcast_to(nf[...].astype(F32)[None], (16, 256)).astype(BF)
     greet(zs + ys + xs + [mate, other_mate])
     seg_z = [k.send(SG, SEGS.at[xl, z, c], to) for to in zs]
     x_ring = Gather(k, q, "z", halves(x), ring_halves(XV))
@@ -636,17 +646,20 @@
             hT[...], gv[:, :, lanes(1 - c, j)].reshape(rows, 256)
         ).astype(BF)
         sent2.append(k.send(W2.at[:, lanes(1, j)], W2.at[:, lanes(0, j)], mate))
+
+    def back_half(j):
+        at = slice(1024 * j, 1024 * j + 1024)
+        dn = nt(bv[...], W[j].reshape(1024, 2 * FZ))
+        part[:, :, at] = dn.astype(BF).reshape(RING, TOK, 1024)
+
+    back_half(0)
     for j in range(4):
         sent2[j].wait_recv()
         at = slice(256 * j, 256 * j + 256)
         own = dot(hT[...], gv[:, :, lanes(c, j)].reshape(rows, 256))
         W2[:, at] = (own + W2[:, at].astype(F32)).astype(BF)
     start(0)
-    out_sum.relay(outs.at[(z + 1) % 4, TOP], outs.at[(z + 3) % 4, LOW], (v2, v3))
-    for j in range(2):
-        at = slice(1024 * j, 1024 * j + 1024)
-        dn = nt(bv[...], W[j].reshape(1024, 2 * FZ))
-        part[:, :, at] = dn.astype(BF).reshape(RING, TOK, 1024)
+    back_half(1)
     z_sum = Sum(k, q, "z", ring_halves(part), halves(below), halves(above), (p0, p1))
     pl.semaphore_signal(used.at[1], inc=1, device_id=mate, device_id_type=MESH)
     pl.semaphore_wait(used.at[1], 1)
@@ -654,17 +667,17 @@
     for j in range(4):
         W[1, j] = tn(N2[:, :, lanes(1 - c, j)].reshape(rows, 256), bv[...]).astype(BF).reshape(shape)
         sent13.append(k.send(W.at[1, j], W.at[0, j], mate))
-        if j == 0:
+        if j == 1:
             relay(0)
+    z_sum.relay(part.at[(z + 1) % 4, TOP], part.at[(z + 3) % 4, LOW], (v0, v1))
     for j in range(4):
         sent13[j].wait_recv()
         own = tn(N2[:, :, lanes(c, j)].reshape(rows, 256), bv[...]).reshape(shape)
         W[0, j] = (own + W[0, j].astype(F32)).astype(BF)
         if j == 1:
-            z_sum.relay(part.at[(z + 1) % 4, TOP], part.at[(z + 3) % 4, LOW], (v0, v1))
+            out_sum.relay(outs.at[(z + 1) % 4, TOP], outs.at[(z + 3) % 4, LOW], (v2, v3))
     start(1)
     start(2)
-    end(0)
     z_sum.end()
     dn = from_pieces(
         part[z].astype(F32) + (below[...].astype(F32) + above[...].astype(F32))
@@ -675,6 +688,7 @@
     GAIN[...] = gain_grad
     vv[z] = total.astype(BF)
     v_ring = Gather(k, q, "z", halves(vv.at[z]), ring_halves(vv))
+    end(0)
     out_sum.end()
     OUT[...] = hf[...] + (
         outs[z].astype(F32) + (out_below[...].astype(F32) + out_above[...].astype(F32))
@@ -707,7 +721,8 @@
     (
         wv, nv, ov, gv, R, dm, dn, p0, p1, v0, v1, below, above, mate_o, sum_o, mate_q, sum_q,
         ob0, ob1, ob2, ob3, qb0, qb1, qb2, qb3, la, lb, l2, pa, pb, p2, t2, lo, lq, fo, fq,
-        po, pq, to_, gains, s0, s1, s2, s3, s4, total, ss, rs,
+        po, pq, to_, gains, s0, s1, s2, s3, s4, total,
+        kv_own, kv_low, cv, sv, xv, dv, fav, fbv, f2v, ss, rs,
     ) = scratch
     q = coords()
     y, xx, xh, xl, z, c = q["y"], q["x"], q["xh"], q["xl"], q["z"], q["c"]
@@ -715,10 +730,77 @@
     mate, other, cross = device(q, c=1 - c), device(q, x=xx ^ 1), device(q, x=3 - xx)
     other_mate = device(q, x=xx ^ 1, c=1 - c)
     steps = (1, 3, 2)
+    rows_all = RING * TOK
     k = Copies(ss, rs)
     get_o, get_g = k.local(o, ov), k.local(dho, gv)
-    get_w, get_n = k.local(wq, wv), k.local(n1, nv)
+    r, cc = quarter(xx, 704)
+    get_f = [k.local(fb.at[xx], fbv), k.local(fa.at[y], fav), k.local(f2.at[r, cc], f2v)]
+    get_kv = [k.local(dkv.at[xl, :, c], kv_own), k.local(dkv.at[0, :, c], kv_low)]
+    get_d = [
+        k.local(dq, dm.at[:, :, pl.ds(0, QZ)]),
+        k.local(cosine, cv),
+        k.local(sine, sv),
+        k.local(wq, wv),
+    ]
+    get_n = k.local(n1, nv)
+    get_x = [k.local(x, xv), k.local(dh, dv)]
     greet(zs + ys + xs + [mate, other_mate], q)
+    leg_b = [k.send(fb.at[(xx + s) % 4], lb.at[i], xs[i]) for i, s in enumerate(steps)]
+    leg_a = [k.send(fa.at[(y + s) % 4], la.at[i], ys[i]) for i, s in enumerate(steps)]
+    lanes = lambda cc, j: pl.ds(pl.multiple_of(1024 * cc + 256 * j, 256), 256)
+    get_o.wait()
+    get_g.wait()
+    swaps = []
+    for j in range(4):
+        mate_o[j] = tn(ov[...], gv[:, lanes(1 - c, j)]).astype(BF)
+        swaps.append(k.send(mate_o.at[j], sum_o.at[j], mate))
+    leg_2 = []
+    for i, s in enumerate(steps):
+        r, cc = quarter((xx + s) % 4, 704)
+        leg_2.append(k.send(f2.at[r, cc], l2.at[i], xs[i]))
+    for j in range(4):
+        swaps[j].wait_recv()
+        sum_o[j] = (tn(ov[...], gv[:, lanes(c, j)]) + sum_o[j].astype(F32)).astype(BF)
+    half = lambda ref: lambda h: ref.at[h]
+    o_block = lambda j, h: sum_o.at[j, pl.ds(256 * h, 256)]
+    q_block = lambda j, h: sum_q.at[j, pl.ds(2 * h, 2)]
+    o_sum = Sum(k, q, "y", o_block, half(ob2), half(ob3), (ob0.at[0], ob0.at[1]))
+    at = lambda zz, off, n: pl.ds(pl.multiple_of(FZ * zz + off, 128), n)
+    rows = pl.ds(pl.multiple_of(128 * c + 64 * xl, 64), 64)
+    pair = pl.ds(pl.multiple_of(128 * c, 128), 128)
+    f1 = pl.ds(0, FZ)
+    rest = SPLIT - FZ
+    quarter_rows = lambda h: pl.ds(pl.multiple_of(128 * c + 64 * xl + 32 * h, 32), 32)
+
+    def over_z(src, ref, off, n):
+        return Gather(
+            k, q, "z", lambda h: src.at[pl.ds(32 * h, 32)],
+            lambda j, h: ref.at[quarter_rows(h), at(j, off, n)],
+        )
+
+    spans = [(G1, 0, FZ), (G3, 0, rest), (G3, rest, FZ - rest)]
+    pieces = [pa.at[:, f1], pa.at[:, pl.ds(FZ, rest)], pb]
+    block = lambda i, j: spans[i][0].at[rows, at(j, spans[i][1], spans[i][2])]
+    rings, to_x, heres = [None] * 3, [], []
+
+    def across(i, j):
+        to_x.append(k.send(block(i, j), block(i, j), other))
+
+    def own_across(i):
+        to_x.append(k.send(pieces[i], block(i, z), other))
+        heres.append(k.local(pieces[i], block(i, z)))
+
+    def onward(i):
+        rings[i].near()
+        across(i, rings[i].below)
+        across(i, rings[i].above)
+
+    for cp in get_f:
+        cp.wait()
+    for cp in leg_b:
+        cp.wait_recv()
+    pb[...] = add4(fbv[...], lb[0], lb[1], lb[2])
+    rings[2] = over_z(pieces[2], *spans[2])
     near = k.send(dkv.at[xl, :, 1 - c], R.at[0], mate)
     n = k.n
     k.n += 2
@@ -740,68 +822,30 @@
     def _():
         pre.start()
 
-    leg_2 = []
-    for i, s in enumerate(steps):
-        r, cc = quarter((xx + s) % 4, 704)
-        leg_2.append(k.send(f2.at[r, cc], l2.at[i], xs[i]))
-    leg_a = [k.send(fa.at[(y + s) % 4], la.at[i], ys[i]) for i, s in enumerate(steps)]
-    leg_b = [k.send(fb.at[(xx + s) % 4], lb.at[i], xs[i]) for i, s in enumerate(steps)]
-    lanes = lambda cc, j: pl.ds(pl.multiple_of(1024 * cc + 256 * j, 256), 256)
-    get_o.wait()
-    get_g.wait()
-    swaps = []
-    for j in range(4):
-        mate_o[j] = tn(ov[...], gv[:, lanes(1 - c, j)]).astype(BF)
-        swaps.append(k.send(mate_o.at[j], sum_o.at[j], mate))
+    for cp in get_kv:
+        cp.wait()
+    rings[2].relay()
+    o_sum.relay(o_block((y + 1) % 4, 0), o_block((y + 3) % 4, 1), (ob1.at[0], ob1.at[1]))
 
     @pl.when(xl == 1)
     def _():
         R[3] = jnp.zeros(R.shape[1:], BF)
         pre.wait()
         for i in range(RING):
-            R[2, i] = (dkv[0, i, c].astype(F32) + R[1, i].astype(F32)).astype(BF)
+            R[2, i] = (kv_low[i].astype(F32) + R[1, i].astype(F32)).astype(BF)
         far.start()
 
-    for j in range(4):
-        swaps[j].wait_recv()
-        sum_o[j] = (tn(ov[...], gv[:, lanes(c, j)]) + sum_o[j].astype(F32)).astype(BF)
-    half = lambda ref: lambda h: ref.at[h]
-    o_block = lambda j, h: sum_o.at[j, pl.ds(256 * h, 256)]
-    q_block = lambda j, h: sum_q.at[j, pl.ds(2 * h, 2)]
-    o_sum = Sum(k, q, "y", o_block, half(ob2), half(ob3), (ob0.at[0], ob0.at[1]))
+    for cp in leg_a:
+        cp.wait_recv()
+    pa[...] = add4(fav[...], la[0], la[1], la[2])
+    rings[0] = over_z(pieces[0], *spans[0])
+    rings[1] = over_z(pieces[1], *spans[1])
     for cp in leg_2:
         cp.wait_recv()
-    r, cc = quarter(xx, 704)
-    p2[...] = add4(f2[r, cc], l2[0], l2[1], l2[2])
+    p2[...] = add4(f2v[...], l2[0], l2[1], l2[2])
     turned = turn(k, q, [(p2, t2)])
-    at = lambda zz, off, n: pl.ds(pl.multiple_of(FZ * zz + off, 128), n)
-    rows = pl.ds(pl.multiple_of(128 * c + 64 * xl, 64), 64)
-    pair = pl.ds(pl.multiple_of(128 * c, 128), 128)
-    f1 = pl.ds(0, FZ)
-    rest = SPLIT - FZ
-    quarter_rows = lambda h: pl.ds(pl.multiple_of(128 * c + 64 * xl + 32 * h, 32), 32)
-
-    def over_z(src, ref, off, n):
-        return Gather(
-            k, q, "z", lambda h: src.at[pl.ds(32 * h, 32)],
-            lambda j, h: ref.at[quarter_rows(h), at(j, off, n)],
-        )
-
-    spans = [(G1, 0, FZ), (G3, 0, rest), (G3, rest, FZ - rest)]
-    pieces = [pa.at[:, f1], pa.at[:, pl.ds(FZ, rest)], pb]
-    block = lambda i, j: spans[i][0].at[rows, at(j, spans[i][1], spans[i][2])]
-    for cp in leg_a:
-        cp.wait_recv()
-    pa[...] = add4(fa[y], la[0], la[1], la[2])
-    rings = [over_z(pieces[i], *spans[i]) for i in range(2)]
-    to_x = [k.send(pieces[i], block(i, z), other) for i in range(2)]
-    for cp in leg_b:
-        cp.wait_recv()
-    pb[...] = add4(fb[xx], lb[0], lb[1], lb[2])
-    rings.append(over_z(pieces[2], *spans[2]))
-    to_x.append(k.send(pieces[2], block(2, z), other))
-    heres = [k.local(pieces[i], block(i, z)) for i in range(3)]
-    o_sum.relay(o_block((y + 1) % 4, 0), o_block((y + 3) % 4, 1), (ob1.at[0], ob1.at[1]))
+    onward(2)
+    own_across(2)
 
     @pl.when(xl == 1)
     def _():
@@ -812,42 +856,28 @@
         far.wait_recv()
 
     near.wait_recv()
+    for cp in get_d:
+        cp.wait()
     for i in range(RING):
-        part = slice(TOK * i, TOK * i + TOK)
-        w = dkv[xl, i, c].astype(F32) + (R[0, i].astype(F32) + R[3, i].astype(F32))
+        w = kv_own[i].astype(F32) + (R[0, i].astype(F32) + R[3, i].astype(F32))
         lane = lax.broadcasted_iota(jnp.int32, w.shape, 1)
-        dm[part, :QZ] = dq[i]
-        dm[part, QZ:] = jnp.where(
-            lane < HEAD_DIM, w * cosine[i] - swapped(w) * sine[i], w
+        dm[i, :, QZ:] = jnp.where(
+            lane < HEAD_DIM, w * cv[i] - swapped(w) * sv[i], w
         ).astype(BF)
-    get_w.wait()
-    dn[...] = nt(dm[...], wv[...]).astype(BF).reshape(RING, TOK, D)
+    dmixed = dm[...].reshape(rows_all, MZ)
+    dn[...] = nt(dmixed, wv[...]).astype(BF).reshape(RING, TOK, D)
     z_sum = Sum(k, q, "z", ring_halves(dn), halves(below), halves(above), (p0, p1))
+    onward(0)
+    rings[1].relay()
     get_n.wait()
     cols = lambda cc: pl.ds(pl.multiple_of(1024 * cc, 1024), 1024)
     shape = (4, 4, 64, MZ)
-    mate_q[...] = tn(nv[:, cols(1 - c)], dm[...]).astype(BF).reshape(shape)
+    mate_q[...] = tn(nv[:, cols(1 - c)], dmixed).astype(BF).reshape(shape)
     swap = k.send(mate_q, sum_q, mate)
-
-    def onward(i):
-        rings[i].near()
-        for j in (rings[i].below, rings[i].above):
-            to_x.append(k.send(block(i, j), block(i, j), other))
-
-    rings[0].relay()
-    onward(0)
-    rings[1].relay()
-    onward(1)
+    own = tn(nv[:, cols(c)], dmixed).reshape(shape)
     swap.wait_recv()
-    own = tn(nv[:, cols(c)], dm[...]).reshape(shape)
     sum_q[...] = (own + sum_q[...].astype(F32)).astype(BF)
     q_sum = Sum(k, q, "y", q_block, half(qb2), half(qb3), (qb0.at[0], qb0.at[1]))
-    rings[2].relay()
-    turned()
-    col = pl.ds(pl.multiple_of(128 * (c * 8 + z * 2 + xl), 128), 128)
-    down_x = k.send(t2, G2.at[:, col], other)
-    down_here = k.local(t2, G2.at[:, col])
-    onward(2)
     o_sum.end()
     for h in range(2):
         part = o_block(y, h)[...].astype(F32) + (ob2[h].astype(F32) + ob3[h].astype(F32))
@@ -856,44 +886,50 @@
     for i, s in enumerate(steps):
         r, cc = quarter((xx + s) % 4, 256)
         leg_o.append(k.send(fo.at[r, cc], lo.at[i], xs[i]))
+    turned()
+    col = pl.ds(pl.multiple_of(128 * (c * 8 + z * 2 + xl), 128), 128)
+    down_x = k.send(t2, G2.at[:, col], other)
+    down_here = k.local(t2, G2.at[:, col])
+    z_sum.relay(dn.at[(z + 1) % 4, TOP], dn.at[(z + 3) % 4, LOW], (v0, v1))
     q_sum.relay(q_block((y + 1) % 4, 0), q_block((y + 3) % 4, 1), (qb1.at[0], qb1.at[1]))
-    z_sum.relay(dn.at[(z + 1) % 4, TOP], dn.at[(z + 3) % 4, LOW], (v0, v1))
+    onward(1)
+    for cp in leg_o:
+        cp.wait_recv()
+    r, cc = quarter(xx, 256)
+    po[...] = add4(fo[r, cc], lo[0], lo[1], lo[2])
+    o_turned = turn(k, q, [(po, to_)])
     q_sum.end()
     for h in range(2):
         part = q_block(y, h)[...].astype(F32) + (qb2[h].astype(F32) + qb3[h].astype(F32))
         fq[pl.ds(2 * h, 2)] = part.astype(BF)
     for i, s in enumerate(steps):
         leg_q.append(k.send(fq.at[(xx + s) % 4], lq.at[i], xs[i]))
-    rings[0].end()
-    to_x.append(k.send(block(0, rings[0].far), block(0, rings[0].far), other))
+    rings[1].end()
+    across(1, rings[1].far)
+    rings[0].relay()
+    z_sum.end()
+    for cp in get_x:
+        cp.wait()
+    back, gain1 = rms_back(
+        xv[...].astype(F32),
+        gain[...],
+        from_pieces(dn[z].astype(F32) + (below[...].astype(F32) + above[...].astype(F32))),
+    )
+    IG[...] = dv[...] + back
+    gains[...] = jnp.zeros_like(gains)
+    for d in range(8):
+        gains[d // 2, d % 2, 0:1] = gain1[:, 256 * d : 256 * d + 256]
+        gains[d // 2, d % 2, 1:2] = gain2[:, 256 * d : 256 * d + 256]
+    gain_y = [k.send(gains.at[(y + s) % 4], s0.at[y], ys[i]) for i, s in enumerate(steps)]
+    gain_here = k.local(gains.at[y], s0.at[y])
     down_x.wait_recv()
     down_here.wait()
     down_half = lambda j, h: G2.at[
         pl.ds(352 * h, 352), pl.ds(pl.multiple_of(128 * (c * 8 + j * 2), 256), 256)
     ]
     down_ring = Gather(k, q, "z", lambda h: down_half(z, h), down_half)
-    for i in (1, 2):
-        rings[i].end()
-        to_x.append(k.send(block(i, rings[i].far), block(i, rings[i].far), other))
-    z_sum.end()
-    back, gain1 = rms_back(
-        x[...].astype(F32),
-        gain[...],
-        from_pieces(dn[z].astype(F32) + (below[...].astype(F32) + above[...].astype(F32))),
-    )
-    IG[...] = dh[...] + back
-    gains[...] = jnp.zeros_like(gains)
-    for d in range(8):
-        gains[d // 2, d % 2, 0:1] = gain1[:, 256 * d : 256 * d + 256]
-        gains[d // 2, d % 2, 1:2] = gain2[:, 256 * d : 256 * d + 256]
-    gain_y = [k.send(gains.at[(y + s) % 4], s0.at[y], ys[i]) for i, s in enumerate(steps)]
-    gain_here = k.local(gains.at[y], s0.at[y])
-    for cp in leg_o:
-        cp.wait_recv()
-    r, cc = quarter(xx, 256)
-    po[...] = add4(fo[r, cc], lo[0], lo[1], lo[2])
-    o_turned = turn(k, q, [(po, to_)])
-    down_ring.relay()
+    own_across(0)
+    own_across(1)
     for cp in leg_q:
         cp.wait_recv()
     pq[...] = add4(fq[xx], lq[0], lq[1], lq[2])
@@ -905,6 +941,9 @@
     ]
     q_x = [k.send(src, dst, other) for src, dst in q_pieces]
     q_here = [k.local(src, dst) for src, dst in q_pieces]
+    o_turned()
+    o_x = k.send(to_, GO.at[:, col], other)
+    o_here = k.local(to_, GO.at[:, col])
     for cp in gain_y:
         cp.wait_recv()
     gain_here.wait()
@@ -913,14 +952,15 @@
     gain_x.wait_recv()
     s2[z] = s1[0, xh] + s1[1, 0]
     gain_z = [k.send(s2.at[z], s2.at[z], to) for to in zs]
-    o_turned()
-    o_x = k.send(to_, GO.at[:, col], other)
-    o_here = k.local(to_, GO.at[:, col])
-    for cp in to_x:
-        cp.wait_recv()
-    for cp in heres:
-        cp.wait()
-    last = [k.send(ref.at[pair], ref.at[pair], mate) for ref in (G1, G3)]
+    down_ring.relay()
+    rings[0].end()
+    across(0, rings[0].far)
+    o_x.wait_recv()
+    o_here.wait()
+    o_half = lambda j, h: GO.at[
+        pl.ds(128 * h, 128), pl.ds(pl.multiple_of(128 * (c * 8 + j * 2), 256), 256)
+    ]
+    o_ring = Gather(k, q, "z", lambda h: o_half(z, h), o_half)
     for cp in q_x:
         cp.wait_recv()
     for cp in q_here:
@@ -928,34 +968,37 @@
     half_rows = lambda h: pl.ds(pl.multiple_of(128 * c + 64 * h, 64), 64)
     q_half = lambda j, h: GQ.at[half_rows(h), qc(j)]
     kv_half = lambda j, h: GKV.at[half_rows(h), kc(j)]
-    last_rings = [
+    q_rings = [
         Gather(k, q, "z", lambda h: q_half(z, h), q_half),
         Gather(k, q, "z", lambda h: kv_half(z, h), kv_half),
     ]
+    rings[2].end()
+    across(2, rings[2].far)
     down_ring.near()
     down_ring.end()
-    last.append(k.send(G2.at[:, cols(c)], G2.at[:, cols(c)], mate))
-    o_x.wait_recv()
-    o_here.wait()
-    o_half = lambda j, h: GO.at[
-        pl.ds(128 * h, 128), pl.ds(pl.multiple_of(128 * (c * 8 + j * 2), 256), 256)
-    ]
-    last_rings.append(Gather(k, q, "z", lambda h: o_half(z, h), o_half))
+    last = [k.send(G2.at[:, cols(c)], G2.at[:, cols(c)], mate)]
+    for cp in to_x:
+        cp.wait_recv()
+    for cp in heres:
+        cp.wait()
+    last += [k.send(ref.at[pair], ref.at[pair], mate) for ref in (G1, G3)]
+    o_ring.relay()
     for cp in gain_z:
         cp.wait_recv()
     s3[0] = (s2[0] + s2[1]) + (s2[2] + s2[3])
     gain_x = k.send(s3.at[0], s3.at[1], other)
-    last_rings[0].relay()
-    last_rings[1].relay()
+    for one in q_rings:
+        one.relay()
+    o_ring.near()
+    o_ring.end()
+    last.append(k.send(GO.at[:, cols(c)], GO.at[:, cols(c)], mate))
     gain_x.wait_recv()
     s4[0] = s3[0] + s3[1]
     gain_c = k.send(s4.at[0], s4.at[1], mate)
-    last_rings[2].relay()
-    for r in last_rings:
-        r.near()
-        r.end()
-    refs = [GQ.at[pair], GKV.at[pair], GO.at[:, cols(c)]]
-    last += [k.send(ref, ref, mate) for ref in refs]
+    for one in q_rings:
+        one.near()
+        one.end()
+    last += [k.send(ref.at[pair], ref.at[pair], mate) for ref in (GQ, GKV)]
     gain_c.wait_recv()
     total[...] = s4[0] + s4[1]
     gain_done = k.local(total, gain_out)
@@ -1181,7 +1224,11 @@
     return scale * (inner - unit * jnp.mean(inner * unit, axis=-1, keepdims=True)), gain_grad
 
 
-def finish_kernel(a, b, g1, g3, g2, go, gq, gkv, out, grad, gate, up, down, proj, qkv):
+def finish_kernel(
+    a, b, g1, g3, g2, go, gq, gkv, gains, out, grad, gate, up, down, proj, qkv, gain1, gain2
+):
+    gain1[...] = gains[0]
+    gain2[...] = gains[1]
     out[...] = a[...]
     grad[...] = b[...]
     for src, dst in ((g1, gate), (g3, up), (g2, down), (go, proj)):
@@ -1201,16 +1248,17 @@
 def finish(*arrays):
     steps = 4
     spec = lambda v: pl.BlockSpec((v.shape[0] // steps, v.shape[1]), lambda i: (i, 0))
-    outs = [jax.ShapeDtypeStruct(v.shape, F32) for v in arrays[:-2]]
+    outs = [jax.ShapeDtypeStruct(v.shape, F32) for v in arrays[:-3]]
     outs.append(jax.ShapeDtypeStruct((256, QDIM + 2 * KVDIM), F32))
+    gain = jax.ShapeDtypeStruct((256,), F32)
     return pl.pallas_call(
         finish_kernel,
         name="finish",
         cost_estimate=cost(12),
         grid=(steps,),
-        in_specs=[spec(v) for v in arrays],
-        out_specs=[spec(v) for v in outs],
-        out_shape=outs,
+        in_specs=[spec(v) for v in arrays[:-1]] + [pl.BlockSpec((8, 256), lambda i: (0, 0))],
+        out_specs=[spec(v) for v in outs] + [pl.BlockSpec((256,), lambda i: (0,))] * 2,
+        out_shape=outs + [gain] * 2,
         compiler_params=PARAMS,
     )(*arrays)
 
@@ -1228,8 +1276,8 @@
     y, xx, xl, z, c = q["y"], q["x"], q["xl"], q["z"], q["c"]
     x = tokens[0]
     g = cotangent[0]
-    lane = jnp.arange(128)
-    freq = THETA ** (-(lane % 32).astype(F32) * 2.0 / HEAD_DIM)
+    freq = THETA ** (-(np.arange(128) % 32) * 2.0 / HEAD_DIM)
+    freq = jnp.asarray(freq[None], F32)
     table = ((RING, TOK, 128), F32)
     G, WQ, WO, W13, t2, n1, query, KV, cosine, sine, start, gain_attn, gain_ffn = talk(
         front_kernel,
@@ -1238,7 +1286,7 @@
         46,
         120,
         (
-            x, g, segments, norm_attn[None], norm_ffn[None], freq[None],
+            x, g, segments, norm_attn, norm_ffn, freq,
             wqkv, wo, w1, w3, w2,
         ),
         [
@@ -1360,7 +1408,7 @@
             pltpu.VMEM((RING * TOK, QZ), BF),
             pltpu.VMEM((RING * TOK, D), BF),
             pltpu.VMEM((4, RING, TOK, 128), BF),
-            pltpu.VMEM((RING * TOK, MZ), BF),
+            pltpu.VMEM((RING, TOK, MZ), BF),
             pltpu.VMEM((RING, TOK, D), BF),
             *[pltpu.VMEM(HALF, BF)] * 4,
             *[pltpu.VMEM((TOK, D), BF)] * 2,
@@ -1389,18 +1437,25 @@
             pltpu.VMEM((2,) + small, F32),
             pltpu.VMEM((2,) + small, F32),
             pltpu.VMEM(small, F32),
+            *[pltpu.VMEM((RING, TOK, 128), BF)] * 2,
+            *[pltpu.VMEM((RING, TOK, 128), F32)] * 2,
+            pltpu.VMEM((TOK, D), BF),
+            pltpu.VMEM((TOK, D), F32),
+            pltpu.VMEM((64, SPLIT), BF),
+            pltpu.VMEM((64, rest), BF),
+            pltpu.VMEM((704, 128), BF),
         ],
-        near=tuple(range(11)),
+        near=(6, 7),
         near_out=(0,),
     )
-    output, input_grad, gate_grad, up_grad, down_grad, out_grad, qkv_grad = finish(
-        output, input_grad, G1, G3, G2, GO, GQ, GKV
+    output, input_grad, gate_grad, up_grad, down_grad, out_grad, qkv_grad, gain1, gain2 = finish(
+        output, input_grad, G1, G3, G2, GO, GQ, GKV, gain_out
     )
     return (
         output[None],
         input_grad[None],
-        gain_out[0],
-        gain_out[1],
+        gain1,
+        gain2,
         qkv_grad,
         out_grad,
         gate_grad,

time: 298 us -> 296 us (level)
  local copies, waits for them, and re-layouts: 3.78 us -> 0 us
where the time goes in v7:
time: 296 us; the launch traced here: 290 us
  Pallas kernels  289 us (98%)
    pallas_call x3, Pallas kernels, talk(): pl.pallas_call(kernel, name=name, out_shape=[jax.ShapeDtypeStruct(s, t) f...  250 us
    pallas_call x1, Pallas kernels, attend_back(): pl.pallas_call(attend_back_kernel, name='attend_back', cost_estimate=cost...  14.4 us
    pallas_call x1, Pallas kernels, finish(): pl.pallas_call(finish_kernel, name='finish', cost_estimate=cost(12), grid...  12.7 us
    pallas_call x1, Pallas kernels, attend(): pl.pallas_call(attend_kernel, name='attend', cost_estimate=cost(12), grid...  11.9 us

profile of v7, /device:TPU:1, one launch (start us, length us, event | category | flops | bytes accessed | tf_op | source)
XLA Modules:
  0.0 290.1 jit_solution(5476011009638043373)
XLA Ops:
  0.6 46.1 %front.1 = (bf16[4,128,2048]{2,1,0:T(8,128)(2,1)}, bf16[2,4,2,2,64,640]{5,4,3,2,1,0:T(8,128)(2,1)}, bf16[2,256,2048]{2,1,0:T(8,128)(2,1)}, bf16[2,4,2,2,64,2816]...) custom-call(bf16[128,2048]{1,0:T(8,128)(2,1)} %bitcast.16, ...), custom_call_target="tpu_custom_call" | custom-call | flops 46000001024 | tf_op jit(solution)/shard_map/front/pallas_call | solution.py:281
  46.7 11.9 %attend.1 = (bf16[4,128,512]{2,1,0:T(8,128)(2,1)}, f32[4,1,1024]{2,1,0:T(1,128)}) custom-call(bf16[4,128,512]{2,1,0:T(8,128)(2,1)} %get-tuple-element.51.query, bf16[16,128,128]{2,1,0:T(8,128)(2,1)} %bitcast.29, s32[4,1,128]{2,1,0:T(1,128)} %get-tuple-element.53.start), custom_call_target="tpu_custom_call" | custom-call | flops 12000000000 | tf_op jit(solution)/shard_map/attend/pallas_call | solution.py:1130
  58.7 118.7 %core.1 = (bf16[4,128,2048]{2,1,0:T(8,128)(2,1)}, bf16[2,2,64,1536]{3,2,1,0:T(8,128)(2,1)}, bf16[2,2,64,1280]{3,2,1,0:T(8,128)(2,1)}, bf16[2,704,256]{2,1,0:T(8,...) custom-call(bf16[4,128,512]{2,1,0:T(8,128)(2,1)} %get-tuple-element.54.o.ou, ...), custom_call_target="tpu_custom_call" | custom-call | flops 120000004096 | tf_op jit(solution)/shard_map/core/pallas_call | solution.py:281
  177.4 14.4 %attend_back.1 = (bf16[4,128,512]{2,1,0:T(8,128)(2,1)}, bf16[16,128,128]{2,1,0:T(8,128)(2,1)}) custom-call(bf16[4,128,512]{2,1,0:T(8,128)(2,1)} %get-tuple-element.51.query, bf16[16,128,128]{2,1,0:T(8,128)(2,1)} %bitcast.30, s32[4,1,128]{2,1,0:T(1,128)} %get-tuple-element.53.start, bf16[4,128,512]{2,1,0:T(8,128)(2,1)} %get-tuple-element.54.o.out, ...), custom_call_target="tpu_custom_call" | custom-call | flops 15000000512 | tf_op jit(solution)/shard_map/attend_back/pallas_call | solution.py:1194
  191.9 85.0 %tail.1 = (f32[128,2048]{1,0:T(8,128)}, bf16[256,5632]{1,0:T(8,128)(2,1)}, bf16[256,5632]{1,0:T(8,128)(2,1)}, bf16[704,2048]{1,0:T(8,128)(2,1)}, bf16[256,2048]{...) custom-call(bf16[2,4,2,128,128]{4,3,2,1,0:T(8,128)(2,1)} %bitcast.31, ...), custom_call_target="tpu_custom_call" | custom-call | flops 74999996416 | tf_op jit(solution)/shard_map/tail/pallas_call | solution.py:281
  276.9 12.7 %finish.1 = (f32[128,2048]{1,0:T(8,128)}, f32[128,2048]{1,0:T(8,128)}, f32[256,5632]{1,0:T(8,128)}, f32[256,5632]{1,0:T(8,128)}, f32[704,2048]{1,0:T(8,128)}, /*...) custom-call(f32[128,2048]{1,0:T(8,128)} %get-tuple-element.60.a, ...), custom_call_target="tpu_custom_call" | custom-call | flops 12000000000 | tf_op jit(solution)/shard_map/finish/pallas_call | solution.py:1254

commit v8 on v7

--- a/solution.py
+++ b/solution.py
@@ -432,6 +432,10 @@
         r.near()
         r.end()
     q3 = k.send(WV.at[c], WV.at[c], mate)
+    w2_dealt()
+    t_half = lambda h: pl.ds(352 * h, 352)
+    t_y = Gather(k, q, "y", lambda h: TV.at[t_half(h)], lambda j, h: T2.at[j, t_half(h)])
+    done.append(k.local(TV, T2.at[y]))
     g_ring.relay()
     q3.wait_recv()
     done.append(k.local(WV, WQ))
@@ -466,12 +470,11 @@
         far.start()
 
     done += [k.local(KVV, KV.at[xl, :, c]), k.local(QV, Q)]
+    t_y.relay()
     o_y.near()
     o_y.end()
     part = WO.at[:, :, pl.ds(pl.multiple_of(1024 * c, 1024), 1024)]
     o3 = k.send(part, part, mate)
-    w2_dealt()
-    done.append(k.local(TV, T2))
 
     @pl.when(xl == 0)
     def _():
@@ -489,7 +492,7 @@
         cp.wait_recv()
     for cp in heres + done:
         cp.wait()
-    for r in (gate_x, g_ring):
+    for r in (gate_x, g_ring, t_y):
         r.near()
         r.end()
     k.close()
@@ -518,76 +521,106 @@
     get_wo, get_o = k.local(wo_in, wo), k.local(o, ov)
     loads = [k.local(x, xb), k.local(gate_at(w13, y), gate_at(W, y))]
     loads += [k.local(up_at(w13, j), up_at(W, j)) for j in (xx, lower, higher)]
+    cols = lambda j, n: pl.ds(pl.multiple_of(128 * (8 * c + j), 128 * n), 128 * n)
+    frows = lambda j, h: pl.ds(pl.multiple_of(704 * (j // 2) + 352 * h, 32), 352)
+    own_rows = pl.ds(pl.multiple_of(704 * xh, 64), 704)
+    get_t = [k.local(t2.at[j], W2.at[own_rows, cols(xl * 4 + j, 1)]) for j in range(4)]
     get_g = k.local(G, gv)
     greet(ys + xs + [up, down, mate])
-    cols = lambda j, n: pl.ds(pl.multiple_of(128 * (8 * c + j), 128 * n), 128 * n)
-    frows = lambda j, h: pl.ds(pl.multiple_of(704 * (j // 2) + 352 * h, 32), 352)
-    w2_here = k.local(t2, W2.at[pl.ds(pl.multiple_of(704 * xh, 64), 704), cols(xl * 4 + y, 1)])
-    w2y = Gather(
-        k, q, "y", lambda h: t2.at[pl.ds(352 * h, 352)],
-        lambda j, h: W2.at[frows(xx, h), cols(xl * 4 + j, 1)],
-    )
-    far = [
-        k.send(up_half(w13, lower, 0), up_half(W, lower, 0), xs[0]),
-        k.send(up_half(w13, higher, 1), up_half(W, higher, 1), xs[1]),
-    ]
-    sent = [k.send(up_at(w13, j), up_at(W, j), mate) for j in (xx, lower, higher)]
-    get_wo.wait()
-    get_o.wait()
-    rows = RING * TOK
-    part[...] = dot(ov[...].reshape(rows, QZ), wo[...]).astype(BF).reshape(RING, TOK, D)
-    z_sum = Sum(k, q, "z", ring_halves(part), halves(below), halves(above), (p0, p1))
-    w2y.relay()
     gate = Gather(
         k, q, "y", lambda h: gate_half(w13, y, h), lambda j, h: gate_half(W, j, h)
     )
-    sent.append(k.send(gate_at(w13, y), gate_at(W, y), mate))
-    w2_here.wait()
-    w2y.near()
-    w2y.end()
+    for cp in get_t:
+        cp.wait()
     down2 = lambda j: W2.at[
         pl.ds(pl.multiple_of(704 * (j // 2), 64), 704), cols((j % 2) * 4, 4)
     ]
     down_half = lambda j, h: W2.at[frows(j, h), cols((j % 2) * 4, 4)]
     down_ring = Gather(k, q, "x", lambda h: down_half(xx, h), down_half)
-    sent.append(k.send(down2(xx), down2(xx), mate))
-    z_sum.relay(part.at[(z + 1) % 4, TOP], part.at[(z + 3) % 4, LOW], (v0, v1))
-    z_sum.end()
+    sent_down = []
+    sent = [k.send(up_at(w13, j), up_at(W, j), mate) for j in (xx, lower, higher)]
+    sent.append(k.send(gate_at(w13, y), gate_at(W, y), mate))
+    sent_down.append(k.send(down2(xx), down2(xx), mate))
+    get_wo.wait()
+    get_o.wait()
+    rows = RING * TOK
+    part[...] = dot(ov[...].reshape(rows, QZ), wo[...]).astype(BF).reshape(RING, TOK, D)
+
+    def part_rows(i, h):
+        return pl.ds(64 * i + 32 * h, 32)
+
+    def sum_of(i):
+        at = pl.ds(32 * i, 32)
+        return Sum(
+            k, q, "z", lambda j, h: part.at[j, part_rows(i, h)],
+            lambda h: below.at[part_rows(i, h)], lambda h: above.at[part_rows(i, h)],
+            (p0.at[at], p1.at[at]),
+        )
+
+    def relay_of(one, i):
+        at = pl.ds(32 * i, 32)
+        one.relay(
+            part.at[(z + 1) % 4, part_rows(i, 0)], part.at[(z + 3) % 4, part_rows(i, 1)],
+            (v0.at[at], v1.at[at]),
+        )
+
+    def gather_of(ref, i):
+        return Gather(
+            k, q, "z", lambda h: ref.at[z, part_rows(i, h)], lambda j, h: ref.at[j, part_rows(i, h)]
+        )
+
+    def summed(at):
+        return part[z, at].astype(F32) + (below[at].astype(F32) + above[at].astype(F32))
+
+    z_low = sum_of(0)
+    relay_of(z_low, 0)
+    z_high = sum_of(1)
+    gate.relay()
+    down_ring.relay()
+    far = [
+        k.send(up_half(w13, lower, 0), up_half(W, lower, 0), xs[0]),
+        k.send(up_half(w13, higher, 1), up_half(W, higher, 1), xs[1]),
+    ]
+    relay_of(z_high, 1)
     for cp in loads:
         cp.wait()
-    total = xb[...].astype(F32) + (
-        part[z].astype(F32) + (below[...].astype(F32) + above[...].astype(F32))
-    )
-    hf[...] = total
-    scale = lax.rsqrt(jnp.mean(total * total, axis=-1, keepdims=True) + EPS)
-    N2[z] = to_pieces((total * scale * gain[...]).astype(BF))
-    n2_ring = Gather(k, q, "z", halves(N2.at[z]), ring_halves(N2))
-    gate.relay()
-    down_ring.relay()
-    for cp in far:
-        cp.wait_recv()
-    ref = up_at(W, (xx + 2) % 4)
-    sent.append(k.send(ref, ref, mate))
+    n2_rings = []
+    for i, one in enumerate((z_low, z_high)):
+        one.end()
+        at = slice(64 * i, 64 * i + 64)
+        total = xb[at].astype(F32) + summed(at)
+        hf[at] = total
+        scale = lax.rsqrt(jnp.mean(total * total, axis=-1, keepdims=True) + EPS)
+        N2[z, at] = to_pieces((total * scale * gain[...]).astype(BF))
+        n2_rings.append(gather_of(N2, i))
+    n2_rings[0].relay()
     gate.near()
     for j in (gate.below, gate.above):
         sent.append(k.send(gate_at(W, j), gate_at(W, j), mate))
     down_ring.near()
     for j in (down_ring.below, down_ring.above):
-        sent.append(k.send(down2(j), down2(j), mate))
-    n2_ring.relay()
+        sent_down.append(k.send(down2(j), down2(j), mate))
+    down_ring.end()
+    sent_down.append(k.send(down2(down_ring.far), down2(down_ring.far), mate))
+    n2_rings[1].relay()
     gate.end()
     sent.append(k.send(gate_at(W, gate.far), gate_at(W, gate.far), mate))
-    down_ring.end()
-    sent.append(k.send(down2(down_ring.far), down2(down_ring.far), mate))
+    for cp in far:
+        cp.wait_recv()
+    ref = up_at(W, (xx + 2) % 4)
+    sent.append(k.send(ref, ref, mate))
     get_g.wait()
-    for cp in sent:
+    for cp in sent_down:
         cp.wait_recv()
     tiles = [(256 * i, min(256 * i + 256, FZ)) for i in range(6)]
     gs = gv[...].reshape(rows, D)
     for a, b in tiles:
         bv[:, a:b] = nt(gs, W2[a:b]).astype(BF)
-    n2_ring.near()
-    n2_ring.end()
+    for cp in sent:
+        cp.wait_recv()
+    for one in n2_rings:
+        one.near()
+        one.end()
     k.close()
     n2 = N2[...].reshape(rows, D)
     for a, b in tiles:
@@ -646,20 +679,17 @@
             hT[...], gv[:, :, lanes(1 - c, j)].reshape(rows, 256)
         ).astype(BF)
         sent2.append(k.send(W2.at[:, lanes(1, j)], W2.at[:, lanes(0, j)], mate))
-
-    def back_half(j):
-        at = slice(1024 * j, 1024 * j + 1024)
-        dn = nt(bv[...], W[j].reshape(1024, 2 * FZ))
-        part[:, :, at] = dn.astype(BF).reshape(RING, TOK, 1024)
-
-    back_half(0)
     for j in range(4):
         sent2[j].wait_recv()
         at = slice(256 * j, 256 * j + 256)
         own = dot(hT[...], gv[:, :, lanes(c, j)].reshape(rows, 256))
         W2[:, at] = (own + W2[:, at].astype(F32)).astype(BF)
     start(0)
-    back_half(1)
+    out_sum.relay(outs.at[(z + 1) % 4, TOP], outs.at[(z + 3) % 4, LOW], (v2, v3))
+    for j in range(2):
+        at = slice(1024 * j, 1024 * j + 1024)
+        dn = nt(bv[...], W[j].reshape(1024, 2 * FZ))
+        part[:, :, at] = dn.astype(BF).reshape(RING, TOK, 1024)
     z_sum = Sum(k, q, "z", ring_halves(part), halves(below), halves(above), (p0, p1))
     pl.semaphore_signal(used.at[1], inc=1, device_id=mate, device_id_type=MESH)
     pl.semaphore_wait(used.at[1], 1)
@@ -667,17 +697,17 @@
     for j in range(4):
         W[1, j] = tn(N2[:, :, lanes(1 - c, j)].reshape(rows, 256), bv[...]).astype(BF).reshape(shape)
         sent13.append(k.send(W.at[1, j], W.at[0, j], mate))
-        if j == 1:
+        if j == 0:
             relay(0)
-    z_sum.relay(part.at[(z + 1) % 4, TOP], part.at[(z + 3) % 4, LOW], (v0, v1))
     for j in range(4):
         sent13[j].wait_recv()
         own = tn(N2[:, :, lanes(c, j)].reshape(rows, 256), bv[...]).reshape(shape)
         W[0, j] = (own + W[0, j].astype(F32)).astype(BF)
         if j == 1:
-            out_sum.relay(outs.at[(z + 1) % 4, TOP], outs.at[(z + 3) % 4, LOW], (v2, v3))
+            z_sum.relay(part.at[(z + 1) % 4, TOP], part.at[(z + 3) % 4, LOW], (v0, v1))
     start(1)
     start(2)
+    end(0)
     z_sum.end()
     dn = from_pieces(
         part[z].astype(F32) + (below[...].astype(F32) + above[...].astype(F32))
@@ -688,7 +718,6 @@
     GAIN[...] = gain_grad
     vv[z] = total.astype(BF)
     v_ring = Gather(k, q, "z", halves(vv.at[z]), ring_halves(vv))
-    end(0)
     out_sum.end()
     OUT[...] = hf[...] + (
         outs[z].astype(F32) + (out_below[...].astype(F32) + out_above[...].astype(F32))
@@ -1294,7 +1323,7 @@
             ((2, 4, 2, 2, 64, MZ), BF),
             ((2, 256, D), BF),
             ((2, 4, 2, 2, 64, 2 * FZ), BF),
-            ((704, 128), BF),
+            ((4, 704, 128), BF),
             ((RING, TOK, D), BF),
             ((RING, TOK, QZ), BF),
             ((2, 4, 2, TOK, 128), BF),

time: 296 us -> 293 us (0.990)
  Pallas kernels: 289 us -> 286 us
where the time goes in v8:
time: 293 us; the launch traced here: 287 us
  Pallas kernels  286 us (98%)
    pallas_call x3, Pallas kernels, talk(): pl.pallas_call(kernel, name=name, out_shape=[jax.ShapeDtypeStruct(s, t) f...  247 us
    pallas_call x1, Pallas kernels, attend_back(): pl.pallas_call(attend_back_kernel, name='attend_back', cost_estimate=cost...  14.5 us
    pallas_call x1, Pallas kernels, finish(): pl.pallas_call(finish_kernel, name='finish', cost_estimate=cost(12), grid...  12.6 us
    pallas_call x1, Pallas kernels, attend(): pl.pallas_call(attend_kernel, name='attend', cost_estimate=cost(12), grid...  11.9 us

profile of v8, /device:TPU:1, one launch (start us, length us, event | category | flops | bytes accessed | tf_op | source)
XLA Modules:
  0.0 287.1 jit_solution(12333280798867842016)
XLA Ops:
  0.6 47.6 %front.1 = (bf16[4,128,2048]{2,1,0:T(8,128)(2,1)}, bf16[2,4,2,2,64,640]{5,4,3,2,1,0:T(8,128)(2,1)}, bf16[2,256,2048]{2,1,0:T(8,128)(2,1)}, bf16[2,4,2,2,64,2816]...) custom-call(bf16[128,2048]{1,0:T(8,128)(2,1)} %bitcast.16, ...), custom_call_target="tpu_custom_call" | custom-call | flops 46000001024 | tf_op jit(solution)/shard_map/front/pallas_call | solution.py:281
  48.3 11.9 %attend.1 = (bf16[4,128,512]{2,1,0:T(8,128)(2,1)}, f32[4,1,1024]{2,1,0:T(1,128)}) custom-call(bf16[4,128,512]{2,1,0:T(8,128)(2,1)} %get-tuple-element.51.query, bf16[16,128,128]{2,1,0:T(8,128)(2,1)} %bitcast.29, s32[4,1,128]{2,1,0:T(1,128)} %get-tuple-element.53.start), custom_call_target="tpu_custom_call" | custom-call | flops 12000000000 | tf_op jit(solution)/shard_map/attend/pallas_call | solution.py:1159
  60.2 115.9 %core.1 = (bf16[4,128,2048]{2,1,0:T(8,128)(2,1)}, bf16[2,2,64,1536]{3,2,1,0:T(8,128)(2,1)}, bf16[2,2,64,1280]{3,2,1,0:T(8,128)(2,1)}, bf16[2,704,256]{2,1,0:T(8,...) custom-call(bf16[4,128,512]{2,1,0:T(8,128)(2,1)} %get-tuple-element.54.o.ou, ...), custom_call_target="tpu_custom_call" | custom-call | flops 120000004096 | tf_op jit(solution)/shard_map/core/pallas_call | solution.py:281
  176.2 14.5 %attend_back.1 = (bf16[4,128,512]{2,1,0:T(8,128)(2,1)}, bf16[16,128,128]{2,1,0:T(8,128)(2,1)}) custom-call(bf16[4,128,512]{2,1,0:T(8,128)(2,1)} %get-tuple-element.51.query, bf16[16,128,128]{2,1,0:T(8,128)(2,1)} %bitcast.30, s32[4,1,128]{2,1,0:T(1,128)} %get-tuple-element.53.start, bf16[4,128,512]{2,1,0:T(8,128)(2,1)} %get-tuple-element.54.o.out, ...), custom_call_target="tpu_custom_call" | custom-call | flops 15000000512 | tf_op jit(solution)/shard_map/attend_back/pallas_call | solution.py:1223
  190.6 83.3 %tail.1 = (f32[128,2048]{1,0:T(8,128)}, bf16[256,5632]{1,0:T(8,128)(2,1)}, bf16[256,5632]{1,0:T(8,128)(2,1)}, bf16[704,2048]{1,0:T(8,128)(2,1)}, bf16[256,2048]{...) custom-call(bf16[2,4,2,128,128]{4,3,2,1,0:T(8,128)(2,1)} %bitcast.31, ...), custom_call_target="tpu_custom_call" | custom-call | flops 74999996416 | tf_op jit(solution)/shard_map/tail/pallas_call | solution.py:281
  274.0 12.6 %finish.1 = (f32[128,2048]{1,0:T(8,128)}, f32[128,2048]{1,0:T(8,128)}, f32[256,5632]{1,0:T(8,128)}, f32[256,5632]{1,0:T(8,128)}, f32[704,2048]{1,0:T(8,128)}, /*...) custom-call(f32[128,2048]{1,0:T(8,128)} %get-tuple-element.60.a, ...), custom_call_target="tpu_custom_call" | custom-call | flops 12000000000 | tf_op jit(solution)/shard_map/finish/pallas_call | solution.py:1283

commit v9 on v7

--- a/solution.py
+++ b/solution.py
@@ -499,7 +499,7 @@
     o, x, gain, t2, w13, wo_in, G, V, FA, FB, F2, DO, OUT, DH, GAIN, *scratch
 ):
     (
-        W, W2, N2, gv, hv, hT, bv, part, outs, wo, ov, vv, hf, xb,
+        W, W2, N2, gv, hv, hT, bv, part, outs, wo, ov, vv, hf, xb, outf, dhf,
         p0, p1, p2, p3, v0, v1, v2, v3, below, above, out_below, out_above, *rest_of,
     ) = scratch
     bufs, (used, ss, rs) = rest_of[:-3], rest_of[-3:]
@@ -646,20 +646,17 @@
             hT[...], gv[:, :, lanes(1 - c, j)].reshape(rows, 256)
         ).astype(BF)
         sent2.append(k.send(W2.at[:, lanes(1, j)], W2.at[:, lanes(0, j)], mate))
-
-    def back_half(j):
-        at = slice(1024 * j, 1024 * j + 1024)
-        dn = nt(bv[...], W[j].reshape(1024, 2 * FZ))
-        part[:, :, at] = dn.astype(BF).reshape(RING, TOK, 1024)
-
-    back_half(0)
     for j in range(4):
         sent2[j].wait_recv()
         at = slice(256 * j, 256 * j + 256)
         own = dot(hT[...], gv[:, :, lanes(c, j)].reshape(rows, 256))
         W2[:, at] = (own + W2[:, at].astype(F32)).astype(BF)
     start(0)
-    back_half(1)
+    out_sum.relay(outs.at[(z + 1) % 4, TOP], outs.at[(z + 3) % 4, LOW], (v2, v3))
+    for j in range(2):
+        at = slice(1024 * j, 1024 * j + 1024)
+        dn = nt(bv[...], W[j].reshape(1024, 2 * FZ))
+        part[:, :, at] = dn.astype(BF).reshape(RING, TOK, 1024)
     z_sum = Sum(k, q, "z", ring_halves(part), halves(below), halves(above), (p0, p1))
     pl.semaphore_signal(used.at[1], inc=1, device_id=mate, device_id_type=MESH)
     pl.semaphore_wait(used.at[1], 1)
@@ -667,32 +664,33 @@
     for j in range(4):
         W[1, j] = tn(N2[:, :, lanes(1 - c, j)].reshape(rows, 256), bv[...]).astype(BF).reshape(shape)
         sent13.append(k.send(W.at[1, j], W.at[0, j], mate))
-        if j == 1:
+        if j == 0:
             relay(0)
-    z_sum.relay(part.at[(z + 1) % 4, TOP], part.at[(z + 3) % 4, LOW], (v0, v1))
     for j in range(4):
         sent13[j].wait_recv()
         own = tn(N2[:, :, lanes(c, j)].reshape(rows, 256), bv[...]).reshape(shape)
         W[0, j] = (own + W[0, j].astype(F32)).astype(BF)
         if j == 1:
-            out_sum.relay(outs.at[(z + 1) % 4, TOP], outs.at[(z + 3) % 4, LOW], (v2, v3))
+            z_sum.relay(part.at[(z + 1) % 4, TOP], part.at[(z + 3) % 4, LOW], (v0, v1))
     start(1)
     start(2)
+    end(0)
     z_sum.end()
     dn = from_pieces(
         part[z].astype(F32) + (below[...].astype(F32) + above[...].astype(F32))
     )
     back, gain_grad = rms_back(hf[...], gain[...], dn)
     total = gv[z].astype(F32) + back
-    DH[...] = total
+    dhf[...] = total
+    done.append(k.local(dhf, DH))
     GAIN[...] = gain_grad
     vv[z] = total.astype(BF)
     v_ring = Gather(k, q, "z", halves(vv.at[z]), ring_halves(vv))
-    end(0)
     out_sum.end()
-    OUT[...] = hf[...] + (
+    outf[...] = hf[...] + (
         outs[z].astype(F32) + (out_below[...].astype(F32) + out_above[...].astype(F32))
     )
+    done.append(k.local(outf, OUT))
     relay(1)
     relay(2)
     v_ring.relay()
@@ -722,7 +720,7 @@
         wv, nv, ov, gv, R, dm, dn, p0, p1, v0, v1, below, above, mate_o, sum_o, mate_q, sum_q,
         ob0, ob1, ob2, ob3, qb0, qb1, qb2, qb3, la, lb, l2, pa, pb, p2, t2, lo, lq, fo, fq,
         po, pq, to_, gains, s0, s1, s2, s3, s4, total,
-        kv_own, kv_low, cv, sv, xv, dv, fav, fbv, f2v, ss, rs,
+        kv_own, kv_low, cv, sv, xv, dv, fav, fbv, f2v, ig, ss, rs,
     ) = scratch
     q = coords()
     y, xx, xh, xl, z, c = q["y"], q["x"], q["xh"], q["xl"], q["z"], q["c"]
@@ -915,7 +913,8 @@
         gain[...],
         from_pieces(dn[z].astype(F32) + (below[...].astype(F32) + above[...].astype(F32))),
     )
-    IG[...] = dv[...] + back
+    ig[...] = dv[...] + back
+    ig_done = k.local(ig, IG)
     gains[...] = jnp.zeros_like(gains)
     for d in range(8):
         gains[d // 2, d % 2, 0:1] = gain1[:, 256 * d : 256 * d + 256]
@@ -1005,6 +1004,7 @@
     for cp in last:
         cp.wait_recv()
     gain_done.wait()
+    ig_done.wait()
     k.close()
 
 
@@ -1367,13 +1367,14 @@
             chunks,
             pltpu.VMEM((TOK, D), F32),
             pltpu.VMEM((TOK, D), BF),
+            *[pltpu.VMEM((TOK, D), F32)] * 2,
             *[pltpu.VMEM(HALF, BF)] * 8,
             *[pltpu.VMEM((TOK, D), BF)] * 4,
             *buffers,
             pltpu.SemaphoreType.REGULAR((2,)),
         ],
         near=(2,),
-        near_out=(4, 5, 6, 7),
+        near_out=(4, 7),
     )
     fa, fb = fa.reshape(4, 64, SPLIT), fb.reshape(4, 64, rest)
     f2 = f2.reshape(1408, 256)
@@ -1444,9 +1445,9 @@
             pltpu.VMEM((64, SPLIT), BF),
             pltpu.VMEM((64, rest), BF),
             pltpu.VMEM((704, 128), BF),
+            pltpu.VMEM((TOK, D), F32),
         ],
         near=(6, 7),
-        near_out=(0,),
     )
     output, input_grad, gate_grad, up_grad, down_grad, out_grad, qkv_grad, gain1, gain2 = finish(
         output, input_grad, G1, G3, G2, GO, GQ, GKV, gain_out

time: 296 us -> 290 us (0.980)
  Pallas kernels: 289 us -> 284 us
    pallas_call x3, Pallas kernels: 250 us -> 244 us  [talk(): pl.pallas_call(kernel, name=name, out_shape=[jax.ShapeDtypeStruct(s, t) f...]
where the time goes in v9:
time: 290 us; the launch traced here: 285 us
  Pallas kernels  284 us (98%)
    pallas_call x3, Pallas kernels, talk(): pl.pallas_call(kernel, name=name, out_shape=[jax.ShapeDtypeStruct(s, t) f...  244 us
    pallas_call x1, Pallas kernels, attend_back(): pl.pallas_call(attend_back_kernel, name='attend_back', cost_estimate=cost...  14.4 us
    pallas_call x1, Pallas kernels, finish(): pl.pallas_call(finish_kernel, name='finish', cost_estimate=cost(12), grid...  12.7 us
    pallas_call x1, Pallas kernels, attend(): pl.pallas_call(attend_kernel, name='attend', cost_estimate=cost(12), grid...  11.9 us

profile of v9, /device:TPU:1, one launch (start us, length us, event | category | flops | bytes accessed | tf_op | source)
XLA Modules:
  0.0 284.7 jit_solution(17111493986646483933)
XLA Ops:
  0.6 46.1 %front.1 = (bf16[4,128,2048]{2,1,0:T(8,128)(2,1)}, bf16[2,4,2,2,64,640]{5,4,3,2,1,0:T(8,128)(2,1)}, bf16[2,256,2048]{2,1,0:T(8,128)(2,1)}, bf16[2,4,2,2,64,2816]...) custom-call(bf16[128,2048]{1,0:T(8,128)(2,1)} %bitcast.16, ...), custom_call_target="tpu_custom_call" | custom-call | flops 46000001024 | tf_op jit(solution)/shard_map/front/pallas_call | solution.py:281
  46.7 11.9 %attend.1 = (bf16[4,128,512]{2,1,0:T(8,128)(2,1)}, f32[4,1,1024]{2,1,0:T(1,128)}) custom-call(bf16[4,128,512]{2,1,0:T(8,128)(2,1)} %get-tuple-element.51.query, bf16[16,128,128]{2,1,0:T(8,128)(2,1)} %bitcast.29, s32[4,1,128]{2,1,0:T(1,128)} %get-tuple-element.53.start), custom_call_target="tpu_custom_call" | custom-call | flops 12000000000 | tf_op jit(solution)/shard_map/attend/pallas_call | solution.py:1130
  58.7 114.7 %core.1 = (bf16[4,128,2048]{2,1,0:T(8,128)(2,1)}, bf16[2,2,64,1536]{3,2,1,0:T(8,128)(2,1)}, bf16[2,2,64,1280]{3,2,1,0:T(8,128)(2,1)}, bf16[2,704,256]{2,1,0:T(8,...) custom-call(bf16[4,128,512]{2,1,0:T(8,128)(2,1)} %get-tuple-element.54.o.ou, ...), custom_call_target="tpu_custom_call" | custom-call | flops 120000004096 | tf_op jit(solution)/shard_map/core/pallas_call | solution.py:281
  173.4 14.4 %attend_back.1 = (bf16[4,128,512]{2,1,0:T(8,128)(2,1)}, bf16[16,128,128]{2,1,0:T(8,128)(2,1)}) custom-call(bf16[4,128,512]{2,1,0:T(8,128)(2,1)} %get-tuple-element.51.query, bf16[16,128,128]{2,1,0:T(8,128)(2,1)} %bitcast.30, s32[4,1,128]{2,1,0:T(1,128)} %get-tuple-element.53.start, bf16[4,128,512]{2,1,0:T(8,128)(2,1)} %get-tuple-element.54.o.out, ...), custom_call_target="tpu_custom_call" | custom-call | flops 15000000512 | tf_op jit(solution)/shard_map/attend_back/pallas_call | solution.py:1194
  187.8 83.7 %tail.1 = (f32[128,2048]{1,0:T(8,128)}, bf16[256,5632]{1,0:T(8,128)(2,1)}, bf16[256,5632]{1,0:T(8,128)(2,1)}, bf16[704,2048]{1,0:T(8,128)(2,1)}, bf16[256,2048]{...) custom-call(bf16[2,4,2,128,128]{4,3,2,1,0:T(8,128)(2,1)} %bitcast.31, ...), custom_call_target="tpu_custom_call" | custom-call | flops 74999996416 | tf_op jit(solution)/shard_map/tail/pallas_call | solution.py:281
  271.6 12.7 %finish.1 = (f32[128,2048]{1,0:T(8,128)}, f32[128,2048]{1,0:T(8,128)}, f32[256,5632]{1,0:T(8,128)}, f32[256,5632]{1,0:T(8,128)}, f32[704,2048]{1,0:T(8,128)}, /*...) custom-call(f32[128,2048]{1,0:T(8,128)} %get-tuple-element.60.a, ...), custom_call_target="tpu_custom_call" | custom-call | flops 12000000000 | tf_op jit(solution)/shard_map/finish/pallas_call | solution.py:1254
